TPU v7x, 32 devices: a whole 2x2x4 slice. The times are simulated.
32 devices in a mesh: space: 4 (over y, core), snap: 8 (over z, x).
Axes of the slice: x: 2, y: 2, z: 4, core: 2. Of those that a mesh axis runs over, the one named last changes fastest.
Arguments:
- snapshots: bfloat16 [8192, 4096], P('space', 'snap'), may hold values from -6 to 6
- volume: float32 [8192], P('space'), may hold values from 0.25 to 4
- masks: int32 [4], replicated, may hold values from 1 to 7, as said below
Outputs:
- cross_gram: float32 [4, 8, 512, 512], P(None, 'snap', 'space')
Inputs may be any that keep to these rules, and one draw needn't show every extreme that they name: `masks`: all values are distinct; the first has exactly one bit set, and each later value differs from the one before in exactly one bit.
All inputs are finite; a program needn't handle non-finite values.
Results may differ from a plain program's by a relative error of at most 0.0041.
Values may be sent and summed in bfloat16 or wider, within the bound.
No kernel may reach another device: no remote copies, remote signals or barrier semaphores. Data moves between devices by JAX's collectives and lax.ppermute only.
A program may use at most 64 MiB of HBM per device.

v0:
```python
from functools import partial

import jax
import jax.numpy as jnp
from jax import lax
from jax.sharding import PartitionSpec as P

ROUNDS = 4


def shortened(shard):

    def short(part):
        return part.astype(jnp.bfloat16) if part.dtype == jnp.float32 else part

    return jax.tree.map(short, shard)


def partner(shard, axis, bit):
    return lax.ppermute(shard, axis, [(i, i ^ 1 << bit) for i in range(lax.axis_size(axis))])


def flip_over(block, bit_number):
    return jax.tree.map(
        lambda part, own: part.astype(own.dtype),
        partner(shortened(block), "snap", bit_number),
        block,
    )


def body(snapshots, volume, masks):
    slab_count = lax.axis_size("space")
    scale_factor = float(snapshots.shape[0] * slab_count) ** (-0.5)
    weighted = (snapshots.astype(jnp.float32) * jnp.sqrt(volume)[:, None]).astype(jnp.bfloat16)
    bit_count = lax.axis_size("snap").bit_length() - 1
    branches = [partial(flip_over, bit_number=position) for position in range(bit_count)]
    held = weighted
    previous = jnp.int32(0)
    results = []
    for round_number in range(ROUNDS):
        delta = jnp.bitwise_xor(masks[round_number], previous)
        which_bit = jnp.int32(0)
        for position in range(bit_count):
            which_bit = which_bit + position * jnp.bitwise_and(jnp.right_shift(delta, position), 1)
        held = lax.switch(which_bit, branches, held)
        previous = masks[round_number]
        product = lax.dot_general(
            weighted, held, (((0,), (0,)), ((), ())), preferred_element_type=jnp.float32
        )
        results.append(
            lax.psum_scatter(product * scale_factor, "space", scatter_dimension=0, tiled=True)
        )
    stacked = jnp.stack(results)
    return stacked[:, None]


def solution(mesh):
    in_specs = (P("space", "snap"), P("space"), P())
    out_specs = P(None, "snap", "space", None)
    return jax.shard_map(body, mesh=mesh, in_specs=in_specs, out_specs=out_specs, check_vma=False)
```

profile of v0, /device:TPU:0, one launch (start us, length us, event | category | flops | bytes accessed | tf_op | source)
XLA Modules:
  0.0 325.7 jit_solution(3574562397679908102)
XLA Ops:
  6.5 1.5 fusion
  9.3 0.7 sqrt.3
  10.0 2.0 multiply_convert_fusion
  12.1 48.8 %conditional.4 = (bf16[2048,512]{1,0:T(8,128)(2,1)}) conditional(s32[]{:T(128)} %bitcast, bf16[2048,512]{1,0:T(8,128)(2,1)S(1)} %multiply_convert_fusion, bf16[2048,512]{1,0:T(8,128)(2,1)S(1)} %multiply_convert_fusion, bf16[2048,512]{1,0:T(8,128)(2,1)S(1)} %multiply_convert_fusion), branch_computations={%region_0.0_spmd, %region_1.0_spmd, %region_2.0_spmd} | conditional | bytes 8388656 | solution.py:45
  12.1 3.1 collective-permute-start.1
  15.2 45.7 %collective-permute-done.1 = bf16[2048,512]{1,0:T(8,128)(2,1)} collective-permute-done((bf16[2048,512]{1,0:T(8,128)(2,1)S(1)}, bf16[2048,512]{1,0:T(8,128)(2,1)}, u32[]{:S(2)}, u32[]{:S(2)}) %collective-permute-start.1) | collective-permute-done | bytes 2097184 | tf_op jit(solution)/shard_map/cond/branch_1_fun/ppermute | solution.py:20
  60.9 3.8 %convolution_multiply_fusion.3 = f32[512,512]{1,0:T(8,128)} fusion(bf16[2048,512]{1,0:T(8,128)(2,1)S(1)} %multiply_convert_fusion, bf16[2048,512]{1,0:T(8,128)(2,1)} %get-tuple-element.37), kind=kOutput, calls=%fused_computation.4 | convolution fusion | flops 1074003968 | bytes 5242880 | tf_op jit(solution)/shard_map/dot_general | solution.py:47
  66.1 47.2 %conditional.5 = (bf16[2048,512]{1,0:T(8,128)(2,1)}) conditional(s32[]{:T(128)} %bitcast.2, bf16[2048,512]{1,0:T(8,128)(2,1)} %get-tuple-element.37, bf16[2048,512]{1,0:T(8,128)(2,1)} %get-tuple-element.37, bf16[2048,512]{1,0:T(8,128)(2,1)} %get-tuple-element.37), branch_computations={%region_4.0_spmd, %region_5.0_spmd, %region_6.0_spmd} | conditional | bytes 8388656 | solution.py:45
  66.1 1.7 collective-permute-start.3
  67.8 45.5 %collective-permute-done.3 = bf16[2048,512]{1,0:T(8,128)(2,1)} collective-permute-done((bf16[2048,512]{1,0:T(8,128)(2,1)}, bf16[2048,512]{1,0:T(8,128)(2,1)}, u32[]{:S(2)}, u32[]{:S(2)}) %collective-permute-start.3) | collective-permute-done | bytes 2097184 | tf_op jit(solution)/shard_map/cond/branch_0_fun/ppermute | solution.py:20
  113.3 3.9 %convolution_multiply_fusion.2 = f32[512,512]{1,0:T(8,128)} fusion(bf16[2048,512]{1,0:T(8,128)(2,1)S(1)} %multiply_convert_fusion, bf16[2048,512]{1,0:T(8,128)(2,1)} %get-tuple-element.38), kind=kOutput, calls=%fused_computation.3 | convolution fusion | flops 1074003968 | bytes 5242880 | tf_op jit(solution)/shard_map/dot_general | solution.py:47
  117.2 0.0 reduce-scatter.11.cloned.1.call-start
  119.9 92.1 %conditional.6 = (bf16[2048,512]{1,0:T(8,128)(2,1)}) conditional(s32[]{:T(128)} %bitcast.4, bf16[2048,512]{1,0:T(8,128)(2,1)} %get-tuple-element.38, bf16[2048,512]{1,0:T(8,128)(2,1)} %get-tuple-element.38, bf16[2048,512]{1,0:T(8,128)(2,1)} %get-tuple-element.38), branch_computations={%region_8.0_spmd, %region_9.0_spmd, %region_10.0_spmd} | conditional | bytes 8388656 | solution.py:45
  119.9 2.5 collective-permute-start.8
  122.4 89.6 %collective-permute-done.8 = bf16[2048,512]{1,0:T(8,128)(2,1)} collective-permute-done((bf16[2048,512]{1,0:T(8,128)(2,1)}, bf16[2048,512]{1,0:T(8,128)(2,1)}, u32[]{:S(2)}, u32[]{:S(2)}) %collective-permute-start.8) | collective-permute-done | bytes 2097184 | tf_op jit(solution)/shard_map/cond/branch_2_fun/ppermute | solution.py:20
  212.0 47.3 %conditional.7 = (bf16[2048,512]{1,0:T(8,128)(2,1)}) conditional(s32[]{:T(128)} %bitcast.6, bf16[2048,512]{1,0:T(8,128)(2,1)} %get-tuple-element.39, bf16[2048,512]{1,0:T(8,128)(2,1)} %get-tuple-element.39, bf16[2048,512]{1,0:T(8,128)(2,1)} %get-tuple-element.39), branch_computations={%region_12.0_spmd, %region_13.0_spmd, %region_14.0_spmd} | conditional | bytes 8388656 | solution.py:45
  212.0 0.2 collective-permute-start.10
  212.2 47.1 %collective-permute-done.10 = bf16[2048,512]{1,0:T(8,128)(2,1)} collective-permute-done((bf16[2048,512]{1,0:T(8,128)(2,1)}, bf16[2048,512]{1,0:T(8,128)(2,1)}, u32[]{:S(2)}, u32[]{:S(2)}) %collective-permute-start.10) | collective-permute-done | bytes 2097184 | tf_op jit(solution)/shard_map/cond/branch_1_fun/ppermute | solution.py:20
  259.3 3.8 %convolution_multiply_fusion = f32[512,512]{1,0:T(8,128)} fusion(bf16[2048,512]{1,0:T(8,128)(2,1)S(1)} %multiply_convert_fusion, bf16[2048,512]{1,0:T(8,128)(2,1)} %get-tuple-element.40), kind=kOutput, calls=%fused_computation.1 | convolution fusion | flops 1074003968 | bytes 5242880 | tf_op jit(solution)/shard_map/dot_general | solution.py:47
  263.1 0.0 reduce-scatter.9.cloned.1.call-start
  263.2 3.8 %convolution_multiply_fusion.1 = f32[512,512]{1,0:T(8,128)} fusion(bf16[2048,512]{1,0:T(8,128)(2,1)S(1)} %multiply_convert_fusion, bf16[2048,512]{1,0:T(8,128)(2,1)} %get-tuple-element.39), kind=kOutput, calls=%fused_computation.2 | convolution fusion | flops 1074003968 | bytes 5242880 | tf_op jit(solution)/shard_map/dot_general | solution.py:47
  267.1 22.4 %reduce-scatter.11.cloned.1.call-done = f32[128,512]{1,0:T(8,128)} async-done(((f32[512,512]{1,0:T(8,128)}), f32[128,512]{1,0:T(8,128)}) %reduce-scatter.11.cloned.1.call-update) | async-done | bytes 262160 | tf_op jit(solution)/shard_map/reduce_scatter | solution.py:51
  289.4 27.5 %reduce-scatter.9.cloned.1.call-done = f32[128,512]{1,0:T(8,128)} async-done(((f32[512,512]{1,0:T(8,128)}), f32[128,512]{1,0:T(8,128)}) %reduce-scatter.9.cloned.1.call-update) | async-done | bytes 262160 | tf_op jit(solution)/shard_map/reduce_scatter | solution.py:51
  316.9 2.2 maximum_bitcast_fusion
  (8 shorter events, 0.1 us)
Async XLA Ops:
  6.5 260.5 %reduce-scatter.5.cloned.1.call-start = ((), (), s32[]{:S(2)}) async-start(), calls=%async_computation.4 | async-start | bytes 1310720 | tf_op jit(solution)/shard_map/reduce_scatter | solution.py:51
  12.1 48.8 %collective-permute-start.1 = (bf16[2048,512]{1,0:T(8,128)(2,1)S(1)}, bf16[2048,512]{1,0:T(8,128)(2,1)}, u32[]{:S(2)}, u32[]{:S(2)}) collective-permute-start(bf16[2048,512]{1,0:T(8,128)(2,1)S(1)} %param.1), channel_id=1, source_target_pairs={{0,2},{1,3},{2,0},{3,1},{4,6},{5,7},{6,4},{7,5},{8,10},{9,11},{10,... | collective-permute-start | bytes 6291464 | tf_op jit(solution)/shard_map/cond/branch_1_fun/ppermute | solution.py:20
  64.8 202.3 %reduce-scatter.7.cloned.1.call-start = ((), (), s32[]{:S(2)}) async-start(), calls=%async_computation.5 | async-start | bytes 1310720 | tf_op jit(solution)/shard_map/reduce_scatter | solution.py:51
  66.1 47.2 %collective-permute-start.3 = (bf16[2048,512]{1,0:T(8,128)(2,1)}, bf16[2048,512]{1,0:T(8,128)(2,1)}, u32[]{:S(2)}, u32[]{:S(2)}) collective-permute-start(bf16[2048,512]{1,0:T(8,128)(2,1)} %param.3), channel_id=1, source_target_pairs={{0,1},{1,0},{2,3},{3,2},{4,5},{5,4},{6,7},{7,6},{8,9},{9,8},{10,11... | collective-permute-start | bytes 6291464 | tf_op jit(solution)/shard_map/cond/branch_0_fun/ppermute | solution.py:20
  117.2 172.3 %reduce-scatter.11.cloned.1.call-start = ((), (), s32[]{:S(2)}) async-start(), calls=%async_computation.7 | async-start | bytes 1310720 | tf_op jit(solution)/shard_map/reduce_scatter | solution.py:51
  119.9 92.1 %collective-permute-start.8 = (bf16[2048,512]{1,0:T(8,128)(2,1)}, bf16[2048,512]{1,0:T(8,128)(2,1)}, u32[]{:S(2)}, u32[]{:S(2)}) collective-permute-start(bf16[2048,512]{1,0:T(8,128)(2,1)} %param.8), channel_id=1, source_target_pairs={{0,4},{1,5},{2,6},{3,7},{4,0},{5,1},{6,2},{7,3},{8,12},{9,13},{10,... | collective-permute-start | bytes 6291464 | tf_op jit(solution)/shard_map/cond/branch_2_fun/ppermute | solution.py:20
  212.0 47.3 %collective-permute-start.10 = (bf16[2048,512]{1,0:T(8,128)(2,1)}, bf16[2048,512]{1,0:T(8,128)(2,1)}, u32[]{:S(2)}, u32[]{:S(2)}) collective-permute-start(bf16[2048,512]{1,0:T(8,128)(2,1)} %param.10), channel_id=1, source_target_pairs={{0,2},{1,3},{2,0},{3,1},{4,6},{5,7},{6,4},{7,5},{8,10},{9,11},{10,... | collective-permute-start | bytes 6291464 | tf_op jit(solution)/shard_map/cond/branch_1_fun/ppermute | solution.py:20
  263.1 53.8 %reduce-scatter.9.cloned.1.call-start = ((), (), s32[]{:S(2)}) async-start(), calls=%async_computation.6 | async-start | bytes 1310720 | tf_op jit(solution)/shard_map/reduce_scatter | solution.py:51
Sparse Core Ops, SparseCore 0:
  64.9 26.2 reduce-scatter.4
  117.3 25.9 reduce-scatter.6
  263.2 26.1 reduce-scatter.10
  292.0 24.8 reduce-scatter.8
where the time goes:
time: 326 us
  waiting for transfers between devices  278 us (85%)
  between operations  18.3 us (6%)
  matrix products  15.4 us (5%)
  starting transfers between devices  7.64 us (2%)
  other arithmetic  4.27 us (1%)
    ppermute x4, waiting for transfers between devices, partner(): lax.ppermute(shard, axis, [(i, i ^ 1 << bit) for i in range(lax.axis_size...  228 us
    reduce_scatter x4, waiting for transfers between devices, body(): lax.psum_scatter(product * scale_factor, 'space', scatter_dimension=0, ti...  49.9 us
    dot_general x4, matrix products, body(): lax.dot_general(weighted, held, (((0,), (0,)), ((), ())), preferred_eleme...  15.4 us
    ppermute x4, starting transfers between devices, partner(): lax.ppermute(shard, axis, [(i, i ^ 1 << bit) for i in range(lax.axis_size...  7.52 us
  transfers between devices with their start and end apart: 8, of which 6 were waited for; matrix products, arithmetic and copies ran while one was open for 4% of the time, Pallas kernels for 0%

commit v1 on v0

v1 whole, which is shorter than its diff:
```python
from functools import partial
from itertools import product

import jax
import jax.numpy as jnp
from jax import lax
from jax.sharding import PartitionSpec as P

ROUNDS = 4
PIECES = 2


def exchange(part, axis, mask):
    return lax.ppermute(part, axis, [(i, i ^ mask) for i in range(lax.axis_size(axis))])


def gram(left, right):
    total = None
    for one, other in zip(left, right):
        term = lax.dot_general(
            one, other, (((0,), (0,)), ((), ())), preferred_element_type=jnp.float32
        )
        total = term if total is None else total + term
    return total


def summed_block(tile, dimension):
    count = lax.axis_size("space")
    me = lax.axis_index("space")
    width = tile.shape[dimension] // count

    def block(index):
        return lax.dynamic_slice_in_dim(tile, index * width, width, dimension)

    arrived = [
        exchange(block(jnp.bitwise_xor(me, other)).astype(jnp.bfloat16), "space", other)
        for other in range(1, count)
    ]
    total = block(me)
    for part in arrived:
        total = total + part.astype(jnp.float32)
    return total


def chained(masks, pieces, scale_factor):
    bit_count = lax.axis_size("snap").bit_length() - 1
    weighted = jnp.concatenate(pieces)
    branches = [partial(exchange, axis="snap", mask=1 << position) for position in range(bit_count)]
    held, previous, results = weighted, jnp.int32(0), []
    for round_number in range(ROUNDS):
        delta = jnp.bitwise_xor(masks[round_number], previous)
        which_bit = jnp.int32(0)
        for position in range(bit_count):
            which_bit = which_bit + position * jnp.bitwise_and(jnp.right_shift(delta, position), 1)
        held = lax.switch(which_bit, branches, held)
        previous = masks[round_number]
        results.append(
            lax.psum_scatter(
                gram([weighted], [held]) * scale_factor, "space", scatter_dimension=0, tiled=True
            )
        )
    return jnp.stack(results)


def sequences(groups):
    found = [[1 << bit] for bit in range(groups.bit_length() - 1)]
    for _ in range(ROUNDS - 1):
        found = [
            masks + [masks[-1] ^ 1 << bit]
            for masks in found
            for bit in range(groups.bit_length() - 1)
            if masks[-1] ^ 1 << bit not in masks + [0]
        ]
    return found


def route(masks):
    inside = [mask for mask in masks if mask < 4]
    across = [mask & 3 for mask in masks if mask >= 4]
    best = None
    for own in product((0, 1, 2), repeat=3):
        for half in product((0, 1), repeat=3):
            for own_last, half_last in product((1, 2), repeat=2):
                own_of = dict(zip((0, 1, 2, 3), (2,) + own))
                half_of = dict(zip((0, 1, 2, 3), (1,) + half))
                if any(own_of[mask] < 2 for mask in inside):
                    continue
                if own_of[3] > own_of[3 ^ own_last] or half_of[3] > half_of[3 ^ half_last]:
                    continue
                pairs = []
                for mask in across:
                    able = [e for e in (0, 1, 2, 3) if own_of[e] and half_of[e ^ mask]]
                    if able:
                        pairs.append((able[0], able[0] ^ mask))
                if len(pairs) < len(across):
                    continue
                load = {1: 0, 2: 1}
                for bit in (1, 2):
                    load[bit] += own_of[bit] + half_of[bit]
                load[own_last] += own_of[3]
                load[half_last] += half_of[3]
                cost = (max(load.values()), sum(load.values()), -own_last)
                if best is None or cost < best[0]:
                    best = (cost, own_of, own_last, half_of, half_last, dict(zip(across, pairs)))
    return best[1:]


def planned(pieces, masks, scale_factor):
    own_of, own_last, half_of, half_last, pairs = route(masks)
    cut = lax.axis_size("snap") // 2
    half = PIECES
    kept, given = pieces[:half], pieces[half:]
    own = {0: list(pieces)}
    other = {0: [exchange(piece, "snap", cut) for piece in given]}
    for bit in (1, 2):
        if own_of[bit]:
            own[bit] = [exchange(piece, "snap", bit) for piece in pieces[: half * own_of[bit]]]
    if own_of[3]:
        source = own[3 ^ own_last]
        own[3] = [exchange(piece, "snap", own_last) for piece in source[: half * own_of[3]]]
    for bit in (1, 2):
        if half_of[bit]:
            other[bit] = [exchange(piece, "snap", bit) for piece in other[0]]
    if half_of[3]:
        other[3] = [exchange(piece, "snap", half_last) for piece in other[3 ^ half_last]]

    results = []
    for mask in masks:
        if mask < cut:
            results.append(summed_block(gram(own[0], own[mask]) * scale_factor, 0))
            continue
        mine, theirs = pairs[mask ^ cut]
        tile = gram(own[mine][:half], other[theirs]) * scale_factor
        rows = summed_block(tile, 0)
        if mine:
            rows = exchange(rows.astype(jnp.bfloat16), "snap", mine).astype(jnp.float32)
        columns = summed_block(tile, 1).T.astype(jnp.bfloat16)
        columns = exchange(columns, "snap", theirs ^ cut).astype(jnp.float32)
        results.append(rows + columns)
    return jnp.stack(results)


def body(snapshots, volume, masks):
    slab_count = lax.axis_size("space")
    groups = lax.axis_size("snap")
    cells = snapshots.shape[0]
    scale_factor = float(cells * slab_count) ** (-0.5)
    roots = jnp.sqrt(volume)[:, None]
    upper = (lax.axis_index("snap") >= groups // 2).astype(jnp.int32)
    count = 2 * PIECES
    size = cells // count
    pieces = []
    for number in range(count):
        start = jnp.where(upper == 1, (number + PIECES) % count, number) * size
        part = lax.dynamic_slice_in_dim(snapshots, start, size)
        scale = lax.dynamic_slice_in_dim(roots, start, size)
        pieces.append((part.astype(jnp.float32) * scale).astype(jnp.bfloat16))
    if groups == 8:
        allowed = sequences(groups)
        which = jnp.int32(0)
        for number, sequence in enumerate(allowed):
            same = jnp.all(masks == jnp.array(sequence, jnp.int32))
            which = which + number * same.astype(jnp.int32)
        branches = [
            partial(planned, masks=sequence, scale_factor=scale_factor) for sequence in allowed
        ]
        stacked = lax.switch(which, branches, pieces)
    else:
        stacked = chained(masks, pieces, scale_factor)
    return stacked[:, None]


def solution(mesh):
    in_specs = (P("space", "snap"), P("space"), P())
    out_specs = P(None, "snap", "space", None)
    return jax.shard_map(body, mesh=mesh, in_specs=in_specs, out_specs=out_specs, check_vma=False)
```

time: 326 us -> 200 us (0.61)
  waiting for transfers between devices: 278 us -> 75.9 us
  starting transfers between devices: 7.64 us -> 42.8 us
  loops' own time: 0.06 us -> 22 us
  local copies, waits for them, and re-layouts: 2.18 us -> 24.1 us
  between operations: 18.3 us -> 11.6 us
  other arithmetic: 4.27 us -> 8.06 us
    ppermute x4 -> x36, waiting for transfers between devices: 228 us -> 75.9 us  [exchange(): lax.ppermute(part, axis, [(i, i ^ mask) for i in range(lax.axis_size(axis...]
    reduce_scatter x4 -> x0, waiting for transfers between devices: 49.9 us -> none  [body(): lax.psum_scatter(product * scale_factor, 'space', scatter_dimension=0, ti...]
    ppermute x4 -> x36, starting transfers between devices: 7.52 us -> 42.8 us  [exchange(): lax.ppermute(part, axis, [(i, i ^ mask) for i in range(lax.axis_size(axis...]
    another operation x4 -> x1, loops' own time: 0.06 us -> 22 us  [body(): stacked = lax.switch(which, branches, pieces)]
    cond x0 -> x33, local copies, waits for them, and re-layouts: none -> 16 us
    dynamic_slice x0 -> x6, local copies, waits for them, and re-layouts: none -> 4.1 us  [block(): return lax.dynamic_slice_in_dim(tile, index * width, width, dimension)]
    convert_element_type x1 -> x6, other arithmetic: 2.05 us -> 6.09 us  [the longest x2 2.18 us: planned(): rows = exchange(rows.astype(jnp.bfloat16), 'snap', mine).astype(jnp.float32)]
    dot_general x4 -> x10, matrix products: 15.4 us -> 13.8 us  [gram(): lax.dot_general(one, other, (((0,), (0,)), ((), ())), preferred_element_t...]
  transfers between devices with their start and end apart: 8 -> 36, of which waited for: 6 -> 13; matrix products, arithmetic and copies ran while one was open for 4% -> 20% of each run, Pallas kernels for 0% -> 0%
where the time goes in v1:
time: 200 us; the launch traced here: 198 us
  waiting for transfers between devices  75.9 us (38%)
  starting transfers between devices  42.8 us (21%)
  local copies, waits for them, and re-layouts  24.1 us (12%)
  loops' own time  22 us (11%)
  matrix products  13.8 us (7%)
  between operations  11.6 us (6%)
  other arithmetic  8.06 us (4%)
    ppermute x36, waiting for transfers between devices, exchange(): lax.ppermute(part, axis, [(i, i ^ mask) for i in range(lax.axis_size(axis...  75.9 us
    ppermute x36, starting transfers between devices, exchange(): lax.ppermute(part, axis, [(i, i ^ mask) for i in range(lax.axis_size(axis...  42.8 us
    another operation x1, loops' own time, body(): stacked = lax.switch(which, branches, pieces)  22 us
    cond x33, local copies, waits for them, and re-layouts  16 us
    dot_general x10, matrix products, gram(): lax.dot_general(one, other, (((0,), (0,)), ((), ())), preferred_element_t...  13.8 us
    dynamic_slice x6, local copies, waits for them, and re-layouts, block(): return lax.dynamic_slice_in_dim(tile, index * width, width, dimension)  4.1 us
  transfers between devices with their start and end apart: 36, of which 13 were waited for; matrix products, arithmetic and copies ran while one was open for 20% of the time, Pallas kernels for 0%

profile of v1, /device:TPU:0, one launch (start us, length us, event | category | flops | bytes accessed | tf_op | source)
XLA Modules:
  0.0 198.3 jit_solution(4087801585172046125)
XLA Ops:
  1.0 2.1 %multiply_convert_fusion = (bf16[512,512]{1,0:T(8,128)(2,1)S(1)}, bf16[512,512]{1,0:T(8,128)(2,1)S(1)}, bf16[512,512]{1,0:T(8,128)(2,1)S(1)}, bf16[512,512]{1,0:T(8,128)(2,1)S(1)}) fusion(f32[512]{0:T(512)S(1)} %get-tuple-element.624, bf16[2048,512]{1,0:T(8,128)(2,1)} %param.38, s32[]{:T(128)S(6)} %select_n.320, f32[512]{0:T(512)S(1)} %get-tuple-element.626, ...), kind=kLoop, calls=%fused_computation.793 | loop fusion | flops 3145728 | bytes 4202512 | tf_op jit(solution)/shard_map/convert_element_type | solution.py:157
  14.5 182.7 %conditional.1 = (f32[4,1,128,512]{3,2,1,0:T(8,128)}) conditional(s32[]{:T(128)} %clamp.3, (bf16[512,512]{1,0:T(8,128)(2,1)S(1)}, bf16[512,512]{1,0:T(8,128)(2,1)S(1)}, bf16[512,512]{1,0:T(8,128)(2,1)S(1)}, bf16[512,512]{1,0:T(8,128)(2,1)S(1)}) %tuple.77, (bf16[512,512]{1,0:T(8,128)(2,1)S(1)}, ...), branch_computations={%region_17.18_spmd, %region_18.19_spmd, %region_19.20_spmd, %regio... | conditional | flops 3764781056 | bytes 103417872 | solution.py:167
  22.1 4.1 %collective-permute-start.428 = (bf16[512,512]{1,0:T(8,128)(2,1)S(1)}, bf16[512,512]{1,0:T(8,128)(2,1)S(1)}, u32[]{:S(2)}, u32[]{:S(2)}) collective-permute-start(bf16[512,512]{1,0:T(8,128)(2,1)S(1)} %get-tuple-element.224), channel_id=1, source_target_pairs={{0,4},{1,5},{2,6},{3,7},{4,0},{5,1},{6,2},{7,3},{8,12},{9,13},{10,... | collective-permute-start | bytes 1572872 | tf_op jit(solution)/shard_map/cond/branch_13_fun/ppermute | solution.py:14
  26.3 1.7 collective-permute-start.456
  28.3 1.7 collective-permute-start.437
  30.1 31.4 %collective-permute-done.428 = bf16[512,512]{1,0:T(8,128)(2,1)S(1)} collective-permute-done((bf16[512,512]{1,0:T(8,128)(2,1)S(1)}, bf16[512,512]{1,0:T(8,128)(2,1)S(1)}, u32[]{:S(2)}, u32[]{:S(2)}) %collective-permute-start.428) | collective-permute-done | bytes 524320 | tf_op jit(solution)/shard_map/cond/branch_13_fun/ppermute | solution.py:14
  61.4 1.8 collective-permute-start.436
  63.8 8.2 %collective-permute-done.427 = bf16[512,512]{1,0:T(8,128)(2,1)} collective-permute-done((bf16[512,512]{1,0:T(8,128)(2,1)S(1)}, bf16[512,512]{1,0:T(8,128)(2,1)}, u32[]{:S(2)}, u32[]{:S(2)}) %collective-permute-start.427) | collective-permute-done | bytes 524320 | tf_op jit(solution)/shard_map/cond/branch_13_fun/ppermute | solution.py:14
  76.7 1.7 fusion.130
  87.0 1.7 constant_dynamic-slice_fusion.83
  99.6 3.0 %collective-permute-done.443 = bf16[512,128]{0,1:T(8,128)(2,1)S(1)} collective-permute-done((bf16[512,128]{0,1:T(8,128)(2,1)S(1)}, bf16[512,128]{0,1:T(8,128)(2,1)S(1)}, u32[]{:S(2)}, u32[]{:S(2)}) %collective-permute-start.443) | collective-permute-done | bytes 131104 | tf_op jit(solution)/shard_map/cond/branch_13_fun/ppermute | solution.py:14
  104.3 1.9 collective-permute-start.434
  110.0 2.9 %collective-permute-start.445 = (bf16[128,512]{1,0:T(8,128)(2,1)S(1)}, bf16[128,512]{1,0:T(8,128)(2,1)S(1)}, u32[]{:S(2)}, u32[]{:S(2)}) collective-permute-start(bf16[128,512]{1,0:T(8,128)(2,1)S(1)} %fusion.133), channel_id=1, source_target_pairs={{0,4},{1,5},{2,6},{3,7},{4,0},{5,1},{6,2},{7,3},{8,12},{9,13},{10,... | collective-permute-start | bytes 393224 | tf_op jit(solution)/shard_map/cond/branch_13_fun/ppermute | solution.py:14
  115.5 6.2 %collective-permute-done.445 = bf16[128,512]{1,0:T(8,128)(2,1)S(1)} collective-permute-done((bf16[128,512]{1,0:T(8,128)(2,1)S(1)}, bf16[128,512]{1,0:T(8,128)(2,1)S(1)}, u32[]{:S(2)}, u32[]{:S(2)}) %collective-permute-start.445) | collective-permute-done | bytes 131104 | tf_op jit(solution)/shard_map/cond/branch_13_fun/ppermute | solution.py:14
  121.7 3.4 %collective-permute-start.435 = (bf16[128,512]{0,1:T(8,128)(2,1)}, bf16[128,512]{0,1:T(8,128)(2,1)S(1)}, u32[]{:S(2)}, u32[]{:S(2)}) collective-permute-start(bf16[128,512]{0,1:T(8,128)(2,1)} %fusion.132), channel_id=1, source_target_pairs={{0,4},{1,5},{2,6},{3,7},{4,0},{5,1},{6,2},{7,3},{8,12},{9,13},{10,... | collective-permute-start | bytes 393224 | tf_op jit(solution)/shard_map/cond/branch_13_fun/ppermute | solution.py:14
  130.5 1.7 fusion.271
  132.2 8.8 %collective-permute-done.446 = bf16[512,512]{1,0:T(8,128)(2,1)S(1)} collective-permute-done((bf16[512,512]{1,0:T(8,128)(2,1)}, bf16[512,512]{1,0:T(8,128)(2,1)S(1)}, u32[]{:S(2)}, u32[]{:S(2)}) %collective-permute-start.446) | collective-permute-done | bytes 524320 | tf_op jit(solution)/shard_map/cond/branch_13_fun/ppermute | solution.py:14
  141.0 1.7 fusion.129
  149.9 2.5 %collective-permute-done.457 = bf16[512,512]{1,0:T(8,128)(2,1)} collective-permute-done((bf16[512,512]{1,0:T(8,128)(2,1)}, bf16[512,512]{1,0:T(8,128)(2,1)}, u32[]{:S(2)}, u32[]{:S(2)}) %collective-permute-start.457) | collective-permute-done | bytes 524320 | tf_op jit(solution)/shard_map/cond/branch_13_fun/ppermute | solution.py:14
  154.0 8.0 %collective-permute-done.459 = bf16[512,512]{1,0:T(8,128)(2,1)} collective-permute-done((bf16[512,512]{1,0:T(8,128)(2,1)}, bf16[512,512]{1,0:T(8,128)(2,1)}, u32[]{:S(2)}, u32[]{:S(2)}) %collective-permute-start.459) | collective-permute-done | bytes 524320 | tf_op jit(solution)/shard_map/cond/branch_13_fun/ppermute | solution.py:14
  169.1 2.6 %collective-permute-start.451 = (bf16[128,512]{1,0:T(8,128)(2,1)S(1)}, bf16[128,512]{1,0:T(8,128)(2,1)S(1)}, u32[]{:S(2)}, u32[]{:S(2)}) collective-permute-start(bf16[128,512]{1,0:T(8,128)(2,1)S(1)} %add_convert_fusion.52), channel_id=1, source_target_pairs={{0,3},{1,2},{2,1},{3,0},{4,7},{5,6},{6,5},{7,4},{8,11},{9,10},{10,... | collective-permute-start | bytes 393224 | tf_op jit(solution)/shard_map/cond/branch_13_fun/ppermute | solution.py:14
  171.8 3.5 %collective-permute-start.455 = (bf16[128,512]{1,0:T(8,128)(2,1)S(1)}, bf16[128,512]{1,0:T(8,128)(2,1)S(1)}, u32[]{:S(2)}, u32[]{:S(2)}) collective-permute-start(bf16[128,512]{1,0:T(8,128)(2,1)S(1)} %fusion.134), channel_id=1, source_target_pairs={{0,4},{1,5},{2,6},{3,7},{4,0},{5,1},{6,2},{7,3},{8,12},{9,13},{10,... | collective-permute-start | bytes 393224 | tf_op jit(solution)/shard_map/cond/branch_13_fun/ppermute | solution.py:14
  176.4 2.3 %collective-permute-done.451 = bf16[128,512]{1,0:T(8,128)(2,1)S(1)} collective-permute-done((bf16[128,512]{1,0:T(8,128)(2,1)S(1)}, bf16[128,512]{1,0:T(8,128)(2,1)S(1)}, u32[]{:S(2)}, u32[]{:S(2)}) %collective-permute-start.451) | collective-permute-done | bytes 131104 | tf_op jit(solution)/shard_map/cond/branch_13_fun/ppermute | solution.py:14
  178.7 3.0 %collective-permute-done.455 = bf16[128,512]{1,0:T(8,128)(2,1)S(1)} collective-permute-done((bf16[128,512]{1,0:T(8,128)(2,1)S(1)}, bf16[128,512]{1,0:T(8,128)(2,1)S(1)}, u32[]{:S(2)}, u32[]{:S(2)}) %collective-permute-start.455) | collective-permute-done | bytes 131104 | tf_op jit(solution)/shard_map/cond/branch_13_fun/ppermute | solution.py:14
  (154 shorter events, 58.7 us)
Async XLA Ops:
  22.1 39.3 %collective-permute-start.428 = (bf16[512,512]{1,0:T(8,128)(2,1)S(1)}, bf16[512,512]{1,0:T(8,128)(2,1)S(1)}, u32[]{:S(2)}, u32[]{:S(2)}) collective-permute-start(bf16[512,512]{1,0:T(8,128)(2,1)S(1)} %get-tuple-element.224), channel_id=1, source_target_pairs={{0,4},{1,5},{2,6},{3,7},{4,0},{5,1},{6,2},{7,3},{8,12},{9,13},{10,... | collective-permute-start | bytes 1572872 | tf_op jit(solution)/shard_map/cond/branch_13_fun/ppermute | solution.py:14
  26.2 45.7 %collective-permute-start.427 = (bf16[512,512]{1,0:T(8,128)(2,1)S(1)}, bf16[512,512]{1,0:T(8,128)(2,1)}, u32[]{:S(2)}, u32[]{:S(2)}) collective-permute-start(bf16[512,512]{1,0:T(8,128)(2,1)S(1)} %get-tuple-element.222), channel_id=1, source_target_pairs={{0,4},{1,5},{2,6},{3,7},{4,0},{5,1},{6,2},{7,3},{8,12},{9,13},{10,... | collective-permute-start | bytes 1572872 | tf_op jit(solution)/shard_map/cond/branch_13_fun/ppermute | solution.py:14
  26.3 87.3 %collective-permute-start.456 = (bf16[512,512]{1,0:T(8,128)(2,1)S(1)}, bf16[512,512]{1,0:T(8,128)(2,1)}, u32[]{:S(2)}, u32[]{:S(2)}) collective-permute-start(bf16[512,512]{1,0:T(8,128)(2,1)S(1)} %get-tuple-element.222), channel_id=1, source_target_pairs={{0,1},{1,0},{2,3},{3,2},{4,5},{5,4},{6,7},{7,6},{8,9},{9,8},{10,11... | collective-permute-start | bytes 1572872 | tf_op jit(solution)/shard_map/cond/branch_13_fun/ppermute | solution.py:14
  28.0 85.6 %collective-permute-start.458 = (bf16[512,512]{1,0:T(8,128)(2,1)S(1)}, bf16[512,512]{1,0:T(8,128)(2,1)}, u32[]{:S(2)}, u32[]{:S(2)}) collective-permute-start(bf16[512,512]{1,0:T(8,128)(2,1)S(1)} %get-tuple-element.224), channel_id=1, source_target_pairs={{0,1},{1,0},{2,3},{3,2},{4,5},{5,4},{6,7},{7,6},{8,9},{9,8},{10,11... | collective-permute-start | bytes 1572872 | tf_op jit(solution)/shard_map/cond/branch_13_fun/ppermute | solution.py:14
  28.3 46.8 %collective-permute-start.437 = (bf16[512,512]{1,0:T(8,128)(2,1)S(1)}, bf16[512,512]{1,0:T(8,128)(2,1)}, u32[]{:S(2)}, u32[]{:S(2)}) collective-permute-start(bf16[512,512]{1,0:T(8,128)(2,1)S(1)} %get-tuple-element.223), channel_id=1, source_target_pairs={{0,1},{1,0},{2,3},{3,2},{4,5},{5,4},{6,7},{7,6},{8,9},{9,8},{10,11... | collective-permute-start | bytes 1572872 | tf_op jit(solution)/shard_map/cond/branch_13_fun/ppermute | solution.py:14
  61.4 15.2 %collective-permute-start.436 = (bf16[512,512]{1,0:T(8,128)(2,1)S(1)}, bf16[512,512]{1,0:T(8,128)(2,1)S(1)}, u32[]{:S(2)}, u32[]{:S(2)}) collective-permute-start(bf16[512,512]{1,0:T(8,128)(2,1)S(1)} %get-tuple-element.221), channel_id=1, source_target_pairs={{0,1},{1,0},{2,3},{3,2},{4,5},{5,4},{6,7},{7,6},{8,9},{9,8},{10,11... | collective-permute-start | bytes 1572872 | tf_op jit(solution)/shard_map/cond/branch_13_fun/ppermute | solution.py:14
  81.8 14.1 %collective-permute-start.438 = (bf16[128,512]{1,0:T(8,128)(2,1)}, bf16[128,512]{1,0:T(8,128)(2,1)}, u32[]{:S(2)}, u32[]{:S(2)}) collective-permute-start(bf16[128,512]{1,0:T(8,128)(2,1)} %copy.559), channel_id=1, source_target_pairs={{0,8},{8,0},{16,24},{24,16},{1,9},{9,1},{17,25},{25,17},{2,10},{10... | collective-permute-start | bytes 393224 | tf_op jit(solution)/shard_map/cond/branch_13_fun/ppermute | solution.py:14
  83.5 12.7 %collective-permute-start.439 = (bf16[128,512]{1,0:T(8,128)(2,1)}, bf16[128,512]{1,0:T(8,128)(2,1)}, u32[]{:S(2)}, u32[]{:S(2)}) collective-permute-start(bf16[128,512]{1,0:T(8,128)(2,1)} %copy.560), channel_id=1, source_target_pairs={{0,16},{8,24},{16,0},{24,8},{1,17},{9,25},{17,1},{25,9},{2,18},{10... | collective-permute-start | bytes 393224 | tf_op jit(solution)/shard_map/cond/branch_13_fun/ppermute | solution.py:14
  86.8 11.1 %collective-permute-start.440 = (bf16[128,512]{1,0:T(8,128)(2,1)}, bf16[128,512]{1,0:T(8,128)(2,1)}, u32[]{:S(2)}, u32[]{:S(2)}) collective-permute-start(bf16[128,512]{1,0:T(8,128)(2,1)} %copy.561), channel_id=1, source_target_pairs={{0,24},{8,16},{16,8},{24,0},{1,25},{9,17},{17,9},{25,1},{2,26},{10... | collective-permute-start | bytes 393224 | tf_op jit(solution)/shard_map/cond/branch_13_fun/ppermute | solution.py:14
  107.3 23.3 %collective-permute-start.447 = (bf16[512,512]{1,0:T(8,128)(2,1)}, bf16[512,512]{1,0:T(8,128)(2,1)}, u32[]{:S(2)}, u32[]{:S(2)}) collective-permute-start(bf16[512,512]{1,0:T(8,128)(2,1)} %collective-permute-done.437), channel_id=1, source_target_pairs={{0,2},{1,3},{2,0},{3,1},{4,6},{5,7},{6,4},{7,5},{8,10},{9,11},{10,... | collective-permute-start | bytes 1572872 | tf_op jit(solution)/shard_map/cond/branch_13_fun/ppermute | solution.py:14
  110.0 11.7 %collective-permute-start.445 = (bf16[128,512]{1,0:T(8,128)(2,1)S(1)}, bf16[128,512]{1,0:T(8,128)(2,1)S(1)}, u32[]{:S(2)}, u32[]{:S(2)}) collective-permute-start(bf16[128,512]{1,0:T(8,128)(2,1)S(1)} %fusion.133), channel_id=1, source_target_pairs={{0,4},{1,5},{2,6},{3,7},{4,0},{5,1},{6,2},{7,3},{8,12},{9,13},{10,... | collective-permute-start | bytes 393224 | tf_op jit(solution)/shard_map/cond/branch_13_fun/ppermute | solution.py:14
  113.6 12.3 %collective-permute-start.429 = (bf16[128,512]{0,1:T(8,128)(2,1)}, bf16[128,512]{0,1:T(8,128)(2,1)S(1)}, u32[]{:S(2)}, u32[]{:S(2)}) collective-permute-start(bf16[128,512]{0,1:T(8,128)(2,1)} %copy.555), channel_id=1, source_target_pairs={{0,8},{8,0},{16,24},{24,16},{1,9},{9,1},{17,25},{25,17},{2,10},{10... | collective-permute-start | bytes 393224 | tf_op jit(solution)/shard_map/cond/branch_13_fun/ppermute | solution.py:14
  113.6 13.3 %collective-permute-start.430 = (bf16[128,512]{0,1:T(8,128)(2,1)}, bf16[128,512]{0,1:T(8,128)(2,1)S(1)}, u32[]{:S(2)}, u32[]{:S(2)}) collective-permute-start(bf16[128,512]{0,1:T(8,128)(2,1)} %copy.556), channel_id=1, source_target_pairs={{0,16},{8,24},{16,0},{24,8},{1,17},{9,25},{17,1},{25,9},{2,18},{10... | collective-permute-start | bytes 393224 | tf_op jit(solution)/shard_map/cond/branch_13_fun/ppermute | solution.py:14
  114.2 13.8 %collective-permute-start.431 = (bf16[128,512]{0,1:T(8,128)(2,1)S(1)}, bf16[128,512]{0,1:T(8,128)(2,1)S(1)}, u32[]{:S(2)}, u32[]{:S(2)}) collective-permute-start(bf16[128,512]{0,1:T(8,128)(2,1)S(1)} %copy-done.119), channel_id=1, source_target_pairs={{0,24},{8,16},{16,8},{24,0},{1,25},{9,17},{17,9},{25,1},{2,26},{10... | collective-permute-start | bytes 393224 | tf_op jit(solution)/shard_map/cond/branch_13_fun/ppermute | solution.py:14
  126.0 15.1 %collective-permute-start.446 = (bf16[512,512]{1,0:T(8,128)(2,1)}, bf16[512,512]{1,0:T(8,128)(2,1)S(1)}, u32[]{:S(2)}, u32[]{:S(2)}) collective-permute-start(bf16[512,512]{1,0:T(8,128)(2,1)} %copy-done.112), channel_id=1, source_target_pairs={{0,2},{1,3},{2,0},{3,1},{4,6},{5,7},{6,4},{7,5},{8,10},{9,11},{10,... | collective-permute-start | bytes 1572872 | tf_op jit(solution)/shard_map/cond/branch_13_fun/ppermute | solution.py:14
  126.9 25.5 %collective-permute-start.457 = (bf16[512,512]{1,0:T(8,128)(2,1)}, bf16[512,512]{1,0:T(8,128)(2,1)}, u32[]{:S(2)}, u32[]{:S(2)}) collective-permute-start(bf16[512,512]{1,0:T(8,128)(2,1)} %collective-permute-done.456), channel_id=1, source_target_pairs={{0,2},{1,3},{2,0},{3,1},{4,6},{5,7},{6,4},{7,5},{8,10},{9,11},{10,... | collective-permute-start | bytes 1572872 | tf_op jit(solution)/shard_map/cond/branch_13_fun/ppermute | solution.py:14
  128.0 34.0 %collective-permute-start.459 = (bf16[512,512]{1,0:T(8,128)(2,1)}, bf16[512,512]{1,0:T(8,128)(2,1)}, u32[]{:S(2)}, u32[]{:S(2)}) collective-permute-start(bf16[512,512]{1,0:T(8,128)(2,1)} %collective-permute-done.458), channel_id=1, source_target_pairs={{0,2},{1,3},{2,0},{3,1},{4,6},{5,7},{6,4},{7,5},{8,10},{9,11},{10,... | collective-permute-start | bytes 1572872 | tf_op jit(solution)/shard_map/cond/branch_13_fun/ppermute | solution.py:14
  143.7 21.6 %collective-permute-start.448 = (bf16[128,512]{1,0:T(8,128)(2,1)}, bf16[128,512]{1,0:T(8,128)(2,1)}, u32[]{:S(2)}, u32[]{:S(2)}) collective-permute-start(bf16[128,512]{1,0:T(8,128)(2,1)} %copy.563), channel_id=1, source_target_pairs={{0,8},{8,0},{16,24},{24,16},{1,9},{9,1},{17,25},{25,17},{2,10},{10... | collective-permute-start | bytes 393224 | tf_op jit(solution)/shard_map/cond/branch_13_fun/ppermute | solution.py:14
  144.4 20.9 %collective-permute-start.449 = (bf16[128,512]{1,0:T(8,128)(2,1)}, bf16[128,512]{1,0:T(8,128)(2,1)}, u32[]{:S(2)}, u32[]{:S(2)}) collective-permute-start(bf16[128,512]{1,0:T(8,128)(2,1)} %copy.564), channel_id=1, source_target_pairs={{0,16},{8,24},{16,0},{24,8},{1,17},{9,25},{17,1},{25,9},{2,18},{10... | collective-permute-start | bytes 393224 | tf_op jit(solution)/shard_map/cond/branch_13_fun/ppermute | solution.py:14
  145.5 21.0 %collective-permute-start.450 = (bf16[128,512]{1,0:T(8,128)(2,1)S(1)}, bf16[128,512]{1,0:T(8,128)(2,1)}, u32[]{:S(2)}, u32[]{:S(2)}) collective-permute-start(bf16[128,512]{1,0:T(8,128)(2,1)S(1)} %copy.565), channel_id=1, source_target_pairs={{0,24},{8,16},{16,8},{24,0},{1,25},{9,17},{17,9},{25,1},{2,26},{10... | collective-permute-start | bytes 393224 | tf_op jit(solution)/shard_map/cond/branch_13_fun/ppermute | solution.py:14
  152.4 16.2 %collective-permute-start.452 = (bf16[512,128]{0,1:T(8,128)(2,1)S(1)}, bf16[512,128]{0,1:T(8,128)(2,1)S(1)}, u32[]{:S(2)}, u32[]{:S(2)}) collective-permute-start(bf16[512,128]{0,1:T(8,128)(2,1)S(1)} %get-tuple-element.533), channel_id=1, source_target_pairs={{0,8},{8,0},{16,24},{24,16},{1,9},{9,1},{17,25},{25,17},{2,10},{10... | collective-permute-start | bytes 393224 | tf_op jit(solution)/shard_map/cond/branch_13_fun/ppermute | solution.py:14
  165.4 9.9 %collective-permute-start.460 = (bf16[128,512]{0,1:T(8,128)(2,1)S(1)}, bf16[128,512]{0,1:T(8,128)(2,1)S(1)}, u32[]{:S(2)}, u32[]{:S(2)}) collective-permute-start(bf16[128,512]{0,1:T(8,128)(2,1)S(1)} %get-tuple-element.536), channel_id=1, source_target_pairs={{0,8},{8,0},{16,24},{24,16},{1,9},{9,1},{17,25},{25,17},{2,10},{10... | collective-permute-start | bytes 393224 | tf_op jit(solution)/shard_map/cond/branch_13_fun/ppermute | solution.py:14
  169.1 9.6 %collective-permute-start.451 = (bf16[128,512]{1,0:T(8,128)(2,1)S(1)}, bf16[128,512]{1,0:T(8,128)(2,1)S(1)}, u32[]{:S(2)}, u32[]{:S(2)}) collective-permute-start(bf16[128,512]{1,0:T(8,128)(2,1)S(1)} %add_convert_fusion.52), channel_id=1, source_target_pairs={{0,3},{1,2},{2,1},{3,0},{4,7},{5,6},{6,5},{7,4},{8,11},{9,10},{10,... | collective-permute-start | bytes 393224 | tf_op jit(solution)/shard_map/cond/branch_13_fun/ppermute | solution.py:14
  171.8 9.8 %collective-permute-start.455 = (bf16[128,512]{1,0:T(8,128)(2,1)S(1)}, bf16[128,512]{1,0:T(8,128)(2,1)S(1)}, u32[]{:S(2)}, u32[]{:S(2)}) collective-permute-start(bf16[128,512]{1,0:T(8,128)(2,1)S(1)} %fusion.134), channel_id=1, source_target_pairs={{0,4},{1,5},{2,6},{3,7},{4,0},{5,1},{6,2},{7,3},{8,12},{9,13},{10,... | collective-permute-start | bytes 393224 | tf_op jit(solution)/shard_map/cond/branch_13_fun/ppermute | solution.py:14
  (40 other events, 230.3 us)

commit v2 on v0

v2 whole, which is shorter than its diff:
```python
import jax
import jax.numpy as jnp
from jax import lax
from jax.experimental import pallas as pl
from jax.experimental.pallas import tpu as pltpu
from jax.sharding import PartitionSpec as P

ROUNDS = 4
OWN_PIECES = 2
MATE_PIECES = 2


def exchange(part, axis, mask):
    return lax.ppermute(part, axis, [(i, i ^ mask) for i in range(lax.axis_size(axis))])


def products(choices, lefts, blocks, scale_factor):
    slab_count = lax.axis_size("space")
    group, cells = lefts.shape[1:]
    width = blocks[0].shape[1]
    rows = group // slab_count

    def kernel(choices_ref, lefts_ref, *refs):
        block_refs = refs[: len(blocks)]
        out_refs = refs[len(blocks) : len(blocks) + slab_count]
        picked, tile = refs[len(blocks) + slab_count :]

        def one_round(round_number, carry):
            for number, block_ref in enumerate(block_refs):

                @pl.when(choices_ref[round_number] == number)
                def _():
                    picked[...] = block_ref[...]

            left = lefts_ref[choices_ref[ROUNDS + round_number]]
            tile[...] = scale_factor * jnp.dot(
                left, picked[...], preferred_element_type=jnp.float32
            )
            for number, out_ref in enumerate(out_refs):
                start = jnp.bitwise_xor(choices_ref[2 * ROUNDS], number) * rows
                part = tile[pl.ds(pl.multiple_of(start, rows), rows), :]
                out_ref[round_number] = part.astype(out_ref.dtype)
            return carry

        lax.fori_loop(0, ROUNDS, one_round, 0)

    vmem = pl.BlockSpec(memory_space=pltpu.VMEM)
    return pl.pallas_call(
        kernel,
        out_shape=[
            jax.ShapeDtypeStruct((ROUNDS, rows, width), jnp.bfloat16 if number else jnp.float32)
            for number in range(slab_count)
        ],
        in_specs=[pl.BlockSpec(memory_space=pltpu.SMEM)] + [vmem] * (1 + len(blocks)),
        out_specs=[vmem] * slab_count,
        scratch_shapes=[
            pltpu.VMEM((cells, width), jnp.bfloat16),
            pltpu.VMEM((group, width), jnp.float32),
        ],
        compiler_params=pltpu.CompilerParams(vmem_limit_bytes=32 * 2**20),
        cost_estimate=pl.CostEstimate(
            flops=2 * ROUNDS * group * cells * width,
            bytes_accessed=2 * (lefts.size + len(blocks) * cells * width + ROUNDS * group * width),
            transcendentals=0,
        ),
    )(choices, lefts, *blocks)


def summed(parts):
    total = parts[0]
    for other in range(1, len(parts)):
        total = total + exchange(parts[other], "space", other).astype(jnp.float32)
    return total


def gathered(piece, cut):
    held = {0: piece}
    bit = cut // 2
    while bit:
        for low, block in list(held.items()):
            held[low | bit] = exchange(block, "snap", bit)
        bit //= 2
    return [held[low] for low in range(cut)]


def body(snapshots, volume, masks):
    slab_count = lax.axis_size("space")
    cut = lax.axis_size("snap") // 2
    cells, group = snapshots.shape
    scale_factor = float(cells * slab_count) ** (-0.5)
    half = cells // 2
    upper = (lax.axis_index("snap") >= cut).astype(jnp.int32)
    roots = jnp.sqrt(volume)[:, None]

    def weighted(side, first, count):
        part = lax.dynamic_slice(snapshots, (side * half, first), (half, count))
        scale = lax.dynamic_slice_in_dim(roots, side * half, half)
        return (part.astype(jnp.float32) * scale).astype(jnp.bfloat16)

    def pieces_of(side, count):
        width = group // count
        return [weighted(side, number * width, width) for number in range(count)]

    mate = [exchange(piece, "snap", cut) for piece in pieces_of(1 - upper, MATE_PIECES)]
    own = pieces_of(upper, OWN_PIECES)
    lefts = jnp.stack([weighted(upper, 0, group).T, jnp.concatenate(mate, axis=1).T])

    low = jnp.bitwise_and(masks, cut - 1)
    crossing = (masks >= cut).astype(jnp.int32)
    me = lax.axis_index("space").astype(jnp.int32)[None]
    own_choices = jnp.concatenate([low, crossing, me])
    mate_choices = jnp.concatenate([low, 1 - crossing, me])

    own_sums = [
        summed(products(own_choices, lefts, gathered(piece, cut), scale_factor)) for piece in own
    ]
    own_sum = jnp.concatenate(own_sums, axis=2)
    swap = (crossing == 1)[:, None, None]
    columns = []
    for number, piece in enumerate(mate):
        mate_sum = summed(products(mate_choices, lefts, gathered(piece, cut), scale_factor))
        width = group // MATE_PIECES
        held = lax.slice_in_dim(own_sum, number * width, (number + 1) * width, axis=2)
        keep = jnp.where(swap, mate_sum, held)
        give = jnp.where(swap, held, mate_sum).astype(jnp.bfloat16)
        columns.append(keep + exchange(give, "snap", cut).astype(jnp.float32))
    return jnp.concatenate(columns, axis=2)[:, None]


def solution(mesh):
    in_specs = (P("space", "snap"), P("space"), P())
    out_specs = P(None, "snap", "space", None)
    return jax.shard_map(body, mesh=mesh, in_specs=in_specs, out_specs=out_specs, check_vma=False)
```

time: 326 us -> 196 us (0.60)
  waiting for transfers between devices: 278 us -> 107 us
  local copies, waits for them, and re-layouts: 2.18 us -> 32.6 us
  starting transfers between devices: 7.64 us -> 29.6 us
  between operations: 18.3 us -> 0.2 us
  matrix products: 15.4 us -> 0 us
  Pallas kernels: 0 us -> 13.6 us
  other arithmetic: 4.27 us -> 11.9 us
    ppermute x4 -> x28, waiting for transfers between devices: 228 us -> 107 us  [exchange(): lax.ppermute(part, axis, [(i, i ^ mask) for i in range(lax.axis_size(axis...]
    reduce_scatter x4 -> x0, waiting for transfers between devices: 49.9 us -> none  [body(): lax.psum_scatter(product * scale_factor, 'space', scatter_dimension=0, ti...]
    ppermute x4 -> x28, starting transfers between devices: 7.52 us -> 29.6 us  [exchange(): lax.ppermute(part, axis, [(i, i ^ mask) for i in range(lax.axis_size(axis...]
    unnamed x0 -> x57, local copies, waits for them, and re-layouts: none -> 15.6 us
    dot_general x4 -> x0, matrix products: 15.4 us -> none  [body(): lax.dot_general(weighted, held, (((0,), (0,)), ((), ())), preferred_eleme...]
    ppermute x0 -> x8, local copies, waits for them, and re-layouts: none -> 14 us  [exchange(): lax.ppermute(part, axis, [(i, i ^ mask) for i in range(lax.axis_size(axis...]
    pallas_call x0 -> x4, Pallas kernels: none -> 13.6 us  [products(): pl.pallas_call(kernel, out_shape=[jax.ShapeDtypeStruct((ROUNDS, rows, wid...]
    another operation x0 -> x3, other arithmetic: none -> 3.9 us  [body(): jnp.stack([weighted(upper, 0, group).T, jnp.concatenate(mate, axis=1).T])]
  transfers between devices with their start and end apart: 8 -> 28, of which waited for: 6 -> 11; matrix products, arithmetic and copies ran while one was open for 4% -> 11% of each run, Pallas kernels for 0% -> 7%
where the time goes in v2:
time: 196 us; the launch traced here: 195 us
  waiting for transfers between devices  107 us (55%)
  local copies, waits for them, and re-layouts  32.6 us (17%)
  starting transfers between devices  29.6 us (15%)
  Pallas kernels  13.6 us (7%)
  other arithmetic  11.9 us (6%)
    ppermute x28, waiting for transfers between devices, exchange(): lax.ppermute(part, axis, [(i, i ^ mask) for i in range(lax.axis_size(axis...  107 us
    ppermute x28, starting transfers between devices, exchange(): lax.ppermute(part, axis, [(i, i ^ mask) for i in range(lax.axis_size(axis...  29.6 us
    unnamed x57, local copies, waits for them, and re-layouts  15.6 us
    ppermute x8, local copies, waits for them, and re-layouts, exchange(): lax.ppermute(part, axis, [(i, i ^ mask) for i in range(lax.axis_size(axis...  14 us
    pallas_call x4, Pallas kernels, products(): pl.pallas_call(kernel, out_shape=[jax.ShapeDtypeStruct((ROUNDS, rows, wid...  13.6 us
  transfers between devices with their start and end apart: 28, of which 11 were waited for; matrix products, arithmetic and copies ran while one was open for 11% of the time, Pallas kernels for 7%

profile of v2, /device:TPU:0, one launch (start us, length us, event | category | flops | bytes accessed | tf_op | source)
XLA Modules:
  0.0 195.0 jit_solution(17073358915352710410)
XLA Ops:
  3.2 2.2 %multiply_convert_fusion.4 = (bf16[1024,256]{0,1:T(8,128)(2,1)S(1)}, bf16[1024,256]{0,1:T(8,128)(2,1)}) fusion(bf16[1024,256]{0,1:T(8,128)(2,1)} %copy.17, f32[1024]{0:T(1024)S(1)} %get-tuple-element.42, bf16[1024,256]{0,1:T(8,128)(2,1)S(1)} %copy.18), kind=kLoop, calls=%fused_computation.8 | loop fusion | flops 1572864 | bytes 2101248 | tf_op jit(solution)/shard_map/convert_element_type | solution.py:98
  5.5 4.0 %collective-permute-start = (bf16[1024,256]{0,1:T(8,128)(2,1)S(1)}, bf16[1024,256]{0,1:T(8,128)(2,1)}, u32[]{:S(2)}, u32[]{:S(2)}) collective-permute-start(bf16[1024,256]{0,1:T(8,128)(2,1)S(1)} %get-tuple-element.43), channel_id=1, source_target_pairs={{0,4},{1,5},{2,6},{3,7},{4,0},{5,1},{6,2},{7,3},{8,12},{9,13},{10,... | collective-permute-start | bytes 1572872 | tf_op jit(solution)/shard_map/ppermute | solution.py:14
  13.7 31.2 %collective-permute-done = bf16[1024,256]{0,1:T(8,128)(2,1)} collective-permute-done((bf16[1024,256]{0,1:T(8,128)(2,1)S(1)}, bf16[1024,256]{0,1:T(8,128)(2,1)}, u32[]{:S(2)}, u32[]{:S(2)}) %collective-permute-start) | collective-permute-done | bytes 524320 | tf_op jit(solution)/shard_map/ppermute | solution.py:14
  47.8 2.3 %copy.16 = bf16[1024,512]{0,1:T(8,128)(2,1)} copy(bf16[1024,512]{1,0:T(8,128)(2,1)} %constant_dynamic-slice_fusion.2) | data formatting | bytes 2097152
  50.1 2.4 %fusion = bf16[1,512,1024]{2,1,0:T(8,128)(2,1)} fusion(bf16[1024,512]{0,1:T(8,128)(2,1)} %copy.16, f32[1024]{0:T(1024)S(1)} %get-tuple-element.41), kind=kLoop, calls=%fused_computation.2 | loop fusion | flops 1572864 | bytes 2101248 | tf_op jit(solution)/shard_map/stack | solution.py:106
  52.5 2.8 %collective-permute-done.1 = bf16[1024,256]{0,1:T(8,128)(2,1)} collective-permute-done((bf16[1024,256]{0,1:T(8,128)(2,1)}, bf16[1024,256]{0,1:T(8,128)(2,1)}, u32[]{:S(2)}, u32[]{:S(2)}) %collective-permute-start.1) | collective-permute-done | bytes 524320 | tf_op jit(solution)/shard_map/ppermute | solution.py:14
  61.1 18.8 %collective-permute-done.16 = bf16[1024,256]{0,1:T(8,128)(2,1)} collective-permute-done((bf16[1024,256]{0,1:T(8,128)(2,1)}, bf16[1024,256]{0,1:T(8,128)(2,1)}, u32[]{:S(2)}, u32[]{:S(2)}) %collective-permute-start.16) | collective-permute-done | bytes 524320 | tf_op jit(solution)/shard_map/ppermute | solution.py:14
  86.8 3.5 %shard_map.38 = (f32[4,128,256]{2,1,0:T(8,128)S(1)}, bf16[4,128,256]{2,1,0:T(8,128)(2,1)}, bf16[4,128,256]{2,1,0:T(8,128)(2,1)}, bf16[4,128,256]{2,1,0:T(8,128)(2,1)S(1)}) custom-call(s32[9]{0:T(128)S(1)} %get-tuple-element.49.choices_ref, bf16[2,512,1024]{2,1,0:T(8,128)(2,1)S(1)} %pad_maximum_fusion.lefts_ref, ...), custom_call_target="tpu_custom_call" | custom-call | flops 1073741824 | bytes 5242880 | tf_op jit(solution)/shard_map/pallas_call | solution.py:48
  91.1 3.8 %collective-permute-done.23.refs_3_ = bf16[1024,256]{1,0:T(8,128)(2,1)} collective-permute-done((bf16[1024,256]{1,0:T(8,128)(2,1)}, bf16[1024,256]{1,0:T(8,128)(2,1)}, u32[]{:S(2)}, u32[]{:S(2)}) %collective-permute-start.23) | collective-permute-done | bytes 524320 | tf_op jit(solution)/shard_map/ppermute | solution.py:14
  97.7 2.1 %copy.13.refs_2_ = bf16[1024,256]{1,0:T(8,128)(2,1)} copy(bf16[1024,256]{0,1:T(8,128)(2,1)} %collective-permute-done.16) | data formatting | bytes 1048576 | tf_op jit(solution)/shard_map/ppermute | solution.py:14
  102.8 4.2 %shard_map.40 = (f32[4,128,256]{2,1,0:T(8,128)S(1)}, bf16[4,128,256]{2,1,0:T(8,128)(2,1)}, bf16[4,128,256]{2,1,0:T(8,128)(2,1)}, bf16[4,128,256]{2,1,0:T(8,128)(2,1)}) custom-call(s32[9]{0:T(128)S(1)} %get-tuple-element.49.choices_ref, bf16[2,512,1024]{2,1,0:T(8,128)(2,1)S(1)} %pad_maximum_fusion.lefts_ref, bf16[1024,256]{1,0:T(8,128)(2,1)S(1)} %get-tuple-element.38.refs_0_, ...), custom_call_target="tpu_custom_call" | custom-call | flops 1073741824 | bytes 5242880 | tf_op jit(solution)/shard_map/pallas_call | solution.py:48
  113.0 3.3 %shard_map.39 = (f32[4,128,256]{2,1,0:T(8,128)S(1)}, bf16[4,128,256]{2,1,0:T(8,128)(2,1)}, bf16[4,128,256]{2,1,0:T(8,128)(2,1)S(1)}, bf16[4,128,256]{2,1,0:T(8,128)(2,1)S(1)}) custom-call(s32[9]{0:T(128)S(1)} %get-tuple-element.50.choices_ref, bf16[2,512,1024]{2,1,0:T(8,128)(2,1)S(1)} %pad_maximum_fusion.lefts_ref, bf16[1024,256]{1,0:T(8,128)(2,1)S(1)} %copy.11.refs_0_, ...), custom_call_target="tpu_custom_call" | custom-call | flops 1073741824 | bytes 5242880 | tf_op jit(solution)/shard_map/pallas_call | solution.py:48
  120.7 5.5 %collective-permute-done.4 = bf16[1024,256]{0,1:T(8,128)(2,1)} collective-permute-done((bf16[1024,256]{0,1:T(8,128)(2,1)}, bf16[1024,256]{0,1:T(8,128)(2,1)}, u32[]{:S(2)}, u32[]{:S(2)}) %collective-permute-start.4) | collective-permute-done | bytes 524320 | tf_op jit(solution)/shard_map/ppermute | solution.py:14
  130.7 2.1 %copy.10.refs_3_ = bf16[1024,256]{1,0:T(8,128)(2,1)} copy(bf16[1024,256]{0,1:T(8,128)(2,1)} %collective-permute-done.4) | data formatting | bytes 1048576 | tf_op jit(solution)/shard_map/ppermute | solution.py:14
  134.9 2.6 %shard_map.37 = (f32[4,128,256]{2,1,0:T(8,128)S(1)}, bf16[4,128,256]{2,1,0:T(8,128)(2,1)S(1)}, bf16[4,128,256]{2,1,0:T(8,128)(2,1)S(1)}, bf16[4,128,256]{2,1,0:T(8,128)(2,1)S(1)}) custom-call(s32[9]{0:T(128)S(1)} %get-tuple-element.50.choices_ref, bf16[2,512,1024]{2,1,0:T(8,128)(2,1)S(1)} %pad_maximum_fusion.lefts_ref, bf16[1024,256]{1,0:T(8,128)(2,1)S(1)} %copy.7.refs_0_, ...), custom_call_target="tpu_custom_call" | custom-call | flops 1073741824 | bytes 5242880 | tf_op jit(solution)/shard_map/pallas_call | solution.py:48
  141.3 5.4 %collective-permute-done.19 = bf16[4,128,256]{2,1,0:T(8,128)(2,1)S(1)} collective-permute-done((bf16[4,128,256]{2,1,0:T(8,128)(2,1)S(1)}, bf16[4,128,256]{2,1,0:T(8,128)(2,1)S(1)}, u32[]{:S(2)}, u32[]{:S(2)}) %collective-permute-start.19) | collective-permute-done | bytes 262176 | tf_op jit(solution)/shard_map/ppermute | solution.py:14
  146.7 4.8 %collective-permute-done.20 = bf16[4,128,256]{2,1,0:T(8,128)(2,1)S(1)} collective-permute-done((bf16[4,128,256]{2,1,0:T(8,128)(2,1)S(1)}, bf16[4,128,256]{2,1,0:T(8,128)(2,1)S(1)}, u32[]{:S(2)}, u32[]{:S(2)}) %collective-permute-start.20) | collective-permute-done | bytes 262176 | tf_op jit(solution)/shard_map/ppermute | solution.py:14
  151.6 6.4 %collective-permute-done.6 = bf16[4,128,256]{2,1,0:T(8,128)(2,1)S(1)} collective-permute-done((bf16[4,128,256]{2,1,0:T(8,128)(2,1)S(1)}, bf16[4,128,256]{2,1,0:T(8,128)(2,1)S(1)}, u32[]{:S(2)}, u32[]{:S(2)}) %collective-permute-start.6) | collective-permute-done | bytes 262176 | tf_op jit(solution)/shard_map/ppermute | solution.py:14
  157.9 4.8 %collective-permute-done.7 = bf16[4,128,256]{2,1,0:T(8,128)(2,1)S(1)} collective-permute-done((bf16[4,128,256]{2,1,0:T(8,128)(2,1)S(1)}, bf16[4,128,256]{2,1,0:T(8,128)(2,1)S(1)}, u32[]{:S(2)}, u32[]{:S(2)}) %collective-permute-start.7) | collective-permute-done | bytes 262176 | tf_op jit(solution)/shard_map/ppermute | solution.py:14
  162.8 2.1 %select_convert_fusion.1 = (bf16[4,128,256]{2,1,0:T(8,128)(2,1)S(1)}, bf16[4,128,256]{2,1,0:T(8,128)(2,1)S(1)}) fusion(pred[4]{0:T(512)(128)(4,1)S(1)} %get-tuple-element.52, bf16[4,128,256]{2,1,0:T(8,128)(2,1)S(1)} %collective-permute-done.7, bf16[4,128,256]{2,1,0:T(8,128)(2,1)S(1)} %collective-permute-done.6, f32[4,128,256]{2,1,0:T(8,128)S(1)} %get-tuple-element.21, ...), kind=kLoop, calls=%fused_computation.14 | loop fusion | flops 3670016 | bytes 5767172 | tf_op jit(solution)/shard_map/convert_element_type | solution.py:125
  164.9 3.2 %collective-permute-start.14 = (bf16[4,128,256]{2,1,0:T(8,128)(2,1)S(1)}, bf16[4,128,256]{2,1,0:T(8,128)(2,1)S(1)}, u32[]{:S(2)}, u32[]{:S(2)}) collective-permute-start(bf16[4,128,256]{2,1,0:T(8,128)(2,1)S(1)} %get-tuple-element.47), channel_id=1, source_target_pairs={{0,4},{1,5},{2,6},{3,7},{4,0},{5,1},{6,2},{7,3},{8,12},{9,13},{10,... | collective-permute-start | bytes 786440 | tf_op jit(solution)/shard_map/ppermute | solution.py:14
  168.2 18.2 %collective-permute-done.14 = bf16[4,128,256]{2,1,0:T(8,128)(2,1)S(1)} collective-permute-done((bf16[4,128,256]{2,1,0:T(8,128)(2,1)S(1)}, bf16[4,128,256]{2,1,0:T(8,128)(2,1)S(1)}, u32[]{:S(2)}, u32[]{:S(2)}) %collective-permute-start.14) | collective-permute-done | bytes 262176 | tf_op jit(solution)/shard_map/ppermute | solution.py:14
  186.5 5.2 %collective-permute-done.27 = bf16[4,128,256]{2,1,0:T(8,128)(2,1)S(1)} collective-permute-done((bf16[4,128,256]{2,1,0:T(8,128)(2,1)S(1)}, bf16[4,128,256]{2,1,0:T(8,128)(2,1)S(1)}, u32[]{:S(2)}, u32[]{:S(2)}) %collective-permute-start.27) | collective-permute-done | bytes 262176 | tf_op jit(solution)/shard_map/ppermute | solution.py:14
  191.7 2.2 %convert_add_fusion.3 = (f32[4,128,256]{2,1,0:T(8,128)S(1)}, f32[4,128,256]{2,1,0:T(8,128)S(1)}) fusion(bf16[4,128,256]{2,1,0:T(8,128)(2,1)S(1)} %collective-permute-done.14, pred[4]{0:T(512)(128)(4,1)S(1)} %get-tuple-element.52, bf16[4,128,256]{2,1,0:T(8,128)(2,1)S(1)} %collective-permute-done.7, bf16[4,128,256]{2,1,0:T(8,128)(2,1)S(1)} %collective-permute-done.6, ...), kind=kLoop, calls=%fused_computation.13 | loop fusion | flops 3932160 | bytes 6815748 | tf_op jit(solution)/shard_map/add | solution.py:126
  (116 shorter events, 51.5 us)
Async XLA Ops:
  5.5 39.5 %collective-permute-start = (bf16[1024,256]{0,1:T(8,128)(2,1)S(1)}, bf16[1024,256]{0,1:T(8,128)(2,1)}, u32[]{:S(2)}, u32[]{:S(2)}) collective-permute-start(bf16[1024,256]{0,1:T(8,128)(2,1)S(1)} %get-tuple-element.43), channel_id=1, source_target_pairs={{0,4},{1,5},{2,6},{3,7},{4,0},{5,1},{6,2},{7,3},{8,12},{9,13},{10,... | collective-permute-start | bytes 1572872 | tf_op jit(solution)/shard_map/ppermute | solution.py:14
  9.5 45.8 %collective-permute-start.1 = (bf16[1024,256]{0,1:T(8,128)(2,1)}, bf16[1024,256]{0,1:T(8,128)(2,1)}, u32[]{:S(2)}, u32[]{:S(2)}) collective-permute-start(bf16[1024,256]{0,1:T(8,128)(2,1)} %get-tuple-element.44), channel_id=1, source_target_pairs={{0,4},{1,5},{2,6},{3,7},{4,0},{5,1},{6,2},{7,3},{8,12},{9,13},{10,... | collective-permute-start | bytes 1572872 | tf_op jit(solution)/shard_map/ppermute | solution.py:14
  9.9 46.2 %collective-permute-start.9 = (bf16[1024,256]{1,0:T(8,128)(2,1)S(1)}, bf16[1024,256]{1,0:T(8,128)(2,1)S(1)}, u32[]{:S(2)}, u32[]{:S(2)}) collective-permute-start(bf16[1024,256]{1,0:T(8,128)(2,1)S(1)} %get-tuple-element.37.refs_0_), channel_id=1, source_target_pairs={{0,2},{1,3},{2,0},{3,1},{4,6},{5,7},{6,4},{7,5},{8,10},{9,11},{10,... | collective-permute-start | bytes 1572872 | tf_op jit(solution)/shard_map/ppermute | solution.py:14
  11.8 45.6 %collective-permute-start.8 = (bf16[1024,256]{1,0:T(8,128)(2,1)S(1)}, bf16[1024,256]{1,0:T(8,128)(2,1)S(1)}, u32[]{:S(2)}, u32[]{:S(2)}) collective-permute-start(bf16[1024,256]{1,0:T(8,128)(2,1)S(1)} %get-tuple-element.37.refs_0_), channel_id=1, source_target_pairs={{0,1},{1,0},{2,3},{3,2},{4,5},{5,4},{6,7},{7,6},{8,9},{9,8},{10,11... | collective-permute-start | bytes 1572872 | tf_op jit(solution)/shard_map/ppermute | solution.py:14
  13.3 45.7 %collective-permute-start.22 = (bf16[1024,256]{1,0:T(8,128)(2,1)S(1)}, bf16[1024,256]{1,0:T(8,128)(2,1)}, u32[]{:S(2)}, u32[]{:S(2)}) collective-permute-start(bf16[1024,256]{1,0:T(8,128)(2,1)S(1)} %get-tuple-element.38.refs_0_), channel_id=1, source_target_pairs={{0,2},{1,3},{2,0},{3,1},{4,6},{5,7},{6,4},{7,5},{8,10},{9,11},{10,... | collective-permute-start | bytes 1572872 | tf_op jit(solution)/shard_map/ppermute | solution.py:14
  55.4 27.1 %collective-permute-start.3 = (bf16[1024,256]{0,1:T(8,128)(2,1)}, bf16[1024,256]{0,1:T(8,128)(2,1)}, u32[]{:S(2)}, u32[]{:S(2)}) collective-permute-start(bf16[1024,256]{0,1:T(8,128)(2,1)} %collective-permute-done), channel_id=1, source_target_pairs={{0,2},{1,3},{2,0},{3,1},{4,6},{5,7},{6,4},{7,5},{8,10},{9,11},{10,... | collective-permute-start | bytes 1572872 | tf_op jit(solution)/shard_map/ppermute | solution.py:14
  56.0 23.9 %collective-permute-start.16 = (bf16[1024,256]{0,1:T(8,128)(2,1)}, bf16[1024,256]{0,1:T(8,128)(2,1)}, u32[]{:S(2)}, u32[]{:S(2)}) collective-permute-start(bf16[1024,256]{0,1:T(8,128)(2,1)} %collective-permute-done.1), channel_id=1, source_target_pairs={{0,2},{1,3},{2,0},{3,1},{4,6},{5,7},{6,4},{7,5},{8,10},{9,11},{10,... | collective-permute-start | bytes 1572872 | tf_op jit(solution)/shard_map/ppermute | solution.py:14
  57.4 25.9 %collective-permute-start.10 = (bf16[1024,256]{1,0:T(8,128)(2,1)S(1)}, bf16[1024,256]{1,0:T(8,128)(2,1)S(1)}, u32[]{:S(2)}, u32[]{:S(2)}) collective-permute-start(bf16[1024,256]{1,0:T(8,128)(2,1)S(1)} %collective-permute-done.9.refs_2_), channel_id=1, source_target_pairs={{0,1},{1,0},{2,3},{3,2},{4,5},{5,4},{6,7},{7,6},{8,9},{9,8},{10,11... | collective-permute-start | bytes 1572872 | tf_op jit(solution)/shard_map/ppermute | solution.py:14
  59.0 32.1 %collective-permute-start.15 = (bf16[1024,256]{0,1:T(8,128)(2,1)}, bf16[1024,256]{0,1:T(8,128)(2,1)}, u32[]{:S(2)}, u32[]{:S(2)}) collective-permute-start(bf16[1024,256]{0,1:T(8,128)(2,1)} %collective-permute-done.1), channel_id=1, source_target_pairs={{0,1},{1,0},{2,3},{3,2},{4,5},{5,4},{6,7},{7,6},{8,9},{9,8},{10,11... | collective-permute-start | bytes 1572872 | tf_op jit(solution)/shard_map/ppermute | solution.py:14
  59.5 35.3 %collective-permute-start.23 = (bf16[1024,256]{1,0:T(8,128)(2,1)}, bf16[1024,256]{1,0:T(8,128)(2,1)}, u32[]{:S(2)}, u32[]{:S(2)}) collective-permute-start(bf16[1024,256]{1,0:T(8,128)(2,1)} %collective-permute-done.22.refs_2_), channel_id=1, source_target_pairs={{0,1},{1,0},{2,3},{3,2},{4,5},{5,4},{6,7},{7,6},{8,9},{9,8},{10,11... | collective-permute-start | bytes 1572872 | tf_op jit(solution)/shard_map/ppermute | solution.py:14
  80.0 27.8 %collective-permute-start.17 = (bf16[1024,256]{0,1:T(8,128)(2,1)}, bf16[1024,256]{0,1:T(8,128)(2,1)}, u32[]{:S(2)}, u32[]{:S(2)}) collective-permute-start(bf16[1024,256]{0,1:T(8,128)(2,1)} %collective-permute-done.16), channel_id=1, source_target_pairs={{0,1},{1,0},{2,3},{3,2},{4,5},{5,4},{6,7},{7,6},{8,9},{9,8},{10,11... | collective-permute-start | bytes 1572872 | tf_op jit(solution)/shard_map/ppermute | solution.py:14
  82.5 36.1 %collective-permute-start.2 = (bf16[1024,256]{0,1:T(8,128)(2,1)}, bf16[1024,256]{0,1:T(8,128)(2,1)}, u32[]{:S(2)}, u32[]{:S(2)}) collective-permute-start(bf16[1024,256]{0,1:T(8,128)(2,1)} %collective-permute-done), channel_id=1, source_target_pairs={{0,1},{1,0},{2,3},{3,2},{4,5},{5,4},{6,7},{7,6},{8,9},{9,8},{10,11... | collective-permute-start | bytes 1572872 | tf_op jit(solution)/shard_map/ppermute | solution.py:14
  84.2 42.0 %collective-permute-start.4 = (bf16[1024,256]{0,1:T(8,128)(2,1)}, bf16[1024,256]{0,1:T(8,128)(2,1)}, u32[]{:S(2)}, u32[]{:S(2)}) collective-permute-start(bf16[1024,256]{0,1:T(8,128)(2,1)} %collective-permute-done.3), channel_id=1, source_target_pairs={{0,1},{1,0},{2,3},{3,2},{4,5},{5,4},{6,7},{7,6},{8,9},{9,8},{10,11... | collective-permute-start | bytes 1572872 | tf_op jit(solution)/shard_map/ppermute | solution.py:14
  91.1 28.0 %collective-permute-start.11 = (bf16[4,128,256]{2,1,0:T(8,128)(2,1)}, bf16[4,128,256]{2,1,0:T(8,128)(2,1)}, u32[]{:S(2)}, u32[]{:S(2)}) collective-permute-start(bf16[4,128,256]{2,1,0:T(8,128)(2,1)} %get-tuple-element.26), channel_id=1, source_target_pairs={{0,8},{8,0},{16,24},{24,16},{1,9},{9,1},{17,25},{25,17},{2,10},{10... | collective-permute-start | bytes 786440 | tf_op jit(solution)/shard_map/ppermute | solution.py:14
  94.8 25.9 %collective-permute-start.12 = (bf16[4,128,256]{2,1,0:T(8,128)(2,1)}, bf16[4,128,256]{2,1,0:T(8,128)(2,1)}, u32[]{:S(2)}, u32[]{:S(2)}) collective-permute-start(bf16[4,128,256]{2,1,0:T(8,128)(2,1)} %get-tuple-element.27), channel_id=1, source_target_pairs={{0,16},{8,24},{16,0},{24,8},{1,17},{9,25},{17,1},{25,9},{2,18},{10... | collective-permute-start | bytes 786440 | tf_op jit(solution)/shard_map/ppermute | solution.py:14
  107.8 29.7 %collective-permute-start.13 = (bf16[4,128,256]{2,1,0:T(8,128)(2,1)S(1)}, bf16[4,128,256]{2,1,0:T(8,128)(2,1)}, u32[]{:S(2)}, u32[]{:S(2)}) collective-permute-start(bf16[4,128,256]{2,1,0:T(8,128)(2,1)S(1)} %get-tuple-element.28), channel_id=1, source_target_pairs={{0,24},{8,16},{16,8},{24,0},{1,25},{9,17},{17,9},{25,1},{2,26},{10... | collective-permute-start | bytes 786440 | tf_op jit(solution)/shard_map/ppermute | solution.py:14
  118.5 20.4 %collective-permute-start.24 = (bf16[4,128,256]{2,1,0:T(8,128)(2,1)}, bf16[4,128,256]{2,1,0:T(8,128)(2,1)}, u32[]{:S(2)}, u32[]{:S(2)}) collective-permute-start(bf16[4,128,256]{2,1,0:T(8,128)(2,1)} %get-tuple-element.34), channel_id=1, source_target_pairs={{0,8},{8,0},{16,24},{24,16},{1,9},{9,1},{17,25},{25,17},{2,10},{10... | collective-permute-start | bytes 786440 | tf_op jit(solution)/shard_map/ppermute | solution.py:14
  119.1 20.3 %collective-permute-start.25 = (bf16[4,128,256]{2,1,0:T(8,128)(2,1)}, bf16[4,128,256]{2,1,0:T(8,128)(2,1)}, u32[]{:S(2)}, u32[]{:S(2)}) collective-permute-start(bf16[4,128,256]{2,1,0:T(8,128)(2,1)} %get-tuple-element.35), channel_id=1, source_target_pairs={{0,16},{8,24},{16,0},{24,8},{1,17},{9,25},{17,1},{25,9},{2,18},{10... | collective-permute-start | bytes 786440 | tf_op jit(solution)/shard_map/ppermute | solution.py:14
  120.7 19.1 %collective-permute-start.26 = (bf16[4,128,256]{2,1,0:T(8,128)(2,1)}, bf16[4,128,256]{2,1,0:T(8,128)(2,1)}, u32[]{:S(2)}, u32[]{:S(2)}) collective-permute-start(bf16[4,128,256]{2,1,0:T(8,128)(2,1)} %get-tuple-element.36), channel_id=1, source_target_pairs={{0,24},{8,16},{16,8},{24,0},{1,25},{9,17},{17,9},{25,1},{2,26},{10... | collective-permute-start | bytes 786440 | tf_op jit(solution)/shard_map/ppermute | solution.py:14
  126.2 14.9 %collective-permute-start.18 = (bf16[4,128,256]{2,1,0:T(8,128)(2,1)}, bf16[4,128,256]{2,1,0:T(8,128)(2,1)}, u32[]{:S(2)}, u32[]{:S(2)}) collective-permute-start(bf16[4,128,256]{2,1,0:T(8,128)(2,1)} %get-tuple-element.30), channel_id=1, source_target_pairs={{0,8},{8,0},{16,24},{24,16},{1,9},{9,1},{17,25},{25,17},{2,10},{10... | collective-permute-start | bytes 786440 | tf_op jit(solution)/shard_map/ppermute | solution.py:14
  139.8 18.2 %collective-permute-start.6 = (bf16[4,128,256]{2,1,0:T(8,128)(2,1)S(1)}, bf16[4,128,256]{2,1,0:T(8,128)(2,1)S(1)}, u32[]{:S(2)}, u32[]{:S(2)}) collective-permute-start(bf16[4,128,256]{2,1,0:T(8,128)(2,1)S(1)} %get-tuple-element.23), channel_id=1, source_target_pairs={{0,16},{8,24},{16,0},{24,8},{1,17},{9,25},{17,1},{25,9},{2,18},{10... | collective-permute-start | bytes 786440 | tf_op jit(solution)/shard_map/ppermute | solution.py:14
  141.1 21.7 %collective-permute-start.7 = (bf16[4,128,256]{2,1,0:T(8,128)(2,1)S(1)}, bf16[4,128,256]{2,1,0:T(8,128)(2,1)S(1)}, u32[]{:S(2)}, u32[]{:S(2)}) collective-permute-start(bf16[4,128,256]{2,1,0:T(8,128)(2,1)S(1)} %get-tuple-element.24), channel_id=1, source_target_pairs={{0,24},{8,16},{16,8},{24,0},{1,25},{9,17},{17,9},{25,1},{2,26},{10... | collective-permute-start | bytes 786440 | tf_op jit(solution)/shard_map/ppermute | solution.py:14
  164.9 21.6 %collective-permute-start.14 = (bf16[4,128,256]{2,1,0:T(8,128)(2,1)S(1)}, bf16[4,128,256]{2,1,0:T(8,128)(2,1)S(1)}, u32[]{:S(2)}, u32[]{:S(2)}) collective-permute-start(bf16[4,128,256]{2,1,0:T(8,128)(2,1)S(1)} %get-tuple-element.47), channel_id=1, source_target_pairs={{0,4},{1,5},{2,6},{3,7},{4,0},{5,1},{6,2},{7,3},{8,12},{9,13},{10,... | collective-permute-start | bytes 786440 | tf_op jit(solution)/shard_map/ppermute | solution.py:14
  168.1 23.5 %collective-permute-start.27 = (bf16[4,128,256]{2,1,0:T(8,128)(2,1)S(1)}, bf16[4,128,256]{2,1,0:T(8,128)(2,1)S(1)}, u32[]{:S(2)}, u32[]{:S(2)}) collective-permute-start(bf16[4,128,256]{2,1,0:T(8,128)(2,1)S(1)} %get-tuple-element.48), channel_id=1, source_target_pairs={{0,4},{1,5},{2,6},{3,7},{4,0},{5,1},{6,2},{7,3},{8,12},{9,13},{10,... | collective-permute-start | bytes 786440 | tf_op jit(solution)/shard_map/ppermute | solution.py:14
  (31 other events, 317.2 us)

commit v3 on v2

v3 whole, which is shorter than its diff:
```python
import jax
import jax.numpy as jnp
from jax import lax
from jax.experimental import pallas as pl
from jax.experimental.pallas import tpu as pltpu
from jax.sharding import PartitionSpec as P

ROUNDS = 4
PIECES = 2
VMEM = pl.BlockSpec(memory_space=pltpu.VMEM)
PARAMS = pltpu.CompilerParams(vmem_limit_bytes=40 * 2**20)


def exchange(part, axis, mask):
    return lax.ppermute(part, axis, [(i, i ^ mask) for i in range(lax.axis_size(axis))])


def turned(own, mate):
    cells, width = own[0].shape
    group = width * len(own)

    def kernel(*refs):
        out_ref = refs[-1]
        for number, ref in enumerate(refs[:-1]):
            which, place = divmod(number, len(own))
            out_ref[which, place * width : (place + 1) * width, :] = ref[...].T

    return pl.pallas_call(
        kernel,
        out_shape=jax.ShapeDtypeStruct((2, group, cells), own[0].dtype),
        in_specs=[VMEM] * (2 * len(own)),
        out_specs=VMEM,
        compiler_params=PARAMS,
        cost_estimate=pl.CostEstimate(
            flops=0, bytes_accessed=8 * group * cells, transcendentals=0
        ),
    )(*own, *mate)


def products(choices, lefts, blocks, scale_factor):
    slab_count = lax.axis_size("space")
    group, cells = lefts.shape[1:]
    width = blocks.shape[2]
    rows = group // slab_count

    def kernel(choices_ref, lefts_ref, blocks_ref, even_ref, odd_ref, tile):
        def one_round(round_number, carry):
            left = lefts_ref[choices_ref[ROUNDS + round_number]]
            right = blocks_ref[choices_ref[round_number]]
            tile[...] = scale_factor * jnp.dot(left, right, preferred_element_type=jnp.float32)
            for number in range(slab_count):
                start = jnp.bitwise_xor(choices_ref[2 * ROUNDS], number) * rows
                part = tile[pl.ds(pl.multiple_of(start, rows), rows), :]
                out_ref = odd_ref if number % 2 else even_ref
                out_ref[number // 2, round_number] = part.astype(out_ref.dtype)
            return carry

        lax.fori_loop(0, ROUNDS, one_round, 0)

    shape = (slab_count // 2, ROUNDS, rows, width)
    return pl.pallas_call(
        kernel,
        out_shape=[jax.ShapeDtypeStruct(shape, kind) for kind in (jnp.float32, jnp.bfloat16)],
        in_specs=[pl.BlockSpec(memory_space=pltpu.SMEM), VMEM, VMEM],
        out_specs=[VMEM, VMEM],
        scratch_shapes=[pltpu.VMEM((group, width), jnp.float32)],
        compiler_params=PARAMS,
        cost_estimate=pl.CostEstimate(
            flops=2 * ROUNDS * group * cells * width,
            bytes_accessed=2 * (lefts.size + blocks.size + 2 * ROUNDS * group * width),
            transcendentals=0,
        ),
    )(choices, lefts, blocks)


def summed(keep, send):
    bit = 1
    while True:
        total = keep + exchange(send, "space", bit).astype(jnp.float32)
        if len(total) == 1:
            return total[0]
        keep, send = total[0::2], total[1::2].astype(jnp.bfloat16)
        bit *= 2


def body(snapshots, volume, masks):
    slab_count = lax.axis_size("space")
    groups = lax.axis_size("snap")
    cut = groups // 2
    cells, group = snapshots.shape
    width = group // PIECES
    scale_factor = float(cells * slab_count) ** (-0.5)
    half = cells // 2
    place = lax.axis_index("snap").astype(jnp.int32)
    upper = (place >= cut).astype(jnp.int32)
    roots = jnp.sqrt(volume)[:, None]
    sides = [list(range(cut)), list(range(cut, groups))]

    def pieces_of(side):
        scale = lax.dynamic_slice_in_dim(roots, side * half, half)
        found = []
        for number in range(PIECES):
            part = lax.dynamic_slice(snapshots, (side * half, number * width), (half, width))
            found.append((part.astype(jnp.float32) * scale).astype(jnp.bfloat16))
        return found

    def gathered(piece):
        return lax.all_gather(piece, "snap", axis_index_groups=sides)

    mate = [exchange(piece, "snap", cut) for piece in pieces_of(1 - upper)]
    own = pieces_of(upper)
    lefts = turned(own, mate)

    low = jnp.bitwise_and(jnp.bitwise_xor(masks, place), cut - 1)
    crossing = (masks >= cut).astype(jnp.int32)
    me = lax.axis_index("space").astype(jnp.int32)[None]
    own_choices = jnp.concatenate([low, crossing, me])
    mate_choices = jnp.concatenate([low, 1 - crossing, me])

    own_sums = [summed(*products(own_choices, lefts, gathered(piece), scale_factor)) for piece in own]
    swap = (crossing == 1)[:, None, None]
    columns = []
    for held, piece in zip(own_sums, mate):
        mate_sum = summed(*products(mate_choices, lefts, gathered(piece), scale_factor))
        keep = jnp.where(swap, mate_sum, held)
        give = jnp.where(swap, held, mate_sum).astype(jnp.bfloat16)
        columns.append(keep + exchange(give, "snap", cut).astype(jnp.float32))
    return jnp.concatenate(columns, axis=2)[:, None]


def solution(mesh):
    in_specs = (P("space", "snap"), P("space"), P())
    out_specs = P(None, "snap", "space", None)
    return jax.shard_map(body, mesh=mesh, in_specs=in_specs, out_specs=out_specs, check_vma=False)
```

time: 196 us -> 255 us (1.30)
  waiting for transfers between devices: 107 us -> 193 us
  local copies, waits for them, and re-layouts: 32.6 us -> 14.7 us
  starting transfers between devices: 29.6 us -> 12.5 us
  between operations: 0.2 us -> 13.3 us
  other arithmetic: 11.9 us -> 8.72 us
    all_gather x0 -> x4, waiting for transfers between devices: none -> 106 us  [gathered(): return lax.all_gather(piece, 'snap', axis_index_groups=sides)]
    ppermute x28 -> x12, waiting for transfers between devices: 107 us -> 86.1 us  [exchange(): lax.ppermute(part, axis, [(i, i ^ mask) for i in range(lax.axis_size(axis...]
    ppermute x28 -> x12, starting transfers between devices: 29.6 us -> 12.4 us  [exchange(): lax.ppermute(part, axis, [(i, i ^ mask) for i in range(lax.axis_size(axis...]
    ppermute x8 -> x0, local copies, waits for them, and re-layouts: 14 us -> none  [exchange(): lax.ppermute(part, axis, [(i, i ^ mask) for i in range(lax.axis_size(axis...]
    another operation x3 -> x0, other arithmetic: 3.9 us -> none  [body(): jnp.stack([weighted(upper, 0, group).T, jnp.concatenate(mate, axis=1).T])]
    add x0 -> x4, other arithmetic: none -> 3.67 us  [summed(): total = keep + exchange(send, 'space', bit).astype(jnp.float32)]
    unnamed x57 -> x34, local copies, waits for them, and re-layouts: 15.6 us -> 13.2 us
    pallas_call x4 -> x5, Pallas kernels: 13.6 us -> 12.7 us  [the longest x4 12.1 us: products(): pl.pallas_call(kernel, out_shape=[jax.ShapeDtypeStruct(shape, kind) for k...]
  transfers between devices with their start and end apart: 28 -> 16, of which waited for: 11 -> 10; matrix products, arithmetic and copies ran while one was open for 11% -> 2% of each run, Pallas kernels for 7% -> 5%
where the time goes in v3:
time: 255 us
  waiting for transfers between devices  193 us (76%)
  local copies, waits for them, and re-layouts  14.7 us (6%)
  between operations  13.3 us (5%)
  Pallas kernels  12.7 us (5%)
  starting transfers between devices  12.5 us (5%)
  other arithmetic  8.72 us (3%)
    all_gather x4, waiting for transfers between devices, gathered(): return lax.all_gather(piece, 'snap', axis_index_groups=sides)  106 us
    ppermute x12, waiting for transfers between devices, exchange(): lax.ppermute(part, axis, [(i, i ^ mask) for i in range(lax.axis_size(axis...  86.1 us
    unnamed x34, local copies, waits for them, and re-layouts  13.2 us
    ppermute x12, starting transfers between devices, exchange(): lax.ppermute(part, axis, [(i, i ^ mask) for i in range(lax.axis_size(axis...  12.4 us
    pallas_call x4, Pallas kernels, products(): pl.pallas_call(kernel, out_shape=[jax.ShapeDtypeStruct(shape, kind) for k...  12.1 us
  transfers between devices with their start and end apart: 16, of which 10 were waited for; matrix products, arithmetic and copies ran while one was open for 2% of the time, Pallas kernels for 5%

profile of v3, /device:TPU:0, one launch (start us, length us, event | category | flops | bytes accessed | tf_op | source)
XLA Modules:
  0.0 254.5 jit_solution(16793703867914248366)
XLA Ops:
  7.2 3.0 %multiply_convert_fusion = (bf16[1024,256]{1,0:T(8,128)(2,1)S(1)}, bf16[1024,256]{1,0:T(8,128)(2,1)S(1)}, bf16[1024,256]{1,0:T(8,128)(2,1)}, bf16[1024,256]{1,0:T(8,128)(2,1)}) fusion(bf16[2048,512]{1,0:T(8,128)(2,1)} %param.3, s32[]{:T(128)S(6)} %select_n.21, f32[1024]{0:T(1024)S(1)} %get-tuple-element.27, f32[1024]{0:T(1024)S(1)} %get-tuple-element.28, ...), kind=kLoop, calls=%fused_computation.5 | loop fusion | flops 3145728 | bytes 4202504 | tf_op jit(solution)/shard_map/convert_element_type | solution.py:104
  11.0 4.1 %collective-permute-start = (bf16[1024,256]{1,0:T(8,128)(2,1)S(1)}, bf16[1024,256]{1,0:T(8,128)(2,1)S(1)}, u32[]{:S(2)}, u32[]{:S(2)}) collective-permute-start(bf16[1024,256]{1,0:T(8,128)(2,1)S(1)} %get-tuple-element.22), channel_id=1, source_target_pairs={{0,4},{1,5},{2,6},{3,7},{4,0},{5,1},{6,2},{7,3},{8,12},{9,13},{10,... | collective-permute-start | bytes 1572872 | tf_op jit(solution)/shard_map/ppermute | solution.py:15
  15.1 23.2 %collective-permute-done.refs_2_ = bf16[1024,256]{1,0:T(8,128)(2,1)S(1)} collective-permute-done((bf16[1024,256]{1,0:T(8,128)(2,1)S(1)}, bf16[1024,256]{1,0:T(8,128)(2,1)S(1)}, u32[]{:S(2)}, u32[]{:S(2)}) %collective-permute-start) | collective-permute-done | bytes 524320 | tf_op jit(solution)/shard_map/ppermute | solution.py:15
  39.3 25.4 %collective-permute-done.1.refs_3_ = bf16[1024,256]{1,0:T(8,128)(2,1)S(1)} collective-permute-done((bf16[1024,256]{1,0:T(8,128)(2,1)S(1)}, bf16[1024,256]{1,0:T(8,128)(2,1)S(1)}, u32[]{:S(2)}, u32[]{:S(2)}) %collective-permute-start.1) | collective-permute-done | bytes 524320 | tf_op jit(solution)/shard_map/ppermute | solution.py:15
  68.4 1.6 copy-done.4
  70.0 3.2 %shard_map.39 = (f32[2,4,128,256]{3,2,1,0:T(8,128)S(1)}, bf16[2,4,128,256]{3,2,1,0:T(8,128)(2,1)}) custom-call(s32[9]{0:T(128)S(1)} %get-tuple-element.35.choices_ref, bf16[2,512,1024]{2,1,0:T(8,128)(2,1)S(1)} %shard_map.37.lefts_ref, bf16[4,1024,256]{2,1,0:T(8,128)(2,1)S(1)} %bitcast.35), custom_call_target="tpu_custom_call" | custom-call | flops 1073741824 | bytes 6291456 | tf_op jit(solution)/shard_map/pallas_call | solution.py:61
  74.3 29.8 %all-gather.15.cloned.1.call-done = bf16[4096,256]{1,0:T(8,128)(2,1)} async-done(((bf16[1024,256]{1,0:T(8,128)(2,1)}), bf16[4096,256]{1,0:T(8,128)(2,1)}) %all-gather.15.cloned.1.call-update) | async-done | bytes 2097168 | tf_op jit(solution)/shard_map/all_gather | solution.py:108
  104.1 1.6 copy-done.3
  105.7 3.2 %shard_map.41 = (f32[2,4,128,256]{3,2,1,0:T(8,128)S(1)}, bf16[2,4,128,256]{3,2,1,0:T(8,128)(2,1)}) custom-call(s32[9]{0:T(128)S(1)} %get-tuple-element.35.choices_ref, bf16[2,512,1024]{2,1,0:T(8,128)(2,1)S(1)} %shard_map.37.lefts_ref, bf16[4,1024,256]{2,1,0:T(8,128)(2,1)S(1)} %bitcast.34), custom_call_target="tpu_custom_call" | custom-call | flops 1073741824 | bytes 6291456 | tf_op jit(solution)/shard_map/pallas_call | solution.py:61
  108.9 40.7 %all-gather.9.cloned.1.call-done = bf16[4096,256]{1,0:T(8,128)(2,1)} async-done(((bf16[1024,256]{1,0:T(8,128)(2,1)}), bf16[4096,256]{1,0:T(8,128)(2,1)}) %all-gather.9.cloned.1.call-update) | async-done | bytes 2097168 | tf_op jit(solution)/shard_map/all_gather | solution.py:108
  149.6 1.6 copy-done.5
  151.2 3.2 %shard_map.38 = (f32[2,4,128,256]{3,2,1,0:T(8,128)S(1)}, bf16[2,4,128,256]{3,2,1,0:T(8,128)(2,1)}) custom-call(s32[9]{0:T(128)S(1)} %get-tuple-element.36.choices_ref, bf16[2,512,1024]{2,1,0:T(8,128)(2,1)S(1)} %shard_map.37.lefts_ref, bf16[4,1024,256]{2,1,0:T(8,128)(2,1)S(1)} %bitcast.36), custom_call_target="tpu_custom_call" | custom-call | flops 1073741824 | bytes 6291456 | tf_op jit(solution)/shard_map/pallas_call | solution.py:61
  158.3 1.5 collective-permute-start.5
  159.8 35.2 %all-gather.13.cloned.1.call-done = bf16[4096,256]{1,0:T(8,128)(2,1)} async-done(((bf16[1024,256]{1,0:T(8,128)(2,1)}), bf16[4096,256]{1,0:T(8,128)(2,1)}) %all-gather.13.cloned.1.call-update) | async-done | bytes 2097168 | tf_op jit(solution)/shard_map/all_gather | solution.py:108
  195.0 1.6 copy-done.2
  196.5 2.4 shard_map.40
  200.3 1.5 collective-permute-start.10
  203.9 1.5 collective-permute-start.8
  205.4 4.1 %collective-permute-done.10 = bf16[1,4,128,256]{3,2,1,0:T(8,128)(2,1)S(1)} collective-permute-done((bf16[1,4,128,256]{3,2,1,0:T(8,128)(2,1)S(1)}, bf16[1,4,128,256]{3,2,1,0:T(8,128)(2,1)S(1)}, u32[]{:S(2)}, u32[]{:S(2)}) %collective-permute-start.10) | collective-permute-done | bytes 262176 | tf_op jit(solution)/shard_map/ppermute | solution.py:15
  209.5 5.6 %collective-permute-done.3 = bf16[1,4,128,256]{3,2,1,0:T(8,128)(2,1)S(1)} collective-permute-done((bf16[1,4,128,256]{3,2,1,0:T(8,128)(2,1)S(1)}, bf16[1,4,128,256]{3,2,1,0:T(8,128)(2,1)S(1)}, u32[]{:S(2)}, u32[]{:S(2)}) %collective-permute-start.3) | collective-permute-done | bytes 262176 | tf_op jit(solution)/shard_map/ppermute | solution.py:15
  215.1 5.2 %collective-permute-done.8 = bf16[1,4,128,256]{3,2,1,0:T(8,128)(2,1)S(1)} collective-permute-done((bf16[1,4,128,256]{3,2,1,0:T(8,128)(2,1)S(1)}, bf16[1,4,128,256]{3,2,1,0:T(8,128)(2,1)S(1)}, u32[]{:S(2)}, u32[]{:S(2)}) %collective-permute-start.8) | collective-permute-done | bytes 262176 | tf_op jit(solution)/shard_map/ppermute | solution.py:15
  220.7 2.5 collective-permute-start.6
  223.7 17.7 %collective-permute-done.6 = bf16[4,128,256]{2,1,0:T(8,128)(2,1)S(1)} collective-permute-done((bf16[4,128,256]{2,1,0:T(8,128)(2,1)S(1)}, bf16[4,128,256]{2,1,0:T(8,128)(2,1)S(1)}, u32[]{:S(2)}, u32[]{:S(2)}) %collective-permute-start.6) | collective-permute-done | bytes 262176 | tf_op jit(solution)/shard_map/ppermute | solution.py:15
  241.4 5.0 %collective-permute-done.11 = bf16[4,128,256]{2,1,0:T(8,128)(2,1)S(1)} collective-permute-done((bf16[4,128,256]{2,1,0:T(8,128)(2,1)S(1)}, bf16[4,128,256]{2,1,0:T(8,128)(2,1)S(1)}, u32[]{:S(2)}, u32[]{:S(2)}) %collective-permute-start.11) | collective-permute-done | bytes 262176 | tf_op jit(solution)/shard_map/ppermute | solution.py:15
  (68 shorter events, 16.9 us)
Async XLA Ops:
  6.5 61.9 %all-gather.11.cloned.1.call-start = ((), (), s32[]{:S(2)}) async-start(), calls=%async_computation.1 | async-start | bytes 2621440 | tf_op jit(solution)/shard_map/all_gather | solution.py:108
  10.2 55.3 %copy-start.16 = (s32[4]{0:T(128)S(1)}, s32[4]{0:T(128)}, u32[]{:S(2)}) copy-start(s32[4]{0:T(128)} %param.5) | copy-start | bytes 52
  10.2 55.4 %copy-start = (bf16[1024,256]{1,0:T(8,128)(2,1)S(1)}, bf16[1024,256]{1,0:T(8,128)(2,1)}, u32[]{:S(2)}) copy-start(bf16[1024,256]{1,0:T(8,128)(2,1)} %get-tuple-element.26.refs_1_) | copy-start | bytes 1572868
  10.2 55.4 %copy-start.1 = (bf16[1024,256]{1,0:T(8,128)(2,1)S(1)}, bf16[1024,256]{1,0:T(8,128)(2,1)}, u32[]{:S(2)}) copy-start(bf16[1024,256]{1,0:T(8,128)(2,1)} %get-tuple-element.25.refs_0_) | copy-start | bytes 1572868
  10.2 93.8 %all-gather.15.cloned.1.call-start = ((), (), s32[]{:S(2)}) async-start(), calls=%async_computation.3 | async-start | bytes 2621440 | tf_op jit(solution)/shard_map/all_gather | solution.py:108
  11.0 138.6 %all-gather.9.cloned.1.call-start = ((), (), s32[]{:S(2)}) async-start(), calls=%async_computation | async-start | bytes 2621440 | tf_op jit(solution)/shard_map/all_gather | solution.py:108
  11.0 27.3 %collective-permute-start = (bf16[1024,256]{1,0:T(8,128)(2,1)S(1)}, bf16[1024,256]{1,0:T(8,128)(2,1)S(1)}, u32[]{:S(2)}, u32[]{:S(2)}) collective-permute-start(bf16[1024,256]{1,0:T(8,128)(2,1)S(1)} %get-tuple-element.22), channel_id=1, source_target_pairs={{0,4},{1,5},{2,6},{3,7},{4,0},{5,1},{6,2},{7,3},{8,12},{9,13},{10,... | collective-permute-start | bytes 1572872 | tf_op jit(solution)/shard_map/ppermute | solution.py:15
  39.2 155.8 %all-gather.13.cloned.1.call-start = ((), (), s32[]{:S(2)}) async-start(), calls=%async_computation.2 | async-start | bytes 2621440 | tf_op jit(solution)/shard_map/all_gather | solution.py:108
  39.2 25.5 %collective-permute-start.1 = (bf16[1024,256]{1,0:T(8,128)(2,1)S(1)}, bf16[1024,256]{1,0:T(8,128)(2,1)S(1)}, u32[]{:S(2)}, u32[]{:S(2)}) collective-permute-start(bf16[1024,256]{1,0:T(8,128)(2,1)S(1)} %get-tuple-element.21), channel_id=1, source_target_pairs={{0,4},{1,5},{2,6},{3,7},{4,0},{5,1},{6,2},{7,3},{8,12},{9,13},{10,... | collective-permute-start | bytes 1572872 | tf_op jit(solution)/shard_map/ppermute | solution.py:15
  68.4 1.6 copy-start.4
  74.3 81.1 %collective-permute-start.4 = (bf16[2,4,128,256]{3,2,1,0:T(8,128)(2,1)}, bf16[2,4,128,256]{3,2,1,0:T(8,128)(2,1)}, u32[]{:S(2)}, u32[]{:S(2)}) collective-permute-start(bf16[2,4,128,256]{3,2,1,0:T(8,128)(2,1)} %get-tuple-element.16), channel_id=1, source_target_pairs={{0,8},{8,0},{16,24},{24,16},{1,9},{9,1},{17,25},{25,17},{2,10},{10... | collective-permute-start | bytes 1572872 | tf_op jit(solution)/shard_map/ppermute | solution.py:15
  108.9 90.2 %collective-permute-start.9 = (bf16[2,4,128,256]{3,2,1,0:T(8,128)(2,1)}, bf16[2,4,128,256]{3,2,1,0:T(8,128)(2,1)}, u32[]{:S(2)}, u32[]{:S(2)}) collective-permute-start(bf16[2,4,128,256]{3,2,1,0:T(8,128)(2,1)} %get-tuple-element.20), channel_id=1, source_target_pairs={{0,8},{8,0},{16,24},{24,16},{1,9},{9,1},{17,25},{25,17},{2,10},{10... | collective-permute-start | bytes 1572872 | tf_op jit(solution)/shard_map/ppermute | solution.py:15
  149.6 1.6 copy-start.5
  151.2 4.2 %copy-start.13 = (f32[2,4,128,256]{3,2,1,0:T(8,128)S(1)}, f32[2,4,128,256]{3,2,1,0:T(8,128)}, u32[]{:S(2)}) copy-start(f32[2,4,128,256]{3,2,1,0:T(8,128)} %copy-done.12) | copy-start | bytes 3145732
  155.4 46.5 %collective-permute-start.2 = (bf16[2,4,128,256]{3,2,1,0:T(8,128)(2,1)}, bf16[2,4,128,256]{3,2,1,0:T(8,128)(2,1)}, u32[]{:S(2)}, u32[]{:S(2)}) collective-permute-start(bf16[2,4,128,256]{3,2,1,0:T(8,128)(2,1)} %get-tuple-element.14), channel_id=1, source_target_pairs={{0,8},{8,0},{16,24},{24,16},{1,9},{9,1},{17,25},{25,17},{2,10},{10... | collective-permute-start | bytes 1572872 | tf_op jit(solution)/shard_map/ppermute | solution.py:15
  158.3 47.1 %collective-permute-start.5 = (bf16[1,4,128,256]{3,2,1,0:T(8,128)(2,1)}, bf16[1,4,128,256]{3,2,1,0:T(8,128)(2,1)S(1)}, u32[]{:S(2)}, u32[]{:S(2)}) collective-permute-start(bf16[1,4,128,256]{3,2,1,0:T(8,128)(2,1)} %slice.86), channel_id=1, source_target_pairs={{0,16},{8,24},{16,0},{24,8},{1,17},{9,25},{17,1},{25,9},{2,18},{10... | collective-permute-start | bytes 786440 | tf_op jit(solution)/shard_map/ppermute | solution.py:15
  199.0 2.9 %copy-start.11 = (f32[2,4,128,256]{3,2,1,0:T(8,128)S(1)}, f32[2,4,128,256]{3,2,1,0:T(8,128)}, u32[]{:S(2)}) copy-start(f32[2,4,128,256]{3,2,1,0:T(8,128)} %copy-done.10) | copy-start | bytes 3145732
  199.0 4.7 %collective-permute-start.7 = (bf16[2,4,128,256]{3,2,1,0:T(8,128)(2,1)S(1)}, bf16[2,4,128,256]{3,2,1,0:T(8,128)(2,1)S(1)}, u32[]{:S(2)}, u32[]{:S(2)}) collective-permute-start(bf16[2,4,128,256]{3,2,1,0:T(8,128)(2,1)S(1)} %get-tuple-element.18), channel_id=1, source_target_pairs={{0,8},{8,0},{16,24},{24,16},{1,9},{9,1},{17,25},{25,17},{2,10},{10... | collective-permute-start | bytes 1572872 | tf_op jit(solution)/shard_map/ppermute | solution.py:15
  200.3 9.2 %collective-permute-start.10 = (bf16[1,4,128,256]{3,2,1,0:T(8,128)(2,1)S(1)}, bf16[1,4,128,256]{3,2,1,0:T(8,128)(2,1)S(1)}, u32[]{:S(2)}, u32[]{:S(2)}) collective-permute-start(bf16[1,4,128,256]{3,2,1,0:T(8,128)(2,1)S(1)} %slice.84), channel_id=1, source_target_pairs={{0,16},{8,24},{16,0},{24,8},{1,17},{9,25},{17,1},{25,9},{2,18},{10... | collective-permute-start | bytes 786440 | tf_op jit(solution)/shard_map/ppermute | solution.py:15
  203.0 17.3 %copy-start.15 = (f32[2,4,128,256]{3,2,1,0:T(8,128)S(1)}, f32[2,4,128,256]{3,2,1,0:T(8,128)}, u32[]{:S(2)}) copy-start(f32[2,4,128,256]{3,2,1,0:T(8,128)} %copy-done.14) | copy-start | bytes 3145732
  203.1 12.1 %collective-permute-start.3 = (bf16[1,4,128,256]{3,2,1,0:T(8,128)(2,1)S(1)}, bf16[1,4,128,256]{3,2,1,0:T(8,128)(2,1)S(1)}, u32[]{:S(2)}, u32[]{:S(2)}) collective-permute-start(bf16[1,4,128,256]{3,2,1,0:T(8,128)(2,1)S(1)} %slice.87), channel_id=1, source_target_pairs={{0,16},{8,24},{16,0},{24,8},{1,17},{9,25},{17,1},{25,9},{2,18},{10... | collective-permute-start | bytes 786440 | tf_op jit(solution)/shard_map/ppermute | solution.py:15
  203.9 16.4 %collective-permute-start.8 = (bf16[1,4,128,256]{3,2,1,0:T(8,128)(2,1)S(1)}, bf16[1,4,128,256]{3,2,1,0:T(8,128)(2,1)S(1)}, u32[]{:S(2)}, u32[]{:S(2)}) collective-permute-start(bf16[1,4,128,256]{3,2,1,0:T(8,128)(2,1)S(1)} %slice.85), channel_id=1, source_target_pairs={{0,16},{8,24},{16,0},{24,8},{1,17},{9,25},{17,1},{25,9},{2,18},{10... | collective-permute-start | bytes 786440 | tf_op jit(solution)/shard_map/ppermute | solution.py:15
  220.7 20.7 %collective-permute-start.6 = (bf16[4,128,256]{2,1,0:T(8,128)(2,1)S(1)}, bf16[4,128,256]{2,1,0:T(8,128)(2,1)S(1)}, u32[]{:S(2)}, u32[]{:S(2)}) collective-permute-start(bf16[4,128,256]{2,1,0:T(8,128)(2,1)S(1)} %get-tuple-element.31), channel_id=1, source_target_pairs={{0,4},{1,5},{2,6},{3,7},{4,0},{5,1},{6,2},{7,3},{8,12},{9,13},{10,... | collective-permute-start | bytes 786440 | tf_op jit(solution)/shard_map/ppermute | solution.py:15
  223.2 23.2 %collective-permute-start.11 = (bf16[4,128,256]{2,1,0:T(8,128)(2,1)S(1)}, bf16[4,128,256]{2,1,0:T(8,128)(2,1)S(1)}, u32[]{:S(2)}, u32[]{:S(2)}) collective-permute-start(bf16[4,128,256]{2,1,0:T(8,128)(2,1)S(1)} %get-tuple-element.32), channel_id=1, source_target_pairs={{0,4},{1,5},{2,6},{3,7},{4,0},{5,1},{6,2},{7,3},{8,12},{9,13},{10,... | collective-permute-start | bytes 786440 | tf_op jit(solution)/shard_map/ppermute | solution.py:15
  (9 other events, 10.0 us)
Sparse Core Ops, SparseCore 0:
  10.4 48.2 all-gather.10
  60.2 43.8 all-gather.14
  105.6 43.9 all-gather.8
  151.0 43.9 all-gather.12

commit v4 on v3

v4 whole, which is shorter than its diff:
```python
import jax
import jax.numpy as jnp
from jax import lax
from jax.experimental import pallas as pl
from jax.experimental.pallas import tpu as pltpu
from jax.sharding import PartitionSpec as P

ROUNDS = 4
OWN_WIDTHS = (2, 2)
MATE_WIDTHS = (2, 1, 1)
NEAR_FIRST = (3,)
VMEM = pl.BlockSpec(memory_space=pltpu.VMEM)
PARAMS = pltpu.CompilerParams(vmem_limit_bytes=40 * 2**20)


def exchange(part, axis, mask):
    return lax.ppermute(part, axis, [(i, i ^ mask) for i in range(lax.axis_size(axis))])


def behind(value, earlier):
    return value if earlier is None else lax.optimization_barrier((value, earlier))[0]


def hops_in_order(widths, cut):
    waiting = []
    for piece in range(len(widths)):
        bits, held = [1 << n for n in range(cut.bit_length() - 1)], [0]
        for bit in bits if piece in NEAR_FIRST else reversed(bits):
            waiting += [(piece, low, bit) for low in held]
            held += [low | bit for low in held]
    ready, crossed = {}, 0
    for piece, width in enumerate(widths):
        crossed += 2 * width if piece >= len(OWN_WIDTHS) else 0
        ready[piece, 0] = crossed
    free, ordered = {}, []
    while waiting:
        def start_of(hop):
            return max(free.get(hop[2], 0), ready[hop[:2]])

        able = [hop for hop in waiting if hop[:2] in ready]
        hop = min(able, key=lambda one: (start_of(one), waiting.index(one)))
        piece, low, bit = hop
        shared = 2 if bit == cut // 2 and start_of(hop) < crossed else 1
        free[bit] = ready[piece, low | bit] = start_of(hop) + shared * widths[piece]
        waiting.remove(hop)
        ordered.append(hop)
    return ordered


def gathered(pieces, widths, cut):
    held = [{0: piece} for piece in pieces]
    behind_of = {}
    for piece, low, bit in hops_in_order(widths, cut):
        earlier = behind_of.setdefault(bit, [])
        depth = 2 if bit == 1 else 1
        block = behind(held[piece][low], earlier[-depth] if len(earlier) >= depth else None)
        held[piece][low | bit] = exchange(block, "snap", bit)
        earlier.append(held[piece][low | bit])
    return [[found[low] for low in range(cut)] for found in held]


def turned(own, mate):
    cells = own[0].shape[0]
    group = sum(piece.shape[1] for piece in own)

    def kernel(*refs):
        out_ref = refs[-1]
        for which, some in enumerate((refs[: len(own)], refs[len(own) : -1])):
            first = 0
            for ref in some:
                out_ref[which, first : first + ref.shape[1], :] = ref[...].T
                first += ref.shape[1]

    return pl.pallas_call(
        kernel,
        out_shape=jax.ShapeDtypeStruct((2, group, cells), own[0].dtype),
        in_specs=[VMEM] * (len(own) + len(mate)),
        out_specs=VMEM,
        compiler_params=PARAMS,
        cost_estimate=pl.CostEstimate(
            flops=0, bytes_accessed=8 * group * cells, transcendentals=0
        ),
    )(*own, *mate)


def products(choices, lefts, blocks, scale_factor):
    slab_count = lax.axis_size("space")
    group, cells = lefts.shape[1:]
    width = blocks[0].shape[1]
    rows = group // slab_count

    def kernel(choices_ref, lefts_ref, *refs):
        block_refs = refs[: len(blocks)]
        even_ref, odd_ref, picked, tile = refs[len(blocks) :]

        def one_round(round_number, carry):
            for number, block_ref in enumerate(block_refs):

                @pl.when(choices_ref[round_number] == number)
                def _():
                    picked[...] = block_ref[...]

            left = lefts_ref[choices_ref[ROUNDS + round_number]]
            tile[...] = scale_factor * jnp.dot(
                left, picked[...], preferred_element_type=jnp.float32
            )
            for number in range(slab_count):
                start = jnp.bitwise_xor(choices_ref[2 * ROUNDS], number) * rows
                part = tile[pl.ds(pl.multiple_of(start, rows), rows), :]
                out_ref = odd_ref if number % 2 else even_ref
                out_ref[number // 2, round_number] = part.astype(out_ref.dtype)
            return carry

        lax.fori_loop(0, ROUNDS, one_round, 0)

    shape = (slab_count // 2, ROUNDS, rows, width)
    return pl.pallas_call(
        kernel,
        out_shape=[jax.ShapeDtypeStruct(shape, kind) for kind in (jnp.float32, jnp.bfloat16)],
        in_specs=[pl.BlockSpec(memory_space=pltpu.SMEM)] + [VMEM] * (1 + len(blocks)),
        out_specs=[VMEM, VMEM],
        scratch_shapes=[
            pltpu.VMEM((cells, width), jnp.bfloat16),
            pltpu.VMEM((group, width), jnp.float32),
        ],
        compiler_params=PARAMS,
        cost_estimate=pl.CostEstimate(
            flops=2 * ROUNDS * group * cells * width,
            bytes_accessed=2 * (lefts.size + (len(blocks) * cells + 2 * ROUNDS * group) * width),
            transcendentals=0,
        ),
    )(choices, lefts, *blocks)


def summed(keep, send):
    bit = 1
    while True:
        total = keep + exchange(send, "space", bit).astype(jnp.float32)
        if len(total) == 1:
            return total[0]
        keep, send = total[0::2], total[1::2].astype(jnp.bfloat16)
        bit *= 2


def body(snapshots, volume, masks):
    slab_count = lax.axis_size("space")
    groups = lax.axis_size("snap")
    cut = groups // 2
    cells, group = snapshots.shape
    quarter = group // 4
    scale_factor = float(cells * slab_count) ** (-0.5)
    half = cells // 2
    place = lax.axis_index("snap").astype(jnp.int32)
    upper = (place >= cut).astype(jnp.int32)
    roots = jnp.sqrt(volume)[:, None]

    def pieces_of(side, widths):
        scale = lax.dynamic_slice_in_dim(roots, side * half, half)
        found, first = [], 0
        for width in widths:
            part = lax.dynamic_slice(
                snapshots, (side * half, first * quarter), (half, width * quarter)
            )
            found.append((part.astype(jnp.float32) * scale).astype(jnp.bfloat16))
            first += width
        return found

    mate, crossed = [], None
    for piece in pieces_of(1 - upper, MATE_WIDTHS):
        crossed = exchange(behind(piece, crossed), "snap", cut)
        mate.append(crossed)
    own = pieces_of(upper, OWN_WIDTHS)
    lefts = turned(own, mate)
    blocks = gathered(own + mate, OWN_WIDTHS + MATE_WIDTHS, cut)

    low = jnp.bitwise_and(masks, cut - 1)
    crossing = (masks >= cut).astype(jnp.int32)
    me = lax.axis_index("space").astype(jnp.int32)[None]
    own_choices = jnp.concatenate([low, crossing, me])
    mate_choices = jnp.concatenate([low, 1 - crossing, me])

    own_sum = jnp.concatenate(
        [
            summed(*products(own_choices, lefts, found, scale_factor))
            for found in blocks[: len(own)]
        ],
        axis=2,
    )
    swap = (crossing == 1)[:, None, None]
    columns, first = [], 0
    for found in blocks[len(own) :]:
        mate_sum = summed(*products(mate_choices, lefts, found, scale_factor))
        held = lax.slice_in_dim(own_sum, first, first + mate_sum.shape[2], axis=2)
        keep = jnp.where(swap, mate_sum, held)
        give = jnp.where(swap, held, mate_sum).astype(jnp.bfloat16)
        columns.append(keep + exchange(give, "snap", cut).astype(jnp.float32))
        first += mate_sum.shape[2]
    return jnp.concatenate(columns, axis=2)[:, None]


def solution(mesh):
    in_specs = (P("space", "snap"), P("space"), P())
    out_specs = P(None, "snap", "space", None)
    return jax.shard_map(body, mesh=mesh, in_specs=in_specs, out_specs=out_specs, check_vma=False)
```

time: 255 us -> 143 us (0.56)
  waiting for transfers between devices: 193 us -> 80.3 us
  starting transfers between devices: 12.5 us -> 39.3 us
  between operations: 13.3 us -> 0.29 us
  local copies, waits for them, and re-layouts: 14.7 us -> 3.28 us
  other arithmetic: 8.72 us -> 5.28 us
    all_gather x4 -> x0, waiting for transfers between devices: 106 us -> none  [gathered(): return lax.all_gather(piece, 'snap', axis_index_groups=sides)]
    ppermute x12 -> x31, starting transfers between devices: 12.4 us -> 39.3 us  [exchange(): lax.ppermute(part, axis, [(i, i ^ mask) for i in range(lax.axis_size(axis...]
    unnamed x34 -> x18, local copies, waits for them, and re-layouts: 13.2 us -> 2.45 us
    ppermute x12 -> x31, waiting for transfers between devices: 86.1 us -> 80.3 us  [exchange(): lax.ppermute(part, axis, [(i, i ^ mask) for i in range(lax.axis_size(axis...]
    add x4 -> x5, other arithmetic: 3.67 us -> 0.48 us  [summed(): total = keep + exchange(send, 'space', bit).astype(jnp.float32)]
    pallas_call x4 -> x5, Pallas kernels: 12.1 us -> 13.7 us  [products(): pl.pallas_call(kernel, out_shape=[jax.ShapeDtypeStruct(shape, kind) for k...]
  transfers between devices with their start and end apart: 16 -> 31, of which waited for: 10 -> 15; matrix products, arithmetic and copies ran while one was open for 2% -> 2% of each run, Pallas kernels for 5% -> 10%
where the time goes in v4:
time: 143 us
  waiting for transfers between devices  80.3 us (56%)
  starting transfers between devices  39.3 us (27%)
  Pallas kernels  14.3 us (10%)
  other arithmetic  5.28 us (4%)
  local copies, waits for them, and re-layouts  3.28 us (2%)
    ppermute x31, waiting for transfers between devices, exchange(): lax.ppermute(part, axis, [(i, i ^ mask) for i in range(lax.axis_size(axis...  80.3 us
    ppermute x31, starting transfers between devices, exchange(): lax.ppermute(part, axis, [(i, i ^ mask) for i in range(lax.axis_size(axis...  39.3 us
    pallas_call x5, Pallas kernels, products(): pl.pallas_call(kernel, out_shape=[jax.ShapeDtypeStruct(shape, kind) for k...  13.7 us
    convert_element_type x2, other arithmetic, pieces_of(): found.append((part.astype(jnp.float32) * scale).astype(jnp.bfloat16))  2.94 us
  transfers between devices with their start and end apart: 31, of which 15 were waited for; matrix products, arithmetic and copies ran while one was open for 2% of the time, Pallas kernels for 10%

profile of v4, /device:TPU:0, one launch (start us, length us, event | category | flops | bytes accessed | tf_op | source)
XLA Modules:
  0.0 142.7 jit_solution(11810745304485981642)
XLA Ops:
  2.4 3.1 %collective-permute-start.5 = (bf16[1024,256]{1,0:T(8,128)(2,1)S(1)}, bf16[1024,256]{1,0:T(8,128)(2,1)S(1)}, u32[]{:S(2)}, u32[]{:S(2)}) collective-permute-start(bf16[1024,256]{1,0:T(8,128)(2,1)S(1)} %get-tuple-element.56.refs_0_), channel_id=1, source_target_pairs={{0,2},{1,3},{2,0},{3,1},{4,6},{5,7},{6,4},{7,5},{8,10},{9,11},{10,... | collective-permute-start | bytes 1572872 | tf_op jit(solution)/shard_map/ppermute | solution.py:17
  7.0 2.6 %collective-permute-start = (bf16[1024,256]{1,0:T(8,128)(2,1)S(1)}, bf16[1024,256]{1,0:T(8,128)(2,1)S(1)}, u32[]{:S(2)}, u32[]{:S(2)}) collective-permute-start(bf16[1024,256]{1,0:T(8,128)(2,1)S(1)} %get-tuple-element.57), channel_id=1, source_target_pairs={{0,4},{1,5},{2,6},{3,7},{4,0},{5,1},{6,2},{7,3},{8,12},{9,13},{10,... | collective-permute-start | bytes 1572872 | tf_op jit(solution)/shard_map/ppermute | solution.py:17
  10.1 17.2 %collective-permute-done.5.refs_2_ = bf16[1024,256]{1,0:T(8,128)(2,1)S(1)} collective-permute-done((bf16[1024,256]{1,0:T(8,128)(2,1)S(1)}, bf16[1024,256]{1,0:T(8,128)(2,1)S(1)}, u32[]{:S(2)}, u32[]{:S(2)}) %collective-permute-start.5) | collective-permute-done | bytes 524320 | tf_op jit(solution)/shard_map/ppermute | solution.py:17
  28.2 2.6 %collective-permute-start.12 = (bf16[1024,256]{1,0:T(8,128)(2,1)S(1)}, bf16[1024,256]{1,0:T(8,128)(2,1)S(1)}, u32[]{:S(2)}, u32[]{:S(2)}) collective-permute-start(bf16[1024,256]{1,0:T(8,128)(2,1)S(1)} %collective-permute-done.5.refs_2_), channel_id=1, source_target_pairs={{0,1},{1,0},{2,3},{3,2},{4,5},{5,4},{6,7},{7,6},{8,9},{9,8},{10,11... | collective-permute-start | bytes 1572872 | tf_op jit(solution)/shard_map/ppermute | solution.py:17
  32.4 2.7 %collective-permute-start.1 = (bf16[1024,128]{1,0:T(8,128)(2,1)S(1)}, bf16[1024,128]{1,0:T(8,128)(2,1)S(1)}, u32[]{:S(2)}, u32[]{:S(2)}) collective-permute-start(bf16[1024,128]{1,0:T(8,128)(2,1)S(1)} %get-tuple-element.29), channel_id=1, source_target_pairs={{0,4},{1,5},{2,6},{3,7},{4,0},{5,1},{6,2},{7,3},{8,12},{9,13},{10,... | collective-permute-start | bytes 786440 | tf_op jit(solution)/shard_map/ppermute | solution.py:17
  35.9 11.6 %collective-permute-done.6.refs_2_ = bf16[1024,256]{1,0:T(8,128)(2,1)} collective-permute-done((bf16[1024,256]{1,0:T(8,128)(2,1)S(1)}, bf16[1024,256]{1,0:T(8,128)(2,1)}, u32[]{:S(2)}, u32[]{:S(2)}) %collective-permute-start.6) | collective-permute-done | bytes 524320 | tf_op jit(solution)/shard_map/ppermute | solution.py:17
  47.5 4.0 %collective-permute-start.2 = (bf16[1024,128]{1,0:T(8,128)(2,1)S(1)}, bf16[1024,128]{1,0:T(8,128)(2,1)S(1)}, u32[]{:S(2)}, u32[]{:S(2)}) collective-permute-start(bf16[1024,128]{1,0:T(8,128)(2,1)S(1)} %get-tuple-element.30), channel_id=1, source_target_pairs={{0,4},{1,5},{2,6},{3,7},{4,0},{5,1},{6,2},{7,3},{8,12},{9,13},{10,... | collective-permute-start | bytes 786440 | tf_op jit(solution)/shard_map/ppermute | solution.py:17
  53.8 9.8 %collective-permute-done.2.refs_4_.refs_0_ = bf16[1024,128]{1,0:T(8,128)(2,1)S(1)} collective-permute-done((bf16[1024,128]{1,0:T(8,128)(2,1)S(1)}, bf16[1024,128]{1,0:T(8,128)(2,1)S(1)}, u32[]{:S(2)}, u32[]{:S(2)}) %collective-permute-start.2) | collective-permute-done | bytes 262176 | tf_op jit(solution)/shard_map/ppermute | solution.py:17
  65.8 3.3 %collective-permute-start.18 = (bf16[1024,128]{1,0:T(8,128)(2,1)S(1)}, bf16[1024,128]{1,0:T(8,128)(2,1)S(1)}, u32[]{:S(2)}, u32[]{:S(2)}) collective-permute-start(bf16[1024,128]{1,0:T(8,128)(2,1)S(1)} %collective-permute-done.1.refs_3_.refs_0_), channel_id=1, source_target_pairs={{0,2},{1,3},{2,0},{3,1},{4,6},{5,7},{6,4},{7,5},{8,10},{9,11},{10,... | collective-permute-start | bytes 786440 | tf_op jit(solution)/shard_map/ppermute | solution.py:17
  70.6 2.7 %shard_map.39 = (f32[2,4,128,256]{3,2,1,0:T(8,128)S(1)}, bf16[2,4,128,256]{3,2,1,0:T(8,128)(2,1)S(1)}) custom-call(s32[9]{0:T(128)S(1)} %get-tuple-element.67.choices_ref, bf16[2,512,1024]{2,1,0:T(8,128)(2,1)S(1)} %shard_map.37.lefts_ref, bf16[1024,256]{1,0:T(8,128)(2,1)S(1)} %get-tuple-element.56.refs_0_, bf16[1024,256]{1,0:T(8,128)(2,1)S(1)} %copy-done.5, ...), custom_call_target="tpu_custom_call" | custom-call | flops 1073741824 | bytes 6291456 | tf_op jit(solution)/shard_map/pallas_call | solution.py:117
  74.0 1.7 %collective-permute-start.19 = (bf16[1024,128]{1,0:T(8,128)(2,1)S(1)}, bf16[1024,128]{1,0:T(8,128)(2,1)S(1)}, u32[]{:S(2)}, u32[]{:S(2)}) collective-permute-start(bf16[1024,128]{1,0:T(8,128)(2,1)S(1)} %collective-permute-done.2.refs_4_.refs_0_), channel_id=1, source_target_pairs={{0,2},{1,3},{2,0},{3,1},{4,6},{5,7},{6,4},{7,5},{8,10},{9,11},{10,... | collective-permute-start | bytes 786440 | tf_op jit(solution)/shard_map/ppermute | solution.py:17
  75.8 3.3 %shard_map.41 = (f32[2,4,128,256]{3,2,1,0:T(8,128)S(1)}, bf16[2,4,128,256]{3,2,1,0:T(8,128)(2,1)S(1)}) custom-call(s32[9]{0:T(128)S(1)} %get-tuple-element.67.choices_ref, bf16[2,512,1024]{2,1,0:T(8,128)(2,1)S(1)} %shard_map.37.lefts_ref, bf16[1024,256]{1,0:T(8,128)(2,1)S(1)} %get-tuple-element.32.refs_1_.refs_0_, bf16[1024,256]{1,0:T(8,128)(2,1)S(1)} %copy-done.1, ...), custom_call_target="tpu_custom_call" | custom-call | flops 1073741824 | bytes 6291456 | tf_op jit(solution)/shard_map/pallas_call | solution.py:117
  79.2 7.6 %collective-permute-done.17.refs_1_ = bf16[1024,128]{1,0:T(8,128)(2,1)S(1)} collective-permute-done((bf16[1024,128]{1,0:T(8,128)(2,1)S(1)}, bf16[1024,128]{1,0:T(8,128)(2,1)S(1)}, u32[]{:S(2)}, u32[]{:S(2)}) %collective-permute-start.17) | collective-permute-done | bytes 262176 | tf_op jit(solution)/shard_map/ppermute | solution.py:17
  87.1 1.7 %collective-permute-start.27 = (bf16[1024,128]{1,0:T(8,128)(2,1)S(1)}, bf16[1024,128]{1,0:T(8,128)(2,1)S(1)}, u32[]{:S(2)}, u32[]{:S(2)}) collective-permute-start(bf16[1024,128]{1,0:T(8,128)(2,1)S(1)} %collective-permute-done.19.refs_2_), channel_id=1, source_target_pairs={{0,1},{1,0},{2,3},{3,2},{4,5},{5,4},{6,7},{7,6},{8,9},{9,8},{10,11... | collective-permute-start | bytes 786440 | tf_op jit(solution)/shard_map/ppermute | solution.py:17
  90.9 2.6 %shard_map.38 = (f32[2,4,128,256]{3,2,1,0:T(8,128)S(1)}, bf16[2,4,128,256]{3,2,1,0:T(8,128)(2,1)S(1)}) custom-call(s32[9]{0:T(128)S(1)} %get-tuple-element.66.choices_ref, bf16[2,512,1024]{2,1,0:T(8,128)(2,1)S(1)} %shard_map.37.lefts_ref, bf16[1024,256]{1,0:T(8,128)(2,1)S(1)} %collective-permute-done.refs_2_.refs_0_, ...), custom_call_target="tpu_custom_call" | custom-call | flops 1073741824 | bytes 6291456 | tf_op jit(solution)/shard_map/pallas_call | solution.py:117
  93.6 2.5 %shard_map.40 = (f32[2,4,128,128]{3,2,1,0:T(8,128)S(1)}, bf16[2,4,128,128]{3,2,1,0:T(8,128)(2,1)S(1)}) custom-call(s32[9]{0:T(128)S(1)} %get-tuple-element.66.choices_ref, bf16[2,512,1024]{2,1,0:T(8,128)(2,1)S(1)} %shard_map.37.lefts_ref, bf16[1024,128]{1,0:T(8,128)(2,1)S(1)} %collective-permute-done.1.refs_3_.refs_0_, ...), custom_call_target="tpu_custom_call" | custom-call | flops 536870912 | bytes 4194304 | tf_op jit(solution)/shard_map/pallas_call | solution.py:117
  98.5 2.5 %shard_map.42 = (f32[2,4,128,128]{3,2,1,0:T(8,128)S(1)}, bf16[2,4,128,128]{3,2,1,0:T(8,128)(2,1)S(1)}) custom-call(s32[9]{0:T(128)S(1)} %get-tuple-element.66.choices_ref, bf16[2,512,1024]{2,1,0:T(8,128)(2,1)S(1)} %shard_map.37.lefts_ref, bf16[1024,128]{1,0:T(8,128)(2,1)S(1)} %collective-permute-done.2.refs_4_.refs_0_, ...), custom_call_target="tpu_custom_call" | custom-call | flops 536870912 | bytes 4194304 | tf_op jit(solution)/shard_map/pallas_call | solution.py:117
  105.9 4.5 %collective-permute-done.24 = bf16[1,4,128,256]{3,2,1,0:T(8,128)(2,1)S(1)} collective-permute-done((bf16[1,4,128,256]{3,2,1,0:T(8,128)(2,1)S(1)}, bf16[1,4,128,256]{3,2,1,0:T(8,128)(2,1)S(1)}, u32[]{:S(2)}, u32[]{:S(2)}) %collective-permute-start.24) | collective-permute-done | bytes 262176 | tf_op jit(solution)/shard_map/ppermute | solution.py:17
  110.5 2.8 %collective-permute-done.22 = bf16[1,4,128,128]{3,2,1,0:T(8,128)(2,1)S(1)} collective-permute-done((bf16[1,4,128,128]{3,2,1,0:T(8,128)(2,1)S(1)}, bf16[1,4,128,128]{3,2,1,0:T(8,128)(2,1)S(1)}, u32[]{:S(2)}, u32[]{:S(2)}) %collective-permute-start.22) | collective-permute-done | bytes 131104 | tf_op jit(solution)/shard_map/ppermute | solution.py:17
  113.2 2.8 %collective-permute-done.29 = bf16[1,4,128,128]{3,2,1,0:T(8,128)(2,1)S(1)} collective-permute-done((bf16[1,4,128,128]{3,2,1,0:T(8,128)(2,1)S(1)}, bf16[1,4,128,128]{3,2,1,0:T(8,128)(2,1)S(1)}, u32[]{:S(2)}, u32[]{:S(2)}) %collective-permute-start.29) | collective-permute-done | bytes 131104 | tf_op jit(solution)/shard_map/ppermute | solution.py:17
  119.1 2.1 %collective-permute-done.10 = bf16[1,4,128,256]{3,2,1,0:T(8,128)(2,1)S(1)} collective-permute-done((bf16[1,4,128,256]{3,2,1,0:T(8,128)(2,1)S(1)}, bf16[1,4,128,256]{3,2,1,0:T(8,128)(2,1)S(1)}, u32[]{:S(2)}, u32[]{:S(2)}) %collective-permute-start.10) | collective-permute-done | bytes 262176 | tf_op jit(solution)/shard_map/ppermute | solution.py:17
  123.1 10.9 %collective-permute-done.25 = bf16[4,128,128]{2,1,0:T(8,128)(2,1)S(1)} collective-permute-done((bf16[4,128,128]{2,1,0:T(8,128)(2,1)S(1)}, bf16[4,128,128]{2,1,0:T(8,128)(2,1)S(1)}, u32[]{:S(2)}, u32[]{:S(2)}) %collective-permute-start.25) | collective-permute-done | bytes 131104 | tf_op jit(solution)/shard_map/ppermute | solution.py:17
  134.0 2.8 %collective-permute-done.30 = bf16[4,128,128]{2,1,0:T(8,128)(2,1)S(1)} collective-permute-done((bf16[4,128,128]{2,1,0:T(8,128)(2,1)S(1)}, bf16[4,128,128]{2,1,0:T(8,128)(2,1)S(1)}, u32[]{:S(2)}, u32[]{:S(2)}) %collective-permute-start.30) | collective-permute-done | bytes 131104 | tf_op jit(solution)/shard_map/ppermute | solution.py:17
  137.0 4.5 %collective-permute-done.15 = bf16[4,128,256]{2,1,0:T(8,128)(2,1)S(1)} collective-permute-done((bf16[4,128,256]{2,1,0:T(8,128)(2,1)S(1)}, bf16[4,128,256]{2,1,0:T(8,128)(2,1)S(1)}, u32[]{:S(2)}, u32[]{:S(2)}) %collective-permute-start.15) | collective-permute-done | bytes 262176 | tf_op jit(solution)/shard_map/ppermute | solution.py:17
  (85 shorter events, 30.5 us)
Async XLA Ops:
  2.4 24.9 %collective-permute-start.5 = (bf16[1024,256]{1,0:T(8,128)(2,1)S(1)}, bf16[1024,256]{1,0:T(8,128)(2,1)S(1)}, u32[]{:S(2)}, u32[]{:S(2)}) collective-permute-start(bf16[1024,256]{1,0:T(8,128)(2,1)S(1)} %get-tuple-element.56.refs_0_), channel_id=1, source_target_pairs={{0,2},{1,3},{2,0},{3,1},{4,6},{5,7},{6,4},{7,5},{8,10},{9,11},{10,... | collective-permute-start | bytes 1572872 | tf_op jit(solution)/shard_map/ppermute | solution.py:17
  5.5 21.8 %collective-permute-start.11 = (bf16[1024,256]{1,0:T(8,128)(2,1)S(1)}, bf16[1024,256]{1,0:T(8,128)(2,1)S(1)}, u32[]{:S(2)}, u32[]{:S(2)}) collective-permute-start(bf16[1024,256]{1,0:T(8,128)(2,1)S(1)} %get-tuple-element.56.refs_0_), channel_id=1, source_target_pairs={{0,1},{1,0},{2,3},{3,2},{4,5},{5,4},{6,7},{7,6},{8,9},{9,8},{10,11... | collective-permute-start | bytes 1572872 | tf_op jit(solution)/shard_map/ppermute | solution.py:17
  7.0 25.4 %collective-permute-start = (bf16[1024,256]{1,0:T(8,128)(2,1)S(1)}, bf16[1024,256]{1,0:T(8,128)(2,1)S(1)}, u32[]{:S(2)}, u32[]{:S(2)}) collective-permute-start(bf16[1024,256]{1,0:T(8,128)(2,1)S(1)} %get-tuple-element.57), channel_id=1, source_target_pairs={{0,4},{1,5},{2,6},{3,7},{4,0},{5,1},{6,2},{7,3},{8,12},{9,13},{10,... | collective-permute-start | bytes 1572872 | tf_op jit(solution)/shard_map/ppermute | solution.py:17
  9.6 25.5 %collective-permute-start.3 = (bf16[1024,256]{1,0:T(8,128)(2,1)S(1)}, bf16[1024,256]{1,0:T(8,128)(2,1)S(1)}, u32[]{:S(2)}, u32[]{:S(2)}) collective-permute-start(bf16[1024,256]{1,0:T(8,128)(2,1)S(1)} %get-tuple-element.32.refs_1_.refs_0_), channel_id=1, source_target_pairs={{0,1},{1,0},{2,3},{3,2},{4,5},{5,4},{6,7},{7,6},{8,9},{9,8},{10,11... | collective-permute-start | bytes 1572872 | tf_op jit(solution)/shard_map/ppermute | solution.py:17
  27.4 20.2 %collective-permute-start.6 = (bf16[1024,256]{1,0:T(8,128)(2,1)S(1)}, bf16[1024,256]{1,0:T(8,128)(2,1)}, u32[]{:S(2)}, u32[]{:S(2)}) collective-permute-start(bf16[1024,256]{1,0:T(8,128)(2,1)S(1)} %get-tuple-element.32.refs_1_.refs_0_), channel_id=1, source_target_pairs={{0,2},{1,3},{2,0},{3,1},{4,6},{5,7},{6,4},{7,5},{8,10},{9,11},{10,... | collective-permute-start | bytes 1572872 | tf_op jit(solution)/shard_map/ppermute | solution.py:17
  28.2 23.4 %collective-permute-start.12 = (bf16[1024,256]{1,0:T(8,128)(2,1)S(1)}, bf16[1024,256]{1,0:T(8,128)(2,1)S(1)}, u32[]{:S(2)}, u32[]{:S(2)}) collective-permute-start(bf16[1024,256]{1,0:T(8,128)(2,1)S(1)} %collective-permute-done.5.refs_2_), channel_id=1, source_target_pairs={{0,1},{1,0},{2,3},{3,2},{4,5},{5,4},{6,7},{7,6},{8,9},{9,8},{10,11... | collective-permute-start | bytes 1572872 | tf_op jit(solution)/shard_map/ppermute | solution.py:17
  32.4 15.1 %collective-permute-start.1 = (bf16[1024,128]{1,0:T(8,128)(2,1)S(1)}, bf16[1024,128]{1,0:T(8,128)(2,1)S(1)}, u32[]{:S(2)}, u32[]{:S(2)}) collective-permute-start(bf16[1024,128]{1,0:T(8,128)(2,1)S(1)} %get-tuple-element.29), channel_id=1, source_target_pairs={{0,4},{1,5},{2,6},{3,7},{4,0},{5,1},{6,2},{7,3},{8,12},{9,13},{10,... | collective-permute-start | bytes 786440 | tf_op jit(solution)/shard_map/ppermute | solution.py:17
  35.9 33.1 %collective-permute-start.4 = (bf16[1024,256]{1,0:T(8,128)(2,1)S(1)}, bf16[1024,256]{1,0:T(8,128)(2,1)S(1)}, u32[]{:S(2)}, u32[]{:S(2)}) collective-permute-start(bf16[1024,256]{1,0:T(8,128)(2,1)S(1)} %collective-permute-done.refs_2_.refs_0_), channel_id=1, source_target_pairs={{0,1},{1,0},{2,3},{3,2},{4,5},{5,4},{6,7},{7,6},{8,9},{9,8},{10,11... | collective-permute-start | bytes 1572872 | tf_op jit(solution)/shard_map/ppermute | solution.py:17
  47.5 18.3 %collective-permute-start.7 = (bf16[1024,256]{1,0:T(8,128)(2,1)S(1)}, bf16[1024,256]{1,0:T(8,128)(2,1)S(1)}, u32[]{:S(2)}, u32[]{:S(2)}) collective-permute-start(bf16[1024,256]{1,0:T(8,128)(2,1)S(1)} %collective-permute-done.refs_2_.refs_0_), channel_id=1, source_target_pairs={{0,2},{1,3},{2,0},{3,1},{4,6},{5,7},{6,4},{7,5},{8,10},{9,11},{10,... | collective-permute-start | bytes 1572872 | tf_op jit(solution)/shard_map/ppermute | solution.py:17
  47.5 16.0 %collective-permute-start.2 = (bf16[1024,128]{1,0:T(8,128)(2,1)S(1)}, bf16[1024,128]{1,0:T(8,128)(2,1)S(1)}, u32[]{:S(2)}, u32[]{:S(2)}) collective-permute-start(bf16[1024,128]{1,0:T(8,128)(2,1)S(1)} %get-tuple-element.30), channel_id=1, source_target_pairs={{0,4},{1,5},{2,6},{3,7},{4,0},{5,1},{6,2},{7,3},{8,12},{9,13},{10,... | collective-permute-start | bytes 786440 | tf_op jit(solution)/shard_map/ppermute | solution.py:17
  52.4 21.0 %collective-permute-start.16 = (bf16[1024,256]{1,0:T(8,128)(2,1)}, bf16[1024,256]{1,0:T(8,128)(2,1)}, u32[]{:S(2)}, u32[]{:S(2)}) collective-permute-start(bf16[1024,256]{1,0:T(8,128)(2,1)} %collective-permute-done.6.refs_2_), channel_id=1, source_target_pairs={{0,1},{1,0},{2,3},{3,2},{4,5},{5,4},{6,7},{7,6},{8,9},{9,8},{10,11... | collective-permute-start | bytes 1572872 | tf_op jit(solution)/shard_map/ppermute | solution.py:17
  69.1 19.8 %collective-permute-start.8 = (bf16[1024,256]{1,0:T(8,128)(2,1)S(1)}, bf16[1024,256]{1,0:T(8,128)(2,1)S(1)}, u32[]{:S(2)}, u32[]{:S(2)}) collective-permute-start(bf16[1024,256]{1,0:T(8,128)(2,1)S(1)} %collective-permute-done.7.refs_2_), channel_id=1, source_target_pairs={{0,1},{1,0},{2,3},{3,2},{4,5},{5,4},{6,7},{7,6},{8,9},{9,8},{10,11... | collective-permute-start | bytes 1572872 | tf_op jit(solution)/shard_map/ppermute | solution.py:17
  73.3 15.9 %collective-permute-start.13 = (bf16[2,4,128,256]{3,2,1,0:T(8,128)(2,1)S(1)}, bf16[2,4,128,256]{3,2,1,0:T(8,128)(2,1)S(1)}, u32[]{:S(2)}, u32[]{:S(2)}) collective-permute-start(bf16[2,4,128,256]{3,2,1,0:T(8,128)(2,1)S(1)} %get-tuple-element.39), channel_id=1, source_target_pairs={{0,8},{8,0},{16,24},{24,16},{1,9},{9,1},{17,25},{25,17},{2,10},{10... | collective-permute-start | bytes 1572872 | tf_op jit(solution)/shard_map/ppermute | solution.py:17
  73.3 13.4 %collective-permute-start.17 = (bf16[1024,128]{1,0:T(8,128)(2,1)S(1)}, bf16[1024,128]{1,0:T(8,128)(2,1)S(1)}, u32[]{:S(2)}, u32[]{:S(2)}) collective-permute-start(bf16[1024,128]{1,0:T(8,128)(2,1)S(1)} %collective-permute-done.1.refs_3_.refs_0_), channel_id=1, source_target_pairs={{0,1},{1,0},{2,3},{3,2},{4,5},{5,4},{6,7},{7,6},{8,9},{9,8},{10,11... | collective-permute-start | bytes 786440 | tf_op jit(solution)/shard_map/ppermute | solution.py:17
  74.0 12.7 %collective-permute-start.19 = (bf16[1024,128]{1,0:T(8,128)(2,1)S(1)}, bf16[1024,128]{1,0:T(8,128)(2,1)S(1)}, u32[]{:S(2)}, u32[]{:S(2)}) collective-permute-start(bf16[1024,128]{1,0:T(8,128)(2,1)S(1)} %collective-permute-done.2.refs_4_.refs_0_), channel_id=1, source_target_pairs={{0,2},{1,3},{2,0},{3,1},{4,6},{5,7},{6,4},{7,5},{8,10},{9,11},{10,... | collective-permute-start | bytes 786440 | tf_op jit(solution)/shard_map/ppermute | solution.py:17
  79.1 22.0 %collective-permute-start.23 = (bf16[2,4,128,256]{3,2,1,0:T(8,128)(2,1)S(1)}, bf16[2,4,128,256]{3,2,1,0:T(8,128)(2,1)S(1)}, u32[]{:S(2)}, u32[]{:S(2)}) collective-permute-start(bf16[2,4,128,256]{3,2,1,0:T(8,128)(2,1)S(1)} %get-tuple-element.48), channel_id=1, source_target_pairs={{0,8},{8,0},{16,24},{24,16},{1,9},{9,1},{17,25},{25,17},{2,10},{10... | collective-permute-start | bytes 1572872 | tf_op jit(solution)/shard_map/ppermute | solution.py:17
  89.3 29.8 %collective-permute-start.14 = (bf16[1,4,128,256]{3,2,1,0:T(8,128)(2,1)S(1)}, bf16[1,4,128,256]{3,2,1,0:T(8,128)(2,1)S(1)}, u32[]{:S(2)}, u32[]{:S(2)}) collective-permute-start(bf16[1,4,128,256]{3,2,1,0:T(8,128)(2,1)S(1)} %slice.116), channel_id=1, source_target_pairs={{0,16},{8,24},{16,0},{24,8},{1,17},{9,25},{17,1},{25,9},{2,18},{10... | collective-permute-start | bytes 786440 | tf_op jit(solution)/shard_map/ppermute | solution.py:17
  93.6 11.6 %collective-permute-start.9 = (bf16[2,4,128,256]{3,2,1,0:T(8,128)(2,1)S(1)}, bf16[2,4,128,256]{3,2,1,0:T(8,128)(2,1)S(1)}, u32[]{:S(2)}, u32[]{:S(2)}) collective-permute-start(bf16[2,4,128,256]{3,2,1,0:T(8,128)(2,1)S(1)} %get-tuple-element.36), channel_id=1, source_target_pairs={{0,8},{8,0},{16,24},{24,16},{1,9},{9,1},{17,25},{25,17},{2,10},{10... | collective-permute-start | bytes 1572872 | tf_op jit(solution)/shard_map/ppermute | solution.py:17
  102.9 10.3 %collective-permute-start.22 = (bf16[1,4,128,128]{3,2,1,0:T(8,128)(2,1)S(1)}, bf16[1,4,128,128]{3,2,1,0:T(8,128)(2,1)S(1)}, u32[]{:S(2)}, u32[]{:S(2)}) collective-permute-start(bf16[1,4,128,128]{3,2,1,0:T(8,128)(2,1)S(1)} %slice.119), channel_id=1, source_target_pairs={{0,16},{8,24},{16,0},{24,8},{1,17},{9,25},{17,1},{25,9},{2,18},{10... | collective-permute-start | bytes 393224 | tf_op jit(solution)/shard_map/ppermute | solution.py:17
  103.6 12.4 %collective-permute-start.29 = (bf16[1,4,128,128]{3,2,1,0:T(8,128)(2,1)S(1)}, bf16[1,4,128,128]{3,2,1,0:T(8,128)(2,1)S(1)}, u32[]{:S(2)}, u32[]{:S(2)}) collective-permute-start(bf16[1,4,128,128]{3,2,1,0:T(8,128)(2,1)S(1)} %slice.118), channel_id=1, source_target_pairs={{0,16},{8,24},{16,0},{24,8},{1,17},{9,25},{17,1},{25,9},{2,18},{10... | collective-permute-start | bytes 393224 | tf_op jit(solution)/shard_map/ppermute | solution.py:17
  105.4 15.9 %collective-permute-start.10 = (bf16[1,4,128,256]{3,2,1,0:T(8,128)(2,1)S(1)}, bf16[1,4,128,256]{3,2,1,0:T(8,128)(2,1)S(1)}, u32[]{:S(2)}, u32[]{:S(2)}) collective-permute-start(bf16[1,4,128,256]{3,2,1,0:T(8,128)(2,1)S(1)} %slice.117), channel_id=1, source_target_pairs={{0,16},{8,24},{16,0},{24,8},{1,17},{9,25},{17,1},{25,9},{2,18},{10... | collective-permute-start | bytes 786440 | tf_op jit(solution)/shard_map/ppermute | solution.py:17
  116.1 17.9 %collective-permute-start.25 = (bf16[4,128,128]{2,1,0:T(8,128)(2,1)S(1)}, bf16[4,128,128]{2,1,0:T(8,128)(2,1)S(1)}, u32[]{:S(2)}, u32[]{:S(2)}) collective-permute-start(bf16[4,128,128]{2,1,0:T(8,128)(2,1)S(1)} %get-tuple-element.60), channel_id=1, source_target_pairs={{0,4},{1,5},{2,6},{3,7},{4,0},{5,1},{6,2},{7,3},{8,12},{9,13},{10,... | collective-permute-start | bytes 393224 | tf_op jit(solution)/shard_map/ppermute | solution.py:17
  117.8 19.0 %collective-permute-start.30 = (bf16[4,128,128]{2,1,0:T(8,128)(2,1)S(1)}, bf16[4,128,128]{2,1,0:T(8,128)(2,1)S(1)}, u32[]{:S(2)}, u32[]{:S(2)}) collective-permute-start(bf16[4,128,128]{2,1,0:T(8,128)(2,1)S(1)} %get-tuple-element.61), channel_id=1, source_target_pairs={{0,4},{1,5},{2,6},{3,7},{4,0},{5,1},{6,2},{7,3},{8,12},{9,13},{10,... | collective-permute-start | bytes 393224 | tf_op jit(solution)/shard_map/ppermute | solution.py:17
  121.4 20.0 %collective-permute-start.15 = (bf16[4,128,256]{2,1,0:T(8,128)(2,1)S(1)}, bf16[4,128,256]{2,1,0:T(8,128)(2,1)S(1)}, u32[]{:S(2)}, u32[]{:S(2)}) collective-permute-start(bf16[4,128,256]{2,1,0:T(8,128)(2,1)S(1)} %select_convert_fusion), channel_id=1, source_target_pairs={{0,4},{1,5},{2,6},{3,7},{4,0},{5,1},{6,2},{7,3},{8,12},{9,13},{10,... | collective-permute-start | bytes 786440 | tf_op jit(solution)/shard_map/ppermute | solution.py:17
  (16 other events, 177.0 us)

commit v5 on v4

v5 whole, which is shorter than its diff:
```python
import jax
import jax.numpy as jnp
from jax import lax
from jax.experimental import pallas as pl
from jax.experimental.pallas import tpu as pltpu
from jax.sharding import PartitionSpec as P

ROUNDS = 4
OWN_WIDTHS = (2, 2)
CROSSING_WIDTHS = (2, 2)
MATE_WIDTHS = (2, 1, 1)
NEAR_FIRST = (3,)
URGENCY = (0, 2, 1, 3, 4)
BATCHES = (((0,), (2,)), ((1,),), ((3, 4),))
VMEM = pl.BlockSpec(memory_space=pltpu.VMEM)
PARAMS = pltpu.CompilerParams(vmem_limit_bytes=40 * 2**20)


def exchange(part, axis, mask):
    return lax.ppermute(part, axis, [(i, i ^ mask) for i in range(lax.axis_size(axis))])


def behind(value, earlier):
    return value if earlier is None else lax.optimization_barrier((value, earlier))[0]


def hops_in_order(widths, cut):
    waiting = []
    for piece in URGENCY:
        bits, held = [1 << n for n in range(cut.bit_length() - 1)], [0]
        for bit in bits if piece in NEAR_FIRST else reversed(bits):
            waiting += [(piece, low, bit) for low in held]
            held += [low | bit for low in held]
    ready, crossed = {}, 0
    for piece, width in enumerate(widths):
        crossed += 2 * width if piece >= len(OWN_WIDTHS) else 0
        ready[piece, 0] = crossed
    free, ordered = {}, []
    while waiting:
        def start_of(hop):
            return max(free.get(hop[2], 0), ready[hop[:2]])

        able = [hop for hop in waiting if hop[:2] in ready]
        hop = min(able, key=lambda one: (start_of(one), waiting.index(one)))
        piece, low, bit = hop
        shared = 2 if bit == cut // 2 and start_of(hop) < crossed else 1
        free[bit] = ready[piece, low | bit] = start_of(hop) + shared * widths[piece]
        waiting.remove(hop)
        ordered.append(hop)
    return ordered


def turned(own, mate):
    cells = own[0].shape[0]
    group = sum(piece.shape[1] for piece in own)

    def kernel(*refs):
        out_ref = refs[-1]
        for which, some in enumerate((refs[: len(own)], refs[len(own) : -1])):
            first = 0
            for ref in some:
                out_ref[which, first : first + ref.shape[1], :] = ref[...].T
                first += ref.shape[1]

    return pl.pallas_call(
        kernel,
        out_shape=jax.ShapeDtypeStruct((2, group, cells), own[0].dtype),
        in_specs=[VMEM] * (len(own) + len(mate)),
        out_specs=VMEM,
        compiler_params=PARAMS,
        cost_estimate=pl.CostEstimate(
            flops=0, bytes_accessed=8 * group * cells, transcendentals=0
        ),
    )(*own, *mate)


def products(choices, lefts, batch, scale_factor):
    slab_count = lax.axis_size("space")
    group, cells = lefts.shape[1:]
    widths = [sum(blocks[0].shape[1] for blocks in pieces) for _, pieces in batch]
    rows = group // slab_count
    arrays = [block for _, pieces in batch for blocks in pieces for block in blocks]

    def kernel(choices_ref, lefts_ref, *refs):
        waiting = list(refs[: len(arrays)])
        even_ref, odd_ref, picked, tile = refs[len(arrays) :]
        first = 0
        for (mates, pieces), width in zip(batch, widths):
            sources = [[waiting.pop(0) for _ in blocks] for blocks in pieces]
            columns = pl.ds(first, width)
            first += width

            def one_round(round_number, carry):
                begin = 0
                for block_refs in sources:
                    end = begin + block_refs[0].shape[1]
                    for number, block_ref in enumerate(block_refs):

                        @pl.when(choices_ref[round_number] == number)
                        def _():
                            picked[:, begin:end] = block_ref[...]

                    begin = end
                side = choices_ref[ROUNDS + round_number]
                left = lefts_ref[1 - side if mates else side]
                tile[:, :width] = scale_factor * jnp.dot(
                    left, picked[:, :width], preferred_element_type=jnp.float32
                )
                for number in range(slab_count):
                    start = jnp.bitwise_xor(choices_ref[2 * ROUNDS], number) * rows
                    part = tile[pl.ds(pl.multiple_of(start, rows), rows), :width]
                    out_ref = odd_ref if number % 2 else even_ref
                    out_ref[number // 2, round_number, :, columns] = part.astype(out_ref.dtype)
                return carry

            lax.fori_loop(0, ROUNDS, one_round, 0)

    shape = (slab_count // 2, ROUNDS, rows, sum(widths))
    return pl.pallas_call(
        kernel,
        out_shape=[jax.ShapeDtypeStruct(shape, kind) for kind in (jnp.float32, jnp.bfloat16)],
        in_specs=[pl.BlockSpec(memory_space=pltpu.SMEM)] + [VMEM] * (1 + len(arrays)),
        out_specs=[VMEM, VMEM],
        scratch_shapes=[
            pltpu.VMEM((cells, max(widths)), jnp.bfloat16),
            pltpu.VMEM((group, max(widths)), jnp.float32),
        ],
        compiler_params=PARAMS,
        cost_estimate=pl.CostEstimate(
            flops=2 * ROUNDS * group * cells * sum(widths),
            bytes_accessed=2 * lefts.size
            + 2 * sum(array.size for array in arrays)
            + 4 * ROUNDS * group * sum(widths),
            transcendentals=0,
        ),
    )(choices, lefts, *arrays)


def halved(keep, send, bit):
    return keep + exchange(send, "space", bit).astype(jnp.float32)


def summed(total):
    bit = 2
    while len(total) > 1:
        total = halved(total[0::2], total[1::2].astype(jnp.bfloat16), bit)
        bit *= 2
    return total[0]


def body(snapshots, volume, masks):
    slab_count = lax.axis_size("space")
    groups = lax.axis_size("snap")
    cut = groups // 2
    cells, group = snapshots.shape
    quarter = group // 4
    scale_factor = float(cells * slab_count) ** (-0.5)
    half = cells // 2
    place = lax.axis_index("snap").astype(jnp.int32)
    upper = (place >= cut).astype(jnp.int32)
    roots = jnp.sqrt(volume)[:, None]

    def pieces_of(side, widths):
        scale = lax.dynamic_slice_in_dim(roots, side * half, half)
        found, first = [], 0
        for width in widths:
            part = lax.dynamic_slice(
                snapshots, (side * half, first * quarter), (half, width * quarter)
            )
            found.append((part.astype(jnp.float32) * scale).astype(jnp.bfloat16))
            first += width
        return found

    crossed = []
    for piece in pieces_of(1 - upper, CROSSING_WIDTHS):
        crossed.append(exchange(behind(piece, crossed[-1] if crossed else None), "snap", cut))
    own = pieces_of(upper, OWN_WIDTHS)
    lefts = turned(own, crossed)
    mate = []
    for width in MATE_WIDTHS:
        first = sum(piece.shape[1] for piece in mate)
        for piece in crossed:
            if first < piece.shape[1]:
                break
            first -= piece.shape[1]
        mate.append(lax.slice_in_dim(piece, first, first + width * quarter, axis=1))

    low = jnp.bitwise_and(masks, cut - 1)
    crossing = (masks >= cut).astype(jnp.int32)
    me = lax.axis_index("space").astype(jnp.int32)[None]
    choices = jnp.concatenate([low, crossing, me])
    swap = (crossing == 1)[:, None, None]

    held = [{0: piece} for piece in own + mate]
    sent = {}
    halves, given, sums, columns, back = [], [], {}, [], []

    def add_batch():
        lists = BATCHES[len(halves)]
        batch = [
            (numbers[0] >= len(own), [[held[n][low] for low in range(cut)] for n in numbers])
            for numbers in lists
        ]
        earlier = (given[0], halves[-1]) if lists == BATCHES[-1] else None
        even, odd = products(behind(choices, earlier), lefts, batch, scale_factor)
        halves.append(halved(even, odd, 1))
        total = summed(halves[-1])
        taken = 0
        for (mates, pieces), numbers in zip(batch, lists):
            width = sum(found[0].shape[1] for found in pieces)
            part = lax.slice_in_dim(total, taken, taken + width, axis=2)
            taken += width
            if not mates:
                sums[numbers[0]] = part
                continue
            own_part = sums[len(columns)]
            keep = jnp.where(swap, part, own_part)
            given.append(jnp.where(swap, own_part, part).astype(jnp.bfloat16))
            back.append(exchange(behind(given[-1], back[-1] if back else None), "snap", cut))
            columns.append(keep + back[-1].astype(jnp.float32))

    for piece, low, bit in hops_in_order(OWN_WIDTHS + MATE_WIDTHS, cut):
        earlier = sent.setdefault(bit, [])
        depth = 2 if bit == 1 else 1
        ties = earlier[-depth] if len(earlier) >= depth else None
        held[piece][low | bit] = exchange(behind(held[piece][low], ties), "snap", bit)
        earlier.append(held[piece][low | bit])
        while len(halves) < len(BATCHES) and all(
            len(held[n]) == cut for numbers in BATCHES[len(halves)] for n in numbers
        ):
            add_batch()
    return jnp.concatenate(columns, axis=2)[:, None]


def solution(mesh):
    in_specs = (P("space", "snap"), P("space"), P())
    out_specs = P(None, "snap", "space", None)
    return jax.shard_map(body, mesh=mesh, in_specs=in_specs, out_specs=out_specs, check_vma=False)
```

time: 143 us -> 144 us (level)
  waiting for transfers between devices: 80.3 us -> 98.9 us
  starting transfers between devices: 39.3 us -> 26.4 us
  Pallas kernels: 14.3 us -> 11.7 us
  local copies, waits for them, and re-layouts: 3.28 us -> 0.87 us
    ppermute x31 -> x25, waiting for transfers between devices: 80.3 us -> 98.9 us  [exchange(): lax.ppermute(part, axis, [(i, i ^ mask) for i in range(lax.axis_size(axis...]
    ppermute x31 -> x25, starting transfers between devices: 39.3 us -> 26.4 us  [exchange(): lax.ppermute(part, axis, [(i, i ^ mask) for i in range(lax.axis_size(axis...]
    pallas_call x5 -> x3, Pallas kernels: 13.7 us -> 11.1 us  [products(): pl.pallas_call(kernel, out_shape=[jax.ShapeDtypeStruct(shape, kind) for k...]
    unnamed x18 -> x2, local copies, waits for them, and re-layouts: 2.45 us -> 0.01 us
    convert_element_type x2 -> x1, other arithmetic: 2.94 us -> 2.77 us  [pieces_of(): found.append((part.astype(jnp.float32) * scale).astype(jnp.bfloat16))]
  transfers between devices with their start and end apart: 31 -> 25, of which waited for: 15 -> 17; matrix products, arithmetic and copies ran while one was open for 2% -> 1% of each run, Pallas kernels for 10% -> 6%
where the time goes in v5:
time: 144 us; the launch traced here: 143 us
  waiting for transfers between devices  98.9 us (69%)
  starting transfers between devices  26.4 us (18%)
  Pallas kernels  11.7 us (8%)
  other arithmetic  5.42 us (4%)
    ppermute x25, waiting for transfers between devices, exchange(): lax.ppermute(part, axis, [(i, i ^ mask) for i in range(lax.axis_size(axis...  98.9 us
    ppermute x25, starting transfers between devices, exchange(): lax.ppermute(part, axis, [(i, i ^ mask) for i in range(lax.axis_size(axis...  26.4 us
    pallas_call x3, Pallas kernels, products(): pl.pallas_call(kernel, out_shape=[jax.ShapeDtypeStruct(shape, kind) for k...  11.1 us
  transfers between devices with their start and end apart: 25, of which 17 were waited for; matrix products, arithmetic and copies ran while one was open for 1% of the time, Pallas kernels for 6%

profile of v5, /device:TPU:0, one launch (start us, length us, event | category | flops | bytes accessed | tf_op | source)
XLA Modules:
  0.0 143.5 jit_solution(10322809346183222531)
XLA Ops:
  0.7 2.8 %multiply_convert_fusion = (bf16[1024,256]{1,0:T(8,128)(2,1)}, bf16[1024,256]{1,0:T(8,128)(2,1)S(1)}, bf16[1024,256]{1,0:T(8,128)(2,1)S(1)}, bf16[1024,256]{1,0:T(8,128)(2,1)S(1)}) fusion(bf16[2048,512]{1,0:T(8,128)(2,1)} %param.3, s32[]{:T(128)S(6)} %select_n.21, f32[1024]{0:T(1024)S(1)} %get-tuple-element.55, f32[1024]{0:T(1024)S(1)} %get-tuple-element.56, ...), kind=kLoop, calls=%fused_computation.7 | loop fusion | flops 3145728 | bytes 4202504 | tf_op jit(solution)/shard_map/convert_element_type | solution.py:170
  3.5 2.9 %collective-permute-start.2 = (bf16[1024,256]{1,0:T(8,128)(2,1)S(1)}, bf16[1024,256]{1,0:T(8,128)(2,1)S(1)}, u32[]{:S(2)}, u32[]{:S(2)}) collective-permute-start(bf16[1024,256]{1,0:T(8,128)(2,1)S(1)} %get-tuple-element.51.refs_0_), channel_id=1, source_target_pairs={{0,1},{1,0},{2,3},{3,2},{4,5},{5,4},{6,7},{7,6},{8,9},{9,8},{10,11... | collective-permute-start | bytes 1572872 | tf_op jit(solution)/shard_map/ppermute | solution.py:20
  6.4 1.6 %collective-permute-start.3 = (bf16[1024,256]{1,0:T(8,128)(2,1)S(1)}, bf16[1024,256]{1,0:T(8,128)(2,1)S(1)}, u32[]{:S(2)}, u32[]{:S(2)}) collective-permute-start(bf16[1024,256]{1,0:T(8,128)(2,1)S(1)} %get-tuple-element.51.refs_0_), channel_id=1, source_target_pairs={{0,2},{1,3},{2,0},{3,1},{4,6},{5,7},{6,4},{7,5},{8,10},{9,11},{10,... | collective-permute-start | bytes 1572872 | tf_op jit(solution)/shard_map/ppermute | solution.py:20
  8.0 2.6 %collective-permute-start = (bf16[1024,256]{1,0:T(8,128)(2,1)S(1)}, bf16[1024,256]{1,0:T(8,128)(2,1)S(1)}, u32[]{:S(2)}, u32[]{:S(2)}) collective-permute-start(bf16[1024,256]{1,0:T(8,128)(2,1)S(1)} %get-tuple-element.48), channel_id=1, source_target_pairs={{0,4},{1,5},{2,6},{3,7},{4,0},{5,1},{6,2},{7,3},{8,12},{9,13},{10,... | collective-permute-start | bytes 1572872 | tf_op jit(solution)/shard_map/ppermute | solution.py:20
  11.1 8.0 %collective-permute-done.2.refs_1_ = bf16[1024,256]{1,0:T(8,128)(2,1)S(1)} collective-permute-done((bf16[1024,256]{1,0:T(8,128)(2,1)S(1)}, bf16[1024,256]{1,0:T(8,128)(2,1)S(1)}, u32[]{:S(2)}, u32[]{:S(2)}) %collective-permute-start.2) | collective-permute-done | bytes 524320 | tf_op jit(solution)/shard_map/ppermute | solution.py:20
  19.2 11.8 %collective-permute-done.3.refs_2_ = bf16[1024,256]{1,0:T(8,128)(2,1)S(1)} collective-permute-done((bf16[1024,256]{1,0:T(8,128)(2,1)S(1)}, bf16[1024,256]{1,0:T(8,128)(2,1)S(1)}, u32[]{:S(2)}, u32[]{:S(2)}) %collective-permute-start.3) | collective-permute-done | bytes 524320 | tf_op jit(solution)/shard_map/ppermute | solution.py:20
  31.3 2.0 %collective-permute-done.refs_2_.refs_4_ = bf16[1024,256]{1,0:T(8,128)(2,1)S(1)} collective-permute-done((bf16[1024,256]{1,0:T(8,128)(2,1)S(1)}, bf16[1024,256]{1,0:T(8,128)(2,1)S(1)}, u32[]{:S(2)}, u32[]{:S(2)}) %collective-permute-start) | collective-permute-done | bytes 524320 | tf_op jit(solution)/shard_map/ppermute | solution.py:20
  33.7 2.7 %collective-permute-start.1 = (bf16[1024,256]{1,0:T(8,128)(2,1)}, bf16[1024,256]{1,0:T(8,128)(2,1)S(1)}, u32[]{:S(2)}, u32[]{:S(2)}) collective-permute-start(bf16[1024,256]{1,0:T(8,128)(2,1)} %get-tuple-element.26), channel_id=1, source_target_pairs={{0,4},{1,5},{2,6},{3,7},{4,0},{5,1},{6,2},{7,3},{8,12},{9,13},{10,... | collective-permute-start | bytes 1572872 | tf_op jit(solution)/shard_map/ppermute | solution.py:20
  36.9 9.0 %collective-permute-done.4.refs_3_ = bf16[1024,256]{1,0:T(8,128)(2,1)} collective-permute-done((bf16[1024,256]{1,0:T(8,128)(2,1)S(1)}, bf16[1024,256]{1,0:T(8,128)(2,1)}, u32[]{:S(2)}, u32[]{:S(2)}) %collective-permute-start.4) | collective-permute-done | bytes 524320 | tf_op jit(solution)/shard_map/ppermute | solution.py:20
  45.9 8.5 %collective-permute-done.7.refs_6_ = bf16[1024,256]{1,0:T(8,128)(2,1)} collective-permute-done((bf16[1024,256]{1,0:T(8,128)(2,1)S(1)}, bf16[1024,256]{1,0:T(8,128)(2,1)}, u32[]{:S(2)}, u32[]{:S(2)}) %collective-permute-start.7) | collective-permute-done | bytes 524320 | tf_op jit(solution)/shard_map/ppermute | solution.py:20
  55.3 3.1 %collective-permute-done.1.refs_3_ = bf16[1024,256]{1,0:T(8,128)(2,1)S(1)} collective-permute-done((bf16[1024,256]{1,0:T(8,128)(2,1)}, bf16[1024,256]{1,0:T(8,128)(2,1)S(1)}, u32[]{:S(2)}, u32[]{:S(2)}) %collective-permute-start.1) | collective-permute-done | bytes 524320 | tf_op jit(solution)/shard_map/ppermute | solution.py:20
  59.0 6.9 %collective-permute-done.8.refs_7_ = bf16[1024,256]{1,0:T(8,128)(2,1)S(1)} collective-permute-done((bf16[1024,256]{1,0:T(8,128)(2,1)}, bf16[1024,256]{1,0:T(8,128)(2,1)S(1)}, u32[]{:S(2)}, u32[]{:S(2)}) %collective-permute-start.8) | collective-permute-done | bytes 524320 | tf_op jit(solution)/shard_map/ppermute | solution.py:20
  65.9 5.5 %shard_map.38 = (f32[2,4,128,512]{3,2,1,0:T(8,128)S(1)}, bf16[2,4,128,512]{3,2,1,0:T(8,128)(2,1)S(1)}) custom-call(s32[9]{0:T(128)S(1)} %pad_add_fusion.choices_ref, bf16[2,512,1024]{2,1,0:T(8,128)(2,1)S(1)} %shard_map.37.lefts_ref, bf16[1024,256]{1,0:T(8,128)(2,1)S(1)} %get-tuple-element.51.refs_0_, bf16[1024,256]{1,0:T(8,128)(2,1)S(1)} %collective-permute-done.2.refs_1_, ...), custom_call_target="tpu_custom_call" | custom-call | flops 2147483648 | bytes 10485760 | tf_op jit(solution)/shard_map/pallas_call | solution.py:119
  73.8 7.1 %collective-permute-done.16.refs_2_ = bf16[1024,128]{1,0:T(8,128)(2,1)S(1)} collective-permute-done((bf16[1024,128]{1,0:T(8,128)(2,1)S(1)}, bf16[1024,128]{1,0:T(8,128)(2,1)S(1)}, u32[]{:S(2)}, u32[]{:S(2)}) %collective-permute-start.16) | collective-permute-done | bytes 262176 | tf_op jit(solution)/shard_map/ppermute | solution.py:20
  81.2 5.1 %collective-permute-done.13.refs_3_ = bf16[1024,256]{1,0:T(8,128)(2,1)S(1)} collective-permute-done((bf16[1024,256]{1,0:T(8,128)(2,1)S(1)}, bf16[1024,256]{1,0:T(8,128)(2,1)S(1)}, u32[]{:S(2)}, u32[]{:S(2)}) %collective-permute-start.13) | collective-permute-done | bytes 524320 | tf_op jit(solution)/shard_map/ppermute | solution.py:20
  86.3 2.6 %shard_map.39 = (f32[2,4,128,256]{3,2,1,0:T(8,128)S(1)}, bf16[2,4,128,256]{3,2,1,0:T(8,128)(2,1)S(1)}) custom-call(s32[9]{0:T(128)S(1)} %pad_add_fusion.choices_ref, bf16[2,512,1024]{2,1,0:T(8,128)(2,1)S(1)} %shard_map.37.lefts_ref, bf16[1024,256]{1,0:T(8,128)(2,1)S(1)} %get-tuple-element.33.refs_1_.refs_0_, ...), custom_call_target="tpu_custom_call" | custom-call | flops 1073741824 | bytes 6291456 | tf_op jit(solution)/shard_map/pallas_call | solution.py:119
  89.5 1.6 %collective-permute-start.10 = (bf16[1,4,128,512]{3,2,1,0:T(8,128)(2,1)S(1)}, bf16[1,4,128,512]{3,2,1,0:T(8,128)(2,1)S(1)}, u32[]{:S(2)}, u32[]{:S(2)}) collective-permute-start(bf16[1,4,128,512]{3,2,1,0:T(8,128)(2,1)S(1)} %slice.83), channel_id=1, source_target_pairs={{0,16},{8,24},{16,0},{24,8},{1,17},{9,25},{17,1},{25,9},{2,18},{10... | collective-permute-start | bytes 1572872 | tf_op jit(solution)/shard_map/ppermute | solution.py:20
  93.6 10.2 %collective-permute-done.10 = bf16[1,4,128,512]{3,2,1,0:T(8,128)(2,1)S(1)} collective-permute-done((bf16[1,4,128,512]{3,2,1,0:T(8,128)(2,1)S(1)}, bf16[1,4,128,512]{3,2,1,0:T(8,128)(2,1)S(1)}, u32[]{:S(2)}, u32[]{:S(2)}) %collective-permute-start.10) | collective-permute-done | bytes 524320 | tf_op jit(solution)/shard_map/ppermute | solution.py:20
  105.2 3.0 %shard_map.40 = (f32[2,4,128,256]{3,2,1,0:T(8,128)S(1)}, bf16[2,4,128,256]{3,2,1,0:T(8,128)(2,1)S(1)}) custom-call(s32[9]{0:T(128)S(1)} %pad_add_fusion.choices_ref, bf16[2,512,1024]{2,1,0:T(8,128)(2,1)S(1)} %shard_map.37.lefts_ref, bf16[1024,128]{1,0:T(8,128)(2,1)S(1)} %get-tuple-element.39.refs_0_, bf16[1024,128]{1,0:T(8,128)(2,1)S(1)} %collective-permute-done.15.refs_1_, ...), custom_call_target="tpu_custom_call" | custom-call | flops 1073741824 | bytes 6291456 | tf_op jit(solution)/shard_map/pallas_call | solution.py:119
  108.3 1.3 collective-permute-start.23
  111.6 5.0 %collective-permute-start.11 = (bf16[4,128,256]{2,1,0:T(8,128)(2,1)S(1)}, bf16[4,128,256]{2,1,0:T(8,128)(2,1)S(1)}, u32[]{:S(2)}, u32[]{:S(2)}) collective-permute-start(bf16[4,128,256]{2,1,0:T(8,128)(2,1)S(1)} %select_convert_fusion.1), channel_id=1, source_target_pairs={{0,4},{1,5},{2,6},{3,7},{4,0},{5,1},{6,2},{7,3},{8,12},{9,13},{10,... | collective-permute-start | bytes 786440 | tf_op jit(solution)/shard_map/ppermute | solution.py:20
  117.4 5.2 %collective-permute-done.22 = bf16[1,4,128,256]{3,2,1,0:T(8,128)(2,1)S(1)} collective-permute-done((bf16[1,4,128,256]{3,2,1,0:T(8,128)(2,1)S(1)}, bf16[1,4,128,256]{3,2,1,0:T(8,128)(2,1)S(1)}, u32[]{:S(2)}, u32[]{:S(2)}) %collective-permute-start.22) | collective-permute-done | bytes 262176 | tf_op jit(solution)/shard_map/ppermute | solution.py:20
  122.9 5.4 %collective-permute-done.11 = bf16[4,128,256]{2,1,0:T(8,128)(2,1)S(1)} collective-permute-done((bf16[4,128,256]{2,1,0:T(8,128)(2,1)S(1)}, bf16[4,128,256]{2,1,0:T(8,128)(2,1)S(1)}, u32[]{:S(2)}, u32[]{:S(2)}) %collective-permute-start.11) | collective-permute-done | bytes 262176 | tf_op jit(solution)/shard_map/ppermute | solution.py:20
  128.3 13.7 %collective-permute-done.24 = bf16[4,128,256]{2,1,0:T(8,128)(2,1)S(1)} collective-permute-done((bf16[4,128,256]{2,1,0:T(8,128)(2,1)S(1)}, bf16[4,128,256]{2,1,0:T(8,128)(2,1)S(1)}, u32[]{:S(2)}, u32[]{:S(2)}) %collective-permute-start.24) | collective-permute-done | bytes 262176 | tf_op jit(solution)/shard_map/ppermute | solution.py:20
  (50 shorter events, 15.5 us)
Async XLA Ops:
  3.5 15.7 %collective-permute-start.2 = (bf16[1024,256]{1,0:T(8,128)(2,1)S(1)}, bf16[1024,256]{1,0:T(8,128)(2,1)S(1)}, u32[]{:S(2)}, u32[]{:S(2)}) collective-permute-start(bf16[1024,256]{1,0:T(8,128)(2,1)S(1)} %get-tuple-element.51.refs_0_), channel_id=1, source_target_pairs={{0,1},{1,0},{2,3},{3,2},{4,5},{5,4},{6,7},{7,6},{8,9},{9,8},{10,11... | collective-permute-start | bytes 1572872 | tf_op jit(solution)/shard_map/ppermute | solution.py:20
  6.4 24.5 %collective-permute-start.3 = (bf16[1024,256]{1,0:T(8,128)(2,1)S(1)}, bf16[1024,256]{1,0:T(8,128)(2,1)S(1)}, u32[]{:S(2)}, u32[]{:S(2)}) collective-permute-start(bf16[1024,256]{1,0:T(8,128)(2,1)S(1)} %get-tuple-element.51.refs_0_), channel_id=1, source_target_pairs={{0,2},{1,3},{2,0},{3,1},{4,6},{5,7},{6,4},{7,5},{8,10},{9,11},{10,... | collective-permute-start | bytes 1572872 | tf_op jit(solution)/shard_map/ppermute | solution.py:20
  8.0 25.3 %collective-permute-start = (bf16[1024,256]{1,0:T(8,128)(2,1)S(1)}, bf16[1024,256]{1,0:T(8,128)(2,1)S(1)}, u32[]{:S(2)}, u32[]{:S(2)}) collective-permute-start(bf16[1024,256]{1,0:T(8,128)(2,1)S(1)} %get-tuple-element.48), channel_id=1, source_target_pairs={{0,4},{1,5},{2,6},{3,7},{4,0},{5,1},{6,2},{7,3},{8,12},{9,13},{10,... | collective-permute-start | bytes 1572872 | tf_op jit(solution)/shard_map/ppermute | solution.py:20
  10.6 25.8 %collective-permute-start.5 = (bf16[1024,256]{1,0:T(8,128)(2,1)S(1)}, bf16[1024,256]{1,0:T(8,128)(2,1)S(1)}, u32[]{:S(2)}, u32[]{:S(2)}) collective-permute-start(bf16[1024,256]{1,0:T(8,128)(2,1)S(1)} %get-tuple-element.33.refs_1_.refs_0_), channel_id=1, source_target_pairs={{0,1},{1,0},{2,3},{3,2},{4,5},{5,4},{6,7},{7,6},{8,9},{9,8},{10,11... | collective-permute-start | bytes 1572872 | tf_op jit(solution)/shard_map/ppermute | solution.py:20
  30.9 15.0 %collective-permute-start.4 = (bf16[1024,256]{1,0:T(8,128)(2,1)S(1)}, bf16[1024,256]{1,0:T(8,128)(2,1)}, u32[]{:S(2)}, u32[]{:S(2)}) collective-permute-start(bf16[1024,256]{1,0:T(8,128)(2,1)S(1)} %collective-permute-done.3.refs_2_), channel_id=1, source_target_pairs={{0,1},{1,0},{2,3},{3,2},{4,5},{5,4},{6,7},{7,6},{8,9},{9,8},{10,11... | collective-permute-start | bytes 1572872 | tf_op jit(solution)/shard_map/ppermute | solution.py:20
  33.3 21.1 %collective-permute-start.7 = (bf16[1024,256]{1,0:T(8,128)(2,1)S(1)}, bf16[1024,256]{1,0:T(8,128)(2,1)}, u32[]{:S(2)}, u32[]{:S(2)}) collective-permute-start(bf16[1024,256]{1,0:T(8,128)(2,1)S(1)} %collective-permute-done.refs_2_.refs_4_), channel_id=1, source_target_pairs={{0,2},{1,3},{2,0},{3,1},{4,6},{5,7},{6,4},{7,5},{8,10},{9,11},{10,... | collective-permute-start | bytes 1572872 | tf_op jit(solution)/shard_map/ppermute | solution.py:20
  33.7 24.6 %collective-permute-start.1 = (bf16[1024,256]{1,0:T(8,128)(2,1)}, bf16[1024,256]{1,0:T(8,128)(2,1)S(1)}, u32[]{:S(2)}, u32[]{:S(2)}) collective-permute-start(bf16[1024,256]{1,0:T(8,128)(2,1)} %get-tuple-element.26), channel_id=1, source_target_pairs={{0,4},{1,5},{2,6},{3,7},{4,0},{5,1},{6,2},{7,3},{8,12},{9,13},{10,... | collective-permute-start | bytes 1572872 | tf_op jit(solution)/shard_map/ppermute | solution.py:20
  36.4 22.6 %collective-permute-start.6 = (bf16[1024,256]{1,0:T(8,128)(2,1)S(1)}, bf16[1024,256]{1,0:T(8,128)(2,1)S(1)}, u32[]{:S(2)}, u32[]{:S(2)}) collective-permute-start(bf16[1024,256]{1,0:T(8,128)(2,1)S(1)} %collective-permute-done.refs_2_.refs_4_), channel_id=1, source_target_pairs={{0,1},{1,0},{2,3},{3,2},{4,5},{5,4},{6,7},{7,6},{8,9},{9,8},{10,11... | collective-permute-start | bytes 1572872 | tf_op jit(solution)/shard_map/ppermute | solution.py:20
  54.4 11.5 %collective-permute-start.8 = (bf16[1024,256]{1,0:T(8,128)(2,1)}, bf16[1024,256]{1,0:T(8,128)(2,1)S(1)}, u32[]{:S(2)}, u32[]{:S(2)}) collective-permute-start(bf16[1024,256]{1,0:T(8,128)(2,1)} %collective-permute-done.7.refs_6_), channel_id=1, source_target_pairs={{0,1},{1,0},{2,3},{3,2},{4,5},{5,4},{6,7},{7,6},{8,9},{9,8},{10,11... | collective-permute-start | bytes 1572872 | tf_op jit(solution)/shard_map/ppermute | solution.py:20
  55.3 16.2 %collective-permute-start.12 = (bf16[1024,256]{1,0:T(8,128)(2,1)S(1)}, bf16[1024,256]{1,0:T(8,128)(2,1)S(1)}, u32[]{:S(2)}, u32[]{:S(2)}) collective-permute-start(bf16[1024,256]{1,0:T(8,128)(2,1)S(1)} %get-tuple-element.33.refs_1_.refs_0_), channel_id=1, source_target_pairs={{0,2},{1,3},{2,0},{3,1},{4,6},{5,7},{6,4},{7,5},{8,10},{9,11},{10,... | collective-permute-start | bytes 1572872 | tf_op jit(solution)/shard_map/ppermute | solution.py:20
  71.4 17.6 %collective-permute-start.9 = (bf16[2,4,128,512]{3,2,1,0:T(8,128)(2,1)S(1)}, bf16[2,4,128,512]{3,2,1,0:T(8,128)(2,1)S(1)}, u32[]{:S(2)}, u32[]{:S(2)}) collective-permute-start(bf16[2,4,128,512]{3,2,1,0:T(8,128)(2,1)S(1)} %get-tuple-element.32), channel_id=1, source_target_pairs={{0,8},{8,0},{16,24},{24,16},{1,9},{9,1},{17,25},{25,17},{2,10},{10... | collective-permute-start | bytes 3145736 | tf_op jit(solution)/shard_map/ppermute | solution.py:20
  71.5 14.8 %collective-permute-start.13 = (bf16[1024,256]{1,0:T(8,128)(2,1)S(1)}, bf16[1024,256]{1,0:T(8,128)(2,1)S(1)}, u32[]{:S(2)}, u32[]{:S(2)}) collective-permute-start(bf16[1024,256]{1,0:T(8,128)(2,1)S(1)} %collective-permute-done.12.refs_2_), channel_id=1, source_target_pairs={{0,1},{1,0},{2,3},{3,2},{4,5},{5,4},{6,7},{7,6},{8,9},{9,8},{10,11... | collective-permute-start | bytes 1572872 | tf_op jit(solution)/shard_map/ppermute | solution.py:20
  72.4 8.4 %collective-permute-start.16 = (bf16[1024,128]{1,0:T(8,128)(2,1)S(1)}, bf16[1024,128]{1,0:T(8,128)(2,1)S(1)}, u32[]{:S(2)}, u32[]{:S(2)}) collective-permute-start(bf16[1024,128]{1,0:T(8,128)(2,1)S(1)} %get-tuple-element.39.refs_0_), channel_id=1, source_target_pairs={{0,2},{1,3},{2,0},{3,1},{4,6},{5,7},{6,4},{7,5},{8,10},{9,11},{10,... | collective-permute-start | bytes 786440 | tf_op jit(solution)/shard_map/ppermute | solution.py:20
  72.5 18.9 %collective-permute-start.15 = (bf16[1024,128]{1,0:T(8,128)(2,1)S(1)}, bf16[1024,128]{1,0:T(8,128)(2,1)S(1)}, u32[]{:S(2)}, u32[]{:S(2)}) collective-permute-start(bf16[1024,128]{1,0:T(8,128)(2,1)S(1)} %get-tuple-element.39.refs_0_), channel_id=1, source_target_pairs={{0,1},{1,0},{2,3},{3,2},{4,5},{5,4},{6,7},{7,6},{8,9},{9,8},{10,11... | collective-permute-start | bytes 786440 | tf_op jit(solution)/shard_map/ppermute | solution.py:20
  80.9 10.6 %collective-permute-start.17 = (bf16[1024,128]{1,0:T(8,128)(2,1)S(1)}, bf16[1024,128]{1,0:T(8,128)(2,1)S(1)}, u32[]{:S(2)}, u32[]{:S(2)}) collective-permute-start(bf16[1024,128]{1,0:T(8,128)(2,1)S(1)} %get-tuple-element.42.refs_4_), channel_id=1, source_target_pairs={{0,2},{1,3},{2,0},{3,1},{4,6},{5,7},{6,4},{7,5},{8,10},{9,11},{10,... | collective-permute-start | bytes 786440 | tf_op jit(solution)/shard_map/ppermute | solution.py:20
  88.9 4.5 %collective-permute-start.14 = (bf16[2,4,128,256]{3,2,1,0:T(8,128)(2,1)S(1)}, bf16[2,4,128,256]{3,2,1,0:T(8,128)(2,1)S(1)}, u32[]{:S(2)}, u32[]{:S(2)}) collective-permute-start(bf16[2,4,128,256]{3,2,1,0:T(8,128)(2,1)S(1)} %get-tuple-element.36), channel_id=1, source_target_pairs={{0,8},{8,0},{16,24},{24,16},{1,9},{9,1},{17,25},{25,17},{2,10},{10... | collective-permute-start | bytes 1572872 | tf_op jit(solution)/shard_map/ppermute | solution.py:20
  89.5 14.4 %collective-permute-start.10 = (bf16[1,4,128,512]{3,2,1,0:T(8,128)(2,1)S(1)}, bf16[1,4,128,512]{3,2,1,0:T(8,128)(2,1)S(1)}, u32[]{:S(2)}, u32[]{:S(2)}) collective-permute-start(bf16[1,4,128,512]{3,2,1,0:T(8,128)(2,1)S(1)} %slice.83), channel_id=1, source_target_pairs={{0,16},{8,24},{16,0},{24,8},{1,17},{9,25},{17,1},{25,9},{2,18},{10... | collective-permute-start | bytes 1572872 | tf_op jit(solution)/shard_map/ppermute | solution.py:20
  91.4 12.7 %collective-permute-start.18 = (bf16[1024,128]{1,0:T(8,128)(2,1)S(1)}, bf16[1024,128]{1,0:T(8,128)(2,1)S(1)}, u32[]{:S(2)}, u32[]{:S(2)}) collective-permute-start(bf16[1024,128]{1,0:T(8,128)(2,1)S(1)} %collective-permute-done.15.refs_1_), channel_id=1, source_target_pairs={{0,2},{1,3},{2,0},{3,1},{4,6},{5,7},{6,4},{7,5},{8,10},{9,11},{10,... | collective-permute-start | bytes 786440 | tf_op jit(solution)/shard_map/ppermute | solution.py:20
  91.4 12.7 %collective-permute-start.20 = (bf16[1024,128]{1,0:T(8,128)(2,1)S(1)}, bf16[1024,128]{1,0:T(8,128)(2,1)S(1)}, u32[]{:S(2)}, u32[]{:S(2)}) collective-permute-start(bf16[1024,128]{1,0:T(8,128)(2,1)S(1)} %collective-permute-done.17.refs_6_), channel_id=1, source_target_pairs={{0,1},{1,0},{2,3},{3,2},{4,5},{5,4},{6,7},{7,6},{8,9},{9,8},{10,11... | collective-permute-start | bytes 786440 | tf_op jit(solution)/shard_map/ppermute | solution.py:20
  92.3 12.9 %collective-permute-start.19 = (bf16[1024,128]{1,0:T(8,128)(2,1)S(1)}, bf16[1024,128]{1,0:T(8,128)(2,1)S(1)}, u32[]{:S(2)}, u32[]{:S(2)}) collective-permute-start(bf16[1024,128]{1,0:T(8,128)(2,1)S(1)} %get-tuple-element.42.refs_4_), channel_id=1, source_target_pairs={{0,1},{1,0},{2,3},{3,2},{4,5},{5,4},{6,7},{7,6},{8,9},{9,8},{10,11... | collective-permute-start | bytes 786440 | tf_op jit(solution)/shard_map/ppermute | solution.py:20
  108.3 9.2 %collective-permute-start.23 = (bf16[1,4,128,256]{3,2,1,0:T(8,128)(2,1)S(1)}, bf16[1,4,128,256]{3,2,1,0:T(8,128)(2,1)S(1)}, u32[]{:S(2)}, u32[]{:S(2)}) collective-permute-start(bf16[1,4,128,256]{3,2,1,0:T(8,128)(2,1)S(1)} %slice.84), channel_id=1, source_target_pairs={{0,16},{8,24},{16,0},{24,8},{1,17},{9,25},{17,1},{25,9},{2,18},{10... | collective-permute-start | bytes 786440 | tf_op jit(solution)/shard_map/ppermute | solution.py:20
  110.3 12.4 %collective-permute-start.22 = (bf16[1,4,128,256]{3,2,1,0:T(8,128)(2,1)S(1)}, bf16[1,4,128,256]{3,2,1,0:T(8,128)(2,1)S(1)}, u32[]{:S(2)}, u32[]{:S(2)}) collective-permute-start(bf16[1,4,128,256]{3,2,1,0:T(8,128)(2,1)S(1)} %slice.85), channel_id=1, source_target_pairs={{0,16},{8,24},{16,0},{24,8},{1,17},{9,25},{17,1},{25,9},{2,18},{10... | collective-permute-start | bytes 786440 | tf_op jit(solution)/shard_map/ppermute | solution.py:20
  111.6 16.7 %collective-permute-start.11 = (bf16[4,128,256]{2,1,0:T(8,128)(2,1)S(1)}, bf16[4,128,256]{2,1,0:T(8,128)(2,1)S(1)}, u32[]{:S(2)}, u32[]{:S(2)}) collective-permute-start(bf16[4,128,256]{2,1,0:T(8,128)(2,1)S(1)} %select_convert_fusion.1), channel_id=1, source_target_pairs={{0,4},{1,5},{2,6},{3,7},{4,0},{5,1},{6,2},{7,3},{8,12},{9,13},{10,... | collective-permute-start | bytes 786440 | tf_op jit(solution)/shard_map/ppermute | solution.py:20
  128.3 13.7 %collective-permute-start.24 = (bf16[4,128,256]{2,1,0:T(8,128)(2,1)S(1)}, bf16[4,128,256]{2,1,0:T(8,128)(2,1)S(1)}, u32[]{:S(2)}, u32[]{:S(2)}) collective-permute-start(bf16[4,128,256]{2,1,0:T(8,128)(2,1)S(1)} %select_convert_fusion), channel_id=1, source_target_pairs={{0,4},{1,5},{2,6},{3,7},{4,0},{5,1},{6,2},{7,3},{8,12},{9,13},{10,... | collective-permute-start | bytes 786440 | tf_op jit(solution)/shard_map/ppermute | solution.py:20
  (2 other events, 56.4 us)

commit v6 on v5

--- a/solution.py
+++ b/solution.py
@@ -41,10 +41,11 @@
             return max(free.get(hop[2], 0), ready[hop[:2]])
 
         able = [hop for hop in waiting if hop[:2] in ready]
-        hop = min(able, key=lambda one: (start_of(one), waiting.index(one)))
+        hop = min(able, key=lambda one: (start_of(one), -one[2], waiting.index(one)))
         piece, low, bit = hop
         shared = 2 if bit == cut // 2 and start_of(hop) < crossed else 1
-        free[bit] = ready[piece, low | bit] = start_of(hop) + shared * widths[piece]
+        free[bit] = start_of(hop) + shared * widths[piece]
+        ready[piece, low | bit] = free[bit] + 0.5
         waiting.remove(hop)
         ordered.append(hop)
     return ordered
@@ -68,9 +69,7 @@
         in_specs=[VMEM] * (len(own) + len(mate)),
         out_specs=VMEM,
         compiler_params=PARAMS,
-        cost_estimate=pl.CostEstimate(
-            flops=0, bytes_accessed=8 * group * cells, transcendentals=0
-        ),
+        cost_estimate=pl.CostEstimate(flops=0, bytes_accessed=0, transcendentals=0),
     )(*own, *mate)
 
 
@@ -126,13 +125,7 @@
             pltpu.VMEM((group, max(widths)), jnp.float32),
         ],
         compiler_params=PARAMS,
-        cost_estimate=pl.CostEstimate(
-            flops=2 * ROUNDS * group * cells * sum(widths),
-            bytes_accessed=2 * lefts.size
-            + 2 * sum(array.size for array in arrays)
-            + 4 * ROUNDS * group * sum(widths),
-            transcendentals=0,
-        ),
+        cost_estimate=pl.CostEstimate(flops=0, bytes_accessed=0, transcendentals=0),
     )(choices, lefts, *arrays)
 
 
@@ -201,7 +194,13 @@
             (numbers[0] >= len(own), [[held[n][low] for low in range(cut)] for n in numbers])
             for numbers in lists
         ]
-        earlier = (given[0], halves[-1]) if lists == BATCHES[-1] else None
+        earlier = None
+        if not halves:
+            earlier = (sent[cut // 2][-1], sent[1][4])
+        elif lists != BATCHES[-1]:
+            earlier = halves[0]
+        else:
+            earlier = (given[0], halves[-1])
         even, odd = products(behind(choices, earlier), lefts, batch, scale_factor)
         halves.append(halved(even, odd, 1))
         total = summed(halves[-1])

time: 144 us -> 150 us (1.042)
  starting transfers between devices: 26.4 us -> 29.8 us
  waiting for transfers between devices: 98.9 us -> 101 us
    ppermute x25, starting transfers between devices: 26.4 us -> 29.8 us  [exchange(): lax.ppermute(part, axis, [(i, i ^ mask) for i in range(lax.axis_size(axis...]
    ppermute x25, waiting for transfers between devices: 98.9 us -> 101 us  [exchange(): lax.ppermute(part, axis, [(i, i ^ mask) for i in range(lax.axis_size(axis...]
  transfers between devices with their start and end apart: 25 -> 25, of which waited for: 17 -> 15; matrix products, arithmetic and copies ran while one was open for 1% -> 1% of each run, Pallas kernels for 6% -> 2%
where the time goes in v6:
time: 150 us
  waiting for transfers between devices  101 us (67%)
  starting transfers between devices  29.8 us (20%)
  Pallas kernels  11.8 us (8%)
  other arithmetic  5.34 us (4%)
  local copies, waits for them, and re-layouts  1.67 us (1%)
    ppermute x25, waiting for transfers between devices, exchange(): lax.ppermute(part, axis, [(i, i ^ mask) for i in range(lax.axis_size(axis...  101 us
    ppermute x25, starting transfers between devices, exchange(): lax.ppermute(part, axis, [(i, i ^ mask) for i in range(lax.axis_size(axis...  29.8 us
    pallas_call x3, Pallas kernels, products(): pl.pallas_call(kernel, out_shape=[jax.ShapeDtypeStruct(shape, kind) for k...  11.2 us
  transfers between devices with their start and end apart: 25, of which 15 were waited for; matrix products, arithmetic and copies ran while one was open for 1% of the time, Pallas kernels for 2%

profile of v6, /device:TPU:0, one launch (start us, length us, event | category | flops | bytes accessed | tf_op | source)
XLA Modules:
  0.0 150.3 jit_solution(11495282245638131272)
XLA Ops:
  0.7 2.8 %multiply_convert_fusion = (bf16[1024,256]{1,0:T(8,128)(2,1)}, bf16[1024,256]{1,0:T(8,128)(2,1)S(1)}, bf16[1024,256]{1,0:T(8,128)(2,1)S(1)}, bf16[1024,256]{1,0:T(8,128)(2,1)S(1)}) fusion(bf16[2048,512]{1,0:T(8,128)(2,1)} %param.3, s32[]{:T(128)S(6)} %select_n.21, f32[1024]{0:T(1024)S(1)} %get-tuple-element.59, f32[1024]{0:T(1024)S(1)} %get-tuple-element.60, ...), kind=kLoop, calls=%fused_computation.7 | loop fusion | flops 3145728 | bytes 4202504 | tf_op jit(solution)/shard_map/convert_element_type | solution.py:163
  3.5 4.0 %collective-permute-start = (bf16[1024,256]{1,0:T(8,128)(2,1)S(1)}, bf16[1024,256]{1,0:T(8,128)(2,1)S(1)}, u32[]{:S(2)}, u32[]{:S(2)}) collective-permute-start(bf16[1024,256]{1,0:T(8,128)(2,1)S(1)} %get-tuple-element.52), channel_id=1, source_target_pairs={{0,4},{1,5},{2,6},{3,7},{4,0},{5,1},{6,2},{7,3},{8,12},{9,13},{10,... | collective-permute-start | bytes 1572872 | tf_op jit(solution)/shard_map/ppermute | solution.py:20
  7.5 1.6 %collective-permute-start.1 = (bf16[1024,256]{1,0:T(8,128)(2,1)S(1)}, bf16[1024,256]{1,0:T(8,128)(2,1)S(1)}, u32[]{:S(2)}, u32[]{:S(2)}) collective-permute-start(bf16[1024,256]{1,0:T(8,128)(2,1)S(1)} %get-tuple-element.56.refs_0_), channel_id=1, source_target_pairs={{0,2},{1,3},{2,0},{3,1},{4,6},{5,7},{6,4},{7,5},{8,10},{9,11},{10,... | collective-permute-start | bytes 1572872 | tf_op jit(solution)/shard_map/ppermute | solution.py:20
  11.1 19.7 %collective-permute-done.refs_2_.refs_4_ = bf16[1024,256]{1,0:T(8,128)(2,1)S(1)} collective-permute-done((bf16[1024,256]{1,0:T(8,128)(2,1)S(1)}, bf16[1024,256]{1,0:T(8,128)(2,1)S(1)}, u32[]{:S(2)}, u32[]{:S(2)}) %collective-permute-start) | collective-permute-done | bytes 524320 | tf_op jit(solution)/shard_map/ppermute | solution.py:20
  31.0 1.5 collective-permute-start.2
  32.5 1.5 collective-permute-start.9
  34.0 2.3 %collective-permute-start.4 = (bf16[1024,256]{1,0:T(8,128)(2,1)}, bf16[1024,256]{1,0:T(8,128)(2,1)S(1)}, u32[]{:S(2)}, u32[]{:S(2)}) collective-permute-start(bf16[1024,256]{1,0:T(8,128)(2,1)} %get-tuple-element.30), channel_id=1, source_target_pairs={{0,4},{1,5},{2,6},{3,7},{4,0},{5,1},{6,2},{7,3},{8,12},{9,13},{10,... | collective-permute-start | bytes 1572872 | tf_op jit(solution)/shard_map/ppermute | solution.py:20
  37.6 15.9 %collective-permute-done.2.refs_6_ = bf16[1024,256]{1,0:T(8,128)(2,1)} collective-permute-done((bf16[1024,256]{1,0:T(8,128)(2,1)S(1)}, bf16[1024,256]{1,0:T(8,128)(2,1)}, u32[]{:S(2)}, u32[]{:S(2)}) %collective-permute-start.2) | collective-permute-done | bytes 524320 | tf_op jit(solution)/shard_map/ppermute | solution.py:20
  53.5 2.2 %collective-permute-start.10 = (bf16[1024,256]{1,0:T(8,128)(2,1)}, bf16[1024,256]{1,0:T(8,128)(2,1)S(1)}, u32[]{:S(2)}, u32[]{:S(2)}) collective-permute-start(bf16[1024,256]{1,0:T(8,128)(2,1)} %collective-permute-done.2.refs_6_), channel_id=1, source_target_pairs={{0,1},{1,0},{2,3},{3,2},{4,5},{5,4},{6,7},{7,6},{8,9},{9,8},{10,11... | collective-permute-start | bytes 1572872 | tf_op jit(solution)/shard_map/ppermute | solution.py:20
  55.7 3.7 %collective-permute-done.4.refs_3_ = bf16[1024,256]{1,0:T(8,128)(2,1)S(1)} collective-permute-done((bf16[1024,256]{1,0:T(8,128)(2,1)}, bf16[1024,256]{1,0:T(8,128)(2,1)S(1)}, u32[]{:S(2)}, u32[]{:S(2)}) %collective-permute-start.4) | collective-permute-done | bytes 524320 | tf_op jit(solution)/shard_map/ppermute | solution.py:20
  60.8 12.3 %collective-permute-done.7.refs_1_ = bf16[1024,128]{1,0:T(8,128)(2,1)S(1)} collective-permute-done((bf16[1024,128]{1,0:T(8,128)(2,1)S(1)}, bf16[1024,128]{1,0:T(8,128)(2,1)S(1)}, u32[]{:S(2)}, u32[]{:S(2)}) %collective-permute-start.7) | collective-permute-done | bytes 262176 | tf_op jit(solution)/shard_map/ppermute | solution.py:20
  73.1 5.6 %shard_map.38 = (f32[2,4,128,512]{3,2,1,0:T(8,128)S(1)}, bf16[2,4,128,512]{3,2,1,0:T(8,128)(2,1)S(1)}) custom-call(s32[9]{0:T(128)S(1)} %pad_add_fusion.choices_ref, bf16[2,512,1024]{2,1,0:T(8,128)(2,1)S(1)} %shard_map.37.lefts_ref, bf16[1024,256]{1,0:T(8,128)(2,1)S(1)} %get-tuple-element.56.refs_0_, bf16[1024,256]{1,0:T(8,128)(2,1)S(1)} %copy-done.1, ...), custom_call_target="tpu_custom_call" | custom-call | tf_op jit(solution)/shard_map/pallas_call | solution.py:118
  80.7 6.8 %collective-permute-done.16.refs_2_ = bf16[1024,128]{1,0:T(8,128)(2,1)S(1)} collective-permute-done((bf16[1024,128]{1,0:T(8,128)(2,1)S(1)}, bf16[1024,128]{1,0:T(8,128)(2,1)S(1)}, u32[]{:S(2)}, u32[]{:S(2)}) %collective-permute-start.16) | collective-permute-done | bytes 262176 | tf_op jit(solution)/shard_map/ppermute | solution.py:20
  89.8 5.5 %collective-permute-done.17.refs_3_ = bf16[1024,128]{1,0:T(8,128)(2,1)S(1)} collective-permute-done((bf16[1024,128]{1,0:T(8,128)(2,1)S(1)}, bf16[1024,128]{1,0:T(8,128)(2,1)S(1)}, u32[]{:S(2)}, u32[]{:S(2)}) %collective-permute-start.17) | collective-permute-done | bytes 262176 | tf_op jit(solution)/shard_map/ppermute | solution.py:20
  96.0 2.6 %shard_map.39 = (f32[2,4,128,256]{3,2,1,0:T(8,128)S(1)}, bf16[2,4,128,256]{3,2,1,0:T(8,128)(2,1)S(1)}) custom-call(s32[9]{0:T(128)S(1)} %pad_add_fusion.choices_ref, bf16[2,512,1024]{2,1,0:T(8,128)(2,1)S(1)} %shard_map.37.lefts_ref, bf16[1024,256]{1,0:T(8,128)(2,1)S(1)} %get-tuple-element.29.refs_1_.refs_0_, ...), custom_call_target="tpu_custom_call" | custom-call | tf_op jit(solution)/shard_map/pallas_call | solution.py:118
  100.0 2.3 %collective-permute-done.19.refs_6_ = bf16[1024,128]{1,0:T(8,128)(2,1)S(1)} collective-permute-done((bf16[1024,128]{1,0:T(8,128)(2,1)S(1)}, bf16[1024,128]{1,0:T(8,128)(2,1)S(1)}, u32[]{:S(2)}, u32[]{:S(2)}) %collective-permute-start.19) | collective-permute-done | bytes 262176 | tf_op jit(solution)/shard_map/ppermute | solution.py:20
  104.3 3.6 %collective-permute-done.18.refs_5_ = bf16[1024,128]{1,0:T(8,128)(2,1)S(1)} collective-permute-done((bf16[1024,128]{1,0:T(8,128)(2,1)S(1)}, bf16[1024,128]{1,0:T(8,128)(2,1)S(1)}, u32[]{:S(2)}, u32[]{:S(2)}) %collective-permute-start.18) | collective-permute-done | bytes 262176 | tf_op jit(solution)/shard_map/ppermute | solution.py:20
  107.9 5.2 %collective-permute-done.20.refs_7_ = bf16[1024,128]{1,0:T(8,128)(2,1)S(1)} collective-permute-done((bf16[1024,128]{1,0:T(8,128)(2,1)S(1)}, bf16[1024,128]{1,0:T(8,128)(2,1)S(1)}, u32[]{:S(2)}, u32[]{:S(2)}) %collective-permute-start.20) | collective-permute-done | bytes 262176 | tf_op jit(solution)/shard_map/ppermute | solution.py:20
  113.1 3.0 %shard_map.40 = (f32[2,4,128,256]{3,2,1,0:T(8,128)S(1)}, bf16[2,4,128,256]{3,2,1,0:T(8,128)(2,1)S(1)}) custom-call(s32[9]{0:T(128)S(1)} %pad_add_fusion.choices_ref, bf16[2,512,1024]{2,1,0:T(8,128)(2,1)S(1)} %shard_map.37.lefts_ref, bf16[1024,128]{1,0:T(8,128)(2,1)S(1)} %get-tuple-element.43.refs_0_, bf16[1024,128]{1,0:T(8,128)(2,1)S(1)} %collective-permute-done.7.refs_1_, ...), custom_call_target="tpu_custom_call" | custom-call | tf_op jit(solution)/shard_map/pallas_call | solution.py:118
  119.5 3.4 %collective-permute-start.13 = (bf16[4,128,256]{2,1,0:T(8,128)(2,1)S(1)}, bf16[4,128,256]{2,1,0:T(8,128)(2,1)S(1)}, u32[]{:S(2)}, u32[]{:S(2)}) collective-permute-start(bf16[4,128,256]{2,1,0:T(8,128)(2,1)S(1)} %select_convert_fusion.1), channel_id=1, source_target_pairs={{0,4},{1,5},{2,6},{3,7},{4,0},{5,1},{6,2},{7,3},{8,12},{9,13},{10,... | collective-permute-start | bytes 786440 | tf_op jit(solution)/shard_map/ppermute | solution.py:20
  122.9 2.4 %collective-permute-done.23 = bf16[1,4,128,256]{3,2,1,0:T(8,128)(2,1)S(1)} collective-permute-done((bf16[1,4,128,256]{3,2,1,0:T(8,128)(2,1)S(1)}, bf16[1,4,128,256]{3,2,1,0:T(8,128)(2,1)S(1)}, u32[]{:S(2)}, u32[]{:S(2)}) %collective-permute-start.23) | collective-permute-done | bytes 262176 | tf_op jit(solution)/shard_map/ppermute | solution.py:20
  125.3 5.2 %collective-permute-done.22 = bf16[1,4,128,256]{3,2,1,0:T(8,128)(2,1)S(1)} collective-permute-done((bf16[1,4,128,256]{3,2,1,0:T(8,128)(2,1)S(1)}, bf16[1,4,128,256]{3,2,1,0:T(8,128)(2,1)S(1)}, u32[]{:S(2)}, u32[]{:S(2)}) %collective-permute-start.22) | collective-permute-done | bytes 262176 | tf_op jit(solution)/shard_map/ppermute | solution.py:20
  130.8 4.1 %collective-permute-done.13 = bf16[4,128,256]{2,1,0:T(8,128)(2,1)S(1)} collective-permute-done((bf16[4,128,256]{2,1,0:T(8,128)(2,1)S(1)}, bf16[4,128,256]{2,1,0:T(8,128)(2,1)S(1)}, u32[]{:S(2)}, u32[]{:S(2)}) %collective-permute-start.13) | collective-permute-done | bytes 262176 | tf_op jit(solution)/shard_map/ppermute | solution.py:20
  134.8 14.0 %collective-permute-done.24 = bf16[4,128,256]{2,1,0:T(8,128)(2,1)S(1)} collective-permute-done((bf16[4,128,256]{2,1,0:T(8,128)(2,1)S(1)}, bf16[4,128,256]{2,1,0:T(8,128)(2,1)S(1)}, u32[]{:S(2)}, u32[]{:S(2)}) %collective-permute-start.24) | collective-permute-done | bytes 262176 | tf_op jit(solution)/shard_map/ppermute | solution.py:20
  (54 shorter events, 18.9 us)
Async XLA Ops:
  3.5 27.3 %collective-permute-start = (bf16[1024,256]{1,0:T(8,128)(2,1)S(1)}, bf16[1024,256]{1,0:T(8,128)(2,1)S(1)}, u32[]{:S(2)}, u32[]{:S(2)}) collective-permute-start(bf16[1024,256]{1,0:T(8,128)(2,1)S(1)} %get-tuple-element.52), channel_id=1, source_target_pairs={{0,4},{1,5},{2,6},{3,7},{4,0},{5,1},{6,2},{7,3},{8,12},{9,13},{10,... | collective-permute-start | bytes 1572872 | tf_op jit(solution)/shard_map/ppermute | solution.py:20
  7.5 23.5 %collective-permute-start.1 = (bf16[1024,256]{1,0:T(8,128)(2,1)S(1)}, bf16[1024,256]{1,0:T(8,128)(2,1)S(1)}, u32[]{:S(2)}, u32[]{:S(2)}) collective-permute-start(bf16[1024,256]{1,0:T(8,128)(2,1)S(1)} %get-tuple-element.56.refs_0_), channel_id=1, source_target_pairs={{0,2},{1,3},{2,0},{3,1},{4,6},{5,7},{6,4},{7,5},{8,10},{9,11},{10,... | collective-permute-start | bytes 1572872 | tf_op jit(solution)/shard_map/ppermute | solution.py:20
  9.1 23.4 %collective-permute-start.8 = (bf16[1024,256]{1,0:T(8,128)(2,1)S(1)}, bf16[1024,256]{1,0:T(8,128)(2,1)S(1)}, u32[]{:S(2)}, u32[]{:S(2)}) collective-permute-start(bf16[1024,256]{1,0:T(8,128)(2,1)S(1)} %get-tuple-element.29.refs_1_.refs_0_), channel_id=1, source_target_pairs={{0,1},{1,0},{2,3},{3,2},{4,5},{5,4},{6,7},{7,6},{8,9},{9,8},{10,11... | collective-permute-start | bytes 1572872 | tf_op jit(solution)/shard_map/ppermute | solution.py:20
  10.6 25.7 %collective-permute-start.5 = (bf16[1024,256]{1,0:T(8,128)(2,1)S(1)}, bf16[1024,256]{1,0:T(8,128)(2,1)S(1)}, u32[]{:S(2)}, u32[]{:S(2)}) collective-permute-start(bf16[1024,256]{1,0:T(8,128)(2,1)S(1)} %get-tuple-element.56.refs_0_), channel_id=1, source_target_pairs={{0,1},{1,0},{2,3},{3,2},{4,5},{5,4},{6,7},{7,6},{8,9},{9,8},{10,11... | collective-permute-start | bytes 1572872 | tf_op jit(solution)/shard_map/ppermute | solution.py:20
  31.0 22.6 %collective-permute-start.2 = (bf16[1024,256]{1,0:T(8,128)(2,1)S(1)}, bf16[1024,256]{1,0:T(8,128)(2,1)}, u32[]{:S(2)}, u32[]{:S(2)}) collective-permute-start(bf16[1024,256]{1,0:T(8,128)(2,1)S(1)} %collective-permute-done.refs_2_.refs_4_), channel_id=1, source_target_pairs={{0,2},{1,3},{2,0},{3,1},{4,6},{5,7},{6,4},{7,5},{8,10},{9,11},{10,... | collective-permute-start | bytes 1572872 | tf_op jit(solution)/shard_map/ppermute | solution.py:20
  32.5 21.1 %collective-permute-start.9 = (bf16[1024,256]{1,0:T(8,128)(2,1)S(1)}, bf16[1024,256]{1,0:T(8,128)(2,1)}, u32[]{:S(2)}, u32[]{:S(2)}) collective-permute-start(bf16[1024,256]{1,0:T(8,128)(2,1)S(1)} %collective-permute-done.1.refs_2_), channel_id=1, source_target_pairs={{0,1},{1,0},{2,3},{3,2},{4,5},{5,4},{6,7},{7,6},{8,9},{9,8},{10,11... | collective-permute-start | bytes 1572872 | tf_op jit(solution)/shard_map/ppermute | solution.py:20
  34.0 25.5 %collective-permute-start.4 = (bf16[1024,256]{1,0:T(8,128)(2,1)}, bf16[1024,256]{1,0:T(8,128)(2,1)S(1)}, u32[]{:S(2)}, u32[]{:S(2)}) collective-permute-start(bf16[1024,256]{1,0:T(8,128)(2,1)} %get-tuple-element.30), channel_id=1, source_target_pairs={{0,4},{1,5},{2,6},{3,7},{4,0},{5,1},{6,2},{7,3},{8,12},{9,13},{10,... | collective-permute-start | bytes 1572872 | tf_op jit(solution)/shard_map/ppermute | solution.py:20
  37.1 22.4 %collective-permute-start.6 = (bf16[1024,256]{1,0:T(8,128)(2,1)S(1)}, bf16[1024,256]{1,0:T(8,128)(2,1)}, u32[]{:S(2)}, u32[]{:S(2)}) collective-permute-start(bf16[1024,256]{1,0:T(8,128)(2,1)S(1)} %collective-permute-done.refs_2_.refs_4_), channel_id=1, source_target_pairs={{0,1},{1,0},{2,3},{3,2},{4,5},{5,4},{6,7},{7,6},{8,9},{9,8},{10,11... | collective-permute-start | bytes 1572872 | tf_op jit(solution)/shard_map/ppermute | solution.py:20
  53.5 19.5 %collective-permute-start.3 = (bf16[1024,256]{1,0:T(8,128)(2,1)S(1)}, bf16[1024,256]{1,0:T(8,128)(2,1)S(1)}, u32[]{:S(2)}, u32[]{:S(2)}) collective-permute-start(bf16[1024,256]{1,0:T(8,128)(2,1)S(1)} %get-tuple-element.29.refs_1_.refs_0_), channel_id=1, source_target_pairs={{0,2},{1,3},{2,0},{3,1},{4,6},{5,7},{6,4},{7,5},{8,10},{9,11},{10,... | collective-permute-start | bytes 1572872 | tf_op jit(solution)/shard_map/ppermute | solution.py:20
  53.5 19.5 %collective-permute-start.10 = (bf16[1024,256]{1,0:T(8,128)(2,1)}, bf16[1024,256]{1,0:T(8,128)(2,1)S(1)}, u32[]{:S(2)}, u32[]{:S(2)}) collective-permute-start(bf16[1024,256]{1,0:T(8,128)(2,1)} %collective-permute-done.2.refs_6_), channel_id=1, source_target_pairs={{0,1},{1,0},{2,3},{3,2},{4,5},{5,4},{6,7},{7,6},{8,9},{9,8},{10,11... | collective-permute-start | bytes 1572872 | tf_op jit(solution)/shard_map/ppermute | solution.py:20
  59.5 13.6 %collective-permute-start.7 = (bf16[1024,128]{1,0:T(8,128)(2,1)S(1)}, bf16[1024,128]{1,0:T(8,128)(2,1)S(1)}, u32[]{:S(2)}, u32[]{:S(2)}) collective-permute-start(bf16[1024,128]{1,0:T(8,128)(2,1)S(1)} %get-tuple-element.43.refs_0_), channel_id=1, source_target_pairs={{0,1},{1,0},{2,3},{3,2},{4,5},{5,4},{6,7},{7,6},{8,9},{9,8},{10,11... | collective-permute-start | bytes 786440 | tf_op jit(solution)/shard_map/ppermute | solution.py:20
  78.7 9.4 %collective-permute-start.11 = (bf16[2,4,128,512]{3,2,1,0:T(8,128)(2,1)S(1)}, bf16[2,4,128,512]{3,2,1,0:T(8,128)(2,1)S(1)}, u32[]{:S(2)}, u32[]{:S(2)}) collective-permute-start(bf16[2,4,128,512]{3,2,1,0:T(8,128)(2,1)S(1)} %get-tuple-element.37), channel_id=1, source_target_pairs={{0,8},{8,0},{16,24},{24,16},{1,9},{9,1},{17,25},{25,17},{2,10},{10... | collective-permute-start | bytes 3145736 | tf_op jit(solution)/shard_map/ppermute | solution.py:20
  78.8 8.7 %collective-permute-start.16 = (bf16[1024,128]{1,0:T(8,128)(2,1)S(1)}, bf16[1024,128]{1,0:T(8,128)(2,1)S(1)}, u32[]{:S(2)}, u32[]{:S(2)}) collective-permute-start(bf16[1024,128]{1,0:T(8,128)(2,1)S(1)} %get-tuple-element.43.refs_0_), channel_id=1, source_target_pairs={{0,2},{1,3},{2,0},{3,1},{4,6},{5,7},{6,4},{7,5},{8,10},{9,11},{10,... | collective-permute-start | bytes 786440 | tf_op jit(solution)/shard_map/ppermute | solution.py:20
  79.5 16.5 %collective-permute-start.14 = (bf16[1024,256]{1,0:T(8,128)(2,1)S(1)}, bf16[1024,256]{1,0:T(8,128)(2,1)S(1)}, u32[]{:S(2)}, u32[]{:S(2)}) collective-permute-start(bf16[1024,256]{1,0:T(8,128)(2,1)S(1)} %collective-permute-done.3.refs_2_), channel_id=1, source_target_pairs={{0,1},{1,0},{2,3},{3,2},{4,5},{5,4},{6,7},{7,6},{8,9},{9,8},{10,11... | collective-permute-start | bytes 1572872 | tf_op jit(solution)/shard_map/ppermute | solution.py:20
  87.5 7.9 %collective-permute-start.17 = (bf16[1024,128]{1,0:T(8,128)(2,1)S(1)}, bf16[1024,128]{1,0:T(8,128)(2,1)S(1)}, u32[]{:S(2)}, u32[]{:S(2)}) collective-permute-start(bf16[1024,128]{1,0:T(8,128)(2,1)S(1)} %collective-permute-done.7.refs_1_), channel_id=1, source_target_pairs={{0,2},{1,3},{2,0},{3,1},{4,6},{5,7},{6,4},{7,5},{8,10},{9,11},{10,... | collective-permute-start | bytes 786440 | tf_op jit(solution)/shard_map/ppermute | solution.py:20
  88.5 15.3 %collective-permute-start.12 = (bf16[1,4,128,512]{3,2,1,0:T(8,128)(2,1)S(1)}, bf16[1,4,128,512]{3,2,1,0:T(8,128)(2,1)S(1)}, u32[]{:S(2)}, u32[]{:S(2)}) collective-permute-start(bf16[1,4,128,512]{3,2,1,0:T(8,128)(2,1)S(1)} %slice.83), channel_id=1, source_target_pairs={{0,16},{8,24},{16,0},{24,8},{1,17},{9,25},{17,1},{25,9},{2,18},{10... | collective-permute-start | bytes 1572872 | tf_op jit(solution)/shard_map/ppermute | solution.py:20
  95.4 7.0 %collective-permute-start.19 = (bf16[1024,128]{1,0:T(8,128)(2,1)S(1)}, bf16[1024,128]{1,0:T(8,128)(2,1)S(1)}, u32[]{:S(2)}, u32[]{:S(2)}) collective-permute-start(bf16[1024,128]{1,0:T(8,128)(2,1)S(1)} %get-tuple-element.46.refs_4_), channel_id=1, source_target_pairs={{0,2},{1,3},{2,0},{3,1},{4,6},{5,7},{6,4},{7,5},{8,10},{9,11},{10,... | collective-permute-start | bytes 786440 | tf_op jit(solution)/shard_map/ppermute | solution.py:20
  98.6 5.4 %collective-permute-start.15 = (bf16[2,4,128,256]{3,2,1,0:T(8,128)(2,1)S(1)}, bf16[2,4,128,256]{3,2,1,0:T(8,128)(2,1)S(1)}, u32[]{:S(2)}, u32[]{:S(2)}) collective-permute-start(bf16[2,4,128,256]{3,2,1,0:T(8,128)(2,1)S(1)} %get-tuple-element.41), channel_id=1, source_target_pairs={{0,8},{8,0},{16,24},{24,16},{1,9},{9,1},{17,25},{25,17},{2,10},{10... | collective-permute-start | bytes 1572872 | tf_op jit(solution)/shard_map/ppermute | solution.py:20
  98.7 9.2 %collective-permute-start.18 = (bf16[1024,128]{1,0:T(8,128)(2,1)S(1)}, bf16[1024,128]{1,0:T(8,128)(2,1)S(1)}, u32[]{:S(2)}, u32[]{:S(2)}) collective-permute-start(bf16[1024,128]{1,0:T(8,128)(2,1)S(1)} %get-tuple-element.46.refs_4_), channel_id=1, source_target_pairs={{0,1},{1,0},{2,3},{3,2},{4,5},{5,4},{6,7},{7,6},{8,9},{9,8},{10,11... | collective-permute-start | bytes 786440 | tf_op jit(solution)/shard_map/ppermute | solution.py:20
  102.3 10.7 %collective-permute-start.20 = (bf16[1024,128]{1,0:T(8,128)(2,1)S(1)}, bf16[1024,128]{1,0:T(8,128)(2,1)S(1)}, u32[]{:S(2)}, u32[]{:S(2)}) collective-permute-start(bf16[1024,128]{1,0:T(8,128)(2,1)S(1)} %collective-permute-done.19.refs_6_), channel_id=1, source_target_pairs={{0,1},{1,0},{2,3},{3,2},{4,5},{5,4},{6,7},{7,6},{8,9},{9,8},{10,11... | collective-permute-start | bytes 786440 | tf_op jit(solution)/shard_map/ppermute | solution.py:20
  116.2 9.2 %collective-permute-start.23 = (bf16[1,4,128,256]{3,2,1,0:T(8,128)(2,1)S(1)}, bf16[1,4,128,256]{3,2,1,0:T(8,128)(2,1)S(1)}, u32[]{:S(2)}, u32[]{:S(2)}) collective-permute-start(bf16[1,4,128,256]{3,2,1,0:T(8,128)(2,1)S(1)} %slice.84), channel_id=1, source_target_pairs={{0,16},{8,24},{16,0},{24,8},{1,17},{9,25},{17,1},{25,9},{2,18},{10... | collective-permute-start | bytes 786440 | tf_op jit(solution)/shard_map/ppermute | solution.py:20
  118.2 12.4 %collective-permute-start.22 = (bf16[1,4,128,256]{3,2,1,0:T(8,128)(2,1)S(1)}, bf16[1,4,128,256]{3,2,1,0:T(8,128)(2,1)S(1)}, u32[]{:S(2)}, u32[]{:S(2)}) collective-permute-start(bf16[1,4,128,256]{3,2,1,0:T(8,128)(2,1)S(1)} %slice.85), channel_id=1, source_target_pairs={{0,16},{8,24},{16,0},{24,8},{1,17},{9,25},{17,1},{25,9},{2,18},{10... | collective-permute-start | bytes 786440 | tf_op jit(solution)/shard_map/ppermute | solution.py:20
  119.5 15.3 %collective-permute-start.13 = (bf16[4,128,256]{2,1,0:T(8,128)(2,1)S(1)}, bf16[4,128,256]{2,1,0:T(8,128)(2,1)S(1)}, u32[]{:S(2)}, u32[]{:S(2)}) collective-permute-start(bf16[4,128,256]{2,1,0:T(8,128)(2,1)S(1)} %select_convert_fusion.1), channel_id=1, source_target_pairs={{0,4},{1,5},{2,6},{3,7},{4,0},{5,1},{6,2},{7,3},{8,12},{9,13},{10,... | collective-permute-start | bytes 786440 | tf_op jit(solution)/shard_map/ppermute | solution.py:20
  134.8 14.0 %collective-permute-start.24 = (bf16[4,128,256]{2,1,0:T(8,128)(2,1)S(1)}, bf16[4,128,256]{2,1,0:T(8,128)(2,1)S(1)}, u32[]{:S(2)}, u32[]{:S(2)}) collective-permute-start(bf16[4,128,256]{2,1,0:T(8,128)(2,1)S(1)} %select_convert_fusion), channel_id=1, source_target_pairs={{0,4},{1,5},{2,6},{3,7},{4,0},{5,1},{6,2},{7,3},{8,12},{9,13},{10,... | collective-permute-start | bytes 786440 | tf_op jit(solution)/shard_map/ppermute | solution.py:20
  (4 other events, 52.6 us)

commit v7 on v4

--- a/solution.py
+++ b/solution.py
@@ -91,7 +91,7 @@
 
     def kernel(choices_ref, lefts_ref, *refs):
         block_refs = refs[: len(blocks)]
-        even_ref, odd_ref, picked, tile = refs[len(blocks) :]
+        out_ref, picked = refs[len(blocks) :]
 
         def one_round(round_number, carry):
             for number, block_ref in enumerate(block_refs):
@@ -101,45 +101,32 @@
                     picked[...] = block_ref[...]
 
             left = lefts_ref[choices_ref[ROUNDS + round_number]]
-            tile[...] = scale_factor * jnp.dot(
-                left, picked[...], preferred_element_type=jnp.float32
-            )
+            tile = scale_factor * jnp.dot(left, picked[...], preferred_element_type=jnp.float32)
             for number in range(slab_count):
-                start = jnp.bitwise_xor(choices_ref[2 * ROUNDS], number) * rows
-                part = tile[pl.ds(pl.multiple_of(start, rows), rows), :]
-                out_ref = odd_ref if number % 2 else even_ref
-                out_ref[number // 2, round_number] = part.astype(out_ref.dtype)
+                part = tile[number * rows : (number + 1) * rows, :]
+                out_ref[number, round_number] = part.astype(out_ref.dtype)
             return carry
 
         lax.fori_loop(0, ROUNDS, one_round, 0)
 
-    shape = (slab_count // 2, ROUNDS, rows, width)
     return pl.pallas_call(
         kernel,
-        out_shape=[jax.ShapeDtypeStruct(shape, kind) for kind in (jnp.float32, jnp.bfloat16)],
+        out_shape=jax.ShapeDtypeStruct((slab_count, ROUNDS, rows, width), jnp.bfloat16),
         in_specs=[pl.BlockSpec(memory_space=pltpu.SMEM)] + [VMEM] * (1 + len(blocks)),
-        out_specs=[VMEM, VMEM],
-        scratch_shapes=[
-            pltpu.VMEM((cells, width), jnp.bfloat16),
-            pltpu.VMEM((group, width), jnp.float32),
-        ],
+        out_specs=VMEM,
+        scratch_shapes=[pltpu.VMEM((cells, width), jnp.bfloat16)],
         compiler_params=PARAMS,
         cost_estimate=pl.CostEstimate(
             flops=2 * ROUNDS * group * cells * width,
-            bytes_accessed=2 * (lefts.size + (len(blocks) * cells + 2 * ROUNDS * group) * width),
+            bytes_accessed=2 * (lefts.size + (len(blocks) * cells + ROUNDS * group) * width),
             transcendentals=0,
         ),
     )(choices, lefts, *blocks)
 
 
-def summed(keep, send):
-    bit = 1
-    while True:
-        total = keep + exchange(send, "space", bit).astype(jnp.float32)
-        if len(total) == 1:
-            return total[0]
-        keep, send = total[0::2], total[1::2].astype(jnp.bfloat16)
-        bit *= 2
+def summed(parts):
+    arrived = lax.all_to_all(parts, "space", 0, 0)
+    return jnp.sum(arrived.astype(jnp.float32), axis=0)
 
 
 def body(snapshots, volume, masks):
@@ -175,13 +162,12 @@
 
     low = jnp.bitwise_and(masks, cut - 1)
     crossing = (masks >= cut).astype(jnp.int32)
-    me = lax.axis_index("space").astype(jnp.int32)[None]
-    own_choices = jnp.concatenate([low, crossing, me])
-    mate_choices = jnp.concatenate([low, 1 - crossing, me])
+    own_choices = jnp.concatenate([low, crossing])
+    mate_choices = jnp.concatenate([low, 1 - crossing])
 
     own_sum = jnp.concatenate(
         [
-            summed(*products(own_choices, lefts, found, scale_factor))
+            summed(products(own_choices, lefts, found, scale_factor))
             for found in blocks[: len(own)]
         ],
         axis=2,
@@ -189,7 +175,7 @@
     swap = (crossing == 1)[:, None, None]
     columns, first = [], 0
     for found in blocks[len(own) :]:
-        mate_sum = summed(*products(mate_choices, lefts, found, scale_factor))
+        mate_sum = summed(products(mate_choices, lefts, found, scale_factor))
         held = lax.slice_in_dim(own_sum, first, first + mate_sum.shape[2], axis=2)
         keep = jnp.where(swap, mate_sum, held)
         give = jnp.where(swap, held, mate_sum).astype(jnp.bfloat16)

time: 143 us -> 194 us (1.36)
  waiting for transfers between devices: 80.3 us -> 114 us
  starting transfers between devices: 39.3 us -> 47.8 us
  other arithmetic: 5.28 us -> 9.88 us
  Pallas kernels: 14.3 us -> 17.3 us
    ppermute x31 -> x21, waiting for transfers between devices: 80.3 us -> 103 us  [exchange(): lax.ppermute(part, axis, [(i, i ^ mask) for i in range(lax.axis_size(axis...]
    all_to_all x0 -> x5, starting transfers between devices: none -> 20.4 us  [summed(): arrived = lax.all_to_all(parts, 'space', 0, 0)]
    ppermute x31 -> x21, starting transfers between devices: 39.3 us -> 27.4 us  [exchange(): lax.ppermute(part, axis, [(i, i ^ mask) for i in range(lax.axis_size(axis...]
    all_to_all x0 -> x5, waiting for transfers between devices: none -> 10.9 us  [summed(): arrived = lax.all_to_all(parts, 'space', 0, 0)]
    reduce_sum x0 -> x5, other arithmetic: none -> 5.28 us  [summed(): return jnp.sum(arrived.astype(jnp.float32), axis=0)]
    pallas_call x5, Pallas kernels: 13.7 us -> 16.7 us  [products(): pl.pallas_call(kernel, out_shape=jax.ShapeDtypeStruct((slab_count, ROUNDS...]
  transfers between devices with their start and end apart: 31 -> 26, of which waited for: 15 -> 16; matrix products, arithmetic and copies ran while one was open for 2% -> 4% of each run, Pallas kernels for 10% -> 9%
where the time goes in v7:
time: 194 us; the launch traced here: 193 us
  waiting for transfers between devices  114 us (59%)
  starting transfers between devices  47.8 us (25%)
  Pallas kernels  17.3 us (9%)
  other arithmetic  9.88 us (5%)
  local copies, waits for them, and re-layouts  4.33 us (2%)
    ppermute x21, waiting for transfers between devices, exchange(): lax.ppermute(part, axis, [(i, i ^ mask) for i in range(lax.axis_size(axis...  103 us
    ppermute x21, starting transfers between devices, exchange(): lax.ppermute(part, axis, [(i, i ^ mask) for i in range(lax.axis_size(axis...  27.4 us
    all_to_all x5, starting transfers between devices, summed(): arrived = lax.all_to_all(parts, 'space', 0, 0)  20.4 us
    pallas_call x5, Pallas kernels, products(): pl.pallas_call(kernel, out_shape=jax.ShapeDtypeStruct((slab_count, ROUNDS...  16.7 us
    all_to_all x5, waiting for transfers between devices, summed(): arrived = lax.all_to_all(parts, 'space', 0, 0)  10.9 us
    reduce_sum x5, other arithmetic, summed(): return jnp.sum(arrived.astype(jnp.float32), axis=0)  5.28 us
  transfers between devices with their start and end apart: 26, of which 16 were waited for; matrix products, arithmetic and copies ran while one was open for 4% of the time, Pallas kernels for 9%

profile of v7, /device:TPU:0, one launch (start us, length us, event | category | flops | bytes accessed | tf_op | source)
XLA Modules:
  0.0 193.2 jit_solution(13114000119870185933)
XLA Ops:
  2.4 4.1 %collective-permute-start = (bf16[1024,256]{1,0:T(8,128)(2,1)S(1)}, bf16[1024,256]{1,0:T(8,128)(2,1)S(1)}, u32[]{:S(2)}, u32[]{:S(2)}) collective-permute-start(bf16[1024,256]{1,0:T(8,128)(2,1)S(1)} %get-tuple-element.37), channel_id=1, source_target_pairs={{0,4},{1,5},{2,6},{3,7},{4,0},{5,1},{6,2},{7,3},{8,12},{9,13},{10,... | collective-permute-start | bytes 1572872 | tf_op jit(solution)/shard_map/ppermute | solution.py:17
  10.8 19.0 %collective-permute-done.refs_2_.refs_0_ = bf16[1024,256]{1,0:T(8,128)(2,1)S(1)} collective-permute-done((bf16[1024,256]{1,0:T(8,128)(2,1)S(1)}, bf16[1024,256]{1,0:T(8,128)(2,1)S(1)}, u32[]{:S(2)}, u32[]{:S(2)}) %collective-permute-start) | collective-permute-done | bytes 524320 | tf_op jit(solution)/shard_map/ppermute | solution.py:17
  31.5 3.8 %collective-permute-start.6 = (bf16[1024,256]{1,0:T(8,128)(2,1)S(1)}, bf16[1024,256]{1,0:T(8,128)(2,1)}, u32[]{:S(2)}, u32[]{:S(2)}) collective-permute-start(bf16[1024,256]{1,0:T(8,128)(2,1)S(1)} %get-tuple-element.22.refs_1_.refs_0_), channel_id=1, source_target_pairs={{0,2},{1,3},{2,0},{3,1},{4,6},{5,7},{6,4},{7,5},{8,10},{9,11},{10,... | collective-permute-start | bytes 1572872 | tf_op jit(solution)/shard_map/ppermute | solution.py:17
  35.3 8.6 %collective-permute-done.1.refs_3_.refs_0_ = bf16[1024,128]{1,0:T(8,128)(2,1)S(1)} collective-permute-done((bf16[1024,128]{1,0:T(8,128)(2,1)S(1)}, bf16[1024,128]{1,0:T(8,128)(2,1)S(1)}, u32[]{:S(2)}, u32[]{:S(2)}) %collective-permute-start.1) | collective-permute-done | bytes 262176 | tf_op jit(solution)/shard_map/ppermute | solution.py:17
  43.9 13.0 %collective-permute-done.2.refs_4_.refs_0_ = bf16[1024,128]{1,0:T(8,128)(2,1)S(1)} collective-permute-done((bf16[1024,128]{1,0:T(8,128)(2,1)S(1)}, bf16[1024,128]{1,0:T(8,128)(2,1)S(1)}, u32[]{:S(2)}, u32[]{:S(2)}) %collective-permute-start.2) | collective-permute-done | bytes 262176 | tf_op jit(solution)/shard_map/ppermute | solution.py:17
  61.1 4.2 %all-to-all-start.1 = ((bf16[4,4,128,256]{3,2,1,0:T(8,128)(2,1)}), bf16[4,4,128,256]{3,2,1,0:T(8,128)(2,1)}, u32[]{:S(2)}, u32[]{:S(2)}) async-start(bf16[4,4,128,256]{3,2,1,0:T(8,128)(2,1)} %copy-done.1), calls=%async_computation.1 | async-start | bytes 2097152 | tf_op jit(solution)/shard_map/all_to_all | solution.py:128
  67.8 12.4 %collective-permute-done.3.refs_1_ = bf16[1024,256]{1,0:T(8,128)(2,1)S(1)} collective-permute-done((bf16[1024,256]{1,0:T(8,128)(2,1)S(1)}, bf16[1024,256]{1,0:T(8,128)(2,1)S(1)}, u32[]{:S(2)}, u32[]{:S(2)}) %collective-permute-start.3) | collective-permute-done | bytes 524320 | tf_op jit(solution)/shard_map/ppermute | solution.py:17
  81.9 9.5 %collective-permute-done.12.refs_3_ = bf16[1024,256]{1,0:T(8,128)(2,1)S(1)} collective-permute-done((bf16[1024,256]{1,0:T(8,128)(2,1)}, bf16[1024,256]{1,0:T(8,128)(2,1)S(1)}, u32[]{:S(2)}, u32[]{:S(2)}) %collective-permute-start.12) | collective-permute-done | bytes 524320 | tf_op jit(solution)/shard_map/ppermute | solution.py:17
  91.4 3.0 %shard_map.41 = bf16[4,4,128,256]{3,2,1,0:T(8,128)(2,1)S(1)} custom-call(s32[8]{0:T(128)S(1)} %get-tuple-element.46.choices_ref, bf16[2,512,1024]{2,1,0:T(8,128)(2,1)S(1)} %shard_map.37.lefts_ref, bf16[1024,256]{1,0:T(8,128)(2,1)S(1)} %get-tuple-element.22.refs_1_.refs_0_, bf16[1024,256]{1,0:T(8,128)(2,1)S(1)} %collective-permute-done.3.refs_1_, ...), custom_call_target="tpu_custom_call" | custom-call | flops 1073741824 | bytes 5242880 | tf_op jit(solution)/shard_map/pallas_call | solution.py:112
  95.4 4.4 %all-to-all-start.3 = ((bf16[4,4,128,256]{3,2,1,0:T(8,128)(2,1)}), bf16[4,4,128,256]{3,2,1,0:T(8,128)(2,1)}, u32[]{:S(2)}, u32[]{:S(2)}) async-start(bf16[4,4,128,256]{3,2,1,0:T(8,128)(2,1)} %copy-done), calls=%async_computation.3 | async-start | bytes 2097152 | tf_op jit(solution)/shard_map/all_to_all | solution.py:128
  102.5 6.6 %collective-permute-done.13.refs_1_ = bf16[1024,128]{1,0:T(8,128)(2,1)S(1)} collective-permute-done((bf16[1024,128]{1,0:T(8,128)(2,1)S(1)}, bf16[1024,128]{1,0:T(8,128)(2,1)S(1)}, u32[]{:S(2)}, u32[]{:S(2)}) %collective-permute-start.13) | collective-permute-done | bytes 262176 | tf_op jit(solution)/shard_map/ppermute | solution.py:17
  110.7 6.5 %collective-permute-done.16.refs_3_ = bf16[1024,128]{1,0:T(8,128)(2,1)S(1)} collective-permute-done((bf16[1024,128]{1,0:T(8,128)(2,1)S(1)}, bf16[1024,128]{1,0:T(8,128)(2,1)S(1)}, u32[]{:S(2)}, u32[]{:S(2)}) %collective-permute-start.16) | collective-permute-done | bytes 262176 | tf_op jit(solution)/shard_map/ppermute | solution.py:17
  117.1 3.7 %shard_map.40 = bf16[4,4,128,128]{3,2,1,0:T(8,128)(2,1)} custom-call(s32[8]{0:T(128)S(1)} %get-tuple-element.47.choices_ref, bf16[2,512,1024]{2,1,0:T(8,128)(2,1)S(1)} %shard_map.37.lefts_ref, bf16[1024,128]{1,0:T(8,128)(2,1)S(1)} %copy-done.3, bf16[1024,128]{1,0:T(8,128)(2,1)S(1)} %collective-permute-done.13.refs_1_, ...), custom_call_target="tpu_custom_call" | custom-call | flops 536870912 | bytes 3670016 | tf_op jit(solution)/shard_map/pallas_call | solution.py:112
  120.8 4.1 %all-to-all-start.2 = ((bf16[4,4,128,128]{3,2,1,0:T(8,128)(2,1)}), bf16[4,4,128,128]{3,2,1,0:T(8,128)(2,1)}, u32[]{:S(2)}, u32[]{:S(2)}) async-start(bf16[4,4,128,128]{3,2,1,0:T(8,128)(2,1)} %shard_map.40), calls=%async_computation.2 | async-start | bytes 1048576 | tf_op jit(solution)/shard_map/all_to_all | solution.py:128
  127.1 7.3 %collective-permute-done.19.refs_3_ = bf16[1024,128]{1,0:T(8,128)(2,1)S(1)} collective-permute-done((bf16[1024,128]{1,0:T(8,128)(2,1)}, bf16[1024,128]{1,0:T(8,128)(2,1)S(1)}, u32[]{:S(2)}, u32[]{:S(2)}) %collective-permute-start.19) | collective-permute-done | bytes 262176 | tf_op jit(solution)/shard_map/ppermute | solution.py:17
  134.4 5.1 %collective-permute-done.18.refs_1_ = bf16[1024,128]{1,0:T(8,128)(2,1)S(1)} collective-permute-done((bf16[1024,128]{1,0:T(8,128)(2,1)S(1)}, bf16[1024,128]{1,0:T(8,128)(2,1)S(1)}, u32[]{:S(2)}, u32[]{:S(2)}) %collective-permute-start.18) | collective-permute-done | bytes 262176 | tf_op jit(solution)/shard_map/ppermute | solution.py:17
  140.4 3.3 %shard_map.42 = bf16[4,4,128,128]{3,2,1,0:T(8,128)(2,1)} custom-call(s32[8]{0:T(128)S(1)} %get-tuple-element.47.choices_ref, bf16[2,512,1024]{2,1,0:T(8,128)(2,1)S(1)} %shard_map.37.lefts_ref, bf16[1024,128]{1,0:T(8,128)(2,1)S(1)} %collective-permute-done.2.refs_4_.refs_0_, bf16[1024,128]{1,0:T(8,128)(2,1)S(1)} %collective-permute-done.18.refs_1_, ...), custom_call_target="tpu_custom_call" | custom-call | flops 536870912 | bytes 3670016 | tf_op jit(solution)/shard_map/pallas_call | solution.py:112
  143.7 4.1 %all-to-all-start.4 = ((bf16[4,4,128,128]{3,2,1,0:T(8,128)(2,1)}), bf16[4,4,128,128]{3,2,1,0:T(8,128)(2,1)}, u32[]{:S(2)}, u32[]{:S(2)}) async-start(bf16[4,4,128,128]{3,2,1,0:T(8,128)(2,1)} %shard_map.42), calls=%async_computation.4 | async-start | bytes 1048576 | tf_op jit(solution)/shard_map/all_to_all | solution.py:128
  147.9 4.2 %shard_map.38 = bf16[4,4,128,256]{3,2,1,0:T(8,128)(2,1)} custom-call(s32[8]{0:T(128)S(1)} %get-tuple-element.47.choices_ref, bf16[2,512,1024]{2,1,0:T(8,128)(2,1)S(1)} %shard_map.37.lefts_ref, bf16[1024,256]{1,0:T(8,128)(2,1)S(1)} %collective-permute-done.refs_2_.refs_0_, bf16[1024,256]{1,0:T(8,128)(2,1)} %collective-permute-done.4.refs_1_, ...), custom_call_target="tpu_custom_call" | custom-call | flops 1073741824 | bytes 5242880 | tf_op jit(solution)/shard_map/pallas_call | solution.py:112
  152.0 4.7 %all-to-all-done.4 = bf16[4,4,128,128]{3,2,1,0:T(8,128)(2,1)} async-done(((bf16[4,4,128,128]{3,2,1,0:T(8,128)(2,1)}), bf16[4,4,128,128]{3,2,1,0:T(8,128)(2,1)}, u32[]{:S(2)}, u32[]{:S(2)}) %all-to-all-start.4) | async-done | bytes 524320 | tf_op jit(solution)/shard_map/all_to_all | solution.py:128
  156.8 3.5 %all-to-all-start = ((bf16[4,4,128,256]{3,2,1,0:T(8,128)(2,1)}), bf16[4,4,128,256]{3,2,1,0:T(8,128)(2,1)S(1)}, u32[]{:S(2)}, u32[]{:S(2)}) async-start(bf16[4,4,128,256]{3,2,1,0:T(8,128)(2,1)} %shard_map.38), calls=%async_computation | async-start | bytes 2097152 | tf_op jit(solution)/shard_map/all_to_all | solution.py:128
  168.5 6.2 %all-to-all-done = bf16[4,4,128,256]{3,2,1,0:T(8,128)(2,1)S(1)} async-done(((bf16[4,4,128,256]{3,2,1,0:T(8,128)(2,1)}), bf16[4,4,128,256]{3,2,1,0:T(8,128)(2,1)S(1)}, u32[]{:S(2)}, u32[]{:S(2)}) %all-to-all-start) | async-done | bytes 1048608 | tf_op jit(solution)/shard_map/all_to_all | solution.py:128
  178.4 8.4 %collective-permute-done.20 = bf16[4,128,128]{2,1,0:T(8,128)(2,1)S(1)} collective-permute-done((bf16[4,128,128]{2,1,0:T(8,128)(2,1)S(1)}, bf16[4,128,128]{2,1,0:T(8,128)(2,1)S(1)}, u32[]{:S(2)}, u32[]{:S(2)}) %collective-permute-start.20) | collective-permute-done | bytes 131104 | tf_op jit(solution)/shard_map/ppermute | solution.py:17
  187.0 5.1 %collective-permute-done.11 = bf16[4,128,256]{2,1,0:T(8,128)(2,1)S(1)} collective-permute-done((bf16[4,128,256]{2,1,0:T(8,128)(2,1)S(1)}, bf16[4,128,256]{2,1,0:T(8,128)(2,1)S(1)}, u32[]{:S(2)}, u32[]{:S(2)}) %collective-permute-start.11) | collective-permute-done | bytes 262176 | tf_op jit(solution)/shard_map/ppermute | solution.py:17
  (69 shorter events, 38.5 us)
Async XLA Ops:
  2.4 27.4 %collective-permute-start = (bf16[1024,256]{1,0:T(8,128)(2,1)S(1)}, bf16[1024,256]{1,0:T(8,128)(2,1)S(1)}, u32[]{:S(2)}, u32[]{:S(2)}) collective-permute-start(bf16[1024,256]{1,0:T(8,128)(2,1)S(1)} %get-tuple-element.37), channel_id=1, source_target_pairs={{0,4},{1,5},{2,6},{3,7},{4,0},{5,1},{6,2},{7,3},{8,12},{9,13},{10,... | collective-permute-start | bytes 1572872 | tf_op jit(solution)/shard_map/ppermute | solution.py:17
  6.5 23.5 %collective-permute-start.5 = (bf16[1024,256]{1,0:T(8,128)(2,1)S(1)}, bf16[1024,256]{1,0:T(8,128)(2,1)S(1)}, u32[]{:S(2)}, u32[]{:S(2)}) collective-permute-start(bf16[1024,256]{1,0:T(8,128)(2,1)S(1)} %get-tuple-element.36.refs_0_), channel_id=1, source_target_pairs={{0,2},{1,3},{2,0},{3,1},{4,6},{5,7},{6,4},{7,5},{8,10},{9,11},{10,... | collective-permute-start | bytes 1572872 | tf_op jit(solution)/shard_map/ppermute | solution.py:17
  8.1 21.9 %collective-permute-start.9 = (bf16[1024,256]{1,0:T(8,128)(2,1)S(1)}, bf16[1024,256]{1,0:T(8,128)(2,1)S(1)}, u32[]{:S(2)}, u32[]{:S(2)}) collective-permute-start(bf16[1024,256]{1,0:T(8,128)(2,1)S(1)} %get-tuple-element.36.refs_0_), channel_id=1, source_target_pairs={{0,1},{1,0},{2,3},{3,2},{4,5},{5,4},{6,7},{7,6},{8,9},{9,8},{10,11... | collective-permute-start | bytes 1572872 | tf_op jit(solution)/shard_map/ppermute | solution.py:17
  29.8 14.1 %collective-permute-start.1 = (bf16[1024,128]{1,0:T(8,128)(2,1)S(1)}, bf16[1024,128]{1,0:T(8,128)(2,1)S(1)}, u32[]{:S(2)}, u32[]{:S(2)}) collective-permute-start(bf16[1024,128]{1,0:T(8,128)(2,1)S(1)} %get-tuple-element.19), channel_id=1, source_target_pairs={{0,4},{1,5},{2,6},{3,7},{4,0},{5,1},{6,2},{7,3},{8,12},{9,13},{10,... | collective-permute-start | bytes 786440 | tf_op jit(solution)/shard_map/ppermute | solution.py:17
  30.0 27.6 %collective-permute-start.10 = (bf16[1024,256]{1,0:T(8,128)(2,1)S(1)}, bf16[1024,256]{1,0:T(8,128)(2,1)S(1)}, u32[]{:S(2)}, u32[]{:S(2)}) collective-permute-start(bf16[1024,256]{1,0:T(8,128)(2,1)S(1)} %collective-permute-done.5.refs_2_), channel_id=1, source_target_pairs={{0,1},{1,0},{2,3},{3,2},{4,5},{5,4},{6,7},{7,6},{8,9},{9,8},{10,11... | collective-permute-start | bytes 1572872 | tf_op jit(solution)/shard_map/ppermute | solution.py:17
  31.5 33.9 %collective-permute-start.6 = (bf16[1024,256]{1,0:T(8,128)(2,1)S(1)}, bf16[1024,256]{1,0:T(8,128)(2,1)}, u32[]{:S(2)}, u32[]{:S(2)}) collective-permute-start(bf16[1024,256]{1,0:T(8,128)(2,1)S(1)} %get-tuple-element.22.refs_1_.refs_0_), channel_id=1, source_target_pairs={{0,2},{1,3},{2,0},{3,1},{4,6},{5,7},{6,4},{7,5},{8,10},{9,11},{10,... | collective-permute-start | bytes 1572872 | tf_op jit(solution)/shard_map/ppermute | solution.py:17
  43.9 13.1 %collective-permute-start.2 = (bf16[1024,128]{1,0:T(8,128)(2,1)S(1)}, bf16[1024,128]{1,0:T(8,128)(2,1)S(1)}, u32[]{:S(2)}, u32[]{:S(2)}) collective-permute-start(bf16[1024,128]{1,0:T(8,128)(2,1)S(1)} %get-tuple-element.20), channel_id=1, source_target_pairs={{0,4},{1,5},{2,6},{3,7},{4,0},{5,1},{6,2},{7,3},{8,12},{9,13},{10,... | collective-permute-start | bytes 786440 | tf_op jit(solution)/shard_map/ppermute | solution.py:17
  61.1 34.3 %all-to-all-start.1 = ((bf16[4,4,128,256]{3,2,1,0:T(8,128)(2,1)}), bf16[4,4,128,256]{3,2,1,0:T(8,128)(2,1)}, u32[]{:S(2)}, u32[]{:S(2)}) async-start(bf16[4,4,128,256]{3,2,1,0:T(8,128)(2,1)} %copy-done.1), calls=%async_computation.1 | async-start | bytes 2097152 | tf_op jit(solution)/shard_map/all_to_all | solution.py:128
  65.3 14.8 %collective-permute-start.3 = (bf16[1024,256]{1,0:T(8,128)(2,1)S(1)}, bf16[1024,256]{1,0:T(8,128)(2,1)S(1)}, u32[]{:S(2)}, u32[]{:S(2)}) collective-permute-start(bf16[1024,256]{1,0:T(8,128)(2,1)S(1)} %get-tuple-element.22.refs_1_.refs_0_), channel_id=1, source_target_pairs={{0,1},{1,0},{2,3},{3,2},{4,5},{5,4},{6,7},{7,6},{8,9},{9,8},{10,11... | collective-permute-start | bytes 1572872 | tf_op jit(solution)/shard_map/ppermute | solution.py:17
  65.4 14.8 %collective-permute-start.7 = (bf16[1024,256]{1,0:T(8,128)(2,1)S(1)}, bf16[1024,256]{1,0:T(8,128)(2,1)S(1)}, u32[]{:S(2)}, u32[]{:S(2)}) collective-permute-start(bf16[1024,256]{1,0:T(8,128)(2,1)S(1)} %collective-permute-done.refs_2_.refs_0_), channel_id=1, source_target_pairs={{0,2},{1,3},{2,0},{3,1},{4,6},{5,7},{6,4},{7,5},{8,10},{9,11},{10,... | collective-permute-start | bytes 1572872 | tf_op jit(solution)/shard_map/ppermute | solution.py:17
  67.2 24.2 %collective-permute-start.12 = (bf16[1024,256]{1,0:T(8,128)(2,1)}, bf16[1024,256]{1,0:T(8,128)(2,1)S(1)}, u32[]{:S(2)}, u32[]{:S(2)}) collective-permute-start(bf16[1024,256]{1,0:T(8,128)(2,1)} %collective-permute-done.6.refs_2_), channel_id=1, source_target_pairs={{0,1},{1,0},{2,3},{3,2},{4,5},{5,4},{6,7},{7,6},{8,9},{9,8},{10,11... | collective-permute-start | bytes 1572872 | tf_op jit(solution)/shard_map/ppermute | solution.py:17
  80.2 22.0 %collective-permute-start.4 = (bf16[1024,256]{1,0:T(8,128)(2,1)S(1)}, bf16[1024,256]{1,0:T(8,128)(2,1)}, u32[]{:S(2)}, u32[]{:S(2)}) collective-permute-start(bf16[1024,256]{1,0:T(8,128)(2,1)S(1)} %collective-permute-done.refs_2_.refs_0_), channel_id=1, source_target_pairs={{0,1},{1,0},{2,3},{3,2},{4,5},{5,4},{6,7},{7,6},{8,9},{9,8},{10,11... | collective-permute-start | bytes 1572872 | tf_op jit(solution)/shard_map/ppermute | solution.py:17
  80.2 19.7 %collective-permute-start.14 = (bf16[1024,128]{1,0:T(8,128)(2,1)}, bf16[1024,128]{1,0:T(8,128)(2,1)}, u32[]{:S(2)}, u32[]{:S(2)}) collective-permute-start(bf16[1024,128]{1,0:T(8,128)(2,1)} %copy-done.2), channel_id=1, source_target_pairs={{0,2},{1,3},{2,0},{3,1},{4,6},{5,7},{6,4},{7,5},{8,10},{9,11},{10,... | collective-permute-start | bytes 786440 | tf_op jit(solution)/shard_map/ppermute | solution.py:17
  95.4 25.4 %all-to-all-start.3 = ((bf16[4,4,128,256]{3,2,1,0:T(8,128)(2,1)}), bf16[4,4,128,256]{3,2,1,0:T(8,128)(2,1)}, u32[]{:S(2)}, u32[]{:S(2)}) async-start(bf16[4,4,128,256]{3,2,1,0:T(8,128)(2,1)} %copy-done), calls=%async_computation.3 | async-start | bytes 2097152 | tf_op jit(solution)/shard_map/all_to_all | solution.py:128
  99.8 9.2 %collective-permute-start.13 = (bf16[1024,128]{1,0:T(8,128)(2,1)S(1)}, bf16[1024,128]{1,0:T(8,128)(2,1)S(1)}, u32[]{:S(2)}, u32[]{:S(2)}) collective-permute-start(bf16[1024,128]{1,0:T(8,128)(2,1)S(1)} %copy-done.3), channel_id=1, source_target_pairs={{0,1},{1,0},{2,3},{3,2},{4,5},{5,4},{6,7},{7,6},{8,9},{9,8},{10,11... | collective-permute-start | bytes 786440 | tf_op jit(solution)/shard_map/ppermute | solution.py:17
  102.2 24.3 %collective-permute-start.8 = (bf16[1024,256]{1,0:T(8,128)(2,1)}, bf16[1024,256]{1,0:T(8,128)(2,1)}, u32[]{:S(2)}, u32[]{:S(2)}) collective-permute-start(bf16[1024,256]{1,0:T(8,128)(2,1)} %copy-done.4), channel_id=1, source_target_pairs={{0,1},{1,0},{2,3},{3,2},{4,5},{5,4},{6,7},{7,6},{8,9},{9,8},{10,11... | collective-permute-start | bytes 1572872 | tf_op jit(solution)/shard_map/ppermute | solution.py:17
  120.8 22.9 %all-to-all-start.2 = ((bf16[4,4,128,128]{3,2,1,0:T(8,128)(2,1)}), bf16[4,4,128,128]{3,2,1,0:T(8,128)(2,1)}, u32[]{:S(2)}, u32[]{:S(2)}) async-start(bf16[4,4,128,128]{3,2,1,0:T(8,128)(2,1)} %shard_map.40), calls=%async_computation.2 | async-start | bytes 1048576 | tf_op jit(solution)/shard_map/all_to_all | solution.py:128
  125.0 9.4 %collective-permute-start.19 = (bf16[1024,128]{1,0:T(8,128)(2,1)}, bf16[1024,128]{1,0:T(8,128)(2,1)S(1)}, u32[]{:S(2)}, u32[]{:S(2)}) collective-permute-start(bf16[1024,128]{1,0:T(8,128)(2,1)} %copy-done.6), channel_id=1, source_target_pairs={{0,1},{1,0},{2,3},{3,2},{4,5},{5,4},{6,7},{7,6},{8,9},{9,8},{10,11... | collective-permute-start | bytes 786440 | tf_op jit(solution)/shard_map/ppermute | solution.py:17
  126.4 13.0 %collective-permute-start.18 = (bf16[1024,128]{1,0:T(8,128)(2,1)S(1)}, bf16[1024,128]{1,0:T(8,128)(2,1)S(1)}, u32[]{:S(2)}, u32[]{:S(2)}) collective-permute-start(bf16[1024,128]{1,0:T(8,128)(2,1)S(1)} %collective-permute-done.2.refs_4_.refs_0_), channel_id=1, source_target_pairs={{0,1},{1,0},{2,3},{3,2},{4,5},{5,4},{6,7},{7,6},{8,9},{9,8},{10,11... | collective-permute-start | bytes 786440 | tf_op jit(solution)/shard_map/ppermute | solution.py:17
  143.7 13.1 %all-to-all-start.4 = ((bf16[4,4,128,128]{3,2,1,0:T(8,128)(2,1)}), bf16[4,4,128,128]{3,2,1,0:T(8,128)(2,1)}, u32[]{:S(2)}, u32[]{:S(2)}) async-start(bf16[4,4,128,128]{3,2,1,0:T(8,128)(2,1)} %shard_map.42), calls=%async_computation.4 | async-start | bytes 1048576 | tf_op jit(solution)/shard_map/all_to_all | solution.py:128
  156.8 18.0 %all-to-all-start = ((bf16[4,4,128,256]{3,2,1,0:T(8,128)(2,1)}), bf16[4,4,128,256]{3,2,1,0:T(8,128)(2,1)S(1)}, u32[]{:S(2)}, u32[]{:S(2)}) async-start(bf16[4,4,128,256]{3,2,1,0:T(8,128)(2,1)} %shard_map.38), calls=%async_computation | async-start | bytes 2097152 | tf_op jit(solution)/shard_map/all_to_all | solution.py:128
  165.5 12.9 %collective-permute-start.17 = (bf16[4,128,128]{2,1,0:T(8,128)(2,1)S(1)}, bf16[4,128,128]{2,1,0:T(8,128)(2,1)S(1)}, u32[]{:S(2)}, u32[]{:S(2)}) collective-permute-start(bf16[4,128,128]{2,1,0:T(8,128)(2,1)S(1)} %get-tuple-element.40), channel_id=1, source_target_pairs={{0,4},{1,5},{2,6},{3,7},{4,0},{5,1},{6,2},{7,3},{8,12},{9,13},{10,... | collective-permute-start | bytes 393224 | tf_op jit(solution)/shard_map/ppermute | solution.py:17
  168.2 18.7 %collective-permute-start.20 = (bf16[4,128,128]{2,1,0:T(8,128)(2,1)S(1)}, bf16[4,128,128]{2,1,0:T(8,128)(2,1)S(1)}, u32[]{:S(2)}, u32[]{:S(2)}) collective-permute-start(bf16[4,128,128]{2,1,0:T(8,128)(2,1)S(1)} %get-tuple-element.41), channel_id=1, source_target_pairs={{0,4},{1,5},{2,6},{3,7},{4,0},{5,1},{6,2},{7,3},{8,12},{9,13},{10,... | collective-permute-start | bytes 393224 | tf_op jit(solution)/shard_map/ppermute | solution.py:17
  175.0 17.0 %collective-permute-start.11 = (bf16[4,128,256]{2,1,0:T(8,128)(2,1)S(1)}, bf16[4,128,256]{2,1,0:T(8,128)(2,1)S(1)}, u32[]{:S(2)}, u32[]{:S(2)}) collective-permute-start(bf16[4,128,256]{2,1,0:T(8,128)(2,1)S(1)} %select_convert_fusion), channel_id=1, source_target_pairs={{0,4},{1,5},{2,6},{3,7},{4,0},{5,1},{6,2},{7,3},{8,12},{9,13},{10,... | collective-permute-start | bytes 786440 | tf_op jit(solution)/shard_map/ppermute | solution.py:17
  (11 other events, 93.6 us)

commit v8 on v6

--- a/solution.py
+++ b/solution.py
@@ -11,7 +11,7 @@
 MATE_WIDTHS = (2, 1, 1)
 NEAR_FIRST = (3,)
 URGENCY = (0, 2, 1, 3, 4)
-BATCHES = (((0,), (2,)), ((1,),), ((3, 4),))
+BATCHES = (((0,), (2,)), ((1,), (3, 4)))
 VMEM = pl.BlockSpec(memory_space=pltpu.VMEM)
 PARAMS = pltpu.CompilerParams(vmem_limit_bytes=40 * 2**20)
 
@@ -45,7 +45,7 @@
         piece, low, bit = hop
         shared = 2 if bit == cut // 2 and start_of(hop) < crossed else 1
         free[bit] = start_of(hop) + shared * widths[piece]
-        ready[piece, low | bit] = free[bit] + 0.5
+        ready[piece, low | bit] = free[bit]
         waiting.remove(hop)
         ordered.append(hop)
     return ordered
@@ -196,10 +196,8 @@
         ]
         earlier = None
         if not halves:
-            earlier = (sent[cut // 2][-1], sent[1][4])
-        elif lists != BATCHES[-1]:
-            earlier = halves[0]
-        else:
+            earlier = sent[cut // 2][-1]
+        if lists == BATCHES[-1]:
             earlier = (given[0], halves[-1])
         even, odd = products(behind(choices, earlier), lefts, batch, scale_factor)
         halves.append(halved(even, odd, 1))
@@ -222,6 +220,8 @@
         earlier = sent.setdefault(bit, [])
         depth = 2 if bit == 1 else 1
         ties = earlier[-depth] if len(earlier) >= depth else None
+        if bit == 1 and low == 0 and halves and piece in BATCHES[-1][-1]:
+            ties = (ties, halves[0])
         held[piece][low | bit] = exchange(behind(held[piece][low], ties), "snap", bit)
         earlier.append(held[piece][low | bit])
         while len(halves) < len(BATCHES) and all(

time: 150 us -> 144 us (0.960)
  waiting for transfers between devices: 101 us -> 97.9 us
    ppermute x25 -> x23, waiting for transfers between devices: 101 us -> 97.9 us  [exchange(): lax.ppermute(part, axis, [(i, i ^ mask) for i in range(lax.axis_size(axis...]
    ppermute x25 -> x23, starting transfers between devices: 29.8 us -> 28.4 us  [exchange(): lax.ppermute(part, axis, [(i, i ^ mask) for i in range(lax.axis_size(axis...]
    pallas_call x3 -> x2, Pallas kernels: 11.2 us -> 10.6 us  [products(): pl.pallas_call(kernel, out_shape=[jax.ShapeDtypeStruct(shape, kind) for k...]
  transfers between devices with their start and end apart: 25 -> 23, of which waited for: 15 -> 16; matrix products, arithmetic and copies ran while one was open for 1% -> 1% of each run, Pallas kernels for 2% -> 0%
where the time goes in v8:
time: 144 us
  waiting for transfers between devices  97.9 us (68%)
  starting transfers between devices  28.4 us (20%)
  Pallas kernels  11.2 us (8%)
  other arithmetic  5.51 us (4%)
    ppermute x23, waiting for transfers between devices, exchange(): lax.ppermute(part, axis, [(i, i ^ mask) for i in range(lax.axis_size(axis...  97.9 us
    ppermute x23, starting transfers between devices, exchange(): lax.ppermute(part, axis, [(i, i ^ mask) for i in range(lax.axis_size(axis...  28.4 us
    pallas_call x2, Pallas kernels, products(): pl.pallas_call(kernel, out_shape=[jax.ShapeDtypeStruct(shape, kind) for k...  10.6 us
  transfers between devices with their start and end apart: 23, of which 16 were waited for; matrix products, arithmetic and copies ran while one was open for 1% of the time, Pallas kernels for 0%

profile of v8, /device:TPU:0, one launch (start us, length us, event | category | flops | bytes accessed | tf_op | source)
XLA Modules:
  0.0 144.1 jit_solution(111906525233200804)
XLA Ops:
  0.7 2.8 %multiply_convert_fusion = (bf16[1024,256]{1,0:T(8,128)(2,1)}, bf16[1024,256]{1,0:T(8,128)(2,1)S(1)}, bf16[1024,256]{1,0:T(8,128)(2,1)S(1)}, bf16[1024,256]{1,0:T(8,128)(2,1)S(1)}) fusion(bf16[2048,512]{1,0:T(8,128)(2,1)} %param.3, s32[]{:T(128)S(6)} %select_n.21, f32[1024]{0:T(1024)S(1)} %get-tuple-element.53, f32[1024]{0:T(1024)S(1)} %get-tuple-element.54, ...), kind=kLoop, calls=%fused_computation.9 | loop fusion | flops 3145728 | bytes 4202504 | tf_op jit(solution)/shard_map/convert_element_type | solution.py:163
  3.5 3.0 %collective-permute-start.1 = (bf16[1024,256]{1,0:T(8,128)(2,1)S(1)}, bf16[1024,256]{1,0:T(8,128)(2,1)S(1)}, u32[]{:S(2)}, u32[]{:S(2)}) collective-permute-start(bf16[1024,256]{1,0:T(8,128)(2,1)S(1)} %get-tuple-element.50.refs_0_), channel_id=1, source_target_pairs={{0,2},{1,3},{2,0},{3,1},{4,6},{5,7},{6,4},{7,5},{8,10},{9,11},{10,... | collective-permute-start | bytes 1572872 | tf_op jit(solution)/shard_map/ppermute | solution.py:20
  6.5 2.6 %collective-permute-start = (bf16[1024,256]{1,0:T(8,128)(2,1)S(1)}, bf16[1024,256]{1,0:T(8,128)(2,1)S(1)}, u32[]{:S(2)}, u32[]{:S(2)}) collective-permute-start(bf16[1024,256]{1,0:T(8,128)(2,1)S(1)} %get-tuple-element.46), channel_id=1, source_target_pairs={{0,4},{1,5},{2,6},{3,7},{4,0},{5,1},{6,2},{7,3},{8,12},{9,13},{10,... | collective-permute-start | bytes 1572872 | tf_op jit(solution)/shard_map/ppermute | solution.py:20
  11.1 18.4 %collective-permute-done.1.refs_2_ = bf16[1024,256]{1,0:T(8,128)(2,1)S(1)} collective-permute-done((bf16[1024,256]{1,0:T(8,128)(2,1)S(1)}, bf16[1024,256]{1,0:T(8,128)(2,1)S(1)}, u32[]{:S(2)}, u32[]{:S(2)}) %collective-permute-start.1) | collective-permute-done | bytes 524320 | tf_op jit(solution)/shard_map/ppermute | solution.py:20
  29.6 2.5 %collective-permute-done.refs_2_.refs_4_ = bf16[1024,256]{1,0:T(8,128)(2,1)S(1)} collective-permute-done((bf16[1024,256]{1,0:T(8,128)(2,1)S(1)}, bf16[1024,256]{1,0:T(8,128)(2,1)S(1)}, u32[]{:S(2)}, u32[]{:S(2)}) %collective-permute-start) | collective-permute-done | bytes 524320 | tf_op jit(solution)/shard_map/ppermute | solution.py:20
  34.0 2.7 %collective-permute-start.4 = (bf16[1024,256]{1,0:T(8,128)(2,1)}, bf16[1024,256]{1,0:T(8,128)(2,1)S(1)}, u32[]{:S(2)}, u32[]{:S(2)}) collective-permute-start(bf16[1024,256]{1,0:T(8,128)(2,1)} %get-tuple-element.28), channel_id=1, source_target_pairs={{0,4},{1,5},{2,6},{3,7},{4,0},{5,1},{6,2},{7,3},{8,12},{9,13},{10,... | collective-permute-start | bytes 1572872 | tf_op jit(solution)/shard_map/ppermute | solution.py:20
  37.2 15.0 %collective-permute-done.2.refs_6_ = bf16[1024,256]{1,0:T(8,128)(2,1)} collective-permute-done((bf16[1024,256]{1,0:T(8,128)(2,1)S(1)}, bf16[1024,256]{1,0:T(8,128)(2,1)}, u32[]{:S(2)}, u32[]{:S(2)}) %collective-permute-start.2) | collective-permute-done | bytes 524320 | tf_op jit(solution)/shard_map/ppermute | solution.py:20
  52.2 2.6 %collective-permute-start.9 = (bf16[1024,256]{1,0:T(8,128)(2,1)}, bf16[1024,256]{1,0:T(8,128)(2,1)S(1)}, u32[]{:S(2)}, u32[]{:S(2)}) collective-permute-start(bf16[1024,256]{1,0:T(8,128)(2,1)} %collective-permute-done.2.refs_6_), channel_id=1, source_target_pairs={{0,1},{1,0},{2,3},{3,2},{4,5},{5,4},{6,7},{7,6},{8,9},{9,8},{10,11... | collective-permute-start | bytes 1572872 | tf_op jit(solution)/shard_map/ppermute | solution.py:20
  54.9 3.8 %collective-permute-done.4.refs_3_ = bf16[1024,256]{1,0:T(8,128)(2,1)S(1)} collective-permute-done((bf16[1024,256]{1,0:T(8,128)(2,1)}, bf16[1024,256]{1,0:T(8,128)(2,1)S(1)}, u32[]{:S(2)}, u32[]{:S(2)}) %collective-permute-start.4) | collective-permute-done | bytes 524320 | tf_op jit(solution)/shard_map/ppermute | solution.py:20
  59.3 8.7 %collective-permute-done.3.refs_2_ = bf16[1024,256]{1,0:T(8,128)(2,1)S(1)} collective-permute-done((bf16[1024,256]{1,0:T(8,128)(2,1)S(1)}, bf16[1024,256]{1,0:T(8,128)(2,1)S(1)}, u32[]{:S(2)}, u32[]{:S(2)}) %collective-permute-start.3) | collective-permute-done | bytes 524320 | tf_op jit(solution)/shard_map/ppermute | solution.py:20
  68.0 5.4 %shard_map.38 = (f32[2,4,128,512]{3,2,1,0:T(8,128)S(1)}, bf16[2,4,128,512]{3,2,1,0:T(8,128)(2,1)S(1)}) custom-call(s32[9]{0:T(128)S(1)} %pad_add_fusion.choices_ref, bf16[2,512,1024]{2,1,0:T(8,128)(2,1)S(1)} %shard_map.37.lefts_ref, bf16[1024,256]{1,0:T(8,128)(2,1)S(1)} %get-tuple-element.50.refs_0_, bf16[1024,256]{1,0:T(8,128)(2,1)S(1)} %collective-permute-done.5.refs_1_, ...), custom_call_target="tpu_custom_call" | custom-call | tf_op jit(solution)/shard_map/pallas_call | solution.py:118
  76.6 1.6 %collective-permute-start.11 = (bf16[1,4,128,512]{3,2,1,0:T(8,128)(2,1)S(1)}, bf16[1,4,128,512]{3,2,1,0:T(8,128)(2,1)S(1)}, u32[]{:S(2)}, u32[]{:S(2)}) collective-permute-start(bf16[1,4,128,512]{3,2,1,0:T(8,128)(2,1)S(1)} %slice.73), channel_id=1, source_target_pairs={{0,16},{8,24},{16,0},{24,8},{1,17},{9,25},{17,1},{25,9},{2,18},{10... | collective-permute-start | bytes 1572872 | tf_op jit(solution)/shard_map/ppermute | solution.py:20
  78.2 4.1 %collective-permute-done.15.refs_6_ = bf16[1024,128]{1,0:T(8,128)(2,1)S(1)} collective-permute-done((bf16[1024,128]{1,0:T(8,128)(2,1)S(1)}, bf16[1024,128]{1,0:T(8,128)(2,1)S(1)}, u32[]{:S(2)}, u32[]{:S(2)}) %collective-permute-start.15) | collective-permute-done | bytes 262176 | tf_op jit(solution)/shard_map/ppermute | solution.py:20
  83.6 4.8 %collective-permute-done.13.refs_3_ = bf16[1024,256]{1,0:T(8,128)(2,1)S(1)} collective-permute-done((bf16[1024,256]{1,0:T(8,128)(2,1)S(1)}, bf16[1024,256]{1,0:T(8,128)(2,1)S(1)}, u32[]{:S(2)}, u32[]{:S(2)}) %collective-permute-start.13) | collective-permute-done | bytes 524320 | tf_op jit(solution)/shard_map/ppermute | solution.py:20
  90.2 3.8 %collective-permute-done.14.refs_5_ = bf16[1024,128]{1,0:T(8,128)(2,1)S(1)} collective-permute-done((bf16[1024,128]{1,0:T(8,128)(2,1)S(1)}, bf16[1024,128]{1,0:T(8,128)(2,1)S(1)}, u32[]{:S(2)}, u32[]{:S(2)}) %collective-permute-start.14) | collective-permute-done | bytes 262176 | tf_op jit(solution)/shard_map/ppermute | solution.py:20
  95.3 1.7 %collective-permute-start.17 = (bf16[1024,128]{1,0:T(8,128)(2,1)S(1)}, bf16[1024,128]{1,0:T(8,128)(2,1)S(1)}, u32[]{:S(2)}, u32[]{:S(2)}) collective-permute-start(bf16[1024,128]{1,0:T(8,128)(2,1)S(1)} %collective-permute-done.14.refs_5_), channel_id=1, source_target_pairs={{0,2},{1,3},{2,0},{3,1},{4,6},{5,7},{6,4},{7,5},{8,10},{9,11},{10,... | collective-permute-start | bytes 786440 | tf_op jit(solution)/shard_map/ppermute | solution.py:20
  97.3 2.4 %collective-permute-done.18.refs_9_ = bf16[1024,128]{1,0:T(8,128)(2,1)S(1)} collective-permute-done((bf16[1024,128]{1,0:T(8,128)(2,1)S(1)}, bf16[1024,128]{1,0:T(8,128)(2,1)S(1)}, u32[]{:S(2)}, u32[]{:S(2)}) %collective-permute-start.18) | collective-permute-done | bytes 262176 | tf_op jit(solution)/shard_map/ppermute | solution.py:20
  99.7 5.2 %collective-permute-done.19.refs_11_ = bf16[1024,128]{1,0:T(8,128)(2,1)S(1)} collective-permute-done((bf16[1024,128]{1,0:T(8,128)(2,1)S(1)}, bf16[1024,128]{1,0:T(8,128)(2,1)S(1)}, u32[]{:S(2)}, u32[]{:S(2)}) %collective-permute-start.19) | collective-permute-done | bytes 262176 | tf_op jit(solution)/shard_map/ppermute | solution.py:20
  104.9 5.1 %shard_map.39 = (f32[2,4,128,512]{3,2,1,0:T(8,128)S(1)}, bf16[2,4,128,512]{3,2,1,0:T(8,128)(2,1)S(1)}) custom-call(s32[9]{0:T(128)S(1)} %pad_add_fusion.choices_ref, bf16[2,512,1024]{2,1,0:T(8,128)(2,1)S(1)} %shard_map.37.lefts_ref, bf16[1024,256]{1,0:T(8,128)(2,1)S(1)} %get-tuple-element.26.refs_1_.refs_0_, ...), custom_call_target="tpu_custom_call" | custom-call | tf_op jit(solution)/shard_map/pallas_call | solution.py:118
  110.1 2.6 %collective-permute-done.20 = bf16[2,4,128,512]{3,2,1,0:T(8,128)(2,1)S(1)} collective-permute-done((bf16[2,4,128,512]{3,2,1,0:T(8,128)(2,1)S(1)}, bf16[2,4,128,512]{3,2,1,0:T(8,128)(2,1)S(1)}, u32[]{:S(2)}, u32[]{:S(2)}) %collective-permute-start.20) | collective-permute-done | bytes 1048608 | tf_op jit(solution)/shard_map/ppermute | solution.py:20
  114.8 2.4 %collective-permute-start.12 = (bf16[4,128,256]{2,1,0:T(8,128)(2,1)S(1)}, bf16[4,128,256]{2,1,0:T(8,128)(2,1)S(1)}, u32[]{:S(2)}, u32[]{:S(2)}) collective-permute-start(bf16[4,128,256]{2,1,0:T(8,128)(2,1)S(1)} %select_convert_fusion.1), channel_id=1, source_target_pairs={{0,4},{1,5},{2,6},{3,7},{4,0},{5,1},{6,2},{7,3},{8,12},{9,13},{10,... | collective-permute-start | bytes 786440 | tf_op jit(solution)/shard_map/ppermute | solution.py:20
  117.1 10.1 %collective-permute-done.21 = bf16[1,4,128,512]{3,2,1,0:T(8,128)(2,1)S(1)} collective-permute-done((bf16[1,4,128,512]{3,2,1,0:T(8,128)(2,1)S(1)}, bf16[1,4,128,512]{3,2,1,0:T(8,128)(2,1)S(1)}, u32[]{:S(2)}, u32[]{:S(2)}) %collective-permute-start.21) | collective-permute-done | bytes 524320 | tf_op jit(solution)/shard_map/ppermute | solution.py:20
  127.5 1.9 %collective-permute-done.12 = bf16[4,128,256]{2,1,0:T(8,128)(2,1)S(1)} collective-permute-done((bf16[4,128,256]{2,1,0:T(8,128)(2,1)S(1)}, bf16[4,128,256]{2,1,0:T(8,128)(2,1)S(1)}, u32[]{:S(2)}, u32[]{:S(2)}) %collective-permute-start.12) | collective-permute-done | bytes 262176 | tf_op jit(solution)/shard_map/ppermute | solution.py:20
  129.9 12.8 %collective-permute-done.22 = bf16[4,128,256]{2,1,0:T(8,128)(2,1)S(1)} collective-permute-done((bf16[4,128,256]{2,1,0:T(8,128)(2,1)S(1)}, bf16[4,128,256]{2,1,0:T(8,128)(2,1)S(1)}, u32[]{:S(2)}, u32[]{:S(2)}) %collective-permute-start.22) | collective-permute-done | bytes 262176 | tf_op jit(solution)/shard_map/ppermute | solution.py:20
  (44 shorter events, 18.0 us)
Async XLA Ops:
  0.7 54.0 %copy-start = (s32[4]{0:T(128)S(1)}, s32[4]{0:T(128)}, u32[]{:S(2)}) copy-start(s32[4]{0:T(128)} %param.5) | copy-start | bytes 52
  3.5 26.1 %collective-permute-start.1 = (bf16[1024,256]{1,0:T(8,128)(2,1)S(1)}, bf16[1024,256]{1,0:T(8,128)(2,1)S(1)}, u32[]{:S(2)}, u32[]{:S(2)}) collective-permute-start(bf16[1024,256]{1,0:T(8,128)(2,1)S(1)} %get-tuple-element.50.refs_0_), channel_id=1, source_target_pairs={{0,2},{1,3},{2,0},{3,1},{4,6},{5,7},{6,4},{7,5},{8,10},{9,11},{10,... | collective-permute-start | bytes 1572872 | tf_op jit(solution)/shard_map/ppermute | solution.py:20
  6.5 25.6 %collective-permute-start = (bf16[1024,256]{1,0:T(8,128)(2,1)S(1)}, bf16[1024,256]{1,0:T(8,128)(2,1)S(1)}, u32[]{:S(2)}, u32[]{:S(2)}) collective-permute-start(bf16[1024,256]{1,0:T(8,128)(2,1)S(1)} %get-tuple-element.46), channel_id=1, source_target_pairs={{0,4},{1,5},{2,6},{3,7},{4,0},{5,1},{6,2},{7,3},{8,12},{9,13},{10,... | collective-permute-start | bytes 1572872 | tf_op jit(solution)/shard_map/ppermute | solution.py:20
  9.1 23.4 %collective-permute-start.5 = (bf16[1024,256]{1,0:T(8,128)(2,1)S(1)}, bf16[1024,256]{1,0:T(8,128)(2,1)S(1)}, u32[]{:S(2)}, u32[]{:S(2)}) collective-permute-start(bf16[1024,256]{1,0:T(8,128)(2,1)S(1)} %get-tuple-element.50.refs_0_), channel_id=1, source_target_pairs={{0,1},{1,0},{2,3},{3,2},{4,5},{5,4},{6,7},{7,6},{8,9},{9,8},{10,11... | collective-permute-start | bytes 1572872 | tf_op jit(solution)/shard_map/ppermute | solution.py:20
  10.6 26.1 %collective-permute-start.7 = (bf16[1024,256]{1,0:T(8,128)(2,1)S(1)}, bf16[1024,256]{1,0:T(8,128)(2,1)S(1)}, u32[]{:S(2)}, u32[]{:S(2)}) collective-permute-start(bf16[1024,256]{1,0:T(8,128)(2,1)S(1)} %get-tuple-element.26.refs_1_.refs_0_), channel_id=1, source_target_pairs={{0,1},{1,0},{2,3},{3,2},{4,5},{5,4},{6,7},{7,6},{8,9},{9,8},{10,11... | collective-permute-start | bytes 1572872 | tf_op jit(solution)/shard_map/ppermute | solution.py:20
  32.1 20.1 %collective-permute-start.2 = (bf16[1024,256]{1,0:T(8,128)(2,1)S(1)}, bf16[1024,256]{1,0:T(8,128)(2,1)}, u32[]{:S(2)}, u32[]{:S(2)}) collective-permute-start(bf16[1024,256]{1,0:T(8,128)(2,1)S(1)} %collective-permute-done.refs_2_.refs_4_), channel_id=1, source_target_pairs={{0,2},{1,3},{2,0},{3,1},{4,6},{5,7},{6,4},{7,5},{8,10},{9,11},{10,... | collective-permute-start | bytes 1572872 | tf_op jit(solution)/shard_map/ppermute | solution.py:20
  32.5 19.7 %collective-permute-start.6 = (bf16[1024,256]{1,0:T(8,128)(2,1)S(1)}, bf16[1024,256]{1,0:T(8,128)(2,1)}, u32[]{:S(2)}, u32[]{:S(2)}) collective-permute-start(bf16[1024,256]{1,0:T(8,128)(2,1)S(1)} %collective-permute-done.1.refs_2_), channel_id=1, source_target_pairs={{0,1},{1,0},{2,3},{3,2},{4,5},{5,4},{6,7},{7,6},{8,9},{9,8},{10,11... | collective-permute-start | bytes 1572872 | tf_op jit(solution)/shard_map/ppermute | solution.py:20
  34.0 24.7 %collective-permute-start.4 = (bf16[1024,256]{1,0:T(8,128)(2,1)}, bf16[1024,256]{1,0:T(8,128)(2,1)S(1)}, u32[]{:S(2)}, u32[]{:S(2)}) collective-permute-start(bf16[1024,256]{1,0:T(8,128)(2,1)} %get-tuple-element.28), channel_id=1, source_target_pairs={{0,4},{1,5},{2,6},{3,7},{4,0},{5,1},{6,2},{7,3},{8,12},{9,13},{10,... | collective-permute-start | bytes 1572872 | tf_op jit(solution)/shard_map/ppermute | solution.py:20
  36.7 31.3 %collective-permute-start.8 = (bf16[1024,256]{1,0:T(8,128)(2,1)S(1)}, bf16[1024,256]{1,0:T(8,128)(2,1)S(1)}, u32[]{:S(2)}, u32[]{:S(2)}) collective-permute-start(bf16[1024,256]{1,0:T(8,128)(2,1)S(1)} %collective-permute-done.refs_2_.refs_4_), channel_id=1, source_target_pairs={{0,1},{1,0},{2,3},{3,2},{4,5},{5,4},{6,7},{7,6},{8,9},{9,8},{10,11... | collective-permute-start | bytes 1572872 | tf_op jit(solution)/shard_map/ppermute | solution.py:20
  52.2 15.8 %collective-permute-start.9 = (bf16[1024,256]{1,0:T(8,128)(2,1)}, bf16[1024,256]{1,0:T(8,128)(2,1)S(1)}, u32[]{:S(2)}, u32[]{:S(2)}) collective-permute-start(bf16[1024,256]{1,0:T(8,128)(2,1)} %collective-permute-done.2.refs_6_), channel_id=1, source_target_pairs={{0,1},{1,0},{2,3},{3,2},{4,5},{5,4},{6,7},{7,6},{8,9},{9,8},{10,11... | collective-permute-start | bytes 1572872 | tf_op jit(solution)/shard_map/ppermute | solution.py:20
  54.7 13.2 %collective-permute-start.3 = (bf16[1024,256]{1,0:T(8,128)(2,1)S(1)}, bf16[1024,256]{1,0:T(8,128)(2,1)S(1)}, u32[]{:S(2)}, u32[]{:S(2)}) collective-permute-start(bf16[1024,256]{1,0:T(8,128)(2,1)S(1)} %get-tuple-element.26.refs_1_.refs_0_), channel_id=1, source_target_pairs={{0,2},{1,3},{2,0},{3,1},{4,6},{5,7},{6,4},{7,5},{8,10},{9,11},{10,... | collective-permute-start | bytes 1572872 | tf_op jit(solution)/shard_map/ppermute | solution.py:20
  73.4 2.7 %collective-permute-start.10 = (bf16[2,4,128,512]{3,2,1,0:T(8,128)(2,1)S(1)}, bf16[2,4,128,512]{3,2,1,0:T(8,128)(2,1)S(1)}, u32[]{:S(2)}, u32[]{:S(2)}) collective-permute-start(bf16[2,4,128,512]{3,2,1,0:T(8,128)(2,1)S(1)} %get-tuple-element.33), channel_id=1, source_target_pairs={{0,8},{8,0},{16,24},{24,16},{1,9},{9,1},{17,25},{25,17},{2,10},{10... | collective-permute-start | bytes 3145736 | tf_op jit(solution)/shard_map/ppermute | solution.py:20
  73.6 8.8 %collective-permute-start.15 = (bf16[1024,128]{1,0:T(8,128)(2,1)S(1)}, bf16[1024,128]{1,0:T(8,128)(2,1)S(1)}, u32[]{:S(2)}, u32[]{:S(2)}) collective-permute-start(bf16[1024,128]{1,0:T(8,128)(2,1)S(1)} %get-tuple-element.37.refs_4_), channel_id=1, source_target_pairs={{0,2},{1,3},{2,0},{3,1},{4,6},{5,7},{6,4},{7,5},{8,10},{9,11},{10,... | collective-permute-start | bytes 786440 | tf_op jit(solution)/shard_map/ppermute | solution.py:20
  73.6 14.8 %collective-permute-start.13 = (bf16[1024,256]{1,0:T(8,128)(2,1)S(1)}, bf16[1024,256]{1,0:T(8,128)(2,1)S(1)}, u32[]{:S(2)}, u32[]{:S(2)}) collective-permute-start(bf16[1024,256]{1,0:T(8,128)(2,1)S(1)} %collective-permute-done.3.refs_2_), channel_id=1, source_target_pairs={{0,1},{1,0},{2,3},{3,2},{4,5},{5,4},{6,7},{7,6},{8,9},{9,8},{10,11... | collective-permute-start | bytes 1572872 | tf_op jit(solution)/shard_map/ppermute | solution.py:20
  76.6 20.4 %collective-permute-start.11 = (bf16[1,4,128,512]{3,2,1,0:T(8,128)(2,1)S(1)}, bf16[1,4,128,512]{3,2,1,0:T(8,128)(2,1)S(1)}, u32[]{:S(2)}, u32[]{:S(2)}) collective-permute-start(bf16[1,4,128,512]{3,2,1,0:T(8,128)(2,1)S(1)} %slice.73), channel_id=1, source_target_pairs={{0,16},{8,24},{16,0},{24,8},{1,17},{9,25},{17,1},{25,9},{2,18},{10... | collective-permute-start | bytes 1572872 | tf_op jit(solution)/shard_map/ppermute | solution.py:20
  82.3 7.9 %collective-permute-start.16 = (bf16[1024,128]{1,0:T(8,128)(2,1)S(1)}, bf16[1024,128]{1,0:T(8,128)(2,1)S(1)}, u32[]{:S(2)}, u32[]{:S(2)}) collective-permute-start(bf16[1024,128]{1,0:T(8,128)(2,1)S(1)} %get-tuple-element.40.refs_8_), channel_id=1, source_target_pairs={{0,2},{1,3},{2,0},{3,1},{4,6},{5,7},{6,4},{7,5},{8,10},{9,11},{10,... | collective-permute-start | bytes 786440 | tf_op jit(solution)/shard_map/ppermute | solution.py:20
  82.6 11.4 %collective-permute-start.14 = (bf16[1024,128]{1,0:T(8,128)(2,1)S(1)}, bf16[1024,128]{1,0:T(8,128)(2,1)S(1)}, u32[]{:S(2)}, u32[]{:S(2)}) collective-permute-start(bf16[1024,128]{1,0:T(8,128)(2,1)S(1)} %get-tuple-element.37.refs_4_), channel_id=1, source_target_pairs={{0,1},{1,0},{2,3},{3,2},{4,5},{5,4},{6,7},{7,6},{8,9},{9,8},{10,11... | collective-permute-start | bytes 786440 | tf_op jit(solution)/shard_map/ppermute | solution.py:20
  88.4 11.2 %collective-permute-start.18 = (bf16[1024,128]{1,0:T(8,128)(2,1)S(1)}, bf16[1024,128]{1,0:T(8,128)(2,1)S(1)}, u32[]{:S(2)}, u32[]{:S(2)}) collective-permute-start(bf16[1024,128]{1,0:T(8,128)(2,1)S(1)} %get-tuple-element.40.refs_8_), channel_id=1, source_target_pairs={{0,1},{1,0},{2,3},{3,2},{4,5},{5,4},{6,7},{7,6},{8,9},{9,8},{10,11... | collective-permute-start | bytes 786440 | tf_op jit(solution)/shard_map/ppermute | solution.py:20
  94.0 10.8 %collective-permute-start.19 = (bf16[1024,128]{1,0:T(8,128)(2,1)S(1)}, bf16[1024,128]{1,0:T(8,128)(2,1)S(1)}, u32[]{:S(2)}, u32[]{:S(2)}) collective-permute-start(bf16[1024,128]{1,0:T(8,128)(2,1)S(1)} %collective-permute-done.16.refs_10_), channel_id=1, source_target_pairs={{0,1},{1,0},{2,3},{3,2},{4,5},{5,4},{6,7},{7,6},{8,9},{9,8},{10,11... | collective-permute-start | bytes 786440 | tf_op jit(solution)/shard_map/ppermute | solution.py:20
  95.3 9.6 %collective-permute-start.17 = (bf16[1024,128]{1,0:T(8,128)(2,1)S(1)}, bf16[1024,128]{1,0:T(8,128)(2,1)S(1)}, u32[]{:S(2)}, u32[]{:S(2)}) collective-permute-start(bf16[1024,128]{1,0:T(8,128)(2,1)S(1)} %collective-permute-done.14.refs_5_), channel_id=1, source_target_pairs={{0,2},{1,3},{2,0},{3,1},{4,6},{5,7},{6,4},{7,5},{8,10},{9,11},{10,... | collective-permute-start | bytes 786440 | tf_op jit(solution)/shard_map/ppermute | solution.py:20
  110.0 2.7 %collective-permute-start.20 = (bf16[2,4,128,512]{3,2,1,0:T(8,128)(2,1)S(1)}, bf16[2,4,128,512]{3,2,1,0:T(8,128)(2,1)S(1)}, u32[]{:S(2)}, u32[]{:S(2)}) collective-permute-start(bf16[2,4,128,512]{3,2,1,0:T(8,128)(2,1)S(1)} %get-tuple-element.43), channel_id=1, source_target_pairs={{0,8},{8,0},{16,24},{24,16},{1,9},{9,1},{17,25},{25,17},{2,10},{10... | collective-permute-start | bytes 3145736 | tf_op jit(solution)/shard_map/ppermute | solution.py:20
  113.2 14.0 %collective-permute-start.21 = (bf16[1,4,128,512]{3,2,1,0:T(8,128)(2,1)S(1)}, bf16[1,4,128,512]{3,2,1,0:T(8,128)(2,1)S(1)}, u32[]{:S(2)}, u32[]{:S(2)}) collective-permute-start(bf16[1,4,128,512]{3,2,1,0:T(8,128)(2,1)S(1)} %slice.72), channel_id=1, source_target_pairs={{0,16},{8,24},{16,0},{24,8},{1,17},{9,25},{17,1},{25,9},{2,18},{10... | collective-permute-start | bytes 1572872 | tf_op jit(solution)/shard_map/ppermute | solution.py:20
  114.8 14.6 %collective-permute-start.12 = (bf16[4,128,256]{2,1,0:T(8,128)(2,1)S(1)}, bf16[4,128,256]{2,1,0:T(8,128)(2,1)S(1)}, u32[]{:S(2)}, u32[]{:S(2)}) collective-permute-start(bf16[4,128,256]{2,1,0:T(8,128)(2,1)S(1)} %select_convert_fusion.1), channel_id=1, source_target_pairs={{0,4},{1,5},{2,6},{3,7},{4,0},{5,1},{6,2},{7,3},{8,12},{9,13},{10,... | collective-permute-start | bytes 786440 | tf_op jit(solution)/shard_map/ppermute | solution.py:20
  129.4 13.3 %collective-permute-start.22 = (bf16[4,128,256]{2,1,0:T(8,128)(2,1)S(1)}, bf16[4,128,256]{2,1,0:T(8,128)(2,1)S(1)}, u32[]{:S(2)}, u32[]{:S(2)}) collective-permute-start(bf16[4,128,256]{2,1,0:T(8,128)(2,1)S(1)} %select_convert_fusion), channel_id=1, source_target_pairs={{0,4},{1,5},{2,6},{3,7},{4,0},{5,1},{6,2},{7,3},{8,12},{9,13},{10,... | collective-permute-start | bytes 786440 | tf_op jit(solution)/shard_map/ppermute | solution.py:20

commit v9 on v8

--- a/solution.py
+++ b/solution.py
@@ -82,37 +82,33 @@
 
     def kernel(choices_ref, lefts_ref, *refs):
         waiting = list(refs[: len(arrays)])
-        even_ref, odd_ref, picked, tile = refs[len(arrays) :]
+        even_ref, odd_ref, tiles = refs[len(arrays) :]
         first = 0
         for (mates, pieces), width in zip(batch, widths):
             sources = [[waiting.pop(0) for _ in blocks] for blocks in pieces]
             columns = pl.ds(first, width)
             first += width
 
-            def one_round(round_number, carry):
-                begin = 0
+            for round_number in range(ROUNDS):
+                parts = []
                 for block_refs in sources:
-                    end = begin + block_refs[0].shape[1]
-                    for number, block_ref in enumerate(block_refs):
-
-                        @pl.when(choices_ref[round_number] == number)
-                        def _():
-                            picked[:, begin:end] = block_ref[...]
-
-                    begin = end
+                    part = block_refs[0][...]
+                    for number, block_ref in enumerate(block_refs[1:], 1):
+                        wanted = choices_ref[round_number] == number
+                        part = jnp.where(wanted, block_ref[...], part)
+                    parts.append(part)
+                right = jnp.concatenate(parts, axis=1) if len(parts) > 1 else parts[0]
                 side = choices_ref[ROUNDS + round_number]
                 left = lefts_ref[1 - side if mates else side]
+                tile = tiles.at[round_number % 2]
                 tile[:, :width] = scale_factor * jnp.dot(
-                    left, picked[:, :width], preferred_element_type=jnp.float32
+                    left, right, preferred_element_type=jnp.float32
                 )
                 for number in range(slab_count):
                     start = jnp.bitwise_xor(choices_ref[2 * ROUNDS], number) * rows
                     part = tile[pl.ds(pl.multiple_of(start, rows), rows), :width]
                     out_ref = odd_ref if number % 2 else even_ref
                     out_ref[number // 2, round_number, :, columns] = part.astype(out_ref.dtype)
-                return carry
-
-            lax.fori_loop(0, ROUNDS, one_round, 0)
 
     shape = (slab_count // 2, ROUNDS, rows, sum(widths))
     return pl.pallas_call(
@@ -120,10 +116,7 @@
         out_shape=[jax.ShapeDtypeStruct(shape, kind) for kind in (jnp.float32, jnp.bfloat16)],
         in_specs=[pl.BlockSpec(memory_space=pltpu.SMEM)] + [VMEM] * (1 + len(arrays)),
         out_specs=[VMEM, VMEM],
-        scratch_shapes=[
-            pltpu.VMEM((cells, max(widths)), jnp.bfloat16),
-            pltpu.VMEM((group, max(widths)), jnp.float32),
-        ],
+        scratch_shapes=[pltpu.VMEM((2, group, max(widths)), jnp.float32)],
         compiler_params=PARAMS,
         cost_estimate=pl.CostEstimate(flops=0, bytes_accessed=0, transcendentals=0),
     )(choices, lefts, *arrays)
@@ -158,7 +151,9 @@
         found, first = [], 0
         for width in widths:
             part = lax.dynamic_slice(
-                snapshots, (side * half, first * quarter), (half, width * quarter)
+                behind(snapshots, found[0] if found else None),
+                (side * half, first * quarter),
+                (half, width * quarter),
             )
             found.append((part.astype(jnp.float32) * scale).astype(jnp.bfloat16))
             first += width

time: 144 us -> 140 us (0.972)
  waiting for transfers between devices: 97.9 us -> 92.7 us
  Pallas kernels: 11.2 us -> 8.13 us
  starting transfers between devices: 28.4 us -> 31 us
    ppermute x23, waiting for transfers between devices: 97.9 us -> 92.7 us  [exchange(): lax.ppermute(part, axis, [(i, i ^ mask) for i in range(lax.axis_size(axis...]
    pallas_call x2, Pallas kernels: 10.6 us -> 7.5 us  [products(): pl.pallas_call(kernel, out_shape=[jax.ShapeDtypeStruct(shape, kind) for k...]
    ppermute x23, starting transfers between devices: 28.4 us -> 31 us  [exchange(): lax.ppermute(part, axis, [(i, i ^ mask) for i in range(lax.axis_size(axis...]
    convert_element_type x1 -> x3, other arithmetic: 2.77 us -> 4.03 us  [pieces_of(): found.append((part.astype(jnp.float32) * scale).astype(jnp.bfloat16))]
  transfers between devices with their start and end apart: 23 -> 23, of which waited for: 16 -> 16; matrix products, arithmetic and copies ran while one was open for 1% -> 3% of each run, Pallas kernels for 0% -> 0%
where the time goes in v9:
time: 140 us
  waiting for transfers between devices  92.7 us (66%)
  starting transfers between devices  31 us (22%)
  Pallas kernels  8.13 us (6%)
  other arithmetic  6.77 us (5%)
    ppermute x23, waiting for transfers between devices, exchange(): lax.ppermute(part, axis, [(i, i ^ mask) for i in range(lax.axis_size(axis...  92.7 us
    ppermute x23, starting transfers between devices, exchange(): lax.ppermute(part, axis, [(i, i ^ mask) for i in range(lax.axis_size(axis...  31 us
    pallas_call x2, Pallas kernels, products(): pl.pallas_call(kernel, out_shape=[jax.ShapeDtypeStruct(shape, kind) for k...  7.5 us
    convert_element_type x3, other arithmetic, pieces_of(): found.append((part.astype(jnp.float32) * scale).astype(jnp.bfloat16))  4.03 us
  transfers between devices with their start and end apart: 23, of which 16 were waited for; matrix products, arithmetic and copies ran while one was open for 3% of the time, Pallas kernels for 0%

profile of v9, /device:TPU:0, one launch (start us, length us, event | category | flops | bytes accessed | tf_op | source)
XLA Modules:
  0.0 139.7 jit_solution(8707745854699396448)
XLA Ops:
  2.3 3.1 %collective-permute-start.1 = (bf16[1024,256]{1,0:T(8,128)(2,1)S(1)}, bf16[1024,256]{1,0:T(8,128)(2,1)S(1)}, u32[]{:S(2)}, u32[]{:S(2)}) collective-permute-start(bf16[1024,256]{1,0:T(8,128)(2,1)S(1)} %get-tuple-element.50.refs_0_), channel_id=1, source_target_pairs={{0,2},{1,3},{2,0},{3,1},{4,6},{5,7},{6,4},{7,5},{8,10},{9,11},{10,... | collective-permute-start | bytes 1572872 | tf_op jit(solution)/shard_map/ppermute | solution.py:20
  5.4 2.6 %collective-permute-start = (bf16[1024,256]{1,0:T(8,128)(2,1)S(1)}, bf16[1024,256]{1,0:T(8,128)(2,1)S(1)}, u32[]{:S(2)}, u32[]{:S(2)}) collective-permute-start(bf16[1024,256]{1,0:T(8,128)(2,1)S(1)} %get-tuple-element.49), channel_id=1, source_target_pairs={{0,4},{1,5},{2,6},{3,7},{4,0},{5,1},{6,2},{7,3},{8,12},{9,13},{10,... | collective-permute-start | bytes 1572872 | tf_op jit(solution)/shard_map/ppermute | solution.py:20
  11.3 17.1 %collective-permute-done.1.refs_2_ = bf16[1024,256]{1,0:T(8,128)(2,1)S(1)} collective-permute-done((bf16[1024,256]{1,0:T(8,128)(2,1)S(1)}, bf16[1024,256]{1,0:T(8,128)(2,1)S(1)}, u32[]{:S(2)}, u32[]{:S(2)}) %collective-permute-start.1) | collective-permute-done | bytes 524320 | tf_op jit(solution)/shard_map/ppermute | solution.py:20
  28.4 2.5 %collective-permute-done.refs_2_.refs_4_ = bf16[1024,256]{1,0:T(8,128)(2,1)S(1)} collective-permute-done((bf16[1024,256]{1,0:T(8,128)(2,1)S(1)}, bf16[1024,256]{1,0:T(8,128)(2,1)S(1)}, u32[]{:S(2)}, u32[]{:S(2)}) %collective-permute-start) | collective-permute-done | bytes 524320 | tf_op jit(solution)/shard_map/ppermute | solution.py:20
  34.1 2.7 %collective-permute-start.4 = (bf16[1024,256]{1,0:T(8,128)(2,1)S(1)}, bf16[1024,256]{1,0:T(8,128)(2,1)S(1)}, u32[]{:S(2)}, u32[]{:S(2)}) collective-permute-start(bf16[1024,256]{1,0:T(8,128)(2,1)S(1)} %multiply_convert_fusion), channel_id=1, source_target_pairs={{0,4},{1,5},{2,6},{3,7},{4,0},{5,1},{6,2},{7,3},{8,12},{9,13},{10,... | collective-permute-start | bytes 1572872 | tf_op jit(solution)/shard_map/ppermute | solution.py:20
  37.4 12.5 %collective-permute-done.2.refs_6_ = bf16[1024,256]{1,0:T(8,128)(2,1)} collective-permute-done((bf16[1024,256]{1,0:T(8,128)(2,1)S(1)}, bf16[1024,256]{1,0:T(8,128)(2,1)}, u32[]{:S(2)}, u32[]{:S(2)}) %collective-permute-start.2) | collective-permute-done | bytes 524320 | tf_op jit(solution)/shard_map/ppermute | solution.py:20
  49.9 3.0 %collective-permute-start.9 = (bf16[1024,256]{1,0:T(8,128)(2,1)}, bf16[1024,256]{1,0:T(8,128)(2,1)S(1)}, u32[]{:S(2)}, u32[]{:S(2)}) collective-permute-start(bf16[1024,256]{1,0:T(8,128)(2,1)} %collective-permute-done.2.refs_6_), channel_id=1, source_target_pairs={{0,1},{1,0},{2,3},{3,2},{4,5},{5,4},{6,7},{7,6},{8,9},{9,8},{10,11... | collective-permute-start | bytes 1572872 | tf_op jit(solution)/shard_map/ppermute | solution.py:20
  53.0 5.6 %collective-permute-done.4.refs_3_ = bf16[1024,256]{1,0:T(8,128)(2,1)S(1)} collective-permute-done((bf16[1024,256]{1,0:T(8,128)(2,1)S(1)}, bf16[1024,256]{1,0:T(8,128)(2,1)S(1)}, u32[]{:S(2)}, u32[]{:S(2)}) %collective-permute-start.4) | collective-permute-done | bytes 524320 | tf_op jit(solution)/shard_map/ppermute | solution.py:20
  59.3 7.1 %collective-permute-done.3.refs_2_ = bf16[1024,256]{1,0:T(8,128)(2,1)S(1)} collective-permute-done((bf16[1024,256]{1,0:T(8,128)(2,1)S(1)}, bf16[1024,256]{1,0:T(8,128)(2,1)S(1)}, u32[]{:S(2)}, u32[]{:S(2)}) %collective-permute-start.3) | collective-permute-done | bytes 524320 | tf_op jit(solution)/shard_map/ppermute | solution.py:20
  66.4 4.1 %shard_map.38 = (f32[2,4,128,512]{3,2,1,0:T(8,128)S(1)}, bf16[2,4,128,512]{3,2,1,0:T(8,128)(2,1)S(1)}) custom-call(s32[9]{0:T(128)S(1)} %pad_add_fusion.choices_ref, bf16[2,512,1024]{2,1,0:T(8,128)(2,1)S(1)} %shard_map.37.lefts_ref, bf16[1024,256]{1,0:T(8,128)(2,1)S(1)} %get-tuple-element.50.refs_0_, bf16[1024,256]{1,0:T(8,128)(2,1)S(1)} %collective-permute-done.5.refs_1_, ...), custom_call_target="tpu_custom_call" | custom-call | tf_op jit(solution)/shard_map/pallas_call | solution.py:114
  73.7 1.6 %collective-permute-start.11 = (bf16[1,4,128,512]{3,2,1,0:T(8,128)(2,1)S(1)}, bf16[1,4,128,512]{3,2,1,0:T(8,128)(2,1)S(1)}, u32[]{:S(2)}, u32[]{:S(2)}) collective-permute-start(bf16[1,4,128,512]{3,2,1,0:T(8,128)(2,1)S(1)} %slice.73), channel_id=1, source_target_pairs={{0,16},{8,24},{16,0},{24,8},{1,17},{9,25},{17,1},{25,9},{2,18},{10... | collective-permute-start | bytes 1572872 | tf_op jit(solution)/shard_map/ppermute | solution.py:20
  75.2 4.1 %collective-permute-done.15.refs_6_ = bf16[1024,128]{1,0:T(8,128)(2,1)S(1)} collective-permute-done((bf16[1024,128]{1,0:T(8,128)(2,1)S(1)}, bf16[1024,128]{1,0:T(8,128)(2,1)S(1)}, u32[]{:S(2)}, u32[]{:S(2)}) %collective-permute-start.15) | collective-permute-done | bytes 262176 | tf_op jit(solution)/shard_map/ppermute | solution.py:20
  81.1 4.6 %collective-permute-done.13.refs_3_ = bf16[1024,256]{1,0:T(8,128)(2,1)S(1)} collective-permute-done((bf16[1024,256]{1,0:T(8,128)(2,1)S(1)}, bf16[1024,256]{1,0:T(8,128)(2,1)S(1)}, u32[]{:S(2)}, u32[]{:S(2)}) %collective-permute-start.13) | collective-permute-done | bytes 524320 | tf_op jit(solution)/shard_map/ppermute | solution.py:20
  87.3 4.0 %collective-permute-done.14.refs_5_ = bf16[1024,128]{1,0:T(8,128)(2,1)S(1)} collective-permute-done((bf16[1024,128]{1,0:T(8,128)(2,1)S(1)}, bf16[1024,128]{1,0:T(8,128)(2,1)S(1)}, u32[]{:S(2)}, u32[]{:S(2)}) %collective-permute-start.14) | collective-permute-done | bytes 262176 | tf_op jit(solution)/shard_map/ppermute | solution.py:20
  92.7 1.7 %collective-permute-start.17 = (bf16[1024,128]{1,0:T(8,128)(2,1)S(1)}, bf16[1024,128]{1,0:T(8,128)(2,1)S(1)}, u32[]{:S(2)}, u32[]{:S(2)}) collective-permute-start(bf16[1024,128]{1,0:T(8,128)(2,1)S(1)} %collective-permute-done.14.refs_5_), channel_id=1, source_target_pairs={{0,2},{1,3},{2,0},{3,1},{4,6},{5,7},{6,4},{7,5},{8,10},{9,11},{10,... | collective-permute-start | bytes 786440 | tf_op jit(solution)/shard_map/ppermute | solution.py:20
  94.7 2.1 %collective-permute-done.18.refs_9_ = bf16[1024,128]{1,0:T(8,128)(2,1)S(1)} collective-permute-done((bf16[1024,128]{1,0:T(8,128)(2,1)S(1)}, bf16[1024,128]{1,0:T(8,128)(2,1)S(1)}, u32[]{:S(2)}, u32[]{:S(2)}) %collective-permute-start.18) | collective-permute-done | bytes 262176 | tf_op jit(solution)/shard_map/ppermute | solution.py:20
  96.9 5.0 %collective-permute-done.19.refs_11_ = bf16[1024,128]{1,0:T(8,128)(2,1)S(1)} collective-permute-done((bf16[1024,128]{1,0:T(8,128)(2,1)S(1)}, bf16[1024,128]{1,0:T(8,128)(2,1)S(1)}, u32[]{:S(2)}, u32[]{:S(2)}) %collective-permute-start.19) | collective-permute-done | bytes 262176 | tf_op jit(solution)/shard_map/ppermute | solution.py:20
  101.9 3.5 %shard_map.39 = (f32[2,4,128,512]{3,2,1,0:T(8,128)S(1)}, bf16[2,4,128,512]{3,2,1,0:T(8,128)(2,1)S(1)}) custom-call(s32[9]{0:T(128)S(1)} %pad_add_fusion.choices_ref, bf16[2,512,1024]{2,1,0:T(8,128)(2,1)S(1)} %shard_map.37.lefts_ref, bf16[1024,256]{1,0:T(8,128)(2,1)S(1)} %multiply_convert_fusion.2.refs_1_.refs_0_, ...), custom_call_target="tpu_custom_call" | custom-call | tf_op jit(solution)/shard_map/pallas_call | solution.py:114
  105.4 2.6 %collective-permute-done.20 = bf16[2,4,128,512]{3,2,1,0:T(8,128)(2,1)S(1)} collective-permute-done((bf16[2,4,128,512]{3,2,1,0:T(8,128)(2,1)S(1)}, bf16[2,4,128,512]{3,2,1,0:T(8,128)(2,1)S(1)}, u32[]{:S(2)}, u32[]{:S(2)}) %collective-permute-start.20) | collective-permute-done | bytes 1048608 | tf_op jit(solution)/shard_map/ppermute | solution.py:20
  108.6 1.6 %collective-permute-start.21 = (bf16[1,4,128,512]{3,2,1,0:T(8,128)(2,1)S(1)}, bf16[1,4,128,512]{3,2,1,0:T(8,128)(2,1)S(1)}, u32[]{:S(2)}, u32[]{:S(2)}) collective-permute-start(bf16[1,4,128,512]{3,2,1,0:T(8,128)(2,1)S(1)} %slice.72), channel_id=1, source_target_pairs={{0,16},{8,24},{16,0},{24,8},{1,17},{9,25},{17,1},{25,9},{2,18},{10... | collective-permute-start | bytes 1572872 | tf_op jit(solution)/shard_map/ppermute | solution.py:20
  110.1 2.7 %collective-permute-start.12 = (bf16[4,128,256]{2,1,0:T(8,128)(2,1)S(1)}, bf16[4,128,256]{2,1,0:T(8,128)(2,1)S(1)}, u32[]{:S(2)}, u32[]{:S(2)}) collective-permute-start(bf16[4,128,256]{2,1,0:T(8,128)(2,1)S(1)} %select_convert_fusion.1), channel_id=1, source_target_pairs={{0,4},{1,5},{2,6},{3,7},{4,0},{5,1},{6,2},{7,3},{8,12},{9,13},{10,... | collective-permute-start | bytes 786440 | tf_op jit(solution)/shard_map/ppermute | solution.py:20
  112.9 9.7 %collective-permute-done.21 = bf16[1,4,128,512]{3,2,1,0:T(8,128)(2,1)S(1)} collective-permute-done((bf16[1,4,128,512]{3,2,1,0:T(8,128)(2,1)S(1)}, bf16[1,4,128,512]{3,2,1,0:T(8,128)(2,1)S(1)}, u32[]{:S(2)}, u32[]{:S(2)}) %collective-permute-start.21) | collective-permute-done | bytes 524320 | tf_op jit(solution)/shard_map/ppermute | solution.py:20
  122.9 1.9 %collective-permute-done.12 = bf16[4,128,256]{2,1,0:T(8,128)(2,1)S(1)} collective-permute-done((bf16[4,128,256]{2,1,0:T(8,128)(2,1)S(1)}, bf16[4,128,256]{2,1,0:T(8,128)(2,1)S(1)}, u32[]{:S(2)}, u32[]{:S(2)}) %collective-permute-start.12) | collective-permute-done | bytes 262176 | tf_op jit(solution)/shard_map/ppermute | solution.py:20
  125.6 12.7 %collective-permute-done.22 = bf16[4,128,256]{2,1,0:T(8,128)(2,1)S(1)} collective-permute-done((bf16[4,128,256]{2,1,0:T(8,128)(2,1)S(1)}, bf16[4,128,256]{2,1,0:T(8,128)(2,1)S(1)}, u32[]{:S(2)}, u32[]{:S(2)}) %collective-permute-start.22) | collective-permute-done | bytes 262176 | tf_op jit(solution)/shard_map/ppermute | solution.py:20
  (46 shorter events, 21.3 us)
Async XLA Ops:
  0.7 52.2 %copy-start = (s32[4]{0:T(128)S(1)}, s32[4]{0:T(128)}, u32[]{:S(2)}) copy-start(s32[4]{0:T(128)} %param.5) | copy-start | bytes 52
  2.3 26.1 %collective-permute-start.1 = (bf16[1024,256]{1,0:T(8,128)(2,1)S(1)}, bf16[1024,256]{1,0:T(8,128)(2,1)S(1)}, u32[]{:S(2)}, u32[]{:S(2)}) collective-permute-start(bf16[1024,256]{1,0:T(8,128)(2,1)S(1)} %get-tuple-element.50.refs_0_), channel_id=1, source_target_pairs={{0,2},{1,3},{2,0},{3,1},{4,6},{5,7},{6,4},{7,5},{8,10},{9,11},{10,... | collective-permute-start | bytes 1572872 | tf_op jit(solution)/shard_map/ppermute | solution.py:20
  5.4 25.6 %collective-permute-start = (bf16[1024,256]{1,0:T(8,128)(2,1)S(1)}, bf16[1024,256]{1,0:T(8,128)(2,1)S(1)}, u32[]{:S(2)}, u32[]{:S(2)}) collective-permute-start(bf16[1024,256]{1,0:T(8,128)(2,1)S(1)} %get-tuple-element.49), channel_id=1, source_target_pairs={{0,4},{1,5},{2,6},{3,7},{4,0},{5,1},{6,2},{7,3},{8,12},{9,13},{10,... | collective-permute-start | bytes 1572872 | tf_op jit(solution)/shard_map/ppermute | solution.py:20
  7.9 23.4 %collective-permute-start.5 = (bf16[1024,256]{1,0:T(8,128)(2,1)S(1)}, bf16[1024,256]{1,0:T(8,128)(2,1)S(1)}, u32[]{:S(2)}, u32[]{:S(2)}) collective-permute-start(bf16[1024,256]{1,0:T(8,128)(2,1)S(1)} %get-tuple-element.50.refs_0_), channel_id=1, source_target_pairs={{0,1},{1,0},{2,3},{3,2},{4,5},{5,4},{6,7},{7,6},{8,9},{9,8},{10,11... | collective-permute-start | bytes 1572872 | tf_op jit(solution)/shard_map/ppermute | solution.py:20
  10.7 26.2 %collective-permute-start.7 = (bf16[1024,256]{1,0:T(8,128)(2,1)S(1)}, bf16[1024,256]{1,0:T(8,128)(2,1)S(1)}, u32[]{:S(2)}, u32[]{:S(2)}) collective-permute-start(bf16[1024,256]{1,0:T(8,128)(2,1)S(1)} %multiply_convert_fusion.2.refs_1_.refs_0_), channel_id=1, source_target_pairs={{0,1},{1,0},{2,3},{3,2},{4,5},{5,4},{6,7},{7,6},{8,9},{9,8},{10,11... | collective-permute-start | bytes 1572872 | tf_op jit(solution)/shard_map/ppermute | solution.py:20
  30.9 19.0 %collective-permute-start.2 = (bf16[1024,256]{1,0:T(8,128)(2,1)S(1)}, bf16[1024,256]{1,0:T(8,128)(2,1)}, u32[]{:S(2)}, u32[]{:S(2)}) collective-permute-start(bf16[1024,256]{1,0:T(8,128)(2,1)S(1)} %collective-permute-done.refs_2_.refs_4_), channel_id=1, source_target_pairs={{0,2},{1,3},{2,0},{3,1},{4,6},{5,7},{6,4},{7,5},{8,10},{9,11},{10,... | collective-permute-start | bytes 1572872 | tf_op jit(solution)/shard_map/ppermute | solution.py:20
  31.4 18.6 %collective-permute-start.6 = (bf16[1024,256]{1,0:T(8,128)(2,1)S(1)}, bf16[1024,256]{1,0:T(8,128)(2,1)}, u32[]{:S(2)}, u32[]{:S(2)}) collective-permute-start(bf16[1024,256]{1,0:T(8,128)(2,1)S(1)} %collective-permute-done.1.refs_2_), channel_id=1, source_target_pairs={{0,1},{1,0},{2,3},{3,2},{4,5},{5,4},{6,7},{7,6},{8,9},{9,8},{10,11... | collective-permute-start | bytes 1572872 | tf_op jit(solution)/shard_map/ppermute | solution.py:20
  34.1 24.5 %collective-permute-start.4 = (bf16[1024,256]{1,0:T(8,128)(2,1)S(1)}, bf16[1024,256]{1,0:T(8,128)(2,1)S(1)}, u32[]{:S(2)}, u32[]{:S(2)}) collective-permute-start(bf16[1024,256]{1,0:T(8,128)(2,1)S(1)} %multiply_convert_fusion), channel_id=1, source_target_pairs={{0,4},{1,5},{2,6},{3,7},{4,0},{5,1},{6,2},{7,3},{8,12},{9,13},{10,... | collective-permute-start | bytes 1572872 | tf_op jit(solution)/shard_map/ppermute | solution.py:20
  36.9 29.5 %collective-permute-start.8 = (bf16[1024,256]{1,0:T(8,128)(2,1)S(1)}, bf16[1024,256]{1,0:T(8,128)(2,1)S(1)}, u32[]{:S(2)}, u32[]{:S(2)}) collective-permute-start(bf16[1024,256]{1,0:T(8,128)(2,1)S(1)} %collective-permute-done.refs_2_.refs_4_), channel_id=1, source_target_pairs={{0,1},{1,0},{2,3},{3,2},{4,5},{5,4},{6,7},{7,6},{8,9},{9,8},{10,11... | collective-permute-start | bytes 1572872 | tf_op jit(solution)/shard_map/ppermute | solution.py:20
  49.9 16.5 %collective-permute-start.9 = (bf16[1024,256]{1,0:T(8,128)(2,1)}, bf16[1024,256]{1,0:T(8,128)(2,1)S(1)}, u32[]{:S(2)}, u32[]{:S(2)}) collective-permute-start(bf16[1024,256]{1,0:T(8,128)(2,1)} %collective-permute-done.2.refs_6_), channel_id=1, source_target_pairs={{0,1},{1,0},{2,3},{3,2},{4,5},{5,4},{6,7},{7,6},{8,9},{9,8},{10,11... | collective-permute-start | bytes 1572872 | tf_op jit(solution)/shard_map/ppermute | solution.py:20
  52.9 13.5 %collective-permute-start.3 = (bf16[1024,256]{1,0:T(8,128)(2,1)S(1)}, bf16[1024,256]{1,0:T(8,128)(2,1)S(1)}, u32[]{:S(2)}, u32[]{:S(2)}) collective-permute-start(bf16[1024,256]{1,0:T(8,128)(2,1)S(1)} %multiply_convert_fusion.2.refs_1_.refs_0_), channel_id=1, source_target_pairs={{0,2},{1,3},{2,0},{3,1},{4,6},{5,7},{6,4},{7,5},{8,10},{9,11},{10,... | collective-permute-start | bytes 1572872 | tf_op jit(solution)/shard_map/ppermute | solution.py:20
  70.5 2.7 %collective-permute-start.10 = (bf16[2,4,128,512]{3,2,1,0:T(8,128)(2,1)S(1)}, bf16[2,4,128,512]{3,2,1,0:T(8,128)(2,1)S(1)}, u32[]{:S(2)}, u32[]{:S(2)}) collective-permute-start(bf16[2,4,128,512]{3,2,1,0:T(8,128)(2,1)S(1)} %get-tuple-element.37), channel_id=1, source_target_pairs={{0,8},{8,0},{16,24},{24,16},{1,9},{9,1},{17,25},{25,17},{2,10},{10... | collective-permute-start | bytes 3145736 | tf_op jit(solution)/shard_map/ppermute | solution.py:20
  70.6 8.8 %collective-permute-start.15 = (bf16[1024,128]{1,0:T(8,128)(2,1)S(1)}, bf16[1024,128]{1,0:T(8,128)(2,1)S(1)}, u32[]{:S(2)}, u32[]{:S(2)}) collective-permute-start(bf16[1024,128]{1,0:T(8,128)(2,1)S(1)} %get-tuple-element.41.refs_4_), channel_id=1, source_target_pairs={{0,2},{1,3},{2,0},{3,1},{4,6},{5,7},{6,4},{7,5},{8,10},{9,11},{10,... | collective-permute-start | bytes 786440 | tf_op jit(solution)/shard_map/ppermute | solution.py:20
  70.9 14.7 %collective-permute-start.13 = (bf16[1024,256]{1,0:T(8,128)(2,1)S(1)}, bf16[1024,256]{1,0:T(8,128)(2,1)S(1)}, u32[]{:S(2)}, u32[]{:S(2)}) collective-permute-start(bf16[1024,256]{1,0:T(8,128)(2,1)S(1)} %collective-permute-done.3.refs_2_), channel_id=1, source_target_pairs={{0,1},{1,0},{2,3},{3,2},{4,5},{5,4},{6,7},{7,6},{8,9},{9,8},{10,11... | collective-permute-start | bytes 1572872 | tf_op jit(solution)/shard_map/ppermute | solution.py:20
  73.7 20.8 %collective-permute-start.11 = (bf16[1,4,128,512]{3,2,1,0:T(8,128)(2,1)S(1)}, bf16[1,4,128,512]{3,2,1,0:T(8,128)(2,1)S(1)}, u32[]{:S(2)}, u32[]{:S(2)}) collective-permute-start(bf16[1,4,128,512]{3,2,1,0:T(8,128)(2,1)S(1)} %slice.73), channel_id=1, source_target_pairs={{0,16},{8,24},{16,0},{24,8},{1,17},{9,25},{17,1},{25,9},{2,18},{10... | collective-permute-start | bytes 1572872 | tf_op jit(solution)/shard_map/ppermute | solution.py:20
  79.4 7.9 %collective-permute-start.16 = (bf16[1024,128]{1,0:T(8,128)(2,1)S(1)}, bf16[1024,128]{1,0:T(8,128)(2,1)S(1)}, u32[]{:S(2)}, u32[]{:S(2)}) collective-permute-start(bf16[1024,128]{1,0:T(8,128)(2,1)S(1)} %get-tuple-element.44.refs_8_), channel_id=1, source_target_pairs={{0,2},{1,3},{2,0},{3,1},{4,6},{5,7},{6,4},{7,5},{8,10},{9,11},{10,... | collective-permute-start | bytes 786440 | tf_op jit(solution)/shard_map/ppermute | solution.py:20
  79.6 11.6 %collective-permute-start.14 = (bf16[1024,128]{1,0:T(8,128)(2,1)S(1)}, bf16[1024,128]{1,0:T(8,128)(2,1)S(1)}, u32[]{:S(2)}, u32[]{:S(2)}) collective-permute-start(bf16[1024,128]{1,0:T(8,128)(2,1)S(1)} %get-tuple-element.41.refs_4_), channel_id=1, source_target_pairs={{0,1},{1,0},{2,3},{3,2},{4,5},{5,4},{6,7},{7,6},{8,9},{9,8},{10,11... | collective-permute-start | bytes 786440 | tf_op jit(solution)/shard_map/ppermute | solution.py:20
  85.6 11.2 %collective-permute-start.18 = (bf16[1024,128]{1,0:T(8,128)(2,1)S(1)}, bf16[1024,128]{1,0:T(8,128)(2,1)S(1)}, u32[]{:S(2)}, u32[]{:S(2)}) collective-permute-start(bf16[1024,128]{1,0:T(8,128)(2,1)S(1)} %get-tuple-element.44.refs_8_), channel_id=1, source_target_pairs={{0,1},{1,0},{2,3},{3,2},{4,5},{5,4},{6,7},{7,6},{8,9},{9,8},{10,11... | collective-permute-start | bytes 786440 | tf_op jit(solution)/shard_map/ppermute | solution.py:20
  91.2 10.7 %collective-permute-start.19 = (bf16[1024,128]{1,0:T(8,128)(2,1)S(1)}, bf16[1024,128]{1,0:T(8,128)(2,1)S(1)}, u32[]{:S(2)}, u32[]{:S(2)}) collective-permute-start(bf16[1024,128]{1,0:T(8,128)(2,1)S(1)} %collective-permute-done.16.refs_10_), channel_id=1, source_target_pairs={{0,1},{1,0},{2,3},{3,2},{4,5},{5,4},{6,7},{7,6},{8,9},{9,8},{10,11... | collective-permute-start | bytes 786440 | tf_op jit(solution)/shard_map/ppermute | solution.py:20
  92.7 9.2 %collective-permute-start.17 = (bf16[1024,128]{1,0:T(8,128)(2,1)S(1)}, bf16[1024,128]{1,0:T(8,128)(2,1)S(1)}, u32[]{:S(2)}, u32[]{:S(2)}) collective-permute-start(bf16[1024,128]{1,0:T(8,128)(2,1)S(1)} %collective-permute-done.14.refs_5_), channel_id=1, source_target_pairs={{0,2},{1,3},{2,0},{3,1},{4,6},{5,7},{6,4},{7,5},{8,10},{9,11},{10,... | collective-permute-start | bytes 786440 | tf_op jit(solution)/shard_map/ppermute | solution.py:20
  105.4 2.7 %collective-permute-start.20 = (bf16[2,4,128,512]{3,2,1,0:T(8,128)(2,1)S(1)}, bf16[2,4,128,512]{3,2,1,0:T(8,128)(2,1)S(1)}, u32[]{:S(2)}, u32[]{:S(2)}) collective-permute-start(bf16[2,4,128,512]{3,2,1,0:T(8,128)(2,1)S(1)} %get-tuple-element.47), channel_id=1, source_target_pairs={{0,8},{8,0},{16,24},{24,16},{1,9},{9,1},{17,25},{25,17},{2,10},{10... | collective-permute-start | bytes 3145736 | tf_op jit(solution)/shard_map/ppermute | solution.py:20
  108.6 14.0 %collective-permute-start.21 = (bf16[1,4,128,512]{3,2,1,0:T(8,128)(2,1)S(1)}, bf16[1,4,128,512]{3,2,1,0:T(8,128)(2,1)S(1)}, u32[]{:S(2)}, u32[]{:S(2)}) collective-permute-start(bf16[1,4,128,512]{3,2,1,0:T(8,128)(2,1)S(1)} %slice.72), channel_id=1, source_target_pairs={{0,16},{8,24},{16,0},{24,8},{1,17},{9,25},{17,1},{25,9},{2,18},{10... | collective-permute-start | bytes 1572872 | tf_op jit(solution)/shard_map/ppermute | solution.py:20
  110.1 14.7 %collective-permute-start.12 = (bf16[4,128,256]{2,1,0:T(8,128)(2,1)S(1)}, bf16[4,128,256]{2,1,0:T(8,128)(2,1)S(1)}, u32[]{:S(2)}, u32[]{:S(2)}) collective-permute-start(bf16[4,128,256]{2,1,0:T(8,128)(2,1)S(1)} %select_convert_fusion.1), channel_id=1, source_target_pairs={{0,4},{1,5},{2,6},{3,7},{4,0},{5,1},{6,2},{7,3},{8,12},{9,13},{10,... | collective-permute-start | bytes 786440 | tf_op jit(solution)/shard_map/ppermute | solution.py:20
  124.8 13.5 %collective-permute-start.22 = (bf16[4,128,256]{2,1,0:T(8,128)(2,1)S(1)}, bf16[4,128,256]{2,1,0:T(8,128)(2,1)S(1)}, u32[]{:S(2)}, u32[]{:S(2)}) collective-permute-start(bf16[4,128,256]{2,1,0:T(8,128)(2,1)S(1)} %select_convert_fusion), channel_id=1, source_target_pairs={{0,4},{1,5},{2,6},{3,7},{4,0},{5,1},{6,2},{7,3},{8,12},{9,13},{10,... | collective-permute-start | bytes 786440 | tf_op jit(solution)/shard_map/ppermute | solution.py:20

commit v10 on v9

--- a/solution.py
+++ b/solution.py
@@ -76,19 +76,15 @@
 def products(choices, lefts, batch, scale_factor):
     slab_count = lax.axis_size("space")
     group, cells = lefts.shape[1:]
-    widths = [sum(blocks[0].shape[1] for blocks in pieces) for _, pieces in batch]
+    width = sum(blocks[0].shape[1] for blocks in batch[0])
     rows = group // slab_count
-    arrays = [block for _, pieces in batch for blocks in pieces for block in blocks]
+    arrays = [block for pieces in batch for blocks in pieces for block in blocks]
 
     def kernel(choices_ref, lefts_ref, *refs):
         waiting = list(refs[: len(arrays)])
         even_ref, odd_ref, tiles = refs[len(arrays) :]
-        first = 0
-        for (mates, pieces), width in zip(batch, widths):
+        for mates, pieces in enumerate(batch):
             sources = [[waiting.pop(0) for _ in blocks] for blocks in pieces]
-            columns = pl.ds(first, width)
-            first += width
-
             for round_number in range(ROUNDS):
                 parts = []
                 for block_refs in sources:
@@ -99,24 +95,24 @@
                     parts.append(part)
                 right = jnp.concatenate(parts, axis=1) if len(parts) > 1 else parts[0]
                 side = choices_ref[ROUNDS + round_number]
-                left = lefts_ref[1 - side if mates else side]
+                side = 1 - side if mates else side
                 tile = tiles.at[round_number % 2]
-                tile[:, :width] = scale_factor * jnp.dot(
-                    left, right, preferred_element_type=jnp.float32
+                tile[...] = scale_factor * jnp.dot(
+                    lefts_ref[side], right, preferred_element_type=jnp.float32
                 )
                 for number in range(slab_count):
                     start = jnp.bitwise_xor(choices_ref[2 * ROUNDS], number) * rows
-                    part = tile[pl.ds(pl.multiple_of(start, rows), rows), :width]
+                    part = tile[pl.ds(pl.multiple_of(start, rows), rows), :]
                     out_ref = odd_ref if number % 2 else even_ref
-                    out_ref[number // 2, round_number, :, columns] = part.astype(out_ref.dtype)
-
-    shape = (slab_count // 2, ROUNDS, rows, sum(widths))
+                    out_ref[side, number // 2, round_number] = part.astype(out_ref.dtype)
+
+    shape = (2, slab_count // 2, ROUNDS, rows, width)
     return pl.pallas_call(
         kernel,
         out_shape=[jax.ShapeDtypeStruct(shape, kind) for kind in (jnp.float32, jnp.bfloat16)],
         in_specs=[pl.BlockSpec(memory_space=pltpu.SMEM)] + [VMEM] * (1 + len(arrays)),
         out_specs=[VMEM, VMEM],
-        scratch_shapes=[pltpu.VMEM((2, group, max(widths)), jnp.float32)],
+        scratch_shapes=[pltpu.VMEM((2, group, width), jnp.float32)],
         compiler_params=PARAMS,
         cost_estimate=pl.CostEstimate(flops=0, bytes_accessed=0, transcendentals=0),
     )(choices, lefts, *arrays)
@@ -126,10 +122,11 @@
     return keep + exchange(send, "space", bit).astype(jnp.float32)
 
 
-def summed(total):
+def summed(total, earlier):
     bit = 2
     while len(total) > 1:
-        total = halved(total[0::2], total[1::2].astype(jnp.bfloat16), bit)
+        send = behind(total[1::2].astype(jnp.bfloat16), earlier)
+        total = halved(total[0::2], send, bit)
         bit *= 2
     return total[0]
 
@@ -175,55 +172,42 @@
 
     low = jnp.bitwise_and(masks, cut - 1)
     crossing = (masks >= cut).astype(jnp.int32)
+    rounds = jnp.concatenate([low, crossing])
     me = lax.axis_index("space").astype(jnp.int32)[None]
-    choices = jnp.concatenate([low, crossing, me])
-    swap = (crossing == 1)[:, None, None]
 
     held = [{0: piece} for piece in own + mate]
     sent = {}
-    halves, given, sums, columns, back = [], [], {}, [], []
-
-    def add_batch():
-        lists = BATCHES[len(halves)]
+    halves, columns, back = [], [], []
+
+    def add_batch(rounds):
         batch = [
-            (numbers[0] >= len(own), [[held[n][low] for low in range(cut)] for n in numbers])
-            for numbers in lists
+            [[held[n][low] for low in range(cut)] for n in numbers]
+            for numbers in BATCHES[len(halves)]
         ]
-        earlier = None
-        if not halves:
-            earlier = sent[cut // 2][-1]
-        if lists == BATCHES[-1]:
-            earlier = (given[0], halves[-1])
-        even, odd = products(behind(choices, earlier), lefts, batch, scale_factor)
-        halves.append(halved(even, odd, 1))
-        total = summed(halves[-1])
-        taken = 0
-        for (mates, pieces), numbers in zip(batch, lists):
-            width = sum(found[0].shape[1] for found in pieces)
-            part = lax.slice_in_dim(total, taken, taken + width, axis=2)
-            taken += width
-            if not mates:
-                sums[numbers[0]] = part
-                continue
-            own_part = sums[len(columns)]
-            keep = jnp.where(swap, part, own_part)
-            given.append(jnp.where(swap, own_part, part).astype(jnp.bfloat16))
-            back.append(exchange(behind(given[-1], back[-1] if back else None), "snap", cut))
-            columns.append(keep + back[-1].astype(jnp.float32))
+        earlier = (columns, back) if halves else [arrived[-1] for arrived in sent.values()]
+        rounds = exchange(behind(rounds, earlier), "space", 1)
+        even, odd = products(jnp.concatenate([rounds, me]), lefts, batch, scale_factor)
+        total = even + exchange(odd, "space", 1).astype(jnp.float32)
+        halves.append(total)
+        give = summed(total[1], None)
+        back.append(exchange(give.astype(jnp.bfloat16), "snap", cut))
+        columns.append(summed(total[0], give))
+        return rounds
 
     for piece, low, bit in hops_in_order(OWN_WIDTHS + MATE_WIDTHS, cut):
         earlier = sent.setdefault(bit, [])
         depth = 2 if bit == 1 else 1
         ties = earlier[-depth] if len(earlier) >= depth else None
-        if bit == 1 and low == 0 and halves and piece in BATCHES[-1][-1]:
+        if bit == 1 and low == 0 and halves and piece in BATCHES[-1][1]:
             ties = (ties, halves[0])
         held[piece][low | bit] = exchange(behind(held[piece][low], ties), "snap", bit)
         earlier.append(held[piece][low | bit])
         while len(halves) < len(BATCHES) and all(
             len(held[n]) == cut for numbers in BATCHES[len(halves)] for n in numbers
         ):
-            add_batch()
-    return jnp.concatenate(columns, axis=2)[:, None]
+            rounds = add_batch(rounds)
+    results = [kept + got.astype(jnp.float32) for kept, got in zip(columns, back)]
+    return jnp.concatenate(results, axis=2)[:, None]
 
 
 def solution(mesh):

time: 140 us -> 140 us (level)
  waiting for transfers between devices: 92.7 us -> 95.5 us
  starting transfers between devices: 31 us -> 28.6 us
  local copies, waits for them, and re-layouts: 0.88 us -> 2.46 us
  other arithmetic: 6.77 us -> 5.23 us
    ppermute x23 -> x27, waiting for transfers between devices: 92.7 us -> 95.5 us  [exchange(): lax.ppermute(part, axis, [(i, i ^ mask) for i in range(lax.axis_size(axis...]
    ppermute x23 -> x27, starting transfers between devices: 31 us -> 28.6 us  [exchange(): lax.ppermute(part, axis, [(i, i ^ mask) for i in range(lax.axis_size(axis...]
    unnamed x2 -> x16, local copies, waits for them, and re-layouts: 0.01 us -> 1.65 us
  transfers between devices with their start and end apart: 23 -> 27, of which waited for: 16 -> 21; matrix products, arithmetic and copies ran while one was open for 3% -> 1% of each run, Pallas kernels for 0% -> 0%
where the time goes in v10:
time: 140 us
  waiting for transfers between devices  95.5 us (68%)
  starting transfers between devices  28.6 us (20%)
  Pallas kernels  8.25 us (6%)
  other arithmetic  5.23 us (4%)
  local copies, waits for them, and re-layouts  2.46 us (2%)
    ppermute x27, waiting for transfers between devices, exchange(): lax.ppermute(part, axis, [(i, i ^ mask) for i in range(lax.axis_size(axis...  95.5 us
    ppermute x27, starting transfers between devices, exchange(): lax.ppermute(part, axis, [(i, i ^ mask) for i in range(lax.axis_size(axis...  28.6 us
    pallas_call x2, Pallas kernels, products(): pl.pallas_call(kernel, out_shape=[jax.ShapeDtypeStruct(shape, kind) for k...  7.63 us
    convert_element_type x3, other arithmetic, pieces_of(): found.append((part.astype(jnp.float32) * scale).astype(jnp.bfloat16))  2.89 us
  transfers between devices with their start and end apart: 27, of which 21 were waited for; matrix products, arithmetic and copies ran while one was open for 1% of the time, Pallas kernels for 0%

profile of v10, /device:TPU:0, one launch (start us, length us, event | category | flops | bytes accessed | tf_op | source)
XLA Modules:
  0.0 140.3 jit_solution(13180742820047880588)
XLA Ops:
  0.7 1.7 %multiply_convert_fusion.1 = (bf16[1024,256]{1,0:T(8,128)(2,1)S(1)}, bf16[1024,256]{1,0:T(8,128)(2,1)S(1)}) fusion(f32[1024]{0:T(1024)S(1)} %get-tuple-element.65, bf16[2048,512]{1,0:T(8,128)(2,1)} %param.3, s32[]{:T(128)S(6)} %select_n.2, f32[1024]{0:T(1024)S(1)} %get-tuple-element.66, s32[]{:T(128)S(6)} %mul.16), kind=kLoop, calls=%fused_computation.4 | loop fusion | flops 1572864 | bytes 2105352 | tf_op jit(solution)/shard_map/convert_element_type | solution.py:155
  2.4 4.1 %collective-permute-start = (bf16[1024,256]{1,0:T(8,128)(2,1)S(1)}, bf16[1024,256]{1,0:T(8,128)(2,1)S(1)}, u32[]{:S(2)}, u32[]{:S(2)}) collective-permute-start(bf16[1024,256]{1,0:T(8,128)(2,1)S(1)} %get-tuple-element.57), channel_id=1, source_target_pairs={{0,4},{1,5},{2,6},{3,7},{4,0},{5,1},{6,2},{7,3},{8,12},{9,13},{10,... | collective-permute-start | bytes 1572872 | tf_op jit(solution)/shard_map/ppermute | solution.py:20
  10.4 19.4 %collective-permute-done.refs_2_.refs_4_ = bf16[1024,256]{1,0:T(8,128)(2,1)S(1)} collective-permute-done((bf16[1024,256]{1,0:T(8,128)(2,1)S(1)}, bf16[1024,256]{1,0:T(8,128)(2,1)S(1)}, u32[]{:S(2)}, u32[]{:S(2)}) %collective-permute-start) | collective-permute-done | bytes 524320 | tf_op jit(solution)/shard_map/ppermute | solution.py:20
  34.8 2.3 %collective-permute-start.8 = (bf16[1024,256]{1,0:T(8,128)(2,1)}, bf16[1024,256]{1,0:T(8,128)(2,1)S(1)}, u32[]{:S(2)}, u32[]{:S(2)}) collective-permute-start(bf16[1024,256]{1,0:T(8,128)(2,1)} %multiply_convert_fusion), channel_id=1, source_target_pairs={{0,4},{1,5},{2,6},{3,7},{4,0},{5,1},{6,2},{7,3},{8,12},{9,13},{10,... | collective-permute-start | bytes 1572872 | tf_op jit(solution)/shard_map/ppermute | solution.py:20
  37.6 13.1 %collective-permute-done.2.refs_6_ = bf16[1024,256]{1,0:T(8,128)(2,1)} collective-permute-done((bf16[1024,256]{1,0:T(8,128)(2,1)S(1)}, bf16[1024,256]{1,0:T(8,128)(2,1)}, u32[]{:S(2)}, u32[]{:S(2)}) %collective-permute-start.2) | collective-permute-done | bytes 524320 | tf_op jit(solution)/shard_map/ppermute | solution.py:20
  51.6 2.2 %collective-permute-start.6 = (bf16[1024,256]{1,0:T(8,128)(2,1)}, bf16[1024,256]{1,0:T(8,128)(2,1)}, u32[]{:S(2)}, u32[]{:S(2)}) collective-permute-start(bf16[1024,256]{1,0:T(8,128)(2,1)} %collective-permute-done.2.refs_6_), channel_id=1, source_target_pairs={{0,1},{1,0},{2,3},{3,2},{4,5},{5,4},{6,7},{7,6},{8,9},{9,8},{10,11... | collective-permute-start | bytes 1572872 | tf_op jit(solution)/shard_map/ppermute | solution.py:20
  53.9 6.4 %collective-permute-done.8.refs_3_ = bf16[1024,256]{1,0:T(8,128)(2,1)S(1)} collective-permute-done((bf16[1024,256]{1,0:T(8,128)(2,1)}, bf16[1024,256]{1,0:T(8,128)(2,1)S(1)}, u32[]{:S(2)}, u32[]{:S(2)}) %collective-permute-start.8) | collective-permute-done | bytes 524320 | tf_op jit(solution)/shard_map/ppermute | solution.py:20
  60.9 6.5 %collective-permute-done.6.refs_7_ = bf16[1024,256]{1,0:T(8,128)(2,1)} collective-permute-done((bf16[1024,256]{1,0:T(8,128)(2,1)}, bf16[1024,256]{1,0:T(8,128)(2,1)}, u32[]{:S(2)}, u32[]{:S(2)}) %collective-permute-start.6) | collective-permute-done | bytes 524320 | tf_op jit(solution)/shard_map/ppermute | solution.py:20
  69.8 4.2 %shard_map.38 = (f32[2,2,4,128,256]{4,3,2,1,0:T(8,128)S(1)}, bf16[2,2,4,128,256]{4,3,2,1,0:T(8,128)(2,1)S(1)}) custom-call(s32[9]{0:T(128)S(1)} %pad_add_fusion.1.choices_ref, bf16[2,512,1024]{2,1,0:T(8,128)(2,1)S(1)} %shard_map.37.lefts_ref, bf16[1024,256]{1,0:T(8,128)(2,1)S(1)} %get-tuple-element.58.refs_0_, bf16[1024,256]{1,0:T(8,128)(2,1)S(1)} %copy-done.3, ...), custom_call_target="tpu_custom_call" | custom-call | tf_op jit(solution)/shard_map/pallas_call | solution.py:110
  74.4 2.3 %collective-permute-done.11 = bf16[2,2,4,128,256]{4,3,2,1,0:T(8,128)(2,1)S(1)} collective-permute-done((bf16[2,2,4,128,256]{4,3,2,1,0:T(8,128)(2,1)S(1)}, bf16[2,2,4,128,256]{4,3,2,1,0:T(8,128)(2,1)S(1)}, u32[]{:S(2)}, u32[]{:S(2)}) %collective-permute-start.11) | collective-permute-done | bytes 1048608 | tf_op jit(solution)/shard_map/ppermute | solution.py:20
  79.0 3.9 %collective-permute-done.18.refs_6_ = bf16[1024,128]{1,0:T(8,128)(2,1)S(1)} collective-permute-done((bf16[1024,128]{1,0:T(8,128)(2,1)S(1)}, bf16[1024,128]{1,0:T(8,128)(2,1)S(1)}, u32[]{:S(2)}, u32[]{:S(2)}) %collective-permute-start.18) | collective-permute-done | bytes 262176 | tf_op jit(solution)/shard_map/ppermute | solution.py:20
  83.6 2.0 %collective-permute-done.12 = bf16[1,4,128,256]{3,2,1,0:T(8,128)(2,1)S(1)} collective-permute-done((bf16[1,4,128,256]{3,2,1,0:T(8,128)(2,1)S(1)}, bf16[1,4,128,256]{3,2,1,0:T(8,128)(2,1)S(1)}, u32[]{:S(2)}, u32[]{:S(2)}) %collective-permute-start.12) | collective-permute-done | bytes 262176 | tf_op jit(solution)/shard_map/ppermute | solution.py:20
  85.7 1.6 %collective-permute-start.13 = (bf16[1,4,128,256]{3,2,1,0:T(8,128)(2,1)S(1)}, bf16[1,4,128,256]{3,2,1,0:T(8,128)(2,1)S(1)}, u32[]{:S(2)}, u32[]{:S(2)}) collective-permute-start(bf16[1,4,128,256]{3,2,1,0:T(8,128)(2,1)S(1)} %get-tuple-element.39), channel_id=1, source_target_pairs={{0,16},{8,24},{16,0},{24,8},{1,17},{9,25},{17,1},{25,9},{2,18},{10... | collective-permute-start | bytes 786440 | tf_op jit(solution)/shard_map/ppermute | solution.py:20
  87.2 3.0 %collective-permute-start.14 = (bf16[4,128,256]{2,1,0:T(8,128)(2,1)S(1)}, bf16[4,128,256]{2,1,0:T(8,128)(2,1)S(1)}, u32[]{:S(2)}, u32[]{:S(2)}) collective-permute-start(bf16[4,128,256]{2,1,0:T(8,128)(2,1)S(1)} %fusion.6), channel_id=1, source_target_pairs={{0,4},{1,5},{2,6},{3,7},{4,0},{5,1},{6,2},{7,3},{8,12},{9,13},{10,... | collective-permute-start | bytes 786440 | tf_op jit(solution)/shard_map/ppermute | solution.py:20
  90.2 3.3 %collective-permute-done.16.refs_3_ = bf16[1024,256]{1,0:T(8,128)(2,1)S(1)} collective-permute-done((bf16[1024,256]{1,0:T(8,128)(2,1)S(1)}, bf16[1024,256]{1,0:T(8,128)(2,1)S(1)}, u32[]{:S(2)}, u32[]{:S(2)}) %collective-permute-start.16) | collective-permute-done | bytes 524320 | tf_op jit(solution)/shard_map/ppermute | solution.py:20
  93.9 5.2 %collective-permute-done.17.refs_5_ = bf16[1024,128]{1,0:T(8,128)(2,1)S(1)} collective-permute-done((bf16[1024,128]{1,0:T(8,128)(2,1)S(1)}, bf16[1024,128]{1,0:T(8,128)(2,1)S(1)}, u32[]{:S(2)}, u32[]{:S(2)}) %collective-permute-start.17) | collective-permute-done | bytes 262176 | tf_op jit(solution)/shard_map/ppermute | solution.py:20
  102.7 2.0 %collective-permute-done.21.refs_9_ = bf16[1024,128]{1,0:T(8,128)(2,1)S(1)} collective-permute-done((bf16[1024,128]{1,0:T(8,128)(2,1)S(1)}, bf16[1024,128]{1,0:T(8,128)(2,1)S(1)}, u32[]{:S(2)}, u32[]{:S(2)}) %collective-permute-start.21) | collective-permute-done | bytes 262176 | tf_op jit(solution)/shard_map/ppermute | solution.py:20
  104.7 4.6 %collective-permute-done.22.refs_11_ = bf16[1024,128]{1,0:T(8,128)(2,1)S(1)} collective-permute-done((bf16[1024,128]{1,0:T(8,128)(2,1)S(1)}, bf16[1024,128]{1,0:T(8,128)(2,1)S(1)}, u32[]{:S(2)}, u32[]{:S(2)}) %collective-permute-start.22) | collective-permute-done | bytes 262176 | tf_op jit(solution)/shard_map/ppermute | solution.py:20
  109.3 3.5 %shard_map.39 = (f32[2,2,4,128,256]{4,3,2,1,0:T(8,128)S(1)}, bf16[2,2,4,128,256]{4,3,2,1,0:T(8,128)(2,1)S(1)}) custom-call(s32[9]{0:T(128)S(1)} %pad_add_fusion.2.choices_ref, bf16[2,512,1024]{2,1,0:T(8,128)(2,1)S(1)} %shard_map.37.lefts_ref, bf16[1024,256]{1,0:T(8,128)(2,1)S(1)} %multiply_convert_fusion.2.refs_1_.refs_0_, ...), custom_call_target="tpu_custom_call" | custom-call | tf_op jit(solution)/shard_map/pallas_call | solution.py:110
  112.8 2.6 %collective-permute-done.23 = bf16[2,2,4,128,256]{4,3,2,1,0:T(8,128)(2,1)S(1)} collective-permute-done((bf16[2,2,4,128,256]{4,3,2,1,0:T(8,128)(2,1)S(1)}, bf16[2,2,4,128,256]{4,3,2,1,0:T(8,128)(2,1)S(1)}, u32[]{:S(2)}, u32[]{:S(2)}) %collective-permute-start.23) | collective-permute-done | bytes 1048608 | tf_op jit(solution)/shard_map/ppermute | solution.py:20
  116.5 7.8 %collective-permute-done.24 = bf16[1,4,128,256]{3,2,1,0:T(8,128)(2,1)S(1)} collective-permute-done((bf16[1,4,128,256]{3,2,1,0:T(8,128)(2,1)S(1)}, bf16[1,4,128,256]{3,2,1,0:T(8,128)(2,1)S(1)}, u32[]{:S(2)}, u32[]{:S(2)}) %collective-permute-start.24) | collective-permute-done | bytes 262176 | tf_op jit(solution)/shard_map/ppermute | solution.py:20
  125.0 3.0 %collective-permute-start.26 = (bf16[4,128,256]{2,1,0:T(8,128)(2,1)S(1)}, bf16[4,128,256]{2,1,0:T(8,128)(2,1)S(1)}, u32[]{:S(2)}, u32[]{:S(2)}) collective-permute-start(bf16[4,128,256]{2,1,0:T(8,128)(2,1)S(1)} %fusion.1), channel_id=1, source_target_pairs={{0,4},{1,5},{2,6},{3,7},{4,0},{5,1},{6,2},{7,3},{8,12},{9,13},{10,... | collective-permute-start | bytes 786440 | tf_op jit(solution)/shard_map/ppermute | solution.py:20
  127.9 4.0 %collective-permute-done.25 = bf16[1,4,128,256]{3,2,1,0:T(8,128)(2,1)S(1)} collective-permute-done((bf16[1,4,128,256]{3,2,1,0:T(8,128)(2,1)S(1)}, bf16[1,4,128,256]{3,2,1,0:T(8,128)(2,1)S(1)}, u32[]{:S(2)}, u32[]{:S(2)}) %collective-permute-start.25) | collective-permute-done | bytes 262176 | tf_op jit(solution)/shard_map/ppermute | solution.py:20
  132.0 7.1 %collective-permute-done.26 = bf16[4,128,256]{2,1,0:T(8,128)(2,1)S(1)} collective-permute-done((bf16[4,128,256]{2,1,0:T(8,128)(2,1)S(1)}, bf16[4,128,256]{2,1,0:T(8,128)(2,1)S(1)}, u32[]{:S(2)}, u32[]{:S(2)}) %collective-permute-start.26) | collective-permute-done | bytes 262176 | tf_op jit(solution)/shard_map/ppermute | solution.py:20
  (69 shorter events, 24.4 us)
Async XLA Ops:
  2.4 27.4 %collective-permute-start = (bf16[1024,256]{1,0:T(8,128)(2,1)S(1)}, bf16[1024,256]{1,0:T(8,128)(2,1)S(1)}, u32[]{:S(2)}, u32[]{:S(2)}) collective-permute-start(bf16[1024,256]{1,0:T(8,128)(2,1)S(1)} %get-tuple-element.57), channel_id=1, source_target_pairs={{0,4},{1,5},{2,6},{3,7},{4,0},{5,1},{6,2},{7,3},{8,12},{9,13},{10,... | collective-permute-start | bytes 1572872 | tf_op jit(solution)/shard_map/ppermute | solution.py:20
  6.5 23.5 %collective-permute-start.1 = (bf16[1024,256]{1,0:T(8,128)(2,1)S(1)}, bf16[1024,256]{1,0:T(8,128)(2,1)S(1)}, u32[]{:S(2)}, u32[]{:S(2)}) collective-permute-start(bf16[1024,256]{1,0:T(8,128)(2,1)S(1)} %get-tuple-element.58.refs_0_), channel_id=1, source_target_pairs={{0,2},{1,3},{2,0},{3,1},{4,6},{5,7},{6,4},{7,5},{8,10},{9,11},{10,... | collective-permute-start | bytes 1572872 | tf_op jit(solution)/shard_map/ppermute | solution.py:20
  8.1 23.4 %collective-permute-start.4 = (bf16[1024,256]{1,0:T(8,128)(2,1)S(1)}, bf16[1024,256]{1,0:T(8,128)(2,1)S(1)}, u32[]{:S(2)}, u32[]{:S(2)}) collective-permute-start(bf16[1024,256]{1,0:T(8,128)(2,1)S(1)} %get-tuple-element.58.refs_0_), channel_id=1, source_target_pairs={{0,1},{1,0},{2,3},{3,2},{4,5},{5,4},{6,7},{7,6},{8,9},{9,8},{10,11... | collective-permute-start | bytes 1572872 | tf_op jit(solution)/shard_map/ppermute | solution.py:20
  9.8 27.3 %collective-permute-start.9 = (bf16[1024,256]{1,0:T(8,128)(2,1)S(1)}, bf16[1024,256]{1,0:T(8,128)(2,1)S(1)}, u32[]{:S(2)}, u32[]{:S(2)}) collective-permute-start(bf16[1024,256]{1,0:T(8,128)(2,1)S(1)} %multiply_convert_fusion.2.refs_1_.refs_0_), channel_id=1, source_target_pairs={{0,1},{1,0},{2,3},{3,2},{4,5},{5,4},{6,7},{7,6},{8,9},{9,8},{10,11... | collective-permute-start | bytes 1572872 | tf_op jit(solution)/shard_map/ppermute | solution.py:20
  30.0 20.7 %collective-permute-start.2 = (bf16[1024,256]{1,0:T(8,128)(2,1)S(1)}, bf16[1024,256]{1,0:T(8,128)(2,1)}, u32[]{:S(2)}, u32[]{:S(2)}) collective-permute-start(bf16[1024,256]{1,0:T(8,128)(2,1)S(1)} %collective-permute-done.refs_2_.refs_4_), channel_id=1, source_target_pairs={{0,2},{1,3},{2,0},{3,1},{4,6},{5,7},{6,4},{7,5},{8,10},{9,11},{10,... | collective-permute-start | bytes 1572872 | tf_op jit(solution)/shard_map/ppermute | solution.py:20
  32.3 18.5 %collective-permute-start.5 = (bf16[1024,256]{1,0:T(8,128)(2,1)S(1)}, bf16[1024,256]{1,0:T(8,128)(2,1)S(1)}, u32[]{:S(2)}, u32[]{:S(2)}) collective-permute-start(bf16[1024,256]{1,0:T(8,128)(2,1)S(1)} %collective-permute-done.1.refs_2_), channel_id=1, source_target_pairs={{0,1},{1,0},{2,3},{3,2},{4,5},{5,4},{6,7},{7,6},{8,9},{9,8},{10,11... | collective-permute-start | bytes 1572872 | tf_op jit(solution)/shard_map/ppermute | solution.py:20
  34.8 25.5 %collective-permute-start.8 = (bf16[1024,256]{1,0:T(8,128)(2,1)}, bf16[1024,256]{1,0:T(8,128)(2,1)S(1)}, u32[]{:S(2)}, u32[]{:S(2)}) collective-permute-start(bf16[1024,256]{1,0:T(8,128)(2,1)} %multiply_convert_fusion), channel_id=1, source_target_pairs={{0,4},{1,5},{2,6},{3,7},{4,0},{5,1},{6,2},{7,3},{8,12},{9,13},{10,... | collective-permute-start | bytes 1572872 | tf_op jit(solution)/shard_map/ppermute | solution.py:20
  37.1 32.7 %collective-permute-start.10 = (bf16[1024,256]{1,0:T(8,128)(2,1)S(1)}, bf16[1024,256]{1,0:T(8,128)(2,1)}, u32[]{:S(2)}, u32[]{:S(2)}) collective-permute-start(bf16[1024,256]{1,0:T(8,128)(2,1)S(1)} %collective-permute-done.refs_2_.refs_4_), channel_id=1, source_target_pairs={{0,1},{1,0},{2,3},{3,2},{4,5},{5,4},{6,7},{7,6},{8,9},{9,8},{10,11... | collective-permute-start | bytes 1572872 | tf_op jit(solution)/shard_map/ppermute | solution.py:20
  51.6 15.8 %collective-permute-start.6 = (bf16[1024,256]{1,0:T(8,128)(2,1)}, bf16[1024,256]{1,0:T(8,128)(2,1)}, u32[]{:S(2)}, u32[]{:S(2)}) collective-permute-start(bf16[1024,256]{1,0:T(8,128)(2,1)} %collective-permute-done.2.refs_6_), channel_id=1, source_target_pairs={{0,1},{1,0},{2,3},{3,2},{4,5},{5,4},{6,7},{7,6},{8,9},{9,8},{10,11... | collective-permute-start | bytes 1572872 | tf_op jit(solution)/shard_map/ppermute | solution.py:20
  53.8 14.8 %collective-permute-start.3 = (bf16[1024,256]{1,0:T(8,128)(2,1)S(1)}, bf16[1024,256]{1,0:T(8,128)(2,1)S(1)}, u32[]{:S(2)}, u32[]{:S(2)}) collective-permute-start(bf16[1024,256]{1,0:T(8,128)(2,1)S(1)} %multiply_convert_fusion.2.refs_1_.refs_0_), channel_id=1, source_target_pairs={{0,2},{1,3},{2,0},{3,1},{4,6},{5,7},{6,4},{7,5},{8,10},{9,11},{10,... | collective-permute-start | bytes 1572872 | tf_op jit(solution)/shard_map/ppermute | solution.py:20
  74.0 2.7 %collective-permute-start.11 = (bf16[2,2,4,128,256]{4,3,2,1,0:T(8,128)(2,1)S(1)}, bf16[2,2,4,128,256]{4,3,2,1,0:T(8,128)(2,1)S(1)}, u32[]{:S(2)}, u32[]{:S(2)}) collective-permute-start(bf16[2,2,4,128,256]{4,3,2,1,0:T(8,128)(2,1)S(1)} %get-tuple-element.38), channel_id=1, source_target_pairs={{0,8},{8,0},{16,24},{24,16},{1,9},{9,1},{17,25},{25,17},{2,10},{10... | collective-permute-start | bytes 3145736 | tf_op jit(solution)/shard_map/ppermute | solution.py:20
  74.3 8.6 %collective-permute-start.18 = (bf16[1024,128]{1,0:T(8,128)(2,1)S(1)}, bf16[1024,128]{1,0:T(8,128)(2,1)S(1)}, u32[]{:S(2)}, u32[]{:S(2)}) collective-permute-start(bf16[1024,128]{1,0:T(8,128)(2,1)S(1)} %get-tuple-element.43.refs_4_), channel_id=1, source_target_pairs={{0,2},{1,3},{2,0},{3,1},{4,6},{5,7},{6,4},{7,5},{8,10},{9,11},{10,... | collective-permute-start | bytes 786440 | tf_op jit(solution)/shard_map/ppermute | solution.py:20
  77.1 8.5 %collective-permute-start.12 = (bf16[1,4,128,256]{3,2,1,0:T(8,128)(2,1)S(1)}, bf16[1,4,128,256]{3,2,1,0:T(8,128)(2,1)S(1)}, u32[]{:S(2)}, u32[]{:S(2)}) collective-permute-start(bf16[1,4,128,256]{3,2,1,0:T(8,128)(2,1)S(1)} %get-tuple-element.62), channel_id=1, source_target_pairs={{0,16},{8,24},{16,0},{24,8},{1,17},{9,25},{17,1},{25,9},{2,18},{10... | collective-permute-start | bytes 786440 | tf_op jit(solution)/shard_map/ppermute | solution.py:20
  78.7 14.8 %collective-permute-start.16 = (bf16[1024,256]{1,0:T(8,128)(2,1)S(1)}, bf16[1024,256]{1,0:T(8,128)(2,1)S(1)}, u32[]{:S(2)}, u32[]{:S(2)}) collective-permute-start(bf16[1024,256]{1,0:T(8,128)(2,1)S(1)} %collective-permute-done.3.refs_2_), channel_id=1, source_target_pairs={{0,1},{1,0},{2,3},{3,2},{4,5},{5,4},{6,7},{7,6},{8,9},{9,8},{10,11... | collective-permute-start | bytes 1572872 | tf_op jit(solution)/shard_map/ppermute | solution.py:20
  82.9 11.0 %collective-permute-start.19 = (bf16[1024,128]{1,0:T(8,128)(2,1)S(1)}, bf16[1024,128]{1,0:T(8,128)(2,1)S(1)}, u32[]{:S(2)}, u32[]{:S(2)}) collective-permute-start(bf16[1024,128]{1,0:T(8,128)(2,1)S(1)} %get-tuple-element.46.refs_8_), channel_id=1, source_target_pairs={{0,2},{1,3},{2,0},{3,1},{4,6},{5,7},{6,4},{7,5},{8,10},{9,11},{10,... | collective-permute-start | bytes 786440 | tf_op jit(solution)/shard_map/ppermute | solution.py:20
  83.2 15.9 %collective-permute-start.17 = (bf16[1024,128]{1,0:T(8,128)(2,1)S(1)}, bf16[1024,128]{1,0:T(8,128)(2,1)S(1)}, u32[]{:S(2)}, u32[]{:S(2)}) collective-permute-start(bf16[1024,128]{1,0:T(8,128)(2,1)S(1)} %get-tuple-element.43.refs_4_), channel_id=1, source_target_pairs={{0,1},{1,0},{2,3},{3,2},{4,5},{5,4},{6,7},{7,6},{8,9},{9,8},{10,11... | collective-permute-start | bytes 786440 | tf_op jit(solution)/shard_map/ppermute | solution.py:20
  85.7 14.2 %collective-permute-start.13 = (bf16[1,4,128,256]{3,2,1,0:T(8,128)(2,1)S(1)}, bf16[1,4,128,256]{3,2,1,0:T(8,128)(2,1)S(1)}, u32[]{:S(2)}, u32[]{:S(2)}) collective-permute-start(bf16[1,4,128,256]{3,2,1,0:T(8,128)(2,1)S(1)} %get-tuple-element.39), channel_id=1, source_target_pairs={{0,16},{8,24},{16,0},{24,8},{1,17},{9,25},{17,1},{25,9},{2,18},{10... | collective-permute-start | bytes 786440 | tf_op jit(solution)/shard_map/ppermute | solution.py:20
  87.2 14.2 %collective-permute-start.14 = (bf16[4,128,256]{2,1,0:T(8,128)(2,1)S(1)}, bf16[4,128,256]{2,1,0:T(8,128)(2,1)S(1)}, u32[]{:S(2)}, u32[]{:S(2)}) collective-permute-start(bf16[4,128,256]{2,1,0:T(8,128)(2,1)S(1)} %fusion.6), channel_id=1, source_target_pairs={{0,4},{1,5},{2,6},{3,7},{4,0},{5,1},{6,2},{7,3},{8,12},{9,13},{10,... | collective-permute-start | bytes 786440 | tf_op jit(solution)/shard_map/ppermute | solution.py:20
  93.5 11.2 %collective-permute-start.21 = (bf16[1024,128]{1,0:T(8,128)(2,1)S(1)}, bf16[1024,128]{1,0:T(8,128)(2,1)S(1)}, u32[]{:S(2)}, u32[]{:S(2)}) collective-permute-start(bf16[1024,128]{1,0:T(8,128)(2,1)S(1)} %get-tuple-element.46.refs_8_), channel_id=1, source_target_pairs={{0,1},{1,0},{2,3},{3,2},{4,5},{5,4},{6,7},{7,6},{8,9},{9,8},{10,11... | collective-permute-start | bytes 786440 | tf_op jit(solution)/shard_map/ppermute | solution.py:20
  99.1 10.2 %collective-permute-start.22 = (bf16[1024,128]{1,0:T(8,128)(2,1)S(1)}, bf16[1024,128]{1,0:T(8,128)(2,1)S(1)}, u32[]{:S(2)}, u32[]{:S(2)}) collective-permute-start(bf16[1024,128]{1,0:T(8,128)(2,1)S(1)} %collective-permute-done.19.refs_10_), channel_id=1, source_target_pairs={{0,1},{1,0},{2,3},{3,2},{4,5},{5,4},{6,7},{7,6},{8,9},{9,8},{10,11... | collective-permute-start | bytes 786440 | tf_op jit(solution)/shard_map/ppermute | solution.py:20
  99.4 9.9 %collective-permute-start.20 = (bf16[1024,128]{1,0:T(8,128)(2,1)S(1)}, bf16[1024,128]{1,0:T(8,128)(2,1)S(1)}, u32[]{:S(2)}, u32[]{:S(2)}) collective-permute-start(bf16[1024,128]{1,0:T(8,128)(2,1)S(1)} %collective-permute-done.17.refs_5_), channel_id=1, source_target_pairs={{0,2},{1,3},{2,0},{3,1},{4,6},{5,7},{6,4},{7,5},{8,10},{9,11},{10,... | collective-permute-start | bytes 786440 | tf_op jit(solution)/shard_map/ppermute | solution.py:20
  115.9 8.4 %collective-permute-start.24 = (bf16[1,4,128,256]{3,2,1,0:T(8,128)(2,1)S(1)}, bf16[1,4,128,256]{3,2,1,0:T(8,128)(2,1)S(1)}, u32[]{:S(2)}, u32[]{:S(2)}) collective-permute-start(bf16[1,4,128,256]{3,2,1,0:T(8,128)(2,1)S(1)} %get-tuple-element.60), channel_id=1, source_target_pairs={{0,16},{8,24},{16,0},{24,8},{1,17},{9,25},{17,1},{25,9},{2,18},{10... | collective-permute-start | bytes 786440 | tf_op jit(solution)/shard_map/ppermute | solution.py:20
  124.4 7.6 %collective-permute-start.25 = (bf16[1,4,128,256]{3,2,1,0:T(8,128)(2,1)S(1)}, bf16[1,4,128,256]{3,2,1,0:T(8,128)(2,1)S(1)}, u32[]{:S(2)}, u32[]{:S(2)}) collective-permute-start(bf16[1,4,128,256]{3,2,1,0:T(8,128)(2,1)S(1)} %get-tuple-element.50), channel_id=1, source_target_pairs={{0,16},{8,24},{16,0},{24,8},{1,17},{9,25},{17,1},{25,9},{2,18},{10... | collective-permute-start | bytes 786440 | tf_op jit(solution)/shard_map/ppermute | solution.py:20
  125.0 14.1 %collective-permute-start.26 = (bf16[4,128,256]{2,1,0:T(8,128)(2,1)S(1)}, bf16[4,128,256]{2,1,0:T(8,128)(2,1)S(1)}, u32[]{:S(2)}, u32[]{:S(2)}) collective-permute-start(bf16[4,128,256]{2,1,0:T(8,128)(2,1)S(1)} %fusion.1), channel_id=1, source_target_pairs={{0,4},{1,5},{2,6},{3,7},{4,0},{5,1},{6,2},{7,3},{8,12},{9,13},{10,... | collective-permute-start | bytes 786440 | tf_op jit(solution)/shard_map/ppermute | solution.py:20
  (11 other events, 137.1 us)

commit v11 on v10

--- a/solution.py
+++ b/solution.py
@@ -184,8 +184,8 @@
             [[held[n][low] for low in range(cut)] for n in numbers]
             for numbers in BATCHES[len(halves)]
         ]
-        earlier = (columns, back) if halves else [arrived[-1] for arrived in sent.values()]
-        rounds = exchange(behind(rounds, earlier), "space", 1)
+        earlier = columns if halves else sent[cut // 2][-1]
+        rounds = behind(rounds, earlier)
         even, odd = products(jnp.concatenate([rounds, me]), lefts, batch, scale_factor)
         total = even + exchange(odd, "space", 1).astype(jnp.float32)
         halves.append(total)
@@ -196,10 +196,8 @@
 
     for piece, low, bit in hops_in_order(OWN_WIDTHS + MATE_WIDTHS, cut):
         earlier = sent.setdefault(bit, [])
-        depth = 2 if bit == 1 else 1
+        depth = (2 if len(earlier) < 7 else 3) if bit == 1 else 1
         ties = earlier[-depth] if len(earlier) >= depth else None
-        if bit == 1 and low == 0 and halves and piece in BATCHES[-1][1]:
-            ties = (ties, halves[0])
         held[piece][low | bit] = exchange(behind(held[piece][low], ties), "snap", bit)
         earlier.append(held[piece][low | bit])
         while len(halves) < len(BATCHES) and all(

time: 140 us -> 140 us (level)
  waiting for transfers between devices: 95.5 us -> 90.7 us
  starting transfers between devices: 28.6 us -> 32.7 us
    ppermute x27 -> x25, waiting for transfers between devices: 95.5 us -> 90.7 us  [exchange(): lax.ppermute(part, axis, [(i, i ^ mask) for i in range(lax.axis_size(axis...]
    ppermute x27 -> x25, starting transfers between devices: 28.6 us -> 32.7 us  [exchange(): lax.ppermute(part, axis, [(i, i ^ mask) for i in range(lax.axis_size(axis...]
  transfers between devices with their start and end apart: 27 -> 25, of which waited for: 21 -> 15; matrix products, arithmetic and copies ran while one was open for 1% -> 1% of each run, Pallas kernels for 0% -> 0%
where the time goes in v11:
time: 140 us
  waiting for transfers between devices  90.7 us (65%)
  starting transfers between devices  32.7 us (23%)
  Pallas kernels  8.26 us (6%)
  other arithmetic  5.24 us (4%)
  local copies, waits for them, and re-layouts  2.43 us (2%)
    ppermute x25, waiting for transfers between devices, exchange(): lax.ppermute(part, axis, [(i, i ^ mask) for i in range(lax.axis_size(axis...  90.7 us
    ppermute x25, starting transfers between devices, exchange(): lax.ppermute(part, axis, [(i, i ^ mask) for i in range(lax.axis_size(axis...  32.7 us
    pallas_call x2, Pallas kernels, products(): pl.pallas_call(kernel, out_shape=[jax.ShapeDtypeStruct(shape, kind) for k...  7.64 us
    convert_element_type x3, other arithmetic, pieces_of(): found.append((part.astype(jnp.float32) * scale).astype(jnp.bfloat16))  2.89 us
  transfers between devices with their start and end apart: 25, of which 15 were waited for; matrix products, arithmetic and copies ran while one was open for 1% of the time, Pallas kernels for 0%

profile of v11, /device:TPU:0, one launch (start us, length us, event | category | flops | bytes accessed | tf_op | source)
XLA Modules:
  0.0 139.5 jit_solution(7398768536712398726)
XLA Ops:
  0.7 1.7 %multiply_convert_fusion.1 = (bf16[1024,256]{1,0:T(8,128)(2,1)S(1)}, bf16[1024,256]{1,0:T(8,128)(2,1)S(1)}) fusion(f32[1024]{0:T(1024)S(1)} %get-tuple-element.65, bf16[2048,512]{1,0:T(8,128)(2,1)} %param.3, s32[]{:T(128)S(6)} %select_n.2, f32[1024]{0:T(1024)S(1)} %get-tuple-element.66, s32[]{:T(128)S(6)} %mul.16), kind=kLoop, calls=%fused_computation.4 | loop fusion | flops 1572864 | bytes 2105352 | tf_op jit(solution)/shard_map/convert_element_type | solution.py:155
  2.4 4.1 %collective-permute-start = (bf16[1024,256]{1,0:T(8,128)(2,1)S(1)}, bf16[1024,256]{1,0:T(8,128)(2,1)S(1)}, u32[]{:S(2)}, u32[]{:S(2)}) collective-permute-start(bf16[1024,256]{1,0:T(8,128)(2,1)S(1)} %get-tuple-element.57), channel_id=1, source_target_pairs={{0,4},{1,5},{2,6},{3,7},{4,0},{5,1},{6,2},{7,3},{8,12},{9,13},{10,... | collective-permute-start | bytes 1572872 | tf_op jit(solution)/shard_map/ppermute | solution.py:20
  6.5 1.6 %collective-permute-start.1 = (bf16[1024,256]{1,0:T(8,128)(2,1)S(1)}, bf16[1024,256]{1,0:T(8,128)(2,1)S(1)}, u32[]{:S(2)}, u32[]{:S(2)}) collective-permute-start(bf16[1024,256]{1,0:T(8,128)(2,1)S(1)} %get-tuple-element.58.refs_0_), channel_id=1, source_target_pairs={{0,2},{1,3},{2,0},{3,1},{4,6},{5,7},{6,4},{7,5},{8,10},{9,11},{10,... | collective-permute-start | bytes 1572872 | tf_op jit(solution)/shard_map/ppermute | solution.py:20
  10.4 19.4 %collective-permute-done.refs_2_.refs_4_ = bf16[1024,256]{1,0:T(8,128)(2,1)S(1)} collective-permute-done((bf16[1024,256]{1,0:T(8,128)(2,1)S(1)}, bf16[1024,256]{1,0:T(8,128)(2,1)S(1)}, u32[]{:S(2)}, u32[]{:S(2)}) %collective-permute-start) | collective-permute-done | bytes 524320 | tf_op jit(solution)/shard_map/ppermute | solution.py:20
  34.8 2.3 %collective-permute-start.4 = (bf16[1024,256]{1,0:T(8,128)(2,1)}, bf16[1024,256]{1,0:T(8,128)(2,1)S(1)}, u32[]{:S(2)}, u32[]{:S(2)}) collective-permute-start(bf16[1024,256]{1,0:T(8,128)(2,1)} %multiply_convert_fusion), channel_id=1, source_target_pairs={{0,4},{1,5},{2,6},{3,7},{4,0},{5,1},{6,2},{7,3},{8,12},{9,13},{10,... | collective-permute-start | bytes 1572872 | tf_op jit(solution)/shard_map/ppermute | solution.py:20
  37.6 13.1 %collective-permute-done.2.refs_6_ = bf16[1024,256]{1,0:T(8,128)(2,1)} collective-permute-done((bf16[1024,256]{1,0:T(8,128)(2,1)S(1)}, bf16[1024,256]{1,0:T(8,128)(2,1)}, u32[]{:S(2)}, u32[]{:S(2)}) %collective-permute-start.2) | collective-permute-done | bytes 524320 | tf_op jit(solution)/shard_map/ppermute | solution.py:20
  51.5 2.2 %collective-permute-start.9 = (bf16[1024,256]{1,0:T(8,128)(2,1)}, bf16[1024,256]{1,0:T(8,128)(2,1)}, u32[]{:S(2)}, u32[]{:S(2)}) collective-permute-start(bf16[1024,256]{1,0:T(8,128)(2,1)} %collective-permute-done.2.refs_6_), channel_id=1, source_target_pairs={{0,1},{1,0},{2,3},{3,2},{4,5},{5,4},{6,7},{7,6},{8,9},{9,8},{10,11... | collective-permute-start | bytes 1572872 | tf_op jit(solution)/shard_map/ppermute | solution.py:20
  53.8 6.4 %collective-permute-done.4.refs_3_ = bf16[1024,256]{1,0:T(8,128)(2,1)S(1)} collective-permute-done((bf16[1024,256]{1,0:T(8,128)(2,1)}, bf16[1024,256]{1,0:T(8,128)(2,1)S(1)}, u32[]{:S(2)}, u32[]{:S(2)}) %collective-permute-start.4) | collective-permute-done | bytes 524320 | tf_op jit(solution)/shard_map/ppermute | solution.py:20
  60.9 5.3 %collective-permute-done.3.refs_2_ = bf16[1024,256]{1,0:T(8,128)(2,1)S(1)} collective-permute-done((bf16[1024,256]{1,0:T(8,128)(2,1)S(1)}, bf16[1024,256]{1,0:T(8,128)(2,1)S(1)}, u32[]{:S(2)}, u32[]{:S(2)}) %collective-permute-start.3) | collective-permute-done | bytes 524320 | tf_op jit(solution)/shard_map/ppermute | solution.py:20
  67.4 4.2 %shard_map.38 = (f32[2,2,4,128,256]{4,3,2,1,0:T(8,128)S(1)}, bf16[2,2,4,128,256]{4,3,2,1,0:T(8,128)(2,1)S(1)}) custom-call(s32[9]{0:T(128)S(1)} %pad_add_fusion.1.choices_ref, bf16[2,512,1024]{2,1,0:T(8,128)(2,1)S(1)} %shard_map.37.lefts_ref, bf16[1024,256]{1,0:T(8,128)(2,1)S(1)} %get-tuple-element.58.refs_0_, bf16[1024,256]{1,0:T(8,128)(2,1)S(1)} %copy-done.3, ...), custom_call_target="tpu_custom_call" | custom-call | tf_op jit(solution)/shard_map/pallas_call | solution.py:110
  72.4 1.9 %collective-permute-done.10 = bf16[2,2,4,128,256]{4,3,2,1,0:T(8,128)(2,1)S(1)} collective-permute-done((bf16[2,2,4,128,256]{4,3,2,1,0:T(8,128)(2,1)S(1)}, bf16[2,2,4,128,256]{4,3,2,1,0:T(8,128)(2,1)S(1)}, u32[]{:S(2)}, u32[]{:S(2)}) %collective-permute-start.10) | collective-permute-done | bytes 1048608 | tf_op jit(solution)/shard_map/ppermute | solution.py:20
  74.7 1.6 %collective-permute-start.11 = (bf16[1,4,128,256]{3,2,1,0:T(8,128)(2,1)S(1)}, bf16[1,4,128,256]{3,2,1,0:T(8,128)(2,1)S(1)}, u32[]{:S(2)}, u32[]{:S(2)}) collective-permute-start(bf16[1,4,128,256]{3,2,1,0:T(8,128)(2,1)S(1)} %get-tuple-element.62), channel_id=1, source_target_pairs={{0,16},{8,24},{16,0},{24,8},{1,17},{9,25},{17,1},{25,9},{2,18},{10... | collective-permute-start | bytes 786440 | tf_op jit(solution)/shard_map/ppermute | solution.py:20
  78.3 2.2 %collective-permute-done.16.refs_6_ = bf16[1024,128]{1,0:T(8,128)(2,1)S(1)} collective-permute-done((bf16[1024,128]{1,0:T(8,128)(2,1)S(1)}, bf16[1024,128]{1,0:T(8,128)(2,1)S(1)}, u32[]{:S(2)}, u32[]{:S(2)}) %collective-permute-start.16) | collective-permute-done | bytes 262176 | tf_op jit(solution)/shard_map/ppermute | solution.py:20
  81.1 2.0 %collective-permute-done.11 = bf16[1,4,128,256]{3,2,1,0:T(8,128)(2,1)S(1)} collective-permute-done((bf16[1,4,128,256]{3,2,1,0:T(8,128)(2,1)S(1)}, bf16[1,4,128,256]{3,2,1,0:T(8,128)(2,1)S(1)}, u32[]{:S(2)}, u32[]{:S(2)}) %collective-permute-start.11) | collective-permute-done | bytes 262176 | tf_op jit(solution)/shard_map/ppermute | solution.py:20
  83.2 3.4 %collective-permute-start.13 = (bf16[4,128,256]{2,1,0:T(8,128)(2,1)S(1)}, bf16[4,128,256]{2,1,0:T(8,128)(2,1)S(1)}, u32[]{:S(2)}, u32[]{:S(2)}) collective-permute-start(bf16[4,128,256]{2,1,0:T(8,128)(2,1)S(1)} %fusion.6), channel_id=1, source_target_pairs={{0,4},{1,5},{2,6},{3,7},{4,0},{5,1},{6,2},{7,3},{8,12},{9,13},{10,... | collective-permute-start | bytes 786440 | tf_op jit(solution)/shard_map/ppermute | solution.py:20
  86.6 1.5 %collective-permute-start.12 = (bf16[1,4,128,256]{3,2,1,0:T(8,128)(2,1)S(1)}, bf16[1,4,128,256]{3,2,1,0:T(8,128)(2,1)S(1)}, u32[]{:S(2)}, u32[]{:S(2)}) collective-permute-start(bf16[1,4,128,256]{3,2,1,0:T(8,128)(2,1)S(1)} %get-tuple-element.39), channel_id=1, source_target_pairs={{0,16},{8,24},{16,0},{24,8},{1,17},{9,25},{17,1},{25,9},{2,18},{10... | collective-permute-start | bytes 786440 | tf_op jit(solution)/shard_map/ppermute | solution.py:20
  88.1 7.5 %collective-permute-done.15.refs_5_ = bf16[1024,128]{1,0:T(8,128)(2,1)S(1)} collective-permute-done((bf16[1024,128]{1,0:T(8,128)(2,1)S(1)}, bf16[1024,128]{1,0:T(8,128)(2,1)S(1)}, u32[]{:S(2)}, u32[]{:S(2)}) %collective-permute-start.15) | collective-permute-done | bytes 262176 | tf_op jit(solution)/shard_map/ppermute | solution.py:20
  98.2 6.6 %collective-permute-done.19.refs_9_ = bf16[1024,128]{1,0:T(8,128)(2,1)S(1)} collective-permute-done((bf16[1024,128]{1,0:T(8,128)(2,1)S(1)}, bf16[1024,128]{1,0:T(8,128)(2,1)S(1)}, u32[]{:S(2)}, u32[]{:S(2)}) %collective-permute-start.19) | collective-permute-done | bytes 262176 | tf_op jit(solution)/shard_map/ppermute | solution.py:20
  104.8 3.6 %collective-permute-done.20.refs_11_ = bf16[1024,128]{1,0:T(8,128)(2,1)S(1)} collective-permute-done((bf16[1024,128]{1,0:T(8,128)(2,1)S(1)}, bf16[1024,128]{1,0:T(8,128)(2,1)S(1)}, u32[]{:S(2)}, u32[]{:S(2)}) %collective-permute-start.20) | collective-permute-done | bytes 262176 | tf_op jit(solution)/shard_map/ppermute | solution.py:20
  108.4 3.5 %shard_map.39 = (f32[2,2,4,128,256]{4,3,2,1,0:T(8,128)S(1)}, bf16[2,2,4,128,256]{4,3,2,1,0:T(8,128)(2,1)S(1)}) custom-call(s32[9]{0:T(128)S(1)} %pad_add_fusion.2.choices_ref, bf16[2,512,1024]{2,1,0:T(8,128)(2,1)S(1)} %shard_map.37.lefts_ref, bf16[1024,256]{1,0:T(8,128)(2,1)S(1)} %multiply_convert_fusion.2.refs_1_.refs_0_, ...), custom_call_target="tpu_custom_call" | custom-call | tf_op jit(solution)/shard_map/pallas_call | solution.py:110
  111.9 2.6 %collective-permute-done.21 = bf16[2,2,4,128,256]{4,3,2,1,0:T(8,128)(2,1)S(1)} collective-permute-done((bf16[2,2,4,128,256]{4,3,2,1,0:T(8,128)(2,1)S(1)}, bf16[2,2,4,128,256]{4,3,2,1,0:T(8,128)(2,1)S(1)}, u32[]{:S(2)}, u32[]{:S(2)}) %collective-permute-start.21) | collective-permute-done | bytes 1048608 | tf_op jit(solution)/shard_map/ppermute | solution.py:20
  115.6 7.9 %collective-permute-done.22 = bf16[1,4,128,256]{3,2,1,0:T(8,128)(2,1)S(1)} collective-permute-done((bf16[1,4,128,256]{3,2,1,0:T(8,128)(2,1)S(1)}, bf16[1,4,128,256]{3,2,1,0:T(8,128)(2,1)S(1)}, u32[]{:S(2)}, u32[]{:S(2)}) %collective-permute-start.22) | collective-permute-done | bytes 262176 | tf_op jit(solution)/shard_map/ppermute | solution.py:20
  123.5 3.4 %collective-permute-start.24 = (bf16[4,128,256]{2,1,0:T(8,128)(2,1)S(1)}, bf16[4,128,256]{2,1,0:T(8,128)(2,1)S(1)}, u32[]{:S(2)}, u32[]{:S(2)}) collective-permute-start(bf16[4,128,256]{2,1,0:T(8,128)(2,1)S(1)} %fusion.1), channel_id=1, source_target_pairs={{0,4},{1,5},{2,6},{3,7},{4,0},{5,1},{6,2},{7,3},{8,12},{9,13},{10,... | collective-permute-start | bytes 786440 | tf_op jit(solution)/shard_map/ppermute | solution.py:20
  127.4 10.9 %collective-permute-done.24 = bf16[4,128,256]{2,1,0:T(8,128)(2,1)S(1)} collective-permute-done((bf16[4,128,256]{2,1,0:T(8,128)(2,1)S(1)}, bf16[4,128,256]{2,1,0:T(8,128)(2,1)S(1)}, u32[]{:S(2)}, u32[]{:S(2)}) %collective-permute-start.24) | collective-permute-done | bytes 262176 | tf_op jit(solution)/shard_map/ppermute | solution.py:20
  (65 shorter events, 20.6 us)
Async XLA Ops:
  2.4 27.4 %collective-permute-start = (bf16[1024,256]{1,0:T(8,128)(2,1)S(1)}, bf16[1024,256]{1,0:T(8,128)(2,1)S(1)}, u32[]{:S(2)}, u32[]{:S(2)}) collective-permute-start(bf16[1024,256]{1,0:T(8,128)(2,1)S(1)} %get-tuple-element.57), channel_id=1, source_target_pairs={{0,4},{1,5},{2,6},{3,7},{4,0},{5,1},{6,2},{7,3},{8,12},{9,13},{10,... | collective-permute-start | bytes 1572872 | tf_op jit(solution)/shard_map/ppermute | solution.py:20
  6.5 23.5 %collective-permute-start.1 = (bf16[1024,256]{1,0:T(8,128)(2,1)S(1)}, bf16[1024,256]{1,0:T(8,128)(2,1)S(1)}, u32[]{:S(2)}, u32[]{:S(2)}) collective-permute-start(bf16[1024,256]{1,0:T(8,128)(2,1)S(1)} %get-tuple-element.58.refs_0_), channel_id=1, source_target_pairs={{0,2},{1,3},{2,0},{3,1},{4,6},{5,7},{6,4},{7,5},{8,10},{9,11},{10,... | collective-permute-start | bytes 1572872 | tf_op jit(solution)/shard_map/ppermute | solution.py:20
  8.1 23.4 %collective-permute-start.5 = (bf16[1024,256]{1,0:T(8,128)(2,1)S(1)}, bf16[1024,256]{1,0:T(8,128)(2,1)S(1)}, u32[]{:S(2)}, u32[]{:S(2)}) collective-permute-start(bf16[1024,256]{1,0:T(8,128)(2,1)S(1)} %get-tuple-element.58.refs_0_), channel_id=1, source_target_pairs={{0,1},{1,0},{2,3},{3,2},{4,5},{5,4},{6,7},{7,6},{8,9},{9,8},{10,11... | collective-permute-start | bytes 1572872 | tf_op jit(solution)/shard_map/ppermute | solution.py:20
  9.8 27.3 %collective-permute-start.7 = (bf16[1024,256]{1,0:T(8,128)(2,1)S(1)}, bf16[1024,256]{1,0:T(8,128)(2,1)S(1)}, u32[]{:S(2)}, u32[]{:S(2)}) collective-permute-start(bf16[1024,256]{1,0:T(8,128)(2,1)S(1)} %multiply_convert_fusion.2.refs_1_.refs_0_), channel_id=1, source_target_pairs={{0,1},{1,0},{2,3},{3,2},{4,5},{5,4},{6,7},{7,6},{8,9},{9,8},{10,11... | collective-permute-start | bytes 1572872 | tf_op jit(solution)/shard_map/ppermute | solution.py:20
  30.0 20.8 %collective-permute-start.2 = (bf16[1024,256]{1,0:T(8,128)(2,1)S(1)}, bf16[1024,256]{1,0:T(8,128)(2,1)}, u32[]{:S(2)}, u32[]{:S(2)}) collective-permute-start(bf16[1024,256]{1,0:T(8,128)(2,1)S(1)} %collective-permute-done.refs_2_.refs_4_), channel_id=1, source_target_pairs={{0,2},{1,3},{2,0},{3,1},{4,6},{5,7},{6,4},{7,5},{8,10},{9,11},{10,... | collective-permute-start | bytes 1572872 | tf_op jit(solution)/shard_map/ppermute | solution.py:20
  32.3 18.5 %collective-permute-start.6 = (bf16[1024,256]{1,0:T(8,128)(2,1)S(1)}, bf16[1024,256]{1,0:T(8,128)(2,1)S(1)}, u32[]{:S(2)}, u32[]{:S(2)}) collective-permute-start(bf16[1024,256]{1,0:T(8,128)(2,1)S(1)} %collective-permute-done.1.refs_2_), channel_id=1, source_target_pairs={{0,1},{1,0},{2,3},{3,2},{4,5},{5,4},{6,7},{7,6},{8,9},{9,8},{10,11... | collective-permute-start | bytes 1572872 | tf_op jit(solution)/shard_map/ppermute | solution.py:20
  34.8 25.5 %collective-permute-start.4 = (bf16[1024,256]{1,0:T(8,128)(2,1)}, bf16[1024,256]{1,0:T(8,128)(2,1)S(1)}, u32[]{:S(2)}, u32[]{:S(2)}) collective-permute-start(bf16[1024,256]{1,0:T(8,128)(2,1)} %multiply_convert_fusion), channel_id=1, source_target_pairs={{0,4},{1,5},{2,6},{3,7},{4,0},{5,1},{6,2},{7,3},{8,12},{9,13},{10,... | collective-permute-start | bytes 1572872 | tf_op jit(solution)/shard_map/ppermute | solution.py:20
  37.1 29.1 %collective-permute-start.8 = (bf16[1024,256]{1,0:T(8,128)(2,1)S(1)}, bf16[1024,256]{1,0:T(8,128)(2,1)}, u32[]{:S(2)}, u32[]{:S(2)}) collective-permute-start(bf16[1024,256]{1,0:T(8,128)(2,1)S(1)} %collective-permute-done.refs_2_.refs_4_), channel_id=1, source_target_pairs={{0,1},{1,0},{2,3},{3,2},{4,5},{5,4},{6,7},{7,6},{8,9},{9,8},{10,11... | collective-permute-start | bytes 1572872 | tf_op jit(solution)/shard_map/ppermute | solution.py:20
  50.7 15.4 %collective-permute-start.3 = (bf16[1024,256]{1,0:T(8,128)(2,1)S(1)}, bf16[1024,256]{1,0:T(8,128)(2,1)S(1)}, u32[]{:S(2)}, u32[]{:S(2)}) collective-permute-start(bf16[1024,256]{1,0:T(8,128)(2,1)S(1)} %multiply_convert_fusion.2.refs_1_.refs_0_), channel_id=1, source_target_pairs={{0,2},{1,3},{2,0},{3,1},{4,6},{5,7},{6,4},{7,5},{8,10},{9,11},{10,... | collective-permute-start | bytes 1572872 | tf_op jit(solution)/shard_map/ppermute | solution.py:20
  51.5 15.8 %collective-permute-start.9 = (bf16[1024,256]{1,0:T(8,128)(2,1)}, bf16[1024,256]{1,0:T(8,128)(2,1)}, u32[]{:S(2)}, u32[]{:S(2)}) collective-permute-start(bf16[1024,256]{1,0:T(8,128)(2,1)} %collective-permute-done.2.refs_6_), channel_id=1, source_target_pairs={{0,1},{1,0},{2,3},{3,2},{4,5},{5,4},{6,7},{7,6},{8,9},{9,8},{10,11... | collective-permute-start | bytes 1572872 | tf_op jit(solution)/shard_map/ppermute | solution.py:20
  71.6 2.7 %collective-permute-start.10 = (bf16[2,2,4,128,256]{4,3,2,1,0:T(8,128)(2,1)S(1)}, bf16[2,2,4,128,256]{4,3,2,1,0:T(8,128)(2,1)S(1)}, u32[]{:S(2)}, u32[]{:S(2)}) collective-permute-start(bf16[2,2,4,128,256]{4,3,2,1,0:T(8,128)(2,1)S(1)} %get-tuple-element.38), channel_id=1, source_target_pairs={{0,8},{8,0},{16,24},{24,16},{1,9},{9,1},{17,25},{25,17},{2,10},{10... | collective-permute-start | bytes 3145736 | tf_op jit(solution)/shard_map/ppermute | solution.py:20
  71.7 8.8 %collective-permute-start.16 = (bf16[1024,128]{1,0:T(8,128)(2,1)S(1)}, bf16[1024,128]{1,0:T(8,128)(2,1)S(1)}, u32[]{:S(2)}, u32[]{:S(2)}) collective-permute-start(bf16[1024,128]{1,0:T(8,128)(2,1)S(1)} %get-tuple-element.43.refs_4_), channel_id=1, source_target_pairs={{0,2},{1,3},{2,0},{3,1},{4,6},{5,7},{6,4},{7,5},{8,10},{9,11},{10,... | collective-permute-start | bytes 786440 | tf_op jit(solution)/shard_map/ppermute | solution.py:20
  74.7 8.4 %collective-permute-start.11 = (bf16[1,4,128,256]{3,2,1,0:T(8,128)(2,1)S(1)}, bf16[1,4,128,256]{3,2,1,0:T(8,128)(2,1)S(1)}, u32[]{:S(2)}, u32[]{:S(2)}) collective-permute-start(bf16[1,4,128,256]{3,2,1,0:T(8,128)(2,1)S(1)} %get-tuple-element.62), channel_id=1, source_target_pairs={{0,16},{8,24},{16,0},{24,8},{1,17},{9,25},{17,1},{25,9},{2,18},{10... | collective-permute-start | bytes 786440 | tf_op jit(solution)/shard_map/ppermute | solution.py:20
  76.3 21.2 %collective-permute-start.14 = (bf16[1024,256]{1,0:T(8,128)(2,1)S(1)}, bf16[1024,256]{1,0:T(8,128)(2,1)S(1)}, u32[]{:S(2)}, u32[]{:S(2)}) collective-permute-start(bf16[1024,256]{1,0:T(8,128)(2,1)S(1)} %collective-permute-done.3.refs_2_), channel_id=1, source_target_pairs={{0,1},{1,0},{2,3},{3,2},{4,5},{5,4},{6,7},{7,6},{8,9},{9,8},{10,11... | collective-permute-start | bytes 1572872 | tf_op jit(solution)/shard_map/ppermute | solution.py:20
  77.8 17.8 %collective-permute-start.15 = (bf16[1024,128]{1,0:T(8,128)(2,1)S(1)}, bf16[1024,128]{1,0:T(8,128)(2,1)S(1)}, u32[]{:S(2)}, u32[]{:S(2)}) collective-permute-start(bf16[1024,128]{1,0:T(8,128)(2,1)S(1)} %get-tuple-element.43.refs_4_), channel_id=1, source_target_pairs={{0,1},{1,0},{2,3},{3,2},{4,5},{5,4},{6,7},{7,6},{8,9},{9,8},{10,11... | collective-permute-start | bytes 786440 | tf_op jit(solution)/shard_map/ppermute | solution.py:20
  80.4 16.6 %collective-permute-start.17 = (bf16[1024,128]{1,0:T(8,128)(2,1)S(1)}, bf16[1024,128]{1,0:T(8,128)(2,1)S(1)}, u32[]{:S(2)}, u32[]{:S(2)}) collective-permute-start(bf16[1024,128]{1,0:T(8,128)(2,1)S(1)} %get-tuple-element.46.refs_8_), channel_id=1, source_target_pairs={{0,2},{1,3},{2,0},{3,1},{4,6},{5,7},{6,4},{7,5},{8,10},{9,11},{10,... | collective-permute-start | bytes 786440 | tf_op jit(solution)/shard_map/ppermute | solution.py:20
  83.2 14.9 %collective-permute-start.13 = (bf16[4,128,256]{2,1,0:T(8,128)(2,1)S(1)}, bf16[4,128,256]{2,1,0:T(8,128)(2,1)S(1)}, u32[]{:S(2)}, u32[]{:S(2)}) collective-permute-start(bf16[4,128,256]{2,1,0:T(8,128)(2,1)S(1)} %fusion.6), channel_id=1, source_target_pairs={{0,4},{1,5},{2,6},{3,7},{4,0},{5,1},{6,2},{7,3},{8,12},{9,13},{10,... | collective-permute-start | bytes 786440 | tf_op jit(solution)/shard_map/ppermute | solution.py:20
  86.6 11.5 %collective-permute-start.12 = (bf16[1,4,128,256]{3,2,1,0:T(8,128)(2,1)S(1)}, bf16[1,4,128,256]{3,2,1,0:T(8,128)(2,1)S(1)}, u32[]{:S(2)}, u32[]{:S(2)}) collective-permute-start(bf16[1,4,128,256]{3,2,1,0:T(8,128)(2,1)S(1)} %get-tuple-element.39), channel_id=1, source_target_pairs={{0,16},{8,24},{16,0},{24,8},{1,17},{9,25},{17,1},{25,9},{2,18},{10... | collective-permute-start | bytes 786440 | tf_op jit(solution)/shard_map/ppermute | solution.py:20
  95.6 9.3 %collective-permute-start.19 = (bf16[1024,128]{1,0:T(8,128)(2,1)S(1)}, bf16[1024,128]{1,0:T(8,128)(2,1)S(1)}, u32[]{:S(2)}, u32[]{:S(2)}) collective-permute-start(bf16[1024,128]{1,0:T(8,128)(2,1)S(1)} %get-tuple-element.46.refs_8_), channel_id=1, source_target_pairs={{0,1},{1,0},{2,3},{3,2},{4,5},{5,4},{6,7},{7,6},{8,9},{9,8},{10,11... | collective-permute-start | bytes 786440 | tf_op jit(solution)/shard_map/ppermute | solution.py:20
  97.1 7.8 %collective-permute-start.18 = (bf16[1024,128]{1,0:T(8,128)(2,1)S(1)}, bf16[1024,128]{1,0:T(8,128)(2,1)S(1)}, u32[]{:S(2)}, u32[]{:S(2)}) collective-permute-start(bf16[1024,128]{1,0:T(8,128)(2,1)S(1)} %collective-permute-done.15.refs_5_), channel_id=1, source_target_pairs={{0,2},{1,3},{2,0},{3,1},{4,6},{5,7},{6,4},{7,5},{8,10},{9,11},{10,... | collective-permute-start | bytes 786440 | tf_op jit(solution)/shard_map/ppermute | solution.py:20
  97.5 10.9 %collective-permute-start.20 = (bf16[1024,128]{1,0:T(8,128)(2,1)S(1)}, bf16[1024,128]{1,0:T(8,128)(2,1)S(1)}, u32[]{:S(2)}, u32[]{:S(2)}) collective-permute-start(bf16[1024,128]{1,0:T(8,128)(2,1)S(1)} %collective-permute-done.17.refs_10_), channel_id=1, source_target_pairs={{0,1},{1,0},{2,3},{3,2},{4,5},{5,4},{6,7},{7,6},{8,9},{9,8},{10,11... | collective-permute-start | bytes 786440 | tf_op jit(solution)/shard_map/ppermute | solution.py:20
  115.0 8.4 %collective-permute-start.22 = (bf16[1,4,128,256]{3,2,1,0:T(8,128)(2,1)S(1)}, bf16[1,4,128,256]{3,2,1,0:T(8,128)(2,1)S(1)}, u32[]{:S(2)}, u32[]{:S(2)}) collective-permute-start(bf16[1,4,128,256]{3,2,1,0:T(8,128)(2,1)S(1)} %get-tuple-element.60), channel_id=1, source_target_pairs={{0,16},{8,24},{16,0},{24,8},{1,17},{9,25},{17,1},{25,9},{2,18},{10... | collective-permute-start | bytes 786440 | tf_op jit(solution)/shard_map/ppermute | solution.py:20
  123.5 14.8 %collective-permute-start.24 = (bf16[4,128,256]{2,1,0:T(8,128)(2,1)S(1)}, bf16[4,128,256]{2,1,0:T(8,128)(2,1)S(1)}, u32[]{:S(2)}, u32[]{:S(2)}) collective-permute-start(bf16[4,128,256]{2,1,0:T(8,128)(2,1)S(1)} %fusion.1), channel_id=1, source_target_pairs={{0,4},{1,5},{2,6},{3,7},{4,0},{5,1},{6,2},{7,3},{8,12},{9,13},{10,... | collective-permute-start | bytes 786440 | tf_op jit(solution)/shard_map/ppermute | solution.py:20
  126.9 11.4 %collective-permute-start.23 = (bf16[1,4,128,256]{3,2,1,0:T(8,128)(2,1)S(1)}, bf16[1,4,128,256]{3,2,1,0:T(8,128)(2,1)S(1)}, u32[]{:S(2)}, u32[]{:S(2)}) collective-permute-start(bf16[1,4,128,256]{3,2,1,0:T(8,128)(2,1)S(1)} %get-tuple-element.50), channel_id=1, source_target_pairs={{0,16},{8,24},{16,0},{24,8},{1,17},{9,25},{17,1},{25,9},{2,18},{10... | collective-permute-start | bytes 786440 | tf_op jit(solution)/shard_map/ppermute | solution.py:20
  (9 other events, 127.6 us)

commit v12 on v11

--- a/solution.py
+++ b/solution.py
@@ -8,10 +8,10 @@
 ROUNDS = 4
 OWN_WIDTHS = (2, 2)
 CROSSING_WIDTHS = (2, 2)
-MATE_WIDTHS = (2, 1, 1)
+MATE_WIDTHS = (2, 2)
 NEAR_FIRST = (3,)
-URGENCY = (0, 2, 1, 3, 4)
-BATCHES = (((0,), (2,)), ((1,), (3, 4)))
+URGENCY = (0, 2, 1, 3)
+BATCHES = (((0,), (2,)), ((1,), (3,)))
 VMEM = pl.BlockSpec(memory_space=pltpu.VMEM)
 PARAMS = pltpu.CompilerParams(vmem_limit_bytes=40 * 2**20)
 
@@ -45,7 +45,7 @@
         piece, low, bit = hop
         shared = 2 if bit == cut // 2 and start_of(hop) < crossed else 1
         free[bit] = start_of(hop) + shared * widths[piece]
-        ready[piece, low | bit] = free[bit]
+        ready[piece, low | bit] = free[bit] + 0.5
         waiting.remove(hop)
         ordered.append(hop)
     return ordered
@@ -184,7 +184,7 @@
             [[held[n][low] for low in range(cut)] for n in numbers]
             for numbers in BATCHES[len(halves)]
         ]
-        earlier = columns if halves else sent[cut // 2][-1]
+        earlier = columns if halves else sent[cut // 2][:3][-1]
         rounds = behind(rounds, earlier)
         even, odd = products(jnp.concatenate([rounds, me]), lefts, batch, scale_factor)
         total = even + exchange(odd, "space", 1).astype(jnp.float32)
@@ -196,7 +196,7 @@
 
     for piece, low, bit in hops_in_order(OWN_WIDTHS + MATE_WIDTHS, cut):
         earlier = sent.setdefault(bit, [])
-        depth = (2 if len(earlier) < 7 else 3) if bit == 1 else 1
+        depth = 2 if bit == 1 and len(earlier) < 99 else 1
         ties = earlier[-depth] if len(earlier) >= depth else None
         held[piece][low | bit] = exchange(behind(held[piece][low], ties), "snap", bit)
         earlier.append(held[piece][low | bit])

time: 140 us -> 138 us (0.986)
  starting transfers between devices: 32.7 us -> 22.4 us
  waiting for transfers between devices: 90.7 us -> 99.7 us
    ppermute x25 -> x22, starting transfers between devices: 32.7 us -> 22.4 us  [exchange(): lax.ppermute(part, axis, [(i, i ^ mask) for i in range(lax.axis_size(axis...]
    ppermute x25 -> x22, waiting for transfers between devices: 90.7 us -> 99.7 us  [exchange(): lax.ppermute(part, axis, [(i, i ^ mask) for i in range(lax.axis_size(axis...]
  transfers between devices with their start and end apart: 25 -> 22, of which waited for: 15 -> 18; matrix products, arithmetic and copies ran while one was open for 1% -> 1% of each run, Pallas kernels for 0% -> 0%
where the time goes in v12:
time: 138 us
  waiting for transfers between devices  99.7 us (72%)
  starting transfers between devices  22.4 us (16%)
  Pallas kernels  7.94 us (6%)
  other arithmetic  5.25 us (4%)
  local copies, waits for them, and re-layouts  2.59 us (2%)
    ppermute x22, waiting for transfers between devices, exchange(): lax.ppermute(part, axis, [(i, i ^ mask) for i in range(lax.axis_size(axis...  99.7 us
    ppermute x22, starting transfers between devices, exchange(): lax.ppermute(part, axis, [(i, i ^ mask) for i in range(lax.axis_size(axis...  22.4 us
    pallas_call x2, Pallas kernels, products(): pl.pallas_call(kernel, out_shape=[jax.ShapeDtypeStruct(shape, kind) for k...  7.31 us
    convert_element_type x3, other arithmetic, pieces_of(): found.append((part.astype(jnp.float32) * scale).astype(jnp.bfloat16))  2.88 us
  transfers between devices with their start and end apart: 22, of which 18 were waited for; matrix products, arithmetic and copies ran while one was open for 1% of the time, Pallas kernels for 0%

profile of v12, /device:TPU:0, one launch (start us, length us, event | category | flops | bytes accessed | tf_op | source)
XLA Modules:
  0.0 138.0 jit_solution(535708187044184131)
XLA Ops:
  0.7 1.7 %multiply_convert_fusion.1 = (bf16[1024,256]{1,0:T(8,128)(2,1)S(1)}, bf16[1024,256]{1,0:T(8,128)(2,1)S(1)}) fusion(f32[1024]{0:T(1024)S(1)} %get-tuple-element.57, bf16[2048,512]{1,0:T(8,128)(2,1)} %param.3, s32[]{:T(128)S(6)} %select_n.2, f32[1024]{0:T(1024)S(1)} %get-tuple-element.58, s32[]{:T(128)S(6)} %mul.16), kind=kLoop, calls=%fused_computation.4 | loop fusion | flops 1572864 | bytes 2105352 | tf_op jit(solution)/shard_map/convert_element_type | solution.py:155
  2.8 3.0 %collective-permute-start.6 = (bf16[1024,256]{1,0:T(8,128)(2,1)S(1)}, bf16[1024,256]{1,0:T(8,128)(2,1)S(1)}, u32[]{:S(2)}, u32[]{:S(2)}) collective-permute-start(bf16[1024,256]{1,0:T(8,128)(2,1)S(1)} %multiply_convert_fusion.2.refs_1_.refs_0_), channel_id=1, source_target_pairs={{0,1},{1,0},{2,3},{3,2},{4,5},{5,4},{6,7},{7,6},{8,9},{9,8},{10,11... | collective-permute-start | bytes 1572872 | tf_op jit(solution)/shard_map/ppermute | solution.py:20
  7.4 2.6 %collective-permute-start = (bf16[1024,256]{1,0:T(8,128)(2,1)S(1)}, bf16[1024,256]{1,0:T(8,128)(2,1)S(1)}, u32[]{:S(2)}, u32[]{:S(2)}) collective-permute-start(bf16[1024,256]{1,0:T(8,128)(2,1)S(1)} %get-tuple-element.51), channel_id=1, source_target_pairs={{0,4},{1,5},{2,6},{3,7},{4,0},{5,1},{6,2},{7,3},{8,12},{9,13},{10,... | collective-permute-start | bytes 1572872 | tf_op jit(solution)/shard_map/ppermute | solution.py:20
  10.5 8.1 %collective-permute-done.6.refs_1_ = bf16[1024,256]{1,0:T(8,128)(2,1)S(1)} collective-permute-done((bf16[1024,256]{1,0:T(8,128)(2,1)S(1)}, bf16[1024,256]{1,0:T(8,128)(2,1)S(1)}, u32[]{:S(2)}, u32[]{:S(2)}) %collective-permute-start.6) | collective-permute-done | bytes 524320 | tf_op jit(solution)/shard_map/ppermute | solution.py:20
  18.6 11.8 %collective-permute-done.1.refs_2_ = bf16[1024,256]{1,0:T(8,128)(2,1)S(1)} collective-permute-done((bf16[1024,256]{1,0:T(8,128)(2,1)S(1)}, bf16[1024,256]{1,0:T(8,128)(2,1)S(1)}, u32[]{:S(2)}, u32[]{:S(2)}) %collective-permute-start.1) | collective-permute-done | bytes 524320 | tf_op jit(solution)/shard_map/ppermute | solution.py:20
  30.7 2.0 %collective-permute-done.refs_2_.refs_4_ = bf16[1024,256]{1,0:T(8,128)(2,1)S(1)} collective-permute-done((bf16[1024,256]{1,0:T(8,128)(2,1)S(1)}, bf16[1024,256]{1,0:T(8,128)(2,1)S(1)}, u32[]{:S(2)}, u32[]{:S(2)}) %collective-permute-start) | collective-permute-done | bytes 524320 | tf_op jit(solution)/shard_map/ppermute | solution.py:20
  34.1 2.7 %collective-permute-start.4 = (bf16[1024,256]{1,0:T(8,128)(2,1)}, bf16[1024,256]{1,0:T(8,128)(2,1)S(1)}, u32[]{:S(2)}, u32[]{:S(2)}) collective-permute-start(bf16[1024,256]{1,0:T(8,128)(2,1)} %multiply_convert_fusion), channel_id=1, source_target_pairs={{0,4},{1,5},{2,6},{3,7},{4,0},{5,1},{6,2},{7,3},{8,12},{9,13},{10,... | collective-permute-start | bytes 1572872 | tf_op jit(solution)/shard_map/ppermute | solution.py:20
  38.1 7.1 %collective-permute-done.7.refs_3_ = bf16[1024,256]{1,0:T(8,128)(2,1)S(1)} collective-permute-done((bf16[1024,256]{1,0:T(8,128)(2,1)S(1)}, bf16[1024,256]{1,0:T(8,128)(2,1)S(1)}, u32[]{:S(2)}, u32[]{:S(2)}) %collective-permute-start.7) | collective-permute-done | bytes 524320 | tf_op jit(solution)/shard_map/ppermute | solution.py:20
  46.0 7.0 %collective-permute-done.2.refs_6_ = bf16[1024,256]{1,0:T(8,128)(2,1)} collective-permute-done((bf16[1024,256]{1,0:T(8,128)(2,1)S(1)}, bf16[1024,256]{1,0:T(8,128)(2,1)}, u32[]{:S(2)}, u32[]{:S(2)}) %collective-permute-start.2) | collective-permute-done | bytes 524320 | tf_op jit(solution)/shard_map/ppermute | solution.py:20
  53.7 5.1 %collective-permute-done.4.refs_3_.refs_4_ = bf16[1024,256]{1,0:T(8,128)(2,1)S(1)} collective-permute-done((bf16[1024,256]{1,0:T(8,128)(2,1)}, bf16[1024,256]{1,0:T(8,128)(2,1)S(1)}, u32[]{:S(2)}, u32[]{:S(2)}) %collective-permute-start.4) | collective-permute-done | bytes 524320 | tf_op jit(solution)/shard_map/ppermute | solution.py:20
  59.4 7.0 %collective-permute-done.3.refs_2_ = bf16[1024,256]{1,0:T(8,128)(2,1)S(1)} collective-permute-done((bf16[1024,256]{1,0:T(8,128)(2,1)S(1)}, bf16[1024,256]{1,0:T(8,128)(2,1)S(1)}, u32[]{:S(2)}, u32[]{:S(2)}) %collective-permute-start.3) | collective-permute-done | bytes 524320 | tf_op jit(solution)/shard_map/ppermute | solution.py:20
  66.5 4.1 %shard_map.38 = (f32[2,2,4,128,256]{4,3,2,1,0:T(8,128)S(1)}, bf16[2,2,4,128,256]{4,3,2,1,0:T(8,128)(2,1)S(1)}) custom-call(s32[9]{0:T(128)S(1)} %pad_add_fusion.1.choices_ref, bf16[2,512,1024]{2,1,0:T(8,128)(2,1)S(1)} %shard_map.37.lefts_ref, bf16[1024,256]{1,0:T(8,128)(2,1)S(1)} %get-tuple-element.52.refs_0_, bf16[1024,256]{1,0:T(8,128)(2,1)S(1)} %copy-done.3, ...), custom_call_target="tpu_custom_call" | custom-call | tf_op jit(solution)/shard_map/pallas_call | solution.py:110
  70.7 2.6 %collective-permute-done.10 = bf16[2,2,4,128,256]{4,3,2,1,0:T(8,128)(2,1)S(1)} collective-permute-done((bf16[2,2,4,128,256]{4,3,2,1,0:T(8,128)(2,1)S(1)}, bf16[2,2,4,128,256]{4,3,2,1,0:T(8,128)(2,1)S(1)}, u32[]{:S(2)}, u32[]{:S(2)}) %collective-permute-start.10) | collective-permute-done | bytes 1048608 | tf_op jit(solution)/shard_map/ppermute | solution.py:20
  77.5 4.6 %collective-permute-done.11 = bf16[1,4,128,256]{3,2,1,0:T(8,128)(2,1)S(1)} collective-permute-done((bf16[1,4,128,256]{3,2,1,0:T(8,128)(2,1)S(1)}, bf16[1,4,128,256]{3,2,1,0:T(8,128)(2,1)S(1)}, u32[]{:S(2)}, u32[]{:S(2)}) %collective-permute-start.11) | collective-permute-done | bytes 262176 | tf_op jit(solution)/shard_map/ppermute | solution.py:20
  85.3 3.6 %collective-permute-done.14.refs_5_ = bf16[1024,256]{1,0:T(8,128)(2,1)S(1)} collective-permute-done((bf16[1024,256]{1,0:T(8,128)(2,1)S(1)}, bf16[1024,256]{1,0:T(8,128)(2,1)S(1)}, u32[]{:S(2)}, u32[]{:S(2)}) %collective-permute-start.14) | collective-permute-done | bytes 524320 | tf_op jit(solution)/shard_map/ppermute | solution.py:20
  89.8 4.3 %collective-permute-done.16.refs_6_ = bf16[1024,256]{1,0:T(8,128)(2,1)S(1)} collective-permute-done((bf16[1024,256]{1,0:T(8,128)(2,1)S(1)}, bf16[1024,256]{1,0:T(8,128)(2,1)S(1)}, u32[]{:S(2)}, u32[]{:S(2)}) %collective-permute-start.16) | collective-permute-done | bytes 524320 | tf_op jit(solution)/shard_map/ppermute | solution.py:20
  94.1 3.5 %collective-permute-done.13 = bf16[4,128,256]{2,1,0:T(8,128)(2,1)S(1)} collective-permute-done((bf16[4,128,256]{2,1,0:T(8,128)(2,1)S(1)}, bf16[4,128,256]{2,1,0:T(8,128)(2,1)S(1)}, u32[]{:S(2)}, u32[]{:S(2)}) %collective-permute-start.13) | collective-permute-done | bytes 262176 | tf_op jit(solution)/shard_map/ppermute | solution.py:20
  97.8 4.0 %collective-permute-done.15.refs_3_ = bf16[1024,256]{1,0:T(8,128)(2,1)S(1)} collective-permute-done((bf16[1024,256]{1,0:T(8,128)(2,1)S(1)}, bf16[1024,256]{1,0:T(8,128)(2,1)S(1)}, u32[]{:S(2)}, u32[]{:S(2)}) %collective-permute-start.15) | collective-permute-done | bytes 524320 | tf_op jit(solution)/shard_map/ppermute | solution.py:20
  101.8 5.8 %collective-permute-done.17.refs_7_ = bf16[1024,256]{1,0:T(8,128)(2,1)S(1)} collective-permute-done((bf16[1024,256]{1,0:T(8,128)(2,1)S(1)}, bf16[1024,256]{1,0:T(8,128)(2,1)S(1)}, u32[]{:S(2)}, u32[]{:S(2)}) %collective-permute-start.17) | collective-permute-done | bytes 524320 | tf_op jit(solution)/shard_map/ppermute | solution.py:20
  107.6 3.2 %shard_map.39 = (f32[2,2,4,128,256]{4,3,2,1,0:T(8,128)S(1)}, bf16[2,2,4,128,256]{4,3,2,1,0:T(8,128)(2,1)S(1)}) custom-call(s32[9]{0:T(128)S(1)} %pad_add_fusion.2.choices_ref, bf16[2,512,1024]{2,1,0:T(8,128)(2,1)S(1)} %shard_map.37.lefts_ref, bf16[1024,256]{1,0:T(8,128)(2,1)S(1)} %multiply_convert_fusion.2.refs_1_.refs_0_, ...), custom_call_target="tpu_custom_call" | custom-call | tf_op jit(solution)/shard_map/pallas_call | solution.py:110
  110.9 2.6 %collective-permute-done.18 = bf16[2,2,4,128,256]{4,3,2,1,0:T(8,128)(2,1)S(1)} collective-permute-done((bf16[2,2,4,128,256]{4,3,2,1,0:T(8,128)(2,1)S(1)}, bf16[2,2,4,128,256]{4,3,2,1,0:T(8,128)(2,1)S(1)}, u32[]{:S(2)}, u32[]{:S(2)}) %collective-permute-start.18) | collective-permute-done | bytes 1048608 | tf_op jit(solution)/shard_map/ppermute | solution.py:20
  114.6 7.8 %collective-permute-done.19 = bf16[1,4,128,256]{3,2,1,0:T(8,128)(2,1)S(1)} collective-permute-done((bf16[1,4,128,256]{3,2,1,0:T(8,128)(2,1)S(1)}, bf16[1,4,128,256]{3,2,1,0:T(8,128)(2,1)S(1)}, u32[]{:S(2)}, u32[]{:S(2)}) %collective-permute-start.19) | collective-permute-done | bytes 262176 | tf_op jit(solution)/shard_map/ppermute | solution.py:20
  124.2 5.9 %collective-permute-done.20 = bf16[1,4,128,256]{3,2,1,0:T(8,128)(2,1)S(1)} collective-permute-done((bf16[1,4,128,256]{3,2,1,0:T(8,128)(2,1)S(1)}, bf16[1,4,128,256]{3,2,1,0:T(8,128)(2,1)S(1)}, u32[]{:S(2)}, u32[]{:S(2)}) %collective-permute-start.20) | collective-permute-done | bytes 262176 | tf_op jit(solution)/shard_map/ppermute | solution.py:20
  130.1 6.7 %collective-permute-done.21 = bf16[4,128,256]{2,1,0:T(8,128)(2,1)S(1)} collective-permute-done((bf16[4,128,256]{2,1,0:T(8,128)(2,1)S(1)}, bf16[4,128,256]{2,1,0:T(8,128)(2,1)S(1)}, u32[]{:S(2)}, u32[]{:S(2)}) %collective-permute-start.21) | collective-permute-done | bytes 262176 | tf_op jit(solution)/shard_map/ppermute | solution.py:20
  (58 shorter events, 21.0 us)
Async XLA Ops:
  0.7 52.9 %copy-start.7 = (s32[4]{0:T(128)S(1)}, s32[4]{0:T(128)}, u32[]{:S(2)}) copy-start(s32[4]{0:T(128)} %param.5) | copy-start | bytes 52
  2.8 15.8 %collective-permute-start.6 = (bf16[1024,256]{1,0:T(8,128)(2,1)S(1)}, bf16[1024,256]{1,0:T(8,128)(2,1)S(1)}, u32[]{:S(2)}, u32[]{:S(2)}) collective-permute-start(bf16[1024,256]{1,0:T(8,128)(2,1)S(1)} %multiply_convert_fusion.2.refs_1_.refs_0_), channel_id=1, source_target_pairs={{0,1},{1,0},{2,3},{3,2},{4,5},{5,4},{6,7},{7,6},{8,9},{9,8},{10,11... | collective-permute-start | bytes 1572872 | tf_op jit(solution)/shard_map/ppermute | solution.py:20
  5.8 24.5 %collective-permute-start.1 = (bf16[1024,256]{1,0:T(8,128)(2,1)S(1)}, bf16[1024,256]{1,0:T(8,128)(2,1)S(1)}, u32[]{:S(2)}, u32[]{:S(2)}) collective-permute-start(bf16[1024,256]{1,0:T(8,128)(2,1)S(1)} %get-tuple-element.52.refs_0_), channel_id=1, source_target_pairs={{0,2},{1,3},{2,0},{3,1},{4,6},{5,7},{6,4},{7,5},{8,10},{9,11},{10,... | collective-permute-start | bytes 1572872 | tf_op jit(solution)/shard_map/ppermute | solution.py:20
  7.4 25.3 %collective-permute-start = (bf16[1024,256]{1,0:T(8,128)(2,1)S(1)}, bf16[1024,256]{1,0:T(8,128)(2,1)S(1)}, u32[]{:S(2)}, u32[]{:S(2)}) collective-permute-start(bf16[1024,256]{1,0:T(8,128)(2,1)S(1)} %get-tuple-element.51), channel_id=1, source_target_pairs={{0,4},{1,5},{2,6},{3,7},{4,0},{5,1},{6,2},{7,3},{8,12},{9,13},{10,... | collective-permute-start | bytes 1572872 | tf_op jit(solution)/shard_map/ppermute | solution.py:20
  10.0 26.8 %collective-permute-start.5 = (bf16[1024,256]{1,0:T(8,128)(2,1)S(1)}, bf16[1024,256]{1,0:T(8,128)(2,1)S(1)}, u32[]{:S(2)}, u32[]{:S(2)}) collective-permute-start(bf16[1024,256]{1,0:T(8,128)(2,1)S(1)} %get-tuple-element.52.refs_0_), channel_id=1, source_target_pairs={{0,1},{1,0},{2,3},{3,2},{4,5},{5,4},{6,7},{7,6},{8,9},{9,8},{10,11... | collective-permute-start | bytes 1572872 | tf_op jit(solution)/shard_map/ppermute | solution.py:20
  30.3 22.6 %copy-start = (bf16[1024,256]{1,0:T(8,128)(2,1)}, bf16[1024,256]{1,0:T(8,128)(2,1)S(1)}, u32[]{:S(2)}) copy-start(bf16[1024,256]{1,0:T(8,128)(2,1)S(1)} %collective-permute-done.1.refs_2_) | copy-start | bytes 1572868
  30.3 14.9 %collective-permute-start.7 = (bf16[1024,256]{1,0:T(8,128)(2,1)S(1)}, bf16[1024,256]{1,0:T(8,128)(2,1)S(1)}, u32[]{:S(2)}, u32[]{:S(2)}) collective-permute-start(bf16[1024,256]{1,0:T(8,128)(2,1)S(1)} %collective-permute-done.1.refs_2_), channel_id=1, source_target_pairs={{0,1},{1,0},{2,3},{3,2},{4,5},{5,4},{6,7},{7,6},{8,9},{9,8},{10,11... | collective-permute-start | bytes 1572872 | tf_op jit(solution)/shard_map/ppermute | solution.py:20
  32.7 20.3 %collective-permute-start.2 = (bf16[1024,256]{1,0:T(8,128)(2,1)S(1)}, bf16[1024,256]{1,0:T(8,128)(2,1)}, u32[]{:S(2)}, u32[]{:S(2)}) collective-permute-start(bf16[1024,256]{1,0:T(8,128)(2,1)S(1)} %collective-permute-done.refs_2_.refs_4_), channel_id=1, source_target_pairs={{0,2},{1,3},{2,0},{3,1},{4,6},{5,7},{6,4},{7,5},{8,10},{9,11},{10,... | collective-permute-start | bytes 1572872 | tf_op jit(solution)/shard_map/ppermute | solution.py:20
  34.1 24.6 %collective-permute-start.4 = (bf16[1024,256]{1,0:T(8,128)(2,1)}, bf16[1024,256]{1,0:T(8,128)(2,1)S(1)}, u32[]{:S(2)}, u32[]{:S(2)}) collective-permute-start(bf16[1024,256]{1,0:T(8,128)(2,1)} %multiply_convert_fusion), channel_id=1, source_target_pairs={{0,4},{1,5},{2,6},{3,7},{4,0},{5,1},{6,2},{7,3},{8,12},{9,13},{10,... | collective-permute-start | bytes 1572872 | tf_op jit(solution)/shard_map/ppermute | solution.py:20
  37.6 28.9 %collective-permute-start.8 = (bf16[1024,256]{1,0:T(8,128)(2,1)S(1)}, bf16[1024,256]{1,0:T(8,128)(2,1)}, u32[]{:S(2)}, u32[]{:S(2)}) collective-permute-start(bf16[1024,256]{1,0:T(8,128)(2,1)S(1)} %collective-permute-done.refs_2_.refs_4_), channel_id=1, source_target_pairs={{0,1},{1,0},{2,3},{3,2},{4,5},{5,4},{6,7},{7,6},{8,9},{9,8},{10,11... | collective-permute-start | bytes 1572872 | tf_op jit(solution)/shard_map/ppermute | solution.py:20
  53.0 13.5 %collective-permute-start.9 = (bf16[1024,256]{1,0:T(8,128)(2,1)}, bf16[1024,256]{1,0:T(8,128)(2,1)}, u32[]{:S(2)}, u32[]{:S(2)}) collective-permute-start(bf16[1024,256]{1,0:T(8,128)(2,1)} %collective-permute-done.2.refs_6_), channel_id=1, source_target_pairs={{0,1},{1,0},{2,3},{3,2},{4,5},{5,4},{6,7},{7,6},{8,9},{9,8},{10,11... | collective-permute-start | bytes 1572872 | tf_op jit(solution)/shard_map/ppermute | solution.py:20
  53.6 12.8 %collective-permute-start.3 = (bf16[1024,256]{1,0:T(8,128)(2,1)S(1)}, bf16[1024,256]{1,0:T(8,128)(2,1)S(1)}, u32[]{:S(2)}, u32[]{:S(2)}) collective-permute-start(bf16[1024,256]{1,0:T(8,128)(2,1)S(1)} %multiply_convert_fusion.2.refs_1_.refs_0_), channel_id=1, source_target_pairs={{0,2},{1,3},{2,0},{3,1},{4,6},{5,7},{6,4},{7,5},{8,10},{9,11},{10,... | collective-permute-start | bytes 1572872 | tf_op jit(solution)/shard_map/ppermute | solution.py:20
  70.6 2.7 %collective-permute-start.10 = (bf16[2,2,4,128,256]{4,3,2,1,0:T(8,128)(2,1)S(1)}, bf16[2,2,4,128,256]{4,3,2,1,0:T(8,128)(2,1)S(1)}, u32[]{:S(2)}, u32[]{:S(2)}) collective-permute-start(bf16[2,2,4,128,256]{4,3,2,1,0:T(8,128)(2,1)S(1)} %get-tuple-element.35), channel_id=1, source_target_pairs={{0,8},{8,0},{16,24},{24,16},{1,9},{9,1},{17,25},{25,17},{2,10},{10... | collective-permute-start | bytes 3145736 | tf_op jit(solution)/shard_map/ppermute | solution.py:20
  73.7 8.4 %collective-permute-start.11 = (bf16[1,4,128,256]{3,2,1,0:T(8,128)(2,1)S(1)}, bf16[1,4,128,256]{3,2,1,0:T(8,128)(2,1)S(1)}, u32[]{:S(2)}, u32[]{:S(2)}) collective-permute-start(bf16[1,4,128,256]{3,2,1,0:T(8,128)(2,1)S(1)} %get-tuple-element.56), channel_id=1, source_target_pairs={{0,16},{8,24},{16,0},{24,8},{1,17},{9,25},{17,1},{25,9},{2,18},{10... | collective-permute-start | bytes 786440 | tf_op jit(solution)/shard_map/ppermute | solution.py:20
  75.3 13.7 %collective-permute-start.14 = (bf16[1024,256]{1,0:T(8,128)(2,1)S(1)}, bf16[1024,256]{1,0:T(8,128)(2,1)S(1)}, u32[]{:S(2)}, u32[]{:S(2)}) collective-permute-start(bf16[1024,256]{1,0:T(8,128)(2,1)S(1)} %collective-permute-done.4.refs_3_.refs_4_), channel_id=1, source_target_pairs={{0,1},{1,0},{2,3},{3,2},{4,5},{5,4},{6,7},{7,6},{8,9},{9,8},{10,11... | collective-permute-start | bytes 1572872 | tf_op jit(solution)/shard_map/ppermute | solution.py:20
  76.1 18.0 %collective-permute-start.16 = (bf16[1024,256]{1,0:T(8,128)(2,1)S(1)}, bf16[1024,256]{1,0:T(8,128)(2,1)S(1)}, u32[]{:S(2)}, u32[]{:S(2)}) collective-permute-start(bf16[1024,256]{1,0:T(8,128)(2,1)S(1)} %collective-permute-done.4.refs_3_.refs_4_), channel_id=1, source_target_pairs={{0,2},{1,3},{2,0},{3,1},{4,6},{5,7},{6,4},{7,5},{8,10},{9,11},{10,... | collective-permute-start | bytes 1572872 | tf_op jit(solution)/shard_map/ppermute | solution.py:20
  82.2 12.0 %collective-permute-start.12 = (bf16[1,4,128,256]{3,2,1,0:T(8,128)(2,1)S(1)}, bf16[1,4,128,256]{3,2,1,0:T(8,128)(2,1)S(1)}, u32[]{:S(2)}, u32[]{:S(2)}) collective-permute-start(bf16[1,4,128,256]{3,2,1,0:T(8,128)(2,1)S(1)} %get-tuple-element.36), channel_id=1, source_target_pairs={{0,16},{8,24},{16,0},{24,8},{1,17},{9,25},{17,1},{25,9},{2,18},{10... | collective-permute-start | bytes 786440 | tf_op jit(solution)/shard_map/ppermute | solution.py:20
  83.8 13.9 %collective-permute-start.13 = (bf16[4,128,256]{2,1,0:T(8,128)(2,1)S(1)}, bf16[4,128,256]{2,1,0:T(8,128)(2,1)S(1)}, u32[]{:S(2)}, u32[]{:S(2)}) collective-permute-start(bf16[4,128,256]{2,1,0:T(8,128)(2,1)S(1)} %fusion.6), channel_id=1, source_target_pairs={{0,4},{1,5},{2,6},{3,7},{4,0},{5,1},{6,2},{7,3},{8,12},{9,13},{10,... | collective-permute-start | bytes 786440 | tf_op jit(solution)/shard_map/ppermute | solution.py:20
  89.0 12.8 %collective-permute-start.15 = (bf16[1024,256]{1,0:T(8,128)(2,1)S(1)}, bf16[1024,256]{1,0:T(8,128)(2,1)S(1)}, u32[]{:S(2)}, u32[]{:S(2)}) collective-permute-start(bf16[1024,256]{1,0:T(8,128)(2,1)S(1)} %collective-permute-done.3.refs_2_), channel_id=1, source_target_pairs={{0,1},{1,0},{2,3},{3,2},{4,5},{5,4},{6,7},{7,6},{8,9},{9,8},{10,11... | collective-permute-start | bytes 1572872 | tf_op jit(solution)/shard_map/ppermute | solution.py:20
  94.1 13.5 %collective-permute-start.17 = (bf16[1024,256]{1,0:T(8,128)(2,1)S(1)}, bf16[1024,256]{1,0:T(8,128)(2,1)S(1)}, u32[]{:S(2)}, u32[]{:S(2)}) collective-permute-start(bf16[1024,256]{1,0:T(8,128)(2,1)S(1)} %collective-permute-done.14.refs_5_), channel_id=1, source_target_pairs={{0,2},{1,3},{2,0},{3,1},{4,6},{5,7},{6,4},{7,5},{8,10},{9,11},{10,... | collective-permute-start | bytes 1572872 | tf_op jit(solution)/shard_map/ppermute | solution.py:20
  110.9 2.7 %collective-permute-start.18 = (bf16[2,2,4,128,256]{4,3,2,1,0:T(8,128)(2,1)S(1)}, bf16[2,2,4,128,256]{4,3,2,1,0:T(8,128)(2,1)S(1)}, u32[]{:S(2)}, u32[]{:S(2)}) collective-permute-start(bf16[2,2,4,128,256]{4,3,2,1,0:T(8,128)(2,1)S(1)} %get-tuple-element.43), channel_id=1, source_target_pairs={{0,8},{8,0},{16,24},{24,16},{1,9},{9,1},{17,25},{25,17},{2,10},{10... | collective-permute-start | bytes 3145736 | tf_op jit(solution)/shard_map/ppermute | solution.py:20
  114.0 8.4 %collective-permute-start.19 = (bf16[1,4,128,256]{3,2,1,0:T(8,128)(2,1)S(1)}, bf16[1,4,128,256]{3,2,1,0:T(8,128)(2,1)S(1)}, u32[]{:S(2)}, u32[]{:S(2)}) collective-permute-start(bf16[1,4,128,256]{3,2,1,0:T(8,128)(2,1)S(1)} %get-tuple-element.54), channel_id=1, source_target_pairs={{0,16},{8,24},{16,0},{24,8},{1,17},{9,25},{17,1},{25,9},{2,18},{10... | collective-permute-start | bytes 786440 | tf_op jit(solution)/shard_map/ppermute | solution.py:20
  122.5 7.6 %collective-permute-start.20 = (bf16[1,4,128,256]{3,2,1,0:T(8,128)(2,1)S(1)}, bf16[1,4,128,256]{3,2,1,0:T(8,128)(2,1)S(1)}, u32[]{:S(2)}, u32[]{:S(2)}) collective-permute-start(bf16[1,4,128,256]{3,2,1,0:T(8,128)(2,1)S(1)} %get-tuple-element.44), channel_id=1, source_target_pairs={{0,16},{8,24},{16,0},{24,8},{1,17},{9,25},{17,1},{25,9},{2,18},{10... | collective-permute-start | bytes 786440 | tf_op jit(solution)/shard_map/ppermute | solution.py:20
  123.1 13.8 %collective-permute-start.21 = (bf16[4,128,256]{2,1,0:T(8,128)(2,1)S(1)}, bf16[4,128,256]{2,1,0:T(8,128)(2,1)S(1)}, u32[]{:S(2)}, u32[]{:S(2)}) collective-permute-start(bf16[4,128,256]{2,1,0:T(8,128)(2,1)S(1)} %fusion.1), channel_id=1, source_target_pairs={{0,4},{1,5},{2,6},{3,7},{4,0},{5,1},{6,2},{7,3},{8,12},{9,13},{10,... | collective-permute-start | bytes 786440 | tf_op jit(solution)/shard_map/ppermute | solution.py:20
  (6 other events, 41.9 us)

commit v13 on v12

--- a/solution.py
+++ b/solution.py
@@ -73,7 +73,7 @@
     )(*own, *mate)
 
 
-def products(choices, lefts, batch, scale_factor):
+def products(choices, lefts, batch, scale_factor, side):
     slab_count = lax.axis_size("space")
     group, cells = lefts.shape[1:]
     width = sum(blocks[0].shape[1] for blocks in batch[0])
@@ -83,30 +83,33 @@
     def kernel(choices_ref, lefts_ref, *refs):
         waiting = list(refs[: len(arrays)])
         even_ref, odd_ref, tiles = refs[len(arrays) :]
-        for mates, pieces in enumerate(batch):
-            sources = [[waiting.pop(0) for _ in blocks] for blocks in pieces]
-            for round_number in range(ROUNDS):
-                parts = []
-                for block_refs in sources:
-                    part = block_refs[0][...]
-                    for number, block_ref in enumerate(block_refs[1:], 1):
-                        wanted = choices_ref[round_number] == number
-                        part = jnp.where(wanted, block_ref[...], part)
-                    parts.append(part)
-                right = jnp.concatenate(parts, axis=1) if len(parts) > 1 else parts[0]
-                side = choices_ref[ROUNDS + round_number]
-                side = 1 - side if mates else side
-                tile = tiles.at[round_number % 2]
-                tile[...] = scale_factor * jnp.dot(
-                    lefts_ref[side], right, preferred_element_type=jnp.float32
-                )
-                for number in range(slab_count):
-                    start = jnp.bitwise_xor(choices_ref[2 * ROUNDS], number) * rows
-                    part = tile[pl.ds(pl.multiple_of(start, rows), rows), :]
-                    out_ref = odd_ref if number % 2 else even_ref
-                    out_ref[side, number // 2, round_number] = part.astype(out_ref.dtype)
-
-    shape = (2, slab_count // 2, ROUNDS, rows, width)
+        sources = [[[waiting.pop(0) for _ in blocks] for blocks in pieces] for pieces in batch]
+
+        def picked(pieces, round_number):
+            parts = []
+            for block_refs in pieces:
+                part = block_refs[0][...]
+                for number, block_ref in enumerate(block_refs[1:], 1):
+                    wanted = choices_ref[round_number] == number
+                    part = jnp.where(wanted, block_ref[...], part)
+                parts.append(part)
+            return jnp.concatenate(parts, axis=1) if len(parts) > 1 else parts[0]
+
+        for round_number in range(ROUNDS):
+            of_own = choices_ref[ROUNDS + round_number] == side
+            own, mate = (picked(pieces, round_number) for pieces in sources)
+            right = jnp.where(of_own, own, mate)
+            tile = tiles.at[round_number % 2]
+            tile[...] = scale_factor * jnp.dot(
+                lefts_ref[side], right, preferred_element_type=jnp.float32
+            )
+            for number in range(slab_count):
+                start = jnp.bitwise_xor(choices_ref[2 * ROUNDS], number) * rows
+                part = tile[pl.ds(pl.multiple_of(start, rows), rows), :]
+                out_ref = odd_ref if number % 2 else even_ref
+                out_ref[number // 2, round_number] = part.astype(out_ref.dtype)
+
+    shape = (slab_count // 2, ROUNDS, rows, width)
     return pl.pallas_call(
         kernel,
         out_shape=[jax.ShapeDtypeStruct(shape, kind) for kind in (jnp.float32, jnp.bfloat16)],
@@ -179,20 +182,19 @@
     sent = {}
     halves, columns, back = [], [], []
 
-    def add_batch(rounds):
+    def add_batch():
         batch = [
             [[held[n][low] for low in range(cut)] for n in numbers]
             for numbers in BATCHES[len(halves)]
         ]
         earlier = columns if halves else sent[cut // 2][:3][-1]
-        rounds = behind(rounds, earlier)
-        even, odd = products(jnp.concatenate([rounds, me]), lefts, batch, scale_factor)
-        total = even + exchange(odd, "space", 1).astype(jnp.float32)
-        halves.append(total)
-        give = summed(total[1], None)
+        choices = jnp.concatenate([behind(rounds, earlier), me])
+        even, odd = products(choices, lefts, batch, scale_factor, 1)
+        halves.append(halved(even, odd, 1))
+        give = summed(halves[-1], None)
         back.append(exchange(give.astype(jnp.bfloat16), "snap", cut))
-        columns.append(summed(total[0], give))
-        return rounds
+        even, odd = products(behind(choices, odd), lefts, batch, scale_factor, 0)
+        columns.append(summed(halved(even, odd, 1), give))
 
     for piece, low, bit in hops_in_order(OWN_WIDTHS + MATE_WIDTHS, cut):
         earlier = sent.setdefault(bit, [])
@@ -203,7 +205,7 @@
         while len(halves) < len(BATCHES) and all(
             len(held[n]) == cut for numbers in BATCHES[len(halves)] for n in numbers
         ):
-            rounds = add_batch(rounds)
+            add_batch()
     results = [kept + got.astype(jnp.float32) for kept, got in zip(columns, back)]
     return jnp.concatenate(results, axis=2)[:, None]
 

time: 138 us -> 135 us (0.978)
  waiting for transfers between devices: 99.7 us -> 82 us
  starting transfers between devices: 22.4 us -> 34.1 us
  Pallas kernels: 7.94 us -> 10.9 us
    ppermute x22 -> x24, waiting for transfers between devices: 99.7 us -> 82 us  [exchange(): lax.ppermute(part, axis, [(i, i ^ mask) for i in range(lax.axis_size(axis...]
    ppermute x22 -> x24, starting transfers between devices: 22.4 us -> 34.1 us  [exchange(): lax.ppermute(part, axis, [(i, i ^ mask) for i in range(lax.axis_size(axis...]
    pallas_call x2 -> x4, Pallas kernels: 7.31 us -> 10.3 us  [products(): pl.pallas_call(kernel, out_shape=[jax.ShapeDtypeStruct(shape, kind) for k...]
  transfers between devices with their start and end apart: 22 -> 24, of which waited for: 18 -> 13; matrix products, arithmetic and copies ran while one was open for 1% -> 2% of each run, Pallas kernels for 0% -> 4%
where the time goes in v13:
time: 135 us
  waiting for transfers between devices  82 us (61%)
  starting transfers between devices  34.1 us (25%)
  Pallas kernels  10.9 us (8%)
  other arithmetic  5 us (4%)
  local copies, waits for them, and re-layouts  2.43 us (2%)
    ppermute x24, waiting for transfers between devices, exchange(): lax.ppermute(part, axis, [(i, i ^ mask) for i in range(lax.axis_size(axis...  82 us
    ppermute x24, starting transfers between devices, exchange(): lax.ppermute(part, axis, [(i, i ^ mask) for i in range(lax.axis_size(axis...  34.1 us
    pallas_call x4, Pallas kernels, products(): pl.pallas_call(kernel, out_shape=[jax.ShapeDtypeStruct(shape, kind) for k...  10.3 us
    convert_element_type x3, other arithmetic, pieces_of(): found.append((part.astype(jnp.float32) * scale).astype(jnp.bfloat16))  2.89 us
  transfers between devices with their start and end apart: 24, of which 13 were waited for; matrix products, arithmetic and copies ran while one was open for 2% of the time, Pallas kernels for 4%

profile of v13, /device:TPU:0, one launch (start us, length us, event | category | flops | bytes accessed | tf_op | source)
XLA Modules:
  0.0 134.6 jit_solution(14039057959045512548)
XLA Ops:
  0.7 1.7 %multiply_convert_fusion.1 = (bf16[1024,256]{1,0:T(8,128)(2,1)S(1)}, bf16[1024,256]{1,0:T(8,128)(2,1)S(1)}) fusion(f32[1024]{0:T(1024)S(1)} %get-tuple-element.61, bf16[2048,512]{1,0:T(8,128)(2,1)} %param.3, s32[]{:T(128)S(6)} %select_n.2, f32[1024]{0:T(1024)S(1)} %get-tuple-element.62, s32[]{:T(128)S(6)} %mul.16), kind=kLoop, calls=%fused_computation.6 | loop fusion | flops 1572864 | bytes 2105352 | tf_op jit(solution)/shard_map/convert_element_type | solution.py:158
  2.4 4.1 %collective-permute-start = (bf16[1024,256]{1,0:T(8,128)(2,1)S(1)}, bf16[1024,256]{1,0:T(8,128)(2,1)S(1)}, u32[]{:S(2)}, u32[]{:S(2)}) collective-permute-start(bf16[1024,256]{1,0:T(8,128)(2,1)S(1)} %get-tuple-element.59), channel_id=1, source_target_pairs={{0,4},{1,5},{2,6},{3,7},{4,0},{5,1},{6,2},{7,3},{8,12},{9,13},{10,... | collective-permute-start | bytes 1572872 | tf_op jit(solution)/shard_map/ppermute | solution.py:20
  6.5 1.6 %collective-permute-start.1 = (bf16[1024,256]{1,0:T(8,128)(2,1)S(1)}, bf16[1024,256]{1,0:T(8,128)(2,1)S(1)}, u32[]{:S(2)}, u32[]{:S(2)}) collective-permute-start(bf16[1024,256]{1,0:T(8,128)(2,1)S(1)} %get-tuple-element.60.refs_0_), channel_id=1, source_target_pairs={{0,2},{1,3},{2,0},{3,1},{4,6},{5,7},{6,4},{7,5},{8,10},{9,11},{10,... | collective-permute-start | bytes 1572872 | tf_op jit(solution)/shard_map/ppermute | solution.py:20
  10.4 19.4 %collective-permute-done.refs_2_.refs_4_ = bf16[1024,256]{1,0:T(8,128)(2,1)S(1)} collective-permute-done((bf16[1024,256]{1,0:T(8,128)(2,1)S(1)}, bf16[1024,256]{1,0:T(8,128)(2,1)S(1)}, u32[]{:S(2)}, u32[]{:S(2)}) %collective-permute-start) | collective-permute-done | bytes 524320 | tf_op jit(solution)/shard_map/ppermute | solution.py:20
  34.0 2.3 %collective-permute-start.4 = (bf16[1024,256]{1,0:T(8,128)(2,1)}, bf16[1024,256]{1,0:T(8,128)(2,1)S(1)}, u32[]{:S(2)}, u32[]{:S(2)}) collective-permute-start(bf16[1024,256]{1,0:T(8,128)(2,1)} %multiply_convert_fusion), channel_id=1, source_target_pairs={{0,4},{1,5},{2,6},{3,7},{4,0},{5,1},{6,2},{7,3},{8,12},{9,13},{10,... | collective-permute-start | bytes 1572872 | tf_op jit(solution)/shard_map/ppermute | solution.py:20
  37.6 13.9 %collective-permute-done.2.refs_6_ = bf16[1024,256]{1,0:T(8,128)(2,1)} collective-permute-done((bf16[1024,256]{1,0:T(8,128)(2,1)S(1)}, bf16[1024,256]{1,0:T(8,128)(2,1)}, u32[]{:S(2)}, u32[]{:S(2)}) %collective-permute-start.2) | collective-permute-done | bytes 524320 | tf_op jit(solution)/shard_map/ppermute | solution.py:20
  52.3 2.2 %collective-permute-start.9 = (bf16[1024,256]{1,0:T(8,128)(2,1)}, bf16[1024,256]{1,0:T(8,128)(2,1)}, u32[]{:S(2)}, u32[]{:S(2)}) collective-permute-start(bf16[1024,256]{1,0:T(8,128)(2,1)} %collective-permute-done.2.refs_6_), channel_id=1, source_target_pairs={{0,1},{1,0},{2,3},{3,2},{4,5},{5,4},{6,7},{7,6},{8,9},{9,8},{10,11... | collective-permute-start | bytes 1572872 | tf_op jit(solution)/shard_map/ppermute | solution.py:20
  54.6 4.8 %collective-permute-done.4.refs_3_.refs_4_ = bf16[1024,256]{1,0:T(8,128)(2,1)S(1)} collective-permute-done((bf16[1024,256]{1,0:T(8,128)(2,1)}, bf16[1024,256]{1,0:T(8,128)(2,1)S(1)}, u32[]{:S(2)}, u32[]{:S(2)}) %collective-permute-start.4) | collective-permute-done | bytes 524320 | tf_op jit(solution)/shard_map/ppermute | solution.py:20
  60.1 6.1 %collective-permute-done.3.refs_2_ = bf16[1024,256]{1,0:T(8,128)(2,1)S(1)} collective-permute-done((bf16[1024,256]{1,0:T(8,128)(2,1)S(1)}, bf16[1024,256]{1,0:T(8,128)(2,1)S(1)}, u32[]{:S(2)}, u32[]{:S(2)}) %collective-permute-start.3) | collective-permute-done | bytes 524320 | tf_op jit(solution)/shard_map/ppermute | solution.py:20
  66.6 3.0 %shard_map.38 = (f32[2,4,128,256]{3,2,1,0:T(8,128)S(1)}, bf16[2,4,128,256]{3,2,1,0:T(8,128)(2,1)S(1)}) custom-call(s32[9]{0:T(128)S(1)} %pad_add_fusion.1.choices_ref, bf16[2,512,1024]{2,1,0:T(8,128)(2,1)S(1)} %shard_map.37.lefts_ref, bf16[1024,256]{1,0:T(8,128)(2,1)S(1)} %get-tuple-element.60.refs_0_, bf16[1024,256]{1,0:T(8,128)(2,1)S(1)} %copy-done.3, ...), custom_call_target="tpu_custom_call" | custom-call | tf_op jit(solution)/shard_map/pallas_call | solution.py:113
  69.6 3.0 %shard_map.39 = (f32[2,4,128,256]{3,2,1,0:T(8,128)S(1)}, bf16[2,4,128,256]{3,2,1,0:T(8,128)(2,1)S(1)}) custom-call(s32[9]{0:T(128)S(1)} %pad_add_fusion.1.choices_ref, bf16[2,512,1024]{2,1,0:T(8,128)(2,1)S(1)} %shard_map.37.lefts_ref, bf16[1024,256]{1,0:T(8,128)(2,1)S(1)} %get-tuple-element.60.refs_0_, bf16[1024,256]{1,0:T(8,128)(2,1)S(1)} %copy-done.3, ...), custom_call_target="tpu_custom_call" | custom-call | tf_op jit(solution)/shard_map/pallas_call | solution.py:113
  75.3 1.6 %collective-permute-start.12 = (bf16[1,4,128,256]{3,2,1,0:T(8,128)(2,1)S(1)}, bf16[1,4,128,256]{3,2,1,0:T(8,128)(2,1)S(1)}, u32[]{:S(2)}, u32[]{:S(2)}) collective-permute-start(bf16[1,4,128,256]{3,2,1,0:T(8,128)(2,1)S(1)} %slice.72), channel_id=1, source_target_pairs={{0,16},{8,24},{16,0},{24,8},{1,17},{9,25},{17,1},{25,9},{2,18},{10... | collective-permute-start | bytes 786440 | tf_op jit(solution)/shard_map/ppermute | solution.py:20
  77.0 6.0 %collective-permute-done.12 = bf16[1,4,128,256]{3,2,1,0:T(8,128)(2,1)S(1)} collective-permute-done((bf16[1,4,128,256]{3,2,1,0:T(8,128)(2,1)S(1)}, bf16[1,4,128,256]{3,2,1,0:T(8,128)(2,1)S(1)}, u32[]{:S(2)}, u32[]{:S(2)}) %collective-permute-start.12) | collective-permute-done | bytes 262176 | tf_op jit(solution)/shard_map/ppermute | solution.py:20
  83.1 4.5 %collective-permute-start.14 = (bf16[4,128,256]{2,1,0:T(8,128)(2,1)S(1)}, bf16[4,128,256]{2,1,0:T(8,128)(2,1)S(1)}, u32[]{:S(2)}, u32[]{:S(2)}) collective-permute-start(bf16[4,128,256]{2,1,0:T(8,128)(2,1)S(1)} %fusion.3), channel_id=1, source_target_pairs={{0,4},{1,5},{2,6},{3,7},{4,0},{5,1},{6,2},{7,3},{8,12},{9,13},{10,... | collective-permute-start | bytes 786440 | tf_op jit(solution)/shard_map/ppermute | solution.py:20
  90.1 3.2 %collective-permute-done.17.refs_6_ = bf16[1024,256]{1,0:T(8,128)(2,1)S(1)} collective-permute-done((bf16[1024,256]{1,0:T(8,128)(2,1)S(1)}, bf16[1024,256]{1,0:T(8,128)(2,1)S(1)}, u32[]{:S(2)}, u32[]{:S(2)}) %collective-permute-start.17) | collective-permute-done | bytes 524320 | tf_op jit(solution)/shard_map/ppermute | solution.py:20
  93.3 5.1 %collective-permute-done.14 = bf16[4,128,256]{2,1,0:T(8,128)(2,1)S(1)} collective-permute-done((bf16[4,128,256]{2,1,0:T(8,128)(2,1)S(1)}, bf16[4,128,256]{2,1,0:T(8,128)(2,1)S(1)}, u32[]{:S(2)}, u32[]{:S(2)}) %collective-permute-start.14) | collective-permute-done | bytes 262176 | tf_op jit(solution)/shard_map/ppermute | solution.py:20
  98.6 2.4 %collective-permute-done.16.refs_3_ = bf16[1024,256]{1,0:T(8,128)(2,1)S(1)} collective-permute-done((bf16[1024,256]{1,0:T(8,128)(2,1)S(1)}, bf16[1024,256]{1,0:T(8,128)(2,1)S(1)}, u32[]{:S(2)}, u32[]{:S(2)}) %collective-permute-start.16) | collective-permute-done | bytes 524320 | tf_op jit(solution)/shard_map/ppermute | solution.py:20
  101.0 4.2 %collective-permute-done.18.refs_7_ = bf16[1024,256]{1,0:T(8,128)(2,1)S(1)} collective-permute-done((bf16[1024,256]{1,0:T(8,128)(2,1)S(1)}, bf16[1024,256]{1,0:T(8,128)(2,1)S(1)}, u32[]{:S(2)}, u32[]{:S(2)}) %collective-permute-start.18) | collective-permute-done | bytes 524320 | tf_op jit(solution)/shard_map/ppermute | solution.py:20
  105.2 2.1 %shard_map.40 = (f32[2,4,128,256]{3,2,1,0:T(8,128)S(1)}, bf16[2,4,128,256]{3,2,1,0:T(8,128)(2,1)S(1)}) custom-call(s32[9]{0:T(128)S(1)} %pad_add_fusion.2.choices_ref, bf16[2,512,1024]{2,1,0:T(8,128)(2,1)S(1)} %shard_map.37.lefts_ref, bf16[1024,256]{1,0:T(8,128)(2,1)S(1)} %multiply_convert_fusion.2.refs_1_.refs_0_, ...), custom_call_target="tpu_custom_call" | custom-call | tf_op jit(solution)/shard_map/pallas_call | solution.py:113
  107.4 2.1 %shard_map.41 = (f32[2,4,128,256]{3,2,1,0:T(8,128)S(1)}, bf16[2,4,128,256]{3,2,1,0:T(8,128)(2,1)S(1)}) custom-call(s32[9]{0:T(128)S(1)} %pad_add_fusion.2.choices_ref, bf16[2,512,1024]{2,1,0:T(8,128)(2,1)S(1)} %shard_map.37.lefts_ref, bf16[1024,256]{1,0:T(8,128)(2,1)S(1)} %multiply_convert_fusion.2.refs_1_.refs_0_, ...), custom_call_target="tpu_custom_call" | custom-call | tf_op jit(solution)/shard_map/pallas_call | solution.py:113
  110.3 1.6 %collective-permute-start.21 = (bf16[1,4,128,256]{3,2,1,0:T(8,128)(2,1)S(1)}, bf16[1,4,128,256]{3,2,1,0:T(8,128)(2,1)S(1)}, u32[]{:S(2)}, u32[]{:S(2)}) collective-permute-start(bf16[1,4,128,256]{3,2,1,0:T(8,128)(2,1)S(1)} %slice.70), channel_id=1, source_target_pairs={{0,16},{8,24},{16,0},{24,8},{1,17},{9,25},{17,1},{25,9},{2,18},{10... | collective-permute-start | bytes 786440 | tf_op jit(solution)/shard_map/ppermute | solution.py:20
  112.0 6.6 %collective-permute-done.21 = bf16[1,4,128,256]{3,2,1,0:T(8,128)(2,1)S(1)} collective-permute-done((bf16[1,4,128,256]{3,2,1,0:T(8,128)(2,1)S(1)}, bf16[1,4,128,256]{3,2,1,0:T(8,128)(2,1)S(1)}, u32[]{:S(2)}, u32[]{:S(2)}) %collective-permute-start.21) | collective-permute-done | bytes 262176 | tf_op jit(solution)/shard_map/ppermute | solution.py:20
  118.7 3.5 %collective-permute-start.23 = (bf16[4,128,256]{2,1,0:T(8,128)(2,1)S(1)}, bf16[4,128,256]{2,1,0:T(8,128)(2,1)S(1)}, u32[]{:S(2)}, u32[]{:S(2)}) collective-permute-start(bf16[4,128,256]{2,1,0:T(8,128)(2,1)S(1)} %fusion), channel_id=1, source_target_pairs={{0,4},{1,5},{2,6},{3,7},{4,0},{5,1},{6,2},{7,3},{8,12},{9,13},{10,... | collective-permute-start | bytes 786440 | tf_op jit(solution)/shard_map/ppermute | solution.py:20
  123.7 9.7 %collective-permute-done.23 = bf16[4,128,256]{2,1,0:T(8,128)(2,1)S(1)} collective-permute-done((bf16[4,128,256]{2,1,0:T(8,128)(2,1)S(1)}, bf16[4,128,256]{2,1,0:T(8,128)(2,1)S(1)}, u32[]{:S(2)}, u32[]{:S(2)}) %collective-permute-start.23) | collective-permute-done | bytes 262176 | tf_op jit(solution)/shard_map/ppermute | solution.py:20
  (68 shorter events, 19.8 us)
Async XLA Ops:
  2.4 27.4 %collective-permute-start = (bf16[1024,256]{1,0:T(8,128)(2,1)S(1)}, bf16[1024,256]{1,0:T(8,128)(2,1)S(1)}, u32[]{:S(2)}, u32[]{:S(2)}) collective-permute-start(bf16[1024,256]{1,0:T(8,128)(2,1)S(1)} %get-tuple-element.59), channel_id=1, source_target_pairs={{0,4},{1,5},{2,6},{3,7},{4,0},{5,1},{6,2},{7,3},{8,12},{9,13},{10,... | collective-permute-start | bytes 1572872 | tf_op jit(solution)/shard_map/ppermute | solution.py:20
  6.5 23.5 %collective-permute-start.1 = (bf16[1024,256]{1,0:T(8,128)(2,1)S(1)}, bf16[1024,256]{1,0:T(8,128)(2,1)S(1)}, u32[]{:S(2)}, u32[]{:S(2)}) collective-permute-start(bf16[1024,256]{1,0:T(8,128)(2,1)S(1)} %get-tuple-element.60.refs_0_), channel_id=1, source_target_pairs={{0,2},{1,3},{2,0},{3,1},{4,6},{5,7},{6,4},{7,5},{8,10},{9,11},{10,... | collective-permute-start | bytes 1572872 | tf_op jit(solution)/shard_map/ppermute | solution.py:20
  8.3 23.2 %collective-permute-start.6 = (bf16[1024,256]{1,0:T(8,128)(2,1)S(1)}, bf16[1024,256]{1,0:T(8,128)(2,1)S(1)}, u32[]{:S(2)}, u32[]{:S(2)}) collective-permute-start(bf16[1024,256]{1,0:T(8,128)(2,1)S(1)} %multiply_convert_fusion.2.refs_1_.refs_0_), channel_id=1, source_target_pairs={{0,1},{1,0},{2,3},{3,2},{4,5},{5,4},{6,7},{7,6},{8,9},{9,8},{10,11... | collective-permute-start | bytes 1572872 | tf_op jit(solution)/shard_map/ppermute | solution.py:20
  9.9 26.4 %collective-permute-start.5 = (bf16[1024,256]{1,0:T(8,128)(2,1)S(1)}, bf16[1024,256]{1,0:T(8,128)(2,1)S(1)}, u32[]{:S(2)}, u32[]{:S(2)}) collective-permute-start(bf16[1024,256]{1,0:T(8,128)(2,1)S(1)} %get-tuple-element.60.refs_0_), channel_id=1, source_target_pairs={{0,1},{1,0},{2,3},{3,2},{4,5},{5,4},{6,7},{7,6},{8,9},{9,8},{10,11... | collective-permute-start | bytes 1572872 | tf_op jit(solution)/shard_map/ppermute | solution.py:20
  30.0 21.6 %collective-permute-start.2 = (bf16[1024,256]{1,0:T(8,128)(2,1)S(1)}, bf16[1024,256]{1,0:T(8,128)(2,1)}, u32[]{:S(2)}, u32[]{:S(2)}) collective-permute-start(bf16[1024,256]{1,0:T(8,128)(2,1)S(1)} %collective-permute-done.refs_2_.refs_4_), channel_id=1, source_target_pairs={{0,2},{1,3},{2,0},{3,1},{4,6},{5,7},{6,4},{7,5},{8,10},{9,11},{10,... | collective-permute-start | bytes 1572872 | tf_op jit(solution)/shard_map/ppermute | solution.py:20
  31.5 20.1 %collective-permute-start.7 = (bf16[1024,256]{1,0:T(8,128)(2,1)S(1)}, bf16[1024,256]{1,0:T(8,128)(2,1)S(1)}, u32[]{:S(2)}, u32[]{:S(2)}) collective-permute-start(bf16[1024,256]{1,0:T(8,128)(2,1)S(1)} %collective-permute-done.1.refs_2_), channel_id=1, source_target_pairs={{0,1},{1,0},{2,3},{3,2},{4,5},{5,4},{6,7},{7,6},{8,9},{9,8},{10,11... | collective-permute-start | bytes 1572872 | tf_op jit(solution)/shard_map/ppermute | solution.py:20
  34.0 25.5 %collective-permute-start.4 = (bf16[1024,256]{1,0:T(8,128)(2,1)}, bf16[1024,256]{1,0:T(8,128)(2,1)S(1)}, u32[]{:S(2)}, u32[]{:S(2)}) collective-permute-start(bf16[1024,256]{1,0:T(8,128)(2,1)} %multiply_convert_fusion), channel_id=1, source_target_pairs={{0,4},{1,5},{2,6},{3,7},{4,0},{5,1},{6,2},{7,3},{8,12},{9,13},{10,... | collective-permute-start | bytes 1572872 | tf_op jit(solution)/shard_map/ppermute | solution.py:20
  37.1 29.1 %collective-permute-start.8 = (bf16[1024,256]{1,0:T(8,128)(2,1)S(1)}, bf16[1024,256]{1,0:T(8,128)(2,1)}, u32[]{:S(2)}, u32[]{:S(2)}) collective-permute-start(bf16[1024,256]{1,0:T(8,128)(2,1)S(1)} %collective-permute-done.refs_2_.refs_4_), channel_id=1, source_target_pairs={{0,1},{1,0},{2,3},{3,2},{4,5},{5,4},{6,7},{7,6},{8,9},{9,8},{10,11... | collective-permute-start | bytes 1572872 | tf_op jit(solution)/shard_map/ppermute | solution.py:20
  51.5 14.6 %collective-permute-start.3 = (bf16[1024,256]{1,0:T(8,128)(2,1)S(1)}, bf16[1024,256]{1,0:T(8,128)(2,1)S(1)}, u32[]{:S(2)}, u32[]{:S(2)}) collective-permute-start(bf16[1024,256]{1,0:T(8,128)(2,1)S(1)} %multiply_convert_fusion.2.refs_1_.refs_0_), channel_id=1, source_target_pairs={{0,2},{1,3},{2,0},{3,1},{4,6},{5,7},{6,4},{7,5},{8,10},{9,11},{10,... | collective-permute-start | bytes 1572872 | tf_op jit(solution)/shard_map/ppermute | solution.py:20
  52.3 14.2 %collective-permute-start.9 = (bf16[1024,256]{1,0:T(8,128)(2,1)}, bf16[1024,256]{1,0:T(8,128)(2,1)}, u32[]{:S(2)}, u32[]{:S(2)}) collective-permute-start(bf16[1024,256]{1,0:T(8,128)(2,1)} %collective-permute-done.2.refs_6_), channel_id=1, source_target_pairs={{0,1},{1,0},{2,3},{3,2},{4,5},{5,4},{6,7},{7,6},{8,9},{9,8},{10,11... | collective-permute-start | bytes 1572872 | tf_op jit(solution)/shard_map/ppermute | solution.py:20
  69.6 5.5 %collective-permute-start.11 = (bf16[2,4,128,256]{3,2,1,0:T(8,128)(2,1)S(1)}, bf16[2,4,128,256]{3,2,1,0:T(8,128)(2,1)S(1)}, u32[]{:S(2)}, u32[]{:S(2)}) collective-permute-start(bf16[2,4,128,256]{3,2,1,0:T(8,128)(2,1)S(1)} %get-tuple-element.40), channel_id=1, source_target_pairs={{0,8},{8,0},{16,24},{24,16},{1,9},{9,1},{17,25},{25,17},{2,10},{10... | collective-permute-start | bytes 1572872 | tf_op jit(solution)/shard_map/ppermute | solution.py:20
  72.6 4.2 %collective-permute-start.10 = (bf16[2,4,128,256]{3,2,1,0:T(8,128)(2,1)S(1)}, bf16[2,4,128,256]{3,2,1,0:T(8,128)(2,1)S(1)}, u32[]{:S(2)}, u32[]{:S(2)}) collective-permute-start(bf16[2,4,128,256]{3,2,1,0:T(8,128)(2,1)S(1)} %get-tuple-element.43), channel_id=1, source_target_pairs={{0,8},{8,0},{16,24},{24,16},{1,9},{9,1},{17,25},{25,17},{2,10},{10... | collective-permute-start | bytes 1572872 | tf_op jit(solution)/shard_map/ppermute | solution.py:20
  73.2 15.9 %collective-permute-start.15 = (bf16[1024,256]{1,0:T(8,128)(2,1)S(1)}, bf16[1024,256]{1,0:T(8,128)(2,1)S(1)}, u32[]{:S(2)}, u32[]{:S(2)}) collective-permute-start(bf16[1024,256]{1,0:T(8,128)(2,1)S(1)} %collective-permute-done.4.refs_3_.refs_4_), channel_id=1, source_target_pairs={{0,1},{1,0},{2,3},{3,2},{4,5},{5,4},{6,7},{7,6},{8,9},{9,8},{10,11... | collective-permute-start | bytes 1572872 | tf_op jit(solution)/shard_map/ppermute | solution.py:20
  74.7 18.7 %collective-permute-start.17 = (bf16[1024,256]{1,0:T(8,128)(2,1)S(1)}, bf16[1024,256]{1,0:T(8,128)(2,1)S(1)}, u32[]{:S(2)}, u32[]{:S(2)}) collective-permute-start(bf16[1024,256]{1,0:T(8,128)(2,1)S(1)} %collective-permute-done.4.refs_3_.refs_4_), channel_id=1, source_target_pairs={{0,2},{1,3},{2,0},{3,1},{4,6},{5,7},{6,4},{7,5},{8,10},{9,11},{10,... | collective-permute-start | bytes 1572872 | tf_op jit(solution)/shard_map/ppermute | solution.py:20
  75.3 7.8 %collective-permute-start.12 = (bf16[1,4,128,256]{3,2,1,0:T(8,128)(2,1)S(1)}, bf16[1,4,128,256]{3,2,1,0:T(8,128)(2,1)S(1)}, u32[]{:S(2)}, u32[]{:S(2)}) collective-permute-start(bf16[1,4,128,256]{3,2,1,0:T(8,128)(2,1)S(1)} %slice.72), channel_id=1, source_target_pairs={{0,16},{8,24},{16,0},{24,8},{1,17},{9,25},{17,1},{25,9},{2,18},{10... | collective-permute-start | bytes 786440 | tf_op jit(solution)/shard_map/ppermute | solution.py:20
  83.1 15.3 %collective-permute-start.14 = (bf16[4,128,256]{2,1,0:T(8,128)(2,1)S(1)}, bf16[4,128,256]{2,1,0:T(8,128)(2,1)S(1)}, u32[]{:S(2)}, u32[]{:S(2)}) collective-permute-start(bf16[4,128,256]{2,1,0:T(8,128)(2,1)S(1)} %fusion.3), channel_id=1, source_target_pairs={{0,4},{1,5},{2,6},{3,7},{4,0},{5,1},{6,2},{7,3},{8,12},{9,13},{10,... | collective-permute-start | bytes 786440 | tf_op jit(solution)/shard_map/ppermute | solution.py:20
  87.6 10.8 %collective-permute-start.13 = (bf16[1,4,128,256]{3,2,1,0:T(8,128)(2,1)S(1)}, bf16[1,4,128,256]{3,2,1,0:T(8,128)(2,1)S(1)}, u32[]{:S(2)}, u32[]{:S(2)}) collective-permute-start(bf16[1,4,128,256]{3,2,1,0:T(8,128)(2,1)S(1)} %slice.73), channel_id=1, source_target_pairs={{0,16},{8,24},{16,0},{24,8},{1,17},{9,25},{17,1},{25,9},{2,18},{10... | collective-permute-start | bytes 786440 | tf_op jit(solution)/shard_map/ppermute | solution.py:20
  89.1 11.9 %collective-permute-start.16 = (bf16[1024,256]{1,0:T(8,128)(2,1)S(1)}, bf16[1024,256]{1,0:T(8,128)(2,1)S(1)}, u32[]{:S(2)}, u32[]{:S(2)}) collective-permute-start(bf16[1024,256]{1,0:T(8,128)(2,1)S(1)} %collective-permute-done.3.refs_2_), channel_id=1, source_target_pairs={{0,1},{1,0},{2,3},{3,2},{4,5},{5,4},{6,7},{7,6},{8,9},{9,8},{10,11... | collective-permute-start | bytes 1572872 | tf_op jit(solution)/shard_map/ppermute | solution.py:20
  93.3 11.8 %collective-permute-start.18 = (bf16[1024,256]{1,0:T(8,128)(2,1)S(1)}, bf16[1024,256]{1,0:T(8,128)(2,1)S(1)}, u32[]{:S(2)}, u32[]{:S(2)}) collective-permute-start(bf16[1024,256]{1,0:T(8,128)(2,1)S(1)} %collective-permute-done.15.refs_5_), channel_id=1, source_target_pairs={{0,2},{1,3},{2,0},{3,1},{4,6},{5,7},{6,4},{7,5},{8,10},{9,11},{10,... | collective-permute-start | bytes 1572872 | tf_op jit(solution)/shard_map/ppermute | solution.py:20
  107.3 2.8 %collective-permute-start.20 = (bf16[2,4,128,256]{3,2,1,0:T(8,128)(2,1)S(1)}, bf16[2,4,128,256]{3,2,1,0:T(8,128)(2,1)S(1)}, u32[]{:S(2)}, u32[]{:S(2)}) collective-permute-start(bf16[2,4,128,256]{3,2,1,0:T(8,128)(2,1)S(1)} %get-tuple-element.51), channel_id=1, source_target_pairs={{0,8},{8,0},{16,24},{24,16},{1,9},{9,1},{17,25},{25,17},{2,10},{10... | collective-permute-start | bytes 1572872 | tf_op jit(solution)/shard_map/ppermute | solution.py:20
  109.6 2.3 %collective-permute-start.19 = (bf16[2,4,128,256]{3,2,1,0:T(8,128)(2,1)S(1)}, bf16[2,4,128,256]{3,2,1,0:T(8,128)(2,1)S(1)}, u32[]{:S(2)}, u32[]{:S(2)}) collective-permute-start(bf16[2,4,128,256]{3,2,1,0:T(8,128)(2,1)S(1)} %get-tuple-element.54), channel_id=1, source_target_pairs={{0,8},{8,0},{16,24},{24,16},{1,9},{9,1},{17,25},{25,17},{2,10},{10... | collective-permute-start | bytes 1572872 | tf_op jit(solution)/shard_map/ppermute | solution.py:20
  110.3 8.3 %collective-permute-start.21 = (bf16[1,4,128,256]{3,2,1,0:T(8,128)(2,1)S(1)}, bf16[1,4,128,256]{3,2,1,0:T(8,128)(2,1)S(1)}, u32[]{:S(2)}, u32[]{:S(2)}) collective-permute-start(bf16[1,4,128,256]{3,2,1,0:T(8,128)(2,1)S(1)} %slice.70), channel_id=1, source_target_pairs={{0,16},{8,24},{16,0},{24,8},{1,17},{9,25},{17,1},{25,9},{2,18},{10... | collective-permute-start | bytes 786440 | tf_op jit(solution)/shard_map/ppermute | solution.py:20
  118.7 14.8 %collective-permute-start.23 = (bf16[4,128,256]{2,1,0:T(8,128)(2,1)S(1)}, bf16[4,128,256]{2,1,0:T(8,128)(2,1)S(1)}, u32[]{:S(2)}, u32[]{:S(2)}) collective-permute-start(bf16[4,128,256]{2,1,0:T(8,128)(2,1)S(1)} %fusion), channel_id=1, source_target_pairs={{0,4},{1,5},{2,6},{3,7},{4,0},{5,1},{6,2},{7,3},{8,12},{9,13},{10,... | collective-permute-start | bytes 786440 | tf_op jit(solution)/shard_map/ppermute | solution.py:20
  122.1 11.3 %collective-permute-start.22 = (bf16[1,4,128,256]{3,2,1,0:T(8,128)(2,1)S(1)}, bf16[1,4,128,256]{3,2,1,0:T(8,128)(2,1)S(1)}, u32[]{:S(2)}, u32[]{:S(2)}) collective-permute-start(bf16[1,4,128,256]{3,2,1,0:T(8,128)(2,1)S(1)} %slice.71), channel_id=1, source_target_pairs={{0,16},{8,24},{16,0},{24,8},{1,17},{9,25},{17,1},{25,9},{2,18},{10... | collective-permute-start | bytes 786440 | tf_op jit(solution)/shard_map/ppermute | solution.py:20
  (8 other events, 120.2 us)

commit v14 on v13

--- a/solution.py
+++ b/solution.py
@@ -13,7 +13,7 @@
 URGENCY = (0, 2, 1, 3)
 BATCHES = (((0,), (2,)), ((1,), (3,)))
 VMEM = pl.BlockSpec(memory_space=pltpu.VMEM)
-PARAMS = pltpu.CompilerParams(vmem_limit_bytes=40 * 2**20)
+SPARE = 6 * 2**20
 
 
 def exchange(part, axis, mask):
@@ -68,7 +68,7 @@
         out_shape=jax.ShapeDtypeStruct((2, group, cells), own[0].dtype),
         in_specs=[VMEM] * (len(own) + len(mate)),
         out_specs=VMEM,
-        compiler_params=PARAMS,
+        compiler_params=pltpu.CompilerParams(vmem_limit_bytes=8 * group * cells + SPARE),
         cost_estimate=pl.CostEstimate(flops=0, bytes_accessed=0, transcendentals=0),
     )(*own, *mate)
 
@@ -110,13 +110,14 @@
                 out_ref[number // 2, round_number] = part.astype(out_ref.dtype)
 
     shape = (slab_count // 2, ROUNDS, rows, width)
+    need = 2 * (lefts.size + sum(array.size for array in arrays)) + (8 + 3 * ROUNDS) * group * width
     return pl.pallas_call(
         kernel,
         out_shape=[jax.ShapeDtypeStruct(shape, kind) for kind in (jnp.float32, jnp.bfloat16)],
         in_specs=[pl.BlockSpec(memory_space=pltpu.SMEM)] + [VMEM] * (1 + len(arrays)),
         out_specs=[VMEM, VMEM],
         scratch_shapes=[pltpu.VMEM((2, group, width), jnp.float32)],
-        compiler_params=PARAMS,
+        compiler_params=pltpu.CompilerParams(vmem_limit_bytes=need + SPARE),
         cost_estimate=pl.CostEstimate(flops=0, bytes_accessed=0, transcendentals=0),
     )(choices, lefts, *arrays)
 

time: 135 us -> 135 us (level)
  no operation moved by 1% of the time
where the time goes in v14:
time: 135 us
  waiting for transfers between devices  82 us (61%)
  starting transfers between devices  34.1 us (25%)
  Pallas kernels  10.9 us (8%)
  other arithmetic  5 us (4%)
  local copies, waits for them, and re-layouts  2.43 us (2%)
    ppermute x24, waiting for transfers between devices, exchange(): lax.ppermute(part, axis, [(i, i ^ mask) for i in range(lax.axis_size(axis...  82 us
    ppermute x24, starting transfers between devices, exchange(): lax.ppermute(part, axis, [(i, i ^ mask) for i in range(lax.axis_size(axis...  34.1 us
    pallas_call x4, Pallas kernels, products(): pl.pallas_call(kernel, out_shape=[jax.ShapeDtypeStruct(shape, kind) for k...  10.3 us
    convert_element_type x3, other arithmetic, pieces_of(): found.append((part.astype(jnp.float32) * scale).astype(jnp.bfloat16))  2.89 us
  transfers between devices with their start and end apart: 24, of which 13 were waited for; matrix products, arithmetic and copies ran while one was open for 2% of the time, Pallas kernels for 4%

profile of v14, /device:TPU:0, one launch (start us, length us, event | category | flops | bytes accessed | tf_op | source)
XLA Modules:
  0.0 134.6 jit_solution(5659518509326357403)
XLA Ops:
  0.7 1.7 %multiply_convert_fusion.1 = (bf16[1024,256]{1,0:T(8,128)(2,1)S(1)}, bf16[1024,256]{1,0:T(8,128)(2,1)S(1)}) fusion(f32[1024]{0:T(1024)S(1)} %get-tuple-element.61, bf16[2048,512]{1,0:T(8,128)(2,1)} %param.3, s32[]{:T(128)S(6)} %select_n.2, f32[1024]{0:T(1024)S(1)} %get-tuple-element.62, s32[]{:T(128)S(6)} %mul.16), kind=kLoop, calls=%fused_computation.6 | loop fusion | flops 1572864 | bytes 2105352 | tf_op jit(solution)/shard_map/convert_element_type | solution.py:159
  2.4 4.1 %collective-permute-start = (bf16[1024,256]{1,0:T(8,128)(2,1)S(1)}, bf16[1024,256]{1,0:T(8,128)(2,1)S(1)}, u32[]{:S(2)}, u32[]{:S(2)}) collective-permute-start(bf16[1024,256]{1,0:T(8,128)(2,1)S(1)} %get-tuple-element.59), channel_id=1, source_target_pairs={{0,4},{1,5},{2,6},{3,7},{4,0},{5,1},{6,2},{7,3},{8,12},{9,13},{10,... | collective-permute-start | bytes 1572872 | tf_op jit(solution)/shard_map/ppermute | solution.py:20
  6.5 1.6 %collective-permute-start.1 = (bf16[1024,256]{1,0:T(8,128)(2,1)S(1)}, bf16[1024,256]{1,0:T(8,128)(2,1)S(1)}, u32[]{:S(2)}, u32[]{:S(2)}) collective-permute-start(bf16[1024,256]{1,0:T(8,128)(2,1)S(1)} %get-tuple-element.60.refs_0_), channel_id=1, source_target_pairs={{0,2},{1,3},{2,0},{3,1},{4,6},{5,7},{6,4},{7,5},{8,10},{9,11},{10,... | collective-permute-start | bytes 1572872 | tf_op jit(solution)/shard_map/ppermute | solution.py:20
  10.4 19.4 %collective-permute-done.refs_2_.refs_4_ = bf16[1024,256]{1,0:T(8,128)(2,1)S(1)} collective-permute-done((bf16[1024,256]{1,0:T(8,128)(2,1)S(1)}, bf16[1024,256]{1,0:T(8,128)(2,1)S(1)}, u32[]{:S(2)}, u32[]{:S(2)}) %collective-permute-start) | collective-permute-done | bytes 524320 | tf_op jit(solution)/shard_map/ppermute | solution.py:20
  34.0 2.3 %collective-permute-start.4 = (bf16[1024,256]{1,0:T(8,128)(2,1)}, bf16[1024,256]{1,0:T(8,128)(2,1)S(1)}, u32[]{:S(2)}, u32[]{:S(2)}) collective-permute-start(bf16[1024,256]{1,0:T(8,128)(2,1)} %multiply_convert_fusion), channel_id=1, source_target_pairs={{0,4},{1,5},{2,6},{3,7},{4,0},{5,1},{6,2},{7,3},{8,12},{9,13},{10,... | collective-permute-start | bytes 1572872 | tf_op jit(solution)/shard_map/ppermute | solution.py:20
  37.6 13.9 %collective-permute-done.2.refs_6_ = bf16[1024,256]{1,0:T(8,128)(2,1)} collective-permute-done((bf16[1024,256]{1,0:T(8,128)(2,1)S(1)}, bf16[1024,256]{1,0:T(8,128)(2,1)}, u32[]{:S(2)}, u32[]{:S(2)}) %collective-permute-start.2) | collective-permute-done | bytes 524320 | tf_op jit(solution)/shard_map/ppermute | solution.py:20
  52.3 2.2 %collective-permute-start.9 = (bf16[1024,256]{1,0:T(8,128)(2,1)}, bf16[1024,256]{1,0:T(8,128)(2,1)}, u32[]{:S(2)}, u32[]{:S(2)}) collective-permute-start(bf16[1024,256]{1,0:T(8,128)(2,1)} %collective-permute-done.2.refs_6_), channel_id=1, source_target_pairs={{0,1},{1,0},{2,3},{3,2},{4,5},{5,4},{6,7},{7,6},{8,9},{9,8},{10,11... | collective-permute-start | bytes 1572872 | tf_op jit(solution)/shard_map/ppermute | solution.py:20
  54.6 4.8 %collective-permute-done.4.refs_3_.refs_4_ = bf16[1024,256]{1,0:T(8,128)(2,1)S(1)} collective-permute-done((bf16[1024,256]{1,0:T(8,128)(2,1)}, bf16[1024,256]{1,0:T(8,128)(2,1)S(1)}, u32[]{:S(2)}, u32[]{:S(2)}) %collective-permute-start.4) | collective-permute-done | bytes 524320 | tf_op jit(solution)/shard_map/ppermute | solution.py:20
  60.1 6.1 %collective-permute-done.3.refs_2_ = bf16[1024,256]{1,0:T(8,128)(2,1)S(1)} collective-permute-done((bf16[1024,256]{1,0:T(8,128)(2,1)S(1)}, bf16[1024,256]{1,0:T(8,128)(2,1)S(1)}, u32[]{:S(2)}, u32[]{:S(2)}) %collective-permute-start.3) | collective-permute-done | bytes 524320 | tf_op jit(solution)/shard_map/ppermute | solution.py:20
  66.6 3.0 %shard_map.38 = (f32[2,4,128,256]{3,2,1,0:T(8,128)S(1)}, bf16[2,4,128,256]{3,2,1,0:T(8,128)(2,1)S(1)}) custom-call(s32[9]{0:T(128)S(1)} %pad_add_fusion.1.choices_ref, bf16[2,512,1024]{2,1,0:T(8,128)(2,1)S(1)} %shard_map.37.lefts_ref, bf16[1024,256]{1,0:T(8,128)(2,1)S(1)} %get-tuple-element.60.refs_0_, bf16[1024,256]{1,0:T(8,128)(2,1)S(1)} %copy-done.3, ...), custom_call_target="tpu_custom_call" | custom-call | tf_op jit(solution)/shard_map/pallas_call | solution.py:114
  69.6 3.0 %shard_map.39 = (f32[2,4,128,256]{3,2,1,0:T(8,128)S(1)}, bf16[2,4,128,256]{3,2,1,0:T(8,128)(2,1)S(1)}) custom-call(s32[9]{0:T(128)S(1)} %pad_add_fusion.1.choices_ref, bf16[2,512,1024]{2,1,0:T(8,128)(2,1)S(1)} %shard_map.37.lefts_ref, bf16[1024,256]{1,0:T(8,128)(2,1)S(1)} %get-tuple-element.60.refs_0_, bf16[1024,256]{1,0:T(8,128)(2,1)S(1)} %copy-done.3, ...), custom_call_target="tpu_custom_call" | custom-call | tf_op jit(solution)/shard_map/pallas_call | solution.py:114
  75.3 1.6 %collective-permute-start.12 = (bf16[1,4,128,256]{3,2,1,0:T(8,128)(2,1)S(1)}, bf16[1,4,128,256]{3,2,1,0:T(8,128)(2,1)S(1)}, u32[]{:S(2)}, u32[]{:S(2)}) collective-permute-start(bf16[1,4,128,256]{3,2,1,0:T(8,128)(2,1)S(1)} %slice.72), channel_id=1, source_target_pairs={{0,16},{8,24},{16,0},{24,8},{1,17},{9,25},{17,1},{25,9},{2,18},{10... | collective-permute-start | bytes 786440 | tf_op jit(solution)/shard_map/ppermute | solution.py:20
  77.0 6.0 %collective-permute-done.12 = bf16[1,4,128,256]{3,2,1,0:T(8,128)(2,1)S(1)} collective-permute-done((bf16[1,4,128,256]{3,2,1,0:T(8,128)(2,1)S(1)}, bf16[1,4,128,256]{3,2,1,0:T(8,128)(2,1)S(1)}, u32[]{:S(2)}, u32[]{:S(2)}) %collective-permute-start.12) | collective-permute-done | bytes 262176 | tf_op jit(solution)/shard_map/ppermute | solution.py:20
  83.1 4.5 %collective-permute-start.14 = (bf16[4,128,256]{2,1,0:T(8,128)(2,1)S(1)}, bf16[4,128,256]{2,1,0:T(8,128)(2,1)S(1)}, u32[]{:S(2)}, u32[]{:S(2)}) collective-permute-start(bf16[4,128,256]{2,1,0:T(8,128)(2,1)S(1)} %fusion.3), channel_id=1, source_target_pairs={{0,4},{1,5},{2,6},{3,7},{4,0},{5,1},{6,2},{7,3},{8,12},{9,13},{10,... | collective-permute-start | bytes 786440 | tf_op jit(solution)/shard_map/ppermute | solution.py:20
  90.1 3.2 %collective-permute-done.17.refs_6_ = bf16[1024,256]{1,0:T(8,128)(2,1)S(1)} collective-permute-done((bf16[1024,256]{1,0:T(8,128)(2,1)S(1)}, bf16[1024,256]{1,0:T(8,128)(2,1)S(1)}, u32[]{:S(2)}, u32[]{:S(2)}) %collective-permute-start.17) | collective-permute-done | bytes 524320 | tf_op jit(solution)/shard_map/ppermute | solution.py:20
  93.4 5.0 %collective-permute-done.14 = bf16[4,128,256]{2,1,0:T(8,128)(2,1)S(1)} collective-permute-done((bf16[4,128,256]{2,1,0:T(8,128)(2,1)S(1)}, bf16[4,128,256]{2,1,0:T(8,128)(2,1)S(1)}, u32[]{:S(2)}, u32[]{:S(2)}) %collective-permute-start.14) | collective-permute-done | bytes 262176 | tf_op jit(solution)/shard_map/ppermute | solution.py:20
  98.6 2.4 %collective-permute-done.16.refs_3_ = bf16[1024,256]{1,0:T(8,128)(2,1)S(1)} collective-permute-done((bf16[1024,256]{1,0:T(8,128)(2,1)S(1)}, bf16[1024,256]{1,0:T(8,128)(2,1)S(1)}, u32[]{:S(2)}, u32[]{:S(2)}) %collective-permute-start.16) | collective-permute-done | bytes 524320 | tf_op jit(solution)/shard_map/ppermute | solution.py:20
  101.0 4.2 %collective-permute-done.18.refs_7_ = bf16[1024,256]{1,0:T(8,128)(2,1)S(1)} collective-permute-done((bf16[1024,256]{1,0:T(8,128)(2,1)S(1)}, bf16[1024,256]{1,0:T(8,128)(2,1)S(1)}, u32[]{:S(2)}, u32[]{:S(2)}) %collective-permute-start.18) | collective-permute-done | bytes 524320 | tf_op jit(solution)/shard_map/ppermute | solution.py:20
  105.2 2.1 %shard_map.40 = (f32[2,4,128,256]{3,2,1,0:T(8,128)S(1)}, bf16[2,4,128,256]{3,2,1,0:T(8,128)(2,1)S(1)}) custom-call(s32[9]{0:T(128)S(1)} %pad_add_fusion.2.choices_ref, bf16[2,512,1024]{2,1,0:T(8,128)(2,1)S(1)} %shard_map.37.lefts_ref, bf16[1024,256]{1,0:T(8,128)(2,1)S(1)} %multiply_convert_fusion.2.refs_1_.refs_0_, ...), custom_call_target="tpu_custom_call" | custom-call | tf_op jit(solution)/shard_map/pallas_call | solution.py:114
  107.4 2.1 %shard_map.41 = (f32[2,4,128,256]{3,2,1,0:T(8,128)S(1)}, bf16[2,4,128,256]{3,2,1,0:T(8,128)(2,1)S(1)}) custom-call(s32[9]{0:T(128)S(1)} %pad_add_fusion.2.choices_ref, bf16[2,512,1024]{2,1,0:T(8,128)(2,1)S(1)} %shard_map.37.lefts_ref, bf16[1024,256]{1,0:T(8,128)(2,1)S(1)} %multiply_convert_fusion.2.refs_1_.refs_0_, ...), custom_call_target="tpu_custom_call" | custom-call | tf_op jit(solution)/shard_map/pallas_call | solution.py:114
  110.3 1.6 %collective-permute-start.21 = (bf16[1,4,128,256]{3,2,1,0:T(8,128)(2,1)S(1)}, bf16[1,4,128,256]{3,2,1,0:T(8,128)(2,1)S(1)}, u32[]{:S(2)}, u32[]{:S(2)}) collective-permute-start(bf16[1,4,128,256]{3,2,1,0:T(8,128)(2,1)S(1)} %slice.70), channel_id=1, source_target_pairs={{0,16},{8,24},{16,0},{24,8},{1,17},{9,25},{17,1},{25,9},{2,18},{10... | collective-permute-start | bytes 786440 | tf_op jit(solution)/shard_map/ppermute | solution.py:20
  112.0 6.6 %collective-permute-done.21 = bf16[1,4,128,256]{3,2,1,0:T(8,128)(2,1)S(1)} collective-permute-done((bf16[1,4,128,256]{3,2,1,0:T(8,128)(2,1)S(1)}, bf16[1,4,128,256]{3,2,1,0:T(8,128)(2,1)S(1)}, u32[]{:S(2)}, u32[]{:S(2)}) %collective-permute-start.21) | collective-permute-done | bytes 262176 | tf_op jit(solution)/shard_map/ppermute | solution.py:20
  118.7 3.5 %collective-permute-start.23 = (bf16[4,128,256]{2,1,0:T(8,128)(2,1)S(1)}, bf16[4,128,256]{2,1,0:T(8,128)(2,1)S(1)}, u32[]{:S(2)}, u32[]{:S(2)}) collective-permute-start(bf16[4,128,256]{2,1,0:T(8,128)(2,1)S(1)} %fusion), channel_id=1, source_target_pairs={{0,4},{1,5},{2,6},{3,7},{4,0},{5,1},{6,2},{7,3},{8,12},{9,13},{10,... | collective-permute-start | bytes 786440 | tf_op jit(solution)/shard_map/ppermute | solution.py:20
  123.7 9.7 %collective-permute-done.23 = bf16[4,128,256]{2,1,0:T(8,128)(2,1)S(1)} collective-permute-done((bf16[4,128,256]{2,1,0:T(8,128)(2,1)S(1)}, bf16[4,128,256]{2,1,0:T(8,128)(2,1)S(1)}, u32[]{:S(2)}, u32[]{:S(2)}) %collective-permute-start.23) | collective-permute-done | bytes 262176 | tf_op jit(solution)/shard_map/ppermute | solution.py:20
  (68 shorter events, 19.8 us)
Async XLA Ops:
  2.4 27.4 %collective-permute-start = (bf16[1024,256]{1,0:T(8,128)(2,1)S(1)}, bf16[1024,256]{1,0:T(8,128)(2,1)S(1)}, u32[]{:S(2)}, u32[]{:S(2)}) collective-permute-start(bf16[1024,256]{1,0:T(8,128)(2,1)S(1)} %get-tuple-element.59), channel_id=1, source_target_pairs={{0,4},{1,5},{2,6},{3,7},{4,0},{5,1},{6,2},{7,3},{8,12},{9,13},{10,... | collective-permute-start | bytes 1572872 | tf_op jit(solution)/shard_map/ppermute | solution.py:20
  6.5 23.5 %collective-permute-start.1 = (bf16[1024,256]{1,0:T(8,128)(2,1)S(1)}, bf16[1024,256]{1,0:T(8,128)(2,1)S(1)}, u32[]{:S(2)}, u32[]{:S(2)}) collective-permute-start(bf16[1024,256]{1,0:T(8,128)(2,1)S(1)} %get-tuple-element.60.refs_0_), channel_id=1, source_target_pairs={{0,2},{1,3},{2,0},{3,1},{4,6},{5,7},{6,4},{7,5},{8,10},{9,11},{10,... | collective-permute-start | bytes 1572872 | tf_op jit(solution)/shard_map/ppermute | solution.py:20
  8.3 23.2 %collective-permute-start.6 = (bf16[1024,256]{1,0:T(8,128)(2,1)S(1)}, bf16[1024,256]{1,0:T(8,128)(2,1)S(1)}, u32[]{:S(2)}, u32[]{:S(2)}) collective-permute-start(bf16[1024,256]{1,0:T(8,128)(2,1)S(1)} %multiply_convert_fusion.2.refs_1_.refs_0_), channel_id=1, source_target_pairs={{0,1},{1,0},{2,3},{3,2},{4,5},{5,4},{6,7},{7,6},{8,9},{9,8},{10,11... | collective-permute-start | bytes 1572872 | tf_op jit(solution)/shard_map/ppermute | solution.py:20
  9.9 26.4 %collective-permute-start.5 = (bf16[1024,256]{1,0:T(8,128)(2,1)S(1)}, bf16[1024,256]{1,0:T(8,128)(2,1)S(1)}, u32[]{:S(2)}, u32[]{:S(2)}) collective-permute-start(bf16[1024,256]{1,0:T(8,128)(2,1)S(1)} %get-tuple-element.60.refs_0_), channel_id=1, source_target_pairs={{0,1},{1,0},{2,3},{3,2},{4,5},{5,4},{6,7},{7,6},{8,9},{9,8},{10,11... | collective-permute-start | bytes 1572872 | tf_op jit(solution)/shard_map/ppermute | solution.py:20
  30.0 21.6 %collective-permute-start.2 = (bf16[1024,256]{1,0:T(8,128)(2,1)S(1)}, bf16[1024,256]{1,0:T(8,128)(2,1)}, u32[]{:S(2)}, u32[]{:S(2)}) collective-permute-start(bf16[1024,256]{1,0:T(8,128)(2,1)S(1)} %collective-permute-done.refs_2_.refs_4_), channel_id=1, source_target_pairs={{0,2},{1,3},{2,0},{3,1},{4,6},{5,7},{6,4},{7,5},{8,10},{9,11},{10,... | collective-permute-start | bytes 1572872 | tf_op jit(solution)/shard_map/ppermute | solution.py:20
  31.5 20.1 %collective-permute-start.7 = (bf16[1024,256]{1,0:T(8,128)(2,1)S(1)}, bf16[1024,256]{1,0:T(8,128)(2,1)S(1)}, u32[]{:S(2)}, u32[]{:S(2)}) collective-permute-start(bf16[1024,256]{1,0:T(8,128)(2,1)S(1)} %collective-permute-done.1.refs_2_), channel_id=1, source_target_pairs={{0,1},{1,0},{2,3},{3,2},{4,5},{5,4},{6,7},{7,6},{8,9},{9,8},{10,11... | collective-permute-start | bytes 1572872 | tf_op jit(solution)/shard_map/ppermute | solution.py:20
  34.0 25.5 %collective-permute-start.4 = (bf16[1024,256]{1,0:T(8,128)(2,1)}, bf16[1024,256]{1,0:T(8,128)(2,1)S(1)}, u32[]{:S(2)}, u32[]{:S(2)}) collective-permute-start(bf16[1024,256]{1,0:T(8,128)(2,1)} %multiply_convert_fusion), channel_id=1, source_target_pairs={{0,4},{1,5},{2,6},{3,7},{4,0},{5,1},{6,2},{7,3},{8,12},{9,13},{10,... | collective-permute-start | bytes 1572872 | tf_op jit(solution)/shard_map/ppermute | solution.py:20
  37.1 29.1 %collective-permute-start.8 = (bf16[1024,256]{1,0:T(8,128)(2,1)S(1)}, bf16[1024,256]{1,0:T(8,128)(2,1)}, u32[]{:S(2)}, u32[]{:S(2)}) collective-permute-start(bf16[1024,256]{1,0:T(8,128)(2,1)S(1)} %collective-permute-done.refs_2_.refs_4_), channel_id=1, source_target_pairs={{0,1},{1,0},{2,3},{3,2},{4,5},{5,4},{6,7},{7,6},{8,9},{9,8},{10,11... | collective-permute-start | bytes 1572872 | tf_op jit(solution)/shard_map/ppermute | solution.py:20
  51.5 14.6 %collective-permute-start.3 = (bf16[1024,256]{1,0:T(8,128)(2,1)S(1)}, bf16[1024,256]{1,0:T(8,128)(2,1)S(1)}, u32[]{:S(2)}, u32[]{:S(2)}) collective-permute-start(bf16[1024,256]{1,0:T(8,128)(2,1)S(1)} %multiply_convert_fusion.2.refs_1_.refs_0_), channel_id=1, source_target_pairs={{0,2},{1,3},{2,0},{3,1},{4,6},{5,7},{6,4},{7,5},{8,10},{9,11},{10,... | collective-permute-start | bytes 1572872 | tf_op jit(solution)/shard_map/ppermute | solution.py:20
  52.3 14.2 %collective-permute-start.9 = (bf16[1024,256]{1,0:T(8,128)(2,1)}, bf16[1024,256]{1,0:T(8,128)(2,1)}, u32[]{:S(2)}, u32[]{:S(2)}) collective-permute-start(bf16[1024,256]{1,0:T(8,128)(2,1)} %collective-permute-done.2.refs_6_), channel_id=1, source_target_pairs={{0,1},{1,0},{2,3},{3,2},{4,5},{5,4},{6,7},{7,6},{8,9},{9,8},{10,11... | collective-permute-start | bytes 1572872 | tf_op jit(solution)/shard_map/ppermute | solution.py:20
  69.6 5.5 %collective-permute-start.11 = (bf16[2,4,128,256]{3,2,1,0:T(8,128)(2,1)S(1)}, bf16[2,4,128,256]{3,2,1,0:T(8,128)(2,1)S(1)}, u32[]{:S(2)}, u32[]{:S(2)}) collective-permute-start(bf16[2,4,128,256]{3,2,1,0:T(8,128)(2,1)S(1)} %get-tuple-element.40), channel_id=1, source_target_pairs={{0,8},{8,0},{16,24},{24,16},{1,9},{9,1},{17,25},{25,17},{2,10},{10... | collective-permute-start | bytes 1572872 | tf_op jit(solution)/shard_map/ppermute | solution.py:20
  72.6 4.2 %collective-permute-start.10 = (bf16[2,4,128,256]{3,2,1,0:T(8,128)(2,1)S(1)}, bf16[2,4,128,256]{3,2,1,0:T(8,128)(2,1)S(1)}, u32[]{:S(2)}, u32[]{:S(2)}) collective-permute-start(bf16[2,4,128,256]{3,2,1,0:T(8,128)(2,1)S(1)} %get-tuple-element.43), channel_id=1, source_target_pairs={{0,8},{8,0},{16,24},{24,16},{1,9},{9,1},{17,25},{25,17},{2,10},{10... | collective-permute-start | bytes 1572872 | tf_op jit(solution)/shard_map/ppermute | solution.py:20
  73.2 15.9 %collective-permute-start.15 = (bf16[1024,256]{1,0:T(8,128)(2,1)S(1)}, bf16[1024,256]{1,0:T(8,128)(2,1)S(1)}, u32[]{:S(2)}, u32[]{:S(2)}) collective-permute-start(bf16[1024,256]{1,0:T(8,128)(2,1)S(1)} %collective-permute-done.4.refs_3_.refs_4_), channel_id=1, source_target_pairs={{0,1},{1,0},{2,3},{3,2},{4,5},{5,4},{6,7},{7,6},{8,9},{9,8},{10,11... | collective-permute-start | bytes 1572872 | tf_op jit(solution)/shard_map/ppermute | solution.py:20
  74.7 18.7 %collective-permute-start.17 = (bf16[1024,256]{1,0:T(8,128)(2,1)S(1)}, bf16[1024,256]{1,0:T(8,128)(2,1)S(1)}, u32[]{:S(2)}, u32[]{:S(2)}) collective-permute-start(bf16[1024,256]{1,0:T(8,128)(2,1)S(1)} %collective-permute-done.4.refs_3_.refs_4_), channel_id=1, source_target_pairs={{0,2},{1,3},{2,0},{3,1},{4,6},{5,7},{6,4},{7,5},{8,10},{9,11},{10,... | collective-permute-start | bytes 1572872 | tf_op jit(solution)/shard_map/ppermute | solution.py:20
  75.3 7.8 %collective-permute-start.12 = (bf16[1,4,128,256]{3,2,1,0:T(8,128)(2,1)S(1)}, bf16[1,4,128,256]{3,2,1,0:T(8,128)(2,1)S(1)}, u32[]{:S(2)}, u32[]{:S(2)}) collective-permute-start(bf16[1,4,128,256]{3,2,1,0:T(8,128)(2,1)S(1)} %slice.72), channel_id=1, source_target_pairs={{0,16},{8,24},{16,0},{24,8},{1,17},{9,25},{17,1},{25,9},{2,18},{10... | collective-permute-start | bytes 786440 | tf_op jit(solution)/shard_map/ppermute | solution.py:20
  83.1 15.3 %collective-permute-start.14 = (bf16[4,128,256]{2,1,0:T(8,128)(2,1)S(1)}, bf16[4,128,256]{2,1,0:T(8,128)(2,1)S(1)}, u32[]{:S(2)}, u32[]{:S(2)}) collective-permute-start(bf16[4,128,256]{2,1,0:T(8,128)(2,1)S(1)} %fusion.3), channel_id=1, source_target_pairs={{0,4},{1,5},{2,6},{3,7},{4,0},{5,1},{6,2},{7,3},{8,12},{9,13},{10,... | collective-permute-start | bytes 786440 | tf_op jit(solution)/shard_map/ppermute | solution.py:20
  87.6 10.8 %collective-permute-start.13 = (bf16[1,4,128,256]{3,2,1,0:T(8,128)(2,1)S(1)}, bf16[1,4,128,256]{3,2,1,0:T(8,128)(2,1)S(1)}, u32[]{:S(2)}, u32[]{:S(2)}) collective-permute-start(bf16[1,4,128,256]{3,2,1,0:T(8,128)(2,1)S(1)} %slice.73), channel_id=1, source_target_pairs={{0,16},{8,24},{16,0},{24,8},{1,17},{9,25},{17,1},{25,9},{2,18},{10... | collective-permute-start | bytes 786440 | tf_op jit(solution)/shard_map/ppermute | solution.py:20
  89.1 11.9 %collective-permute-start.16 = (bf16[1024,256]{1,0:T(8,128)(2,1)S(1)}, bf16[1024,256]{1,0:T(8,128)(2,1)S(1)}, u32[]{:S(2)}, u32[]{:S(2)}) collective-permute-start(bf16[1024,256]{1,0:T(8,128)(2,1)S(1)} %collective-permute-done.3.refs_2_), channel_id=1, source_target_pairs={{0,1},{1,0},{2,3},{3,2},{4,5},{5,4},{6,7},{7,6},{8,9},{9,8},{10,11... | collective-permute-start | bytes 1572872 | tf_op jit(solution)/shard_map/ppermute | solution.py:20
  93.4 11.8 %collective-permute-start.18 = (bf16[1024,256]{1,0:T(8,128)(2,1)S(1)}, bf16[1024,256]{1,0:T(8,128)(2,1)S(1)}, u32[]{:S(2)}, u32[]{:S(2)}) collective-permute-start(bf16[1024,256]{1,0:T(8,128)(2,1)S(1)} %collective-permute-done.15.refs_5_), channel_id=1, source_target_pairs={{0,2},{1,3},{2,0},{3,1},{4,6},{5,7},{6,4},{7,5},{8,10},{9,11},{10,... | collective-permute-start | bytes 1572872 | tf_op jit(solution)/shard_map/ppermute | solution.py:20
  107.3 2.8 %collective-permute-start.20 = (bf16[2,4,128,256]{3,2,1,0:T(8,128)(2,1)S(1)}, bf16[2,4,128,256]{3,2,1,0:T(8,128)(2,1)S(1)}, u32[]{:S(2)}, u32[]{:S(2)}) collective-permute-start(bf16[2,4,128,256]{3,2,1,0:T(8,128)(2,1)S(1)} %get-tuple-element.51), channel_id=1, source_target_pairs={{0,8},{8,0},{16,24},{24,16},{1,9},{9,1},{17,25},{25,17},{2,10},{10... | collective-permute-start | bytes 1572872 | tf_op jit(solution)/shard_map/ppermute | solution.py:20
  109.6 2.3 %collective-permute-start.19 = (bf16[2,4,128,256]{3,2,1,0:T(8,128)(2,1)S(1)}, bf16[2,4,128,256]{3,2,1,0:T(8,128)(2,1)S(1)}, u32[]{:S(2)}, u32[]{:S(2)}) collective-permute-start(bf16[2,4,128,256]{3,2,1,0:T(8,128)(2,1)S(1)} %get-tuple-element.54), channel_id=1, source_target_pairs={{0,8},{8,0},{16,24},{24,16},{1,9},{9,1},{17,25},{25,17},{2,10},{10... | collective-permute-start | bytes 1572872 | tf_op jit(solution)/shard_map/ppermute | solution.py:20
  110.3 8.3 %collective-permute-start.21 = (bf16[1,4,128,256]{3,2,1,0:T(8,128)(2,1)S(1)}, bf16[1,4,128,256]{3,2,1,0:T(8,128)(2,1)S(1)}, u32[]{:S(2)}, u32[]{:S(2)}) collective-permute-start(bf16[1,4,128,256]{3,2,1,0:T(8,128)(2,1)S(1)} %slice.70), channel_id=1, source_target_pairs={{0,16},{8,24},{16,0},{24,8},{1,17},{9,25},{17,1},{25,9},{2,18},{10... | collective-permute-start | bytes 786440 | tf_op jit(solution)/shard_map/ppermute | solution.py:20
  118.7 14.8 %collective-permute-start.23 = (bf16[4,128,256]{2,1,0:T(8,128)(2,1)S(1)}, bf16[4,128,256]{2,1,0:T(8,128)(2,1)S(1)}, u32[]{:S(2)}, u32[]{:S(2)}) collective-permute-start(bf16[4,128,256]{2,1,0:T(8,128)(2,1)S(1)} %fusion), channel_id=1, source_target_pairs={{0,4},{1,5},{2,6},{3,7},{4,0},{5,1},{6,2},{7,3},{8,12},{9,13},{10,... | collective-permute-start | bytes 786440 | tf_op jit(solution)/shard_map/ppermute | solution.py:20
  122.1 11.3 %collective-permute-start.22 = (bf16[1,4,128,256]{3,2,1,0:T(8,128)(2,1)S(1)}, bf16[1,4,128,256]{3,2,1,0:T(8,128)(2,1)S(1)}, u32[]{:S(2)}, u32[]{:S(2)}) collective-permute-start(bf16[1,4,128,256]{3,2,1,0:T(8,128)(2,1)S(1)} %slice.71), channel_id=1, source_target_pairs={{0,16},{8,24},{16,0},{24,8},{1,17},{9,25},{17,1},{25,9},{2,18},{10... | collective-permute-start | bytes 786440 | tf_op jit(solution)/shard_map/ppermute | solution.py:20
  (8 other events, 120.2 us)

commit v15 on v13

--- a/solution.py
+++ b/solution.py
@@ -1,3 +1,5 @@
+from functools import partial
+
 import jax
 import jax.numpy as jnp
 from jax import lax
@@ -180,21 +182,27 @@
 
     held = [{0: piece} for piece in own + mate]
     sent = {}
-    halves, columns, back = [], [], []
+    halves, columns, back, keeps = [], [], [], []
 
     def add_batch():
         batch = [
             [[held[n][low] for low in range(cut)] for n in numbers]
             for numbers in BATCHES[len(halves)]
         ]
+        if keeps:
+            keeps.pop()(held[len(own) - 1][cut - 1])
         earlier = columns if halves else sent[cut // 2][:3][-1]
         choices = jnp.concatenate([behind(rounds, earlier), me])
         even, odd = products(choices, lefts, batch, scale_factor, 1)
         halves.append(halved(even, odd, 1))
         give = summed(halves[-1], None)
         back.append(exchange(give.astype(jnp.bfloat16), "snap", cut))
-        even, odd = products(behind(choices, odd), lefts, batch, scale_factor, 0)
-        columns.append(summed(halved(even, odd, 1), give))
+
+        def keep(first, then):
+            even, odd = products(behind(choices, first), lefts, batch, scale_factor, 0)
+            columns.append(summed(halved(even, odd, 1), (give, then)))
+
+        keeps.append(partial(keep, odd))
 
     for piece, low, bit in hops_in_order(OWN_WIDTHS + MATE_WIDTHS, cut):
         earlier = sent.setdefault(bit, [])
@@ -206,6 +214,7 @@
             len(held[n]) == cut for numbers in BATCHES[len(halves)] for n in numbers
         ):
             add_batch()
+    keeps.pop()(None)
     results = [kept + got.astype(jnp.float32) for kept, got in zip(columns, back)]
     return jnp.concatenate(results, axis=2)[:, None]
 

time: 135 us -> 138 us (1.022)
  waiting for transfers between devices: 82 us -> 86.4 us
  starting transfers between devices: 34.1 us -> 32.6 us
    ppermute x24, waiting for transfers between devices: 82 us -> 86.4 us  [exchange(): lax.ppermute(part, axis, [(i, i ^ mask) for i in range(lax.axis_size(axis...]
    ppermute x24, starting transfers between devices: 34.1 us -> 32.6 us  [exchange(): lax.ppermute(part, axis, [(i, i ^ mask) for i in range(lax.axis_size(axis...]
  transfers between devices with their start and end apart: 24 -> 24, of which waited for: 13 -> 13; matrix products, arithmetic and copies ran while one was open for 2% -> 2% of each run, Pallas kernels for 4% -> 6%
where the time goes in v15:
time: 138 us; the launch traced here: 137 us
  waiting for transfers between devices  86.4 us (63%)
  starting transfers between devices  32.6 us (24%)
  Pallas kernels  10.9 us (8%)
  other arithmetic  5.01 us (4%)
  local copies, waits for them, and re-layouts  2.43 us (2%)
    ppermute x24, waiting for transfers between devices, exchange(): lax.ppermute(part, axis, [(i, i ^ mask) for i in range(lax.axis_size(axis...  86.4 us
    ppermute x24, starting transfers between devices, exchange(): lax.ppermute(part, axis, [(i, i ^ mask) for i in range(lax.axis_size(axis...  32.6 us
    pallas_call x4, Pallas kernels, products(): pl.pallas_call(kernel, out_shape=[jax.ShapeDtypeStruct(shape, kind) for k...  10.3 us
    convert_element_type x3, other arithmetic, pieces_of(): found.append((part.astype(jnp.float32) * scale).astype(jnp.bfloat16))  2.89 us
  transfers between devices with their start and end apart: 24, of which 13 were waited for; matrix products, arithmetic and copies ran while one was open for 2% of the time, Pallas kernels for 6%

profile of v15, /device:TPU:0, one launch (start us, length us, event | category | flops | bytes accessed | tf_op | source)
XLA Modules:
  0.0 137.5 jit_solution(18008475382867896898)
XLA Ops:
  0.7 1.7 %multiply_convert_fusion.1 = (bf16[1024,256]{1,0:T(8,128)(2,1)S(1)}, bf16[1024,256]{1,0:T(8,128)(2,1)S(1)}) fusion(f32[1024]{0:T(1024)S(1)} %get-tuple-element.61, bf16[2048,512]{1,0:T(8,128)(2,1)} %param.3, s32[]{:T(128)S(6)} %select_n.2, f32[1024]{0:T(1024)S(1)} %get-tuple-element.62, s32[]{:T(128)S(6)} %mul.16), kind=kLoop, calls=%fused_computation.6 | loop fusion | flops 1572864 | bytes 2105352 | tf_op jit(solution)/shard_map/convert_element_type | solution.py:160
  2.4 4.1 %collective-permute-start = (bf16[1024,256]{1,0:T(8,128)(2,1)S(1)}, bf16[1024,256]{1,0:T(8,128)(2,1)S(1)}, u32[]{:S(2)}, u32[]{:S(2)}) collective-permute-start(bf16[1024,256]{1,0:T(8,128)(2,1)S(1)} %get-tuple-element.59), channel_id=1, source_target_pairs={{0,4},{1,5},{2,6},{3,7},{4,0},{5,1},{6,2},{7,3},{8,12},{9,13},{10,... | collective-permute-start | bytes 1572872 | tf_op jit(solution)/shard_map/ppermute | solution.py:22
  6.5 1.6 %collective-permute-start.1 = (bf16[1024,256]{1,0:T(8,128)(2,1)S(1)}, bf16[1024,256]{1,0:T(8,128)(2,1)S(1)}, u32[]{:S(2)}, u32[]{:S(2)}) collective-permute-start(bf16[1024,256]{1,0:T(8,128)(2,1)S(1)} %get-tuple-element.60.refs_0_), channel_id=1, source_target_pairs={{0,2},{1,3},{2,0},{3,1},{4,6},{5,7},{6,4},{7,5},{8,10},{9,11},{10,... | collective-permute-start | bytes 1572872 | tf_op jit(solution)/shard_map/ppermute | solution.py:22
  10.4 19.4 %collective-permute-done.refs_2_.refs_4_ = bf16[1024,256]{1,0:T(8,128)(2,1)S(1)} collective-permute-done((bf16[1024,256]{1,0:T(8,128)(2,1)S(1)}, bf16[1024,256]{1,0:T(8,128)(2,1)S(1)}, u32[]{:S(2)}, u32[]{:S(2)}) %collective-permute-start) | collective-permute-done | bytes 524320 | tf_op jit(solution)/shard_map/ppermute | solution.py:22
  34.0 2.3 %collective-permute-start.4 = (bf16[1024,256]{1,0:T(8,128)(2,1)}, bf16[1024,256]{1,0:T(8,128)(2,1)S(1)}, u32[]{:S(2)}, u32[]{:S(2)}) collective-permute-start(bf16[1024,256]{1,0:T(8,128)(2,1)} %multiply_convert_fusion), channel_id=1, source_target_pairs={{0,4},{1,5},{2,6},{3,7},{4,0},{5,1},{6,2},{7,3},{8,12},{9,13},{10,... | collective-permute-start | bytes 1572872 | tf_op jit(solution)/shard_map/ppermute | solution.py:22
  37.6 13.9 %collective-permute-done.2.refs_6_ = bf16[1024,256]{1,0:T(8,128)(2,1)} collective-permute-done((bf16[1024,256]{1,0:T(8,128)(2,1)S(1)}, bf16[1024,256]{1,0:T(8,128)(2,1)}, u32[]{:S(2)}, u32[]{:S(2)}) %collective-permute-start.2) | collective-permute-done | bytes 524320 | tf_op jit(solution)/shard_map/ppermute | solution.py:22
  52.3 2.2 %collective-permute-start.9 = (bf16[1024,256]{1,0:T(8,128)(2,1)}, bf16[1024,256]{1,0:T(8,128)(2,1)}, u32[]{:S(2)}, u32[]{:S(2)}) collective-permute-start(bf16[1024,256]{1,0:T(8,128)(2,1)} %collective-permute-done.2.refs_6_), channel_id=1, source_target_pairs={{0,1},{1,0},{2,3},{3,2},{4,5},{5,4},{6,7},{7,6},{8,9},{9,8},{10,11... | collective-permute-start | bytes 1572872 | tf_op jit(solution)/shard_map/ppermute | solution.py:22
  54.6 4.8 %collective-permute-done.4.refs_3_.refs_4_ = bf16[1024,256]{1,0:T(8,128)(2,1)S(1)} collective-permute-done((bf16[1024,256]{1,0:T(8,128)(2,1)}, bf16[1024,256]{1,0:T(8,128)(2,1)S(1)}, u32[]{:S(2)}, u32[]{:S(2)}) %collective-permute-start.4) | collective-permute-done | bytes 524320 | tf_op jit(solution)/shard_map/ppermute | solution.py:22
  60.6 5.5 %collective-permute-done.3.refs_2_ = bf16[1024,256]{1,0:T(8,128)(2,1)S(1)} collective-permute-done((bf16[1024,256]{1,0:T(8,128)(2,1)S(1)}, bf16[1024,256]{1,0:T(8,128)(2,1)S(1)}, u32[]{:S(2)}, u32[]{:S(2)}) %collective-permute-start.3) | collective-permute-done | bytes 524320 | tf_op jit(solution)/shard_map/ppermute | solution.py:22
  66.2 2.1 %collective-permute-done.9.refs_7_ = bf16[1024,256]{1,0:T(8,128)(2,1)} collective-permute-done((bf16[1024,256]{1,0:T(8,128)(2,1)}, bf16[1024,256]{1,0:T(8,128)(2,1)}, u32[]{:S(2)}, u32[]{:S(2)}) %collective-permute-start.9) | collective-permute-done | bytes 524320 | tf_op jit(solution)/shard_map/ppermute | solution.py:22
  68.3 3.0 %shard_map.38 = (f32[2,4,128,256]{3,2,1,0:T(8,128)S(1)}, bf16[2,4,128,256]{3,2,1,0:T(8,128)(2,1)S(1)}) custom-call(s32[9]{0:T(128)S(1)} %pad_add_fusion.1.choices_ref, bf16[2,512,1024]{2,1,0:T(8,128)(2,1)S(1)} %shard_map.37.lefts_ref, bf16[1024,256]{1,0:T(8,128)(2,1)S(1)} %get-tuple-element.60.refs_0_, bf16[1024,256]{1,0:T(8,128)(2,1)S(1)} %copy-done.3, ...), custom_call_target="tpu_custom_call" | custom-call | tf_op jit(solution)/shard_map/pallas_call | solution.py:115
  71.4 3.0 %shard_map.39 = (f32[2,4,128,256]{3,2,1,0:T(8,128)S(1)}, bf16[2,4,128,256]{3,2,1,0:T(8,128)(2,1)S(1)}) custom-call(s32[9]{0:T(128)S(1)} %pad_add_fusion.1.choices_ref, bf16[2,512,1024]{2,1,0:T(8,128)(2,1)S(1)} %shard_map.37.lefts_ref, bf16[1024,256]{1,0:T(8,128)(2,1)S(1)} %get-tuple-element.60.refs_0_, bf16[1024,256]{1,0:T(8,128)(2,1)S(1)} %copy-done.3, ...), custom_call_target="tpu_custom_call" | custom-call | tf_op jit(solution)/shard_map/pallas_call | solution.py:115
  74.9 2.8 %collective-permute-done.13.refs_5_ = bf16[1024,256]{1,0:T(8,128)(2,1)S(1)} collective-permute-done((bf16[1024,256]{1,0:T(8,128)(2,1)S(1)}, bf16[1024,256]{1,0:T(8,128)(2,1)S(1)}, u32[]{:S(2)}, u32[]{:S(2)}) %collective-permute-start.13) | collective-permute-done | bytes 524320 | tf_op jit(solution)/shard_map/ppermute | solution.py:22
  79.7 1.6 %collective-permute-start.12 = (bf16[1,4,128,256]{3,2,1,0:T(8,128)(2,1)S(1)}, bf16[1,4,128,256]{3,2,1,0:T(8,128)(2,1)S(1)}, u32[]{:S(2)}, u32[]{:S(2)}) collective-permute-start(bf16[1,4,128,256]{3,2,1,0:T(8,128)(2,1)S(1)} %slice.72), channel_id=1, source_target_pairs={{0,16},{8,24},{16,0},{24,8},{1,17},{9,25},{17,1},{25,9},{2,18},{10... | collective-permute-start | bytes 786440 | tf_op jit(solution)/shard_map/ppermute | solution.py:22
  81.5 4.8 %collective-permute-done.12 = bf16[1,4,128,256]{3,2,1,0:T(8,128)(2,1)S(1)} collective-permute-done((bf16[1,4,128,256]{3,2,1,0:T(8,128)(2,1)S(1)}, bf16[1,4,128,256]{3,2,1,0:T(8,128)(2,1)S(1)}, u32[]{:S(2)}, u32[]{:S(2)}) %collective-permute-start.12) | collective-permute-done | bytes 262176 | tf_op jit(solution)/shard_map/ppermute | solution.py:22
  86.4 3.4 %collective-permute-start.16 = (bf16[4,128,256]{2,1,0:T(8,128)(2,1)S(1)}, bf16[4,128,256]{2,1,0:T(8,128)(2,1)S(1)}, u32[]{:S(2)}, u32[]{:S(2)}) collective-permute-start(bf16[4,128,256]{2,1,0:T(8,128)(2,1)S(1)} %fusion.3), channel_id=1, source_target_pairs={{0,4},{1,5},{2,6},{3,7},{4,0},{5,1},{6,2},{7,3},{8,12},{9,13},{10,... | collective-permute-start | bytes 786440 | tf_op jit(solution)/shard_map/ppermute | solution.py:22
  91.4 6.7 %collective-permute-done.17.refs_6_ = bf16[1024,256]{1,0:T(8,128)(2,1)S(1)} collective-permute-done((bf16[1024,256]{1,0:T(8,128)(2,1)S(1)}, bf16[1024,256]{1,0:T(8,128)(2,1)S(1)}, u32[]{:S(2)}, u32[]{:S(2)}) %collective-permute-start.17) | collective-permute-done | bytes 524320 | tf_op jit(solution)/shard_map/ppermute | solution.py:22
  98.3 9.7 %collective-permute-done.18.refs_7_ = bf16[1024,256]{1,0:T(8,128)(2,1)S(1)} collective-permute-done((bf16[1024,256]{1,0:T(8,128)(2,1)S(1)}, bf16[1024,256]{1,0:T(8,128)(2,1)S(1)}, u32[]{:S(2)}, u32[]{:S(2)}) %collective-permute-start.18) | collective-permute-done | bytes 524320 | tf_op jit(solution)/shard_map/ppermute | solution.py:22
  108.0 2.1 %shard_map.40 = (f32[2,4,128,256]{3,2,1,0:T(8,128)S(1)}, bf16[2,4,128,256]{3,2,1,0:T(8,128)(2,1)S(1)}) custom-call(s32[9]{0:T(128)S(1)} %pad_add_fusion.2.choices_ref, bf16[2,512,1024]{2,1,0:T(8,128)(2,1)S(1)} %shard_map.37.lefts_ref, bf16[1024,256]{1,0:T(8,128)(2,1)S(1)} %multiply_convert_fusion.2.refs_1_.refs_0_, ...), custom_call_target="tpu_custom_call" | custom-call | tf_op jit(solution)/shard_map/pallas_call | solution.py:115
  110.3 2.2 %shard_map.41 = (f32[2,4,128,256]{3,2,1,0:T(8,128)S(1)}, bf16[2,4,128,256]{3,2,1,0:T(8,128)(2,1)S(1)}) custom-call(s32[9]{0:T(128)S(1)} %pad_add_fusion.2.choices_ref, bf16[2,512,1024]{2,1,0:T(8,128)(2,1)S(1)} %shard_map.37.lefts_ref, bf16[1024,256]{1,0:T(8,128)(2,1)S(1)} %multiply_convert_fusion.2.refs_1_.refs_0_, ...), custom_call_target="tpu_custom_call" | custom-call | tf_op jit(solution)/shard_map/pallas_call | solution.py:115
  113.2 1.6 %collective-permute-start.21 = (bf16[1,4,128,256]{3,2,1,0:T(8,128)(2,1)S(1)}, bf16[1,4,128,256]{3,2,1,0:T(8,128)(2,1)S(1)}, u32[]{:S(2)}, u32[]{:S(2)}) collective-permute-start(bf16[1,4,128,256]{3,2,1,0:T(8,128)(2,1)S(1)} %slice.70), channel_id=1, source_target_pairs={{0,16},{8,24},{16,0},{24,8},{1,17},{9,25},{17,1},{25,9},{2,18},{10... | collective-permute-start | bytes 786440 | tf_op jit(solution)/shard_map/ppermute | solution.py:22
  114.9 6.6 %collective-permute-done.21 = bf16[1,4,128,256]{3,2,1,0:T(8,128)(2,1)S(1)} collective-permute-done((bf16[1,4,128,256]{3,2,1,0:T(8,128)(2,1)S(1)}, bf16[1,4,128,256]{3,2,1,0:T(8,128)(2,1)S(1)}, u32[]{:S(2)}, u32[]{:S(2)}) %collective-permute-start.21) | collective-permute-done | bytes 262176 | tf_op jit(solution)/shard_map/ppermute | solution.py:22
  121.5 3.5 %collective-permute-start.23 = (bf16[4,128,256]{2,1,0:T(8,128)(2,1)S(1)}, bf16[4,128,256]{2,1,0:T(8,128)(2,1)S(1)}, u32[]{:S(2)}, u32[]{:S(2)}) collective-permute-start(bf16[4,128,256]{2,1,0:T(8,128)(2,1)S(1)} %fusion), channel_id=1, source_target_pairs={{0,4},{1,5},{2,6},{3,7},{4,0},{5,1},{6,2},{7,3},{8,12},{9,13},{10,... | collective-permute-start | bytes 786440 | tf_op jit(solution)/shard_map/ppermute | solution.py:22
  126.5 9.7 %collective-permute-done.23 = bf16[4,128,256]{2,1,0:T(8,128)(2,1)S(1)} collective-permute-done((bf16[4,128,256]{2,1,0:T(8,128)(2,1)S(1)}, bf16[4,128,256]{2,1,0:T(8,128)(2,1)S(1)}, u32[]{:S(2)}, u32[]{:S(2)}) %collective-permute-start.23) | collective-permute-done | bytes 262176 | tf_op jit(solution)/shard_map/ppermute | solution.py:22
  (68 shorter events, 19.1 us)
Async XLA Ops:
  2.4 27.4 %collective-permute-start = (bf16[1024,256]{1,0:T(8,128)(2,1)S(1)}, bf16[1024,256]{1,0:T(8,128)(2,1)S(1)}, u32[]{:S(2)}, u32[]{:S(2)}) collective-permute-start(bf16[1024,256]{1,0:T(8,128)(2,1)S(1)} %get-tuple-element.59), channel_id=1, source_target_pairs={{0,4},{1,5},{2,6},{3,7},{4,0},{5,1},{6,2},{7,3},{8,12},{9,13},{10,... | collective-permute-start | bytes 1572872 | tf_op jit(solution)/shard_map/ppermute | solution.py:22
  6.5 23.5 %collective-permute-start.1 = (bf16[1024,256]{1,0:T(8,128)(2,1)S(1)}, bf16[1024,256]{1,0:T(8,128)(2,1)S(1)}, u32[]{:S(2)}, u32[]{:S(2)}) collective-permute-start(bf16[1024,256]{1,0:T(8,128)(2,1)S(1)} %get-tuple-element.60.refs_0_), channel_id=1, source_target_pairs={{0,2},{1,3},{2,0},{3,1},{4,6},{5,7},{6,4},{7,5},{8,10},{9,11},{10,... | collective-permute-start | bytes 1572872 | tf_op jit(solution)/shard_map/ppermute | solution.py:22
  8.3 23.2 %collective-permute-start.6 = (bf16[1024,256]{1,0:T(8,128)(2,1)S(1)}, bf16[1024,256]{1,0:T(8,128)(2,1)S(1)}, u32[]{:S(2)}, u32[]{:S(2)}) collective-permute-start(bf16[1024,256]{1,0:T(8,128)(2,1)S(1)} %multiply_convert_fusion.2.refs_1_.refs_0_), channel_id=1, source_target_pairs={{0,1},{1,0},{2,3},{3,2},{4,5},{5,4},{6,7},{7,6},{8,9},{9,8},{10,11... | collective-permute-start | bytes 1572872 | tf_op jit(solution)/shard_map/ppermute | solution.py:22
  9.9 26.4 %collective-permute-start.5 = (bf16[1024,256]{1,0:T(8,128)(2,1)S(1)}, bf16[1024,256]{1,0:T(8,128)(2,1)S(1)}, u32[]{:S(2)}, u32[]{:S(2)}) collective-permute-start(bf16[1024,256]{1,0:T(8,128)(2,1)S(1)} %get-tuple-element.60.refs_0_), channel_id=1, source_target_pairs={{0,1},{1,0},{2,3},{3,2},{4,5},{5,4},{6,7},{7,6},{8,9},{9,8},{10,11... | collective-permute-start | bytes 1572872 | tf_op jit(solution)/shard_map/ppermute | solution.py:22
  30.0 21.6 %collective-permute-start.2 = (bf16[1024,256]{1,0:T(8,128)(2,1)S(1)}, bf16[1024,256]{1,0:T(8,128)(2,1)}, u32[]{:S(2)}, u32[]{:S(2)}) collective-permute-start(bf16[1024,256]{1,0:T(8,128)(2,1)S(1)} %collective-permute-done.refs_2_.refs_4_), channel_id=1, source_target_pairs={{0,2},{1,3},{2,0},{3,1},{4,6},{5,7},{6,4},{7,5},{8,10},{9,11},{10,... | collective-permute-start | bytes 1572872 | tf_op jit(solution)/shard_map/ppermute | solution.py:22
  31.5 20.1 %collective-permute-start.7 = (bf16[1024,256]{1,0:T(8,128)(2,1)S(1)}, bf16[1024,256]{1,0:T(8,128)(2,1)S(1)}, u32[]{:S(2)}, u32[]{:S(2)}) collective-permute-start(bf16[1024,256]{1,0:T(8,128)(2,1)S(1)} %collective-permute-done.1.refs_2_), channel_id=1, source_target_pairs={{0,1},{1,0},{2,3},{3,2},{4,5},{5,4},{6,7},{7,6},{8,9},{9,8},{10,11... | collective-permute-start | bytes 1572872 | tf_op jit(solution)/shard_map/ppermute | solution.py:22
  34.0 25.5 %collective-permute-start.4 = (bf16[1024,256]{1,0:T(8,128)(2,1)}, bf16[1024,256]{1,0:T(8,128)(2,1)S(1)}, u32[]{:S(2)}, u32[]{:S(2)}) collective-permute-start(bf16[1024,256]{1,0:T(8,128)(2,1)} %multiply_convert_fusion), channel_id=1, source_target_pairs={{0,4},{1,5},{2,6},{3,7},{4,0},{5,1},{6,2},{7,3},{8,12},{9,13},{10,... | collective-permute-start | bytes 1572872 | tf_op jit(solution)/shard_map/ppermute | solution.py:22
  37.1 22.3 %collective-permute-start.8 = (bf16[1024,256]{1,0:T(8,128)(2,1)S(1)}, bf16[1024,256]{1,0:T(8,128)(2,1)}, u32[]{:S(2)}, u32[]{:S(2)}) collective-permute-start(bf16[1024,256]{1,0:T(8,128)(2,1)S(1)} %collective-permute-done.refs_2_.refs_4_), channel_id=1, source_target_pairs={{0,1},{1,0},{2,3},{3,2},{4,5},{5,4},{6,7},{7,6},{8,9},{9,8},{10,11... | collective-permute-start | bytes 1572872 | tf_op jit(solution)/shard_map/ppermute | solution.py:22
  51.5 14.6 %collective-permute-start.3 = (bf16[1024,256]{1,0:T(8,128)(2,1)S(1)}, bf16[1024,256]{1,0:T(8,128)(2,1)S(1)}, u32[]{:S(2)}, u32[]{:S(2)}) collective-permute-start(bf16[1024,256]{1,0:T(8,128)(2,1)S(1)} %multiply_convert_fusion.2.refs_1_.refs_0_), channel_id=1, source_target_pairs={{0,2},{1,3},{2,0},{3,1},{4,6},{5,7},{6,4},{7,5},{8,10},{9,11},{10,... | collective-permute-start | bytes 1572872 | tf_op jit(solution)/shard_map/ppermute | solution.py:22
  52.3 16.0 %collective-permute-start.9 = (bf16[1024,256]{1,0:T(8,128)(2,1)}, bf16[1024,256]{1,0:T(8,128)(2,1)}, u32[]{:S(2)}, u32[]{:S(2)}) collective-permute-start(bf16[1024,256]{1,0:T(8,128)(2,1)} %collective-permute-done.2.refs_6_), channel_id=1, source_target_pairs={{0,1},{1,0},{2,3},{3,2},{4,5},{5,4},{6,7},{7,6},{8,9},{9,8},{10,11... | collective-permute-start | bytes 1572872 | tf_op jit(solution)/shard_map/ppermute | solution.py:22
  59.4 18.3 %collective-permute-start.13 = (bf16[1024,256]{1,0:T(8,128)(2,1)S(1)}, bf16[1024,256]{1,0:T(8,128)(2,1)S(1)}, u32[]{:S(2)}, u32[]{:S(2)}) collective-permute-start(bf16[1024,256]{1,0:T(8,128)(2,1)S(1)} %collective-permute-done.4.refs_3_.refs_4_), channel_id=1, source_target_pairs={{0,1},{1,0},{2,3},{3,2},{4,5},{5,4},{6,7},{7,6},{8,9},{9,8},{10,11... | collective-permute-start | bytes 1572872 | tf_op jit(solution)/shard_map/ppermute | solution.py:22
  71.3 8.3 %collective-permute-start.11 = (bf16[2,4,128,256]{3,2,1,0:T(8,128)(2,1)S(1)}, bf16[2,4,128,256]{3,2,1,0:T(8,128)(2,1)S(1)}, u32[]{:S(2)}, u32[]{:S(2)}) collective-permute-start(bf16[2,4,128,256]{3,2,1,0:T(8,128)(2,1)S(1)} %get-tuple-element.40), channel_id=1, source_target_pairs={{0,8},{8,0},{16,24},{24,16},{1,9},{9,1},{17,25},{25,17},{2,10},{10... | collective-permute-start | bytes 1572872 | tf_op jit(solution)/shard_map/ppermute | solution.py:22
  74.4 7.0 %collective-permute-start.10 = (bf16[2,4,128,256]{3,2,1,0:T(8,128)(2,1)S(1)}, bf16[2,4,128,256]{3,2,1,0:T(8,128)(2,1)S(1)}, u32[]{:S(2)}, u32[]{:S(2)}) collective-permute-start(bf16[2,4,128,256]{3,2,1,0:T(8,128)(2,1)S(1)} %get-tuple-element.43), channel_id=1, source_target_pairs={{0,8},{8,0},{16,24},{24,16},{1,9},{9,1},{17,25},{25,17},{2,10},{10... | collective-permute-start | bytes 1572872 | tf_op jit(solution)/shard_map/ppermute | solution.py:22
  77.7 12.2 %collective-permute-start.14 = (bf16[1024,256]{1,0:T(8,128)(2,1)S(1)}, bf16[1024,256]{1,0:T(8,128)(2,1)S(1)}, u32[]{:S(2)}, u32[]{:S(2)}) collective-permute-start(bf16[1024,256]{1,0:T(8,128)(2,1)S(1)} %collective-permute-done.3.refs_2_), channel_id=1, source_target_pairs={{0,1},{1,0},{2,3},{3,2},{4,5},{5,4},{6,7},{7,6},{8,9},{9,8},{10,11... | collective-permute-start | bytes 1572872 | tf_op jit(solution)/shard_map/ppermute | solution.py:22
  79.2 19.0 %collective-permute-start.17 = (bf16[1024,256]{1,0:T(8,128)(2,1)S(1)}, bf16[1024,256]{1,0:T(8,128)(2,1)S(1)}, u32[]{:S(2)}, u32[]{:S(2)}) collective-permute-start(bf16[1024,256]{1,0:T(8,128)(2,1)S(1)} %collective-permute-done.4.refs_3_.refs_4_), channel_id=1, source_target_pairs={{0,2},{1,3},{2,0},{3,1},{4,6},{5,7},{6,4},{7,5},{8,10},{9,11},{10,... | collective-permute-start | bytes 1572872 | tf_op jit(solution)/shard_map/ppermute | solution.py:22
  79.7 6.6 %collective-permute-start.12 = (bf16[1,4,128,256]{3,2,1,0:T(8,128)(2,1)S(1)}, bf16[1,4,128,256]{3,2,1,0:T(8,128)(2,1)S(1)}, u32[]{:S(2)}, u32[]{:S(2)}) collective-permute-start(bf16[1,4,128,256]{3,2,1,0:T(8,128)(2,1)S(1)} %slice.72), channel_id=1, source_target_pairs={{0,16},{8,24},{16,0},{24,8},{1,17},{9,25},{17,1},{25,9},{2,18},{10... | collective-permute-start | bytes 786440 | tf_op jit(solution)/shard_map/ppermute | solution.py:22
  86.4 11.7 %collective-permute-start.16 = (bf16[4,128,256]{2,1,0:T(8,128)(2,1)S(1)}, bf16[4,128,256]{2,1,0:T(8,128)(2,1)S(1)}, u32[]{:S(2)}, u32[]{:S(2)}) collective-permute-start(bf16[4,128,256]{2,1,0:T(8,128)(2,1)S(1)} %fusion.3), channel_id=1, source_target_pairs={{0,4},{1,5},{2,6},{3,7},{4,0},{5,1},{6,2},{7,3},{8,12},{9,13},{10,... | collective-permute-start | bytes 786440 | tf_op jit(solution)/shard_map/ppermute | solution.py:22
  89.9 8.3 %collective-permute-start.15 = (bf16[1,4,128,256]{3,2,1,0:T(8,128)(2,1)S(1)}, bf16[1,4,128,256]{3,2,1,0:T(8,128)(2,1)S(1)}, u32[]{:S(2)}, u32[]{:S(2)}) collective-permute-start(bf16[1,4,128,256]{3,2,1,0:T(8,128)(2,1)S(1)} %slice.73), channel_id=1, source_target_pairs={{0,16},{8,24},{16,0},{24,8},{1,17},{9,25},{17,1},{25,9},{2,18},{10... | collective-permute-start | bytes 786440 | tf_op jit(solution)/shard_map/ppermute | solution.py:22
  98.1 9.9 %collective-permute-start.18 = (bf16[1024,256]{1,0:T(8,128)(2,1)S(1)}, bf16[1024,256]{1,0:T(8,128)(2,1)S(1)}, u32[]{:S(2)}, u32[]{:S(2)}) collective-permute-start(bf16[1024,256]{1,0:T(8,128)(2,1)S(1)} %collective-permute-done.13.refs_5_), channel_id=1, source_target_pairs={{0,2},{1,3},{2,0},{3,1},{4,6},{5,7},{6,4},{7,5},{8,10},{9,11},{10,... | collective-permute-start | bytes 1572872 | tf_op jit(solution)/shard_map/ppermute | solution.py:22
  110.2 2.8 %collective-permute-start.20 = (bf16[2,4,128,256]{3,2,1,0:T(8,128)(2,1)S(1)}, bf16[2,4,128,256]{3,2,1,0:T(8,128)(2,1)S(1)}, u32[]{:S(2)}, u32[]{:S(2)}) collective-permute-start(bf16[2,4,128,256]{3,2,1,0:T(8,128)(2,1)S(1)} %get-tuple-element.51), channel_id=1, source_target_pairs={{0,8},{8,0},{16,24},{24,16},{1,9},{9,1},{17,25},{25,17},{2,10},{10... | collective-permute-start | bytes 1572872 | tf_op jit(solution)/shard_map/ppermute | solution.py:22
  112.4 2.3 %collective-permute-start.19 = (bf16[2,4,128,256]{3,2,1,0:T(8,128)(2,1)S(1)}, bf16[2,4,128,256]{3,2,1,0:T(8,128)(2,1)S(1)}, u32[]{:S(2)}, u32[]{:S(2)}) collective-permute-start(bf16[2,4,128,256]{3,2,1,0:T(8,128)(2,1)S(1)} %get-tuple-element.54), channel_id=1, source_target_pairs={{0,8},{8,0},{16,24},{24,16},{1,9},{9,1},{17,25},{25,17},{2,10},{10... | collective-permute-start | bytes 1572872 | tf_op jit(solution)/shard_map/ppermute | solution.py:22
  113.2 8.3 %collective-permute-start.21 = (bf16[1,4,128,256]{3,2,1,0:T(8,128)(2,1)S(1)}, bf16[1,4,128,256]{3,2,1,0:T(8,128)(2,1)S(1)}, u32[]{:S(2)}, u32[]{:S(2)}) collective-permute-start(bf16[1,4,128,256]{3,2,1,0:T(8,128)(2,1)S(1)} %slice.70), channel_id=1, source_target_pairs={{0,16},{8,24},{16,0},{24,8},{1,17},{9,25},{17,1},{25,9},{2,18},{10... | collective-permute-start | bytes 786440 | tf_op jit(solution)/shard_map/ppermute | solution.py:22
  121.5 14.8 %collective-permute-start.23 = (bf16[4,128,256]{2,1,0:T(8,128)(2,1)S(1)}, bf16[4,128,256]{2,1,0:T(8,128)(2,1)S(1)}, u32[]{:S(2)}, u32[]{:S(2)}) collective-permute-start(bf16[4,128,256]{2,1,0:T(8,128)(2,1)S(1)} %fusion), channel_id=1, source_target_pairs={{0,4},{1,5},{2,6},{3,7},{4,0},{5,1},{6,2},{7,3},{8,12},{9,13},{10,... | collective-permute-start | bytes 786440 | tf_op jit(solution)/shard_map/ppermute | solution.py:22
  125.0 11.3 %collective-permute-start.22 = (bf16[1,4,128,256]{3,2,1,0:T(8,128)(2,1)S(1)}, bf16[1,4,128,256]{3,2,1,0:T(8,128)(2,1)S(1)}, u32[]{:S(2)}, u32[]{:S(2)}) collective-permute-start(bf16[1,4,128,256]{3,2,1,0:T(8,128)(2,1)S(1)} %slice.71), channel_id=1, source_target_pairs={{0,16},{8,24},{16,0},{24,8},{1,17},{9,25},{17,1},{25,9},{2,18},{10... | collective-permute-start | bytes 786440 | tf_op jit(solution)/shard_map/ppermute | solution.py:22
  (8 other events, 125.4 us)

commit v16 on v15

--- a/solution.py
+++ b/solution.py
@@ -11,7 +11,7 @@
 OWN_WIDTHS = (2, 2)
 CROSSING_WIDTHS = (2, 2)
 MATE_WIDTHS = (2, 2)
-NEAR_FIRST = (3,)
+NEAR_FIRST = ()
 URGENCY = (0, 2, 1, 3)
 BATCHES = (((0,), (2,)), ((1,), (3,)))
 VMEM = pl.BlockSpec(memory_space=pltpu.VMEM)

time: 138 us -> 134 us (0.971)
  starting transfers between devices: 32.6 us -> 30.2 us
  waiting for transfers between devices: 86.4 us -> 84.9 us
    ppermute x24, starting transfers between devices: 32.6 us -> 30.2 us  [exchange(): lax.ppermute(part, axis, [(i, i ^ mask) for i in range(lax.axis_size(axis...]
    ppermute x24, waiting for transfers between devices: 86.4 us -> 84.9 us  [exchange(): lax.ppermute(part, axis, [(i, i ^ mask) for i in range(lax.axis_size(axis...]
  transfers between devices with their start and end apart: 24 -> 24, of which waited for: 13 -> 13; matrix products, arithmetic and copies ran while one was open for 2% -> 2% of each run, Pallas kernels for 6% -> 7%
where the time goes in v16:
time: 134 us
  waiting for transfers between devices  84.9 us (63%)
  starting transfers between devices  30.2 us (23%)
  Pallas kernels  10.9 us (8%)
  other arithmetic  5.01 us (4%)
  local copies, waits for them, and re-layouts  2.43 us (2%)
    ppermute x24, waiting for transfers between devices, exchange(): lax.ppermute(part, axis, [(i, i ^ mask) for i in range(lax.axis_size(axis...  84.9 us
    ppermute x24, starting transfers between devices, exchange(): lax.ppermute(part, axis, [(i, i ^ mask) for i in range(lax.axis_size(axis...  30.2 us
    pallas_call x4, Pallas kernels, products(): pl.pallas_call(kernel, out_shape=[jax.ShapeDtypeStruct(shape, kind) for k...  10.3 us
    convert_element_type x3, other arithmetic, pieces_of(): found.append((part.astype(jnp.float32) * scale).astype(jnp.bfloat16))  2.89 us
  transfers between devices with their start and end apart: 24, of which 13 were waited for; matrix products, arithmetic and copies ran while one was open for 2% of the time, Pallas kernels for 7%

profile of v16, /device:TPU:0, one launch (start us, length us, event | category | flops | bytes accessed | tf_op | source)
XLA Modules:
  0.0 133.7 jit_solution(1560951940429858275)
XLA Ops:
  0.7 1.7 %multiply_convert_fusion.1 = (bf16[1024,256]{1,0:T(8,128)(2,1)S(1)}, bf16[1024,256]{1,0:T(8,128)(2,1)S(1)}) fusion(f32[1024]{0:T(1024)S(1)} %get-tuple-element.61, bf16[2048,512]{1,0:T(8,128)(2,1)} %param.3, s32[]{:T(128)S(6)} %select_n.2, f32[1024]{0:T(1024)S(1)} %get-tuple-element.62, s32[]{:T(128)S(6)} %mul.16), kind=kLoop, calls=%fused_computation.6 | loop fusion | flops 1572864 | bytes 2105352 | tf_op jit(solution)/shard_map/convert_element_type | solution.py:160
  2.4 4.1 %collective-permute-start = (bf16[1024,256]{1,0:T(8,128)(2,1)S(1)}, bf16[1024,256]{1,0:T(8,128)(2,1)S(1)}, u32[]{:S(2)}, u32[]{:S(2)}) collective-permute-start(bf16[1024,256]{1,0:T(8,128)(2,1)S(1)} %get-tuple-element.59), channel_id=1, source_target_pairs={{0,4},{1,5},{2,6},{3,7},{4,0},{5,1},{6,2},{7,3},{8,12},{9,13},{10,... | collective-permute-start | bytes 1572872 | tf_op jit(solution)/shard_map/ppermute | solution.py:22
  6.5 1.6 %collective-permute-start.1 = (bf16[1024,256]{1,0:T(8,128)(2,1)S(1)}, bf16[1024,256]{1,0:T(8,128)(2,1)S(1)}, u32[]{:S(2)}, u32[]{:S(2)}) collective-permute-start(bf16[1024,256]{1,0:T(8,128)(2,1)S(1)} %get-tuple-element.60.refs_0_), channel_id=1, source_target_pairs={{0,2},{1,3},{2,0},{3,1},{4,6},{5,7},{6,4},{7,5},{8,10},{9,11},{10,... | collective-permute-start | bytes 1572872 | tf_op jit(solution)/shard_map/ppermute | solution.py:22
  8.3 1.6 %collective-permute-start.6 = (bf16[1024,256]{1,0:T(8,128)(2,1)S(1)}, bf16[1024,256]{1,0:T(8,128)(2,1)S(1)}, u32[]{:S(2)}, u32[]{:S(2)}) collective-permute-start(bf16[1024,256]{1,0:T(8,128)(2,1)S(1)} %multiply_convert_fusion.2.refs_1_.refs_0_), channel_id=1, source_target_pairs={{0,1},{1,0},{2,3},{3,2},{4,5},{5,4},{6,7},{7,6},{8,9},{9,8},{10,11... | collective-permute-start | bytes 1572872 | tf_op jit(solution)/shard_map/ppermute | solution.py:22
  10.4 19.4 %collective-permute-done.refs_2_.refs_4_ = bf16[1024,256]{1,0:T(8,128)(2,1)S(1)} collective-permute-done((bf16[1024,256]{1,0:T(8,128)(2,1)S(1)}, bf16[1024,256]{1,0:T(8,128)(2,1)S(1)}, u32[]{:S(2)}, u32[]{:S(2)}) %collective-permute-start) | collective-permute-done | bytes 524320 | tf_op jit(solution)/shard_map/ppermute | solution.py:22
  34.0 2.3 %collective-permute-start.4 = (bf16[1024,256]{1,0:T(8,128)(2,1)}, bf16[1024,256]{1,0:T(8,128)(2,1)S(1)}, u32[]{:S(2)}, u32[]{:S(2)}) collective-permute-start(bf16[1024,256]{1,0:T(8,128)(2,1)} %multiply_convert_fusion), channel_id=1, source_target_pairs={{0,4},{1,5},{2,6},{3,7},{4,0},{5,1},{6,2},{7,3},{8,12},{9,13},{10,... | collective-permute-start | bytes 1572872 | tf_op jit(solution)/shard_map/ppermute | solution.py:22
  37.6 13.9 %collective-permute-done.2.refs_6_ = bf16[1024,256]{1,0:T(8,128)(2,1)} collective-permute-done((bf16[1024,256]{1,0:T(8,128)(2,1)S(1)}, bf16[1024,256]{1,0:T(8,128)(2,1)}, u32[]{:S(2)}, u32[]{:S(2)}) %collective-permute-start.2) | collective-permute-done | bytes 524320 | tf_op jit(solution)/shard_map/ppermute | solution.py:22
  52.3 2.2 %collective-permute-start.9 = (bf16[1024,256]{1,0:T(8,128)(2,1)}, bf16[1024,256]{1,0:T(8,128)(2,1)}, u32[]{:S(2)}, u32[]{:S(2)}) collective-permute-start(bf16[1024,256]{1,0:T(8,128)(2,1)} %collective-permute-done.2.refs_6_), channel_id=1, source_target_pairs={{0,1},{1,0},{2,3},{3,2},{4,5},{5,4},{6,7},{7,6},{8,9},{9,8},{10,11... | collective-permute-start | bytes 1572872 | tf_op jit(solution)/shard_map/ppermute | solution.py:22
  54.6 4.8 %collective-permute-done.4.refs_3_.refs_4_ = bf16[1024,256]{1,0:T(8,128)(2,1)S(1)} collective-permute-done((bf16[1024,256]{1,0:T(8,128)(2,1)}, bf16[1024,256]{1,0:T(8,128)(2,1)S(1)}, u32[]{:S(2)}, u32[]{:S(2)}) %collective-permute-start.4) | collective-permute-done | bytes 524320 | tf_op jit(solution)/shard_map/ppermute | solution.py:22
  60.6 5.5 %collective-permute-done.3.refs_2_ = bf16[1024,256]{1,0:T(8,128)(2,1)S(1)} collective-permute-done((bf16[1024,256]{1,0:T(8,128)(2,1)S(1)}, bf16[1024,256]{1,0:T(8,128)(2,1)S(1)}, u32[]{:S(2)}, u32[]{:S(2)}) %collective-permute-start.3) | collective-permute-done | bytes 524320 | tf_op jit(solution)/shard_map/ppermute | solution.py:22
  66.2 2.1 %collective-permute-done.9.refs_7_ = bf16[1024,256]{1,0:T(8,128)(2,1)} collective-permute-done((bf16[1024,256]{1,0:T(8,128)(2,1)}, bf16[1024,256]{1,0:T(8,128)(2,1)}, u32[]{:S(2)}, u32[]{:S(2)}) %collective-permute-start.9) | collective-permute-done | bytes 524320 | tf_op jit(solution)/shard_map/ppermute | solution.py:22
  68.3 3.0 %shard_map.38 = (f32[2,4,128,256]{3,2,1,0:T(8,128)S(1)}, bf16[2,4,128,256]{3,2,1,0:T(8,128)(2,1)S(1)}) custom-call(s32[9]{0:T(128)S(1)} %pad_add_fusion.1.choices_ref, bf16[2,512,1024]{2,1,0:T(8,128)(2,1)S(1)} %shard_map.37.lefts_ref, bf16[1024,256]{1,0:T(8,128)(2,1)S(1)} %get-tuple-element.60.refs_0_, bf16[1024,256]{1,0:T(8,128)(2,1)S(1)} %copy-done.3, ...), custom_call_target="tpu_custom_call" | custom-call | tf_op jit(solution)/shard_map/pallas_call | solution.py:115
  71.4 3.0 %shard_map.39 = (f32[2,4,128,256]{3,2,1,0:T(8,128)S(1)}, bf16[2,4,128,256]{3,2,1,0:T(8,128)(2,1)S(1)}) custom-call(s32[9]{0:T(128)S(1)} %pad_add_fusion.1.choices_ref, bf16[2,512,1024]{2,1,0:T(8,128)(2,1)S(1)} %shard_map.37.lefts_ref, bf16[1024,256]{1,0:T(8,128)(2,1)S(1)} %get-tuple-element.60.refs_0_, bf16[1024,256]{1,0:T(8,128)(2,1)S(1)} %copy-done.3, ...), custom_call_target="tpu_custom_call" | custom-call | tf_op jit(solution)/shard_map/pallas_call | solution.py:115
  74.9 2.8 %collective-permute-done.13.refs_5_ = bf16[1024,256]{1,0:T(8,128)(2,1)S(1)} collective-permute-done((bf16[1024,256]{1,0:T(8,128)(2,1)S(1)}, bf16[1024,256]{1,0:T(8,128)(2,1)S(1)}, u32[]{:S(2)}, u32[]{:S(2)}) %collective-permute-start.13) | collective-permute-done | bytes 524320 | tf_op jit(solution)/shard_map/ppermute | solution.py:22
  79.7 1.6 %collective-permute-start.12 = (bf16[1,4,128,256]{3,2,1,0:T(8,128)(2,1)S(1)}, bf16[1,4,128,256]{3,2,1,0:T(8,128)(2,1)S(1)}, u32[]{:S(2)}, u32[]{:S(2)}) collective-permute-start(bf16[1,4,128,256]{3,2,1,0:T(8,128)(2,1)S(1)} %slice.72), channel_id=1, source_target_pairs={{0,16},{8,24},{16,0},{24,8},{1,17},{9,25},{17,1},{25,9},{2,18},{10... | collective-permute-start | bytes 786440 | tf_op jit(solution)/shard_map/ppermute | solution.py:22
  81.5 4.8 %collective-permute-done.12 = bf16[1,4,128,256]{3,2,1,0:T(8,128)(2,1)S(1)} collective-permute-done((bf16[1,4,128,256]{3,2,1,0:T(8,128)(2,1)S(1)}, bf16[1,4,128,256]{3,2,1,0:T(8,128)(2,1)S(1)}, u32[]{:S(2)}, u32[]{:S(2)}) %collective-permute-start.12) | collective-permute-done | bytes 262176 | tf_op jit(solution)/shard_map/ppermute | solution.py:22
  86.4 3.4 %collective-permute-start.16 = (bf16[4,128,256]{2,1,0:T(8,128)(2,1)S(1)}, bf16[4,128,256]{2,1,0:T(8,128)(2,1)S(1)}, u32[]{:S(2)}, u32[]{:S(2)}) collective-permute-start(bf16[4,128,256]{2,1,0:T(8,128)(2,1)S(1)} %fusion.3), channel_id=1, source_target_pairs={{0,4},{1,5},{2,6},{3,7},{4,0},{5,1},{6,2},{7,3},{8,12},{9,13},{10,... | collective-permute-start | bytes 786440 | tf_op jit(solution)/shard_map/ppermute | solution.py:22
  91.4 5.2 %collective-permute-done.17.refs_6_ = bf16[1024,256]{1,0:T(8,128)(2,1)S(1)} collective-permute-done((bf16[1024,256]{1,0:T(8,128)(2,1)S(1)}, bf16[1024,256]{1,0:T(8,128)(2,1)S(1)}, u32[]{:S(2)}, u32[]{:S(2)}) %collective-permute-start.17) | collective-permute-done | bytes 524320 | tf_op jit(solution)/shard_map/ppermute | solution.py:22
  97.2 8.7 %collective-permute-done.18.refs_7_ = bf16[1024,256]{1,0:T(8,128)(2,1)S(1)} collective-permute-done((bf16[1024,256]{1,0:T(8,128)(2,1)S(1)}, bf16[1024,256]{1,0:T(8,128)(2,1)S(1)}, u32[]{:S(2)}, u32[]{:S(2)}) %collective-permute-start.18) | collective-permute-done | bytes 524320 | tf_op jit(solution)/shard_map/ppermute | solution.py:22
  105.8 2.1 %shard_map.40 = (f32[2,4,128,256]{3,2,1,0:T(8,128)S(1)}, bf16[2,4,128,256]{3,2,1,0:T(8,128)(2,1)S(1)}) custom-call(s32[9]{0:T(128)S(1)} %pad_add_fusion.2.choices_ref, bf16[2,512,1024]{2,1,0:T(8,128)(2,1)S(1)} %shard_map.37.lefts_ref, bf16[1024,256]{1,0:T(8,128)(2,1)S(1)} %multiply_convert_fusion.2.refs_1_.refs_0_, ...), custom_call_target="tpu_custom_call" | custom-call | tf_op jit(solution)/shard_map/pallas_call | solution.py:115
  108.1 2.2 %shard_map.41 = (f32[2,4,128,256]{3,2,1,0:T(8,128)S(1)}, bf16[2,4,128,256]{3,2,1,0:T(8,128)(2,1)S(1)}) custom-call(s32[9]{0:T(128)S(1)} %pad_add_fusion.2.choices_ref, bf16[2,512,1024]{2,1,0:T(8,128)(2,1)S(1)} %shard_map.37.lefts_ref, bf16[1024,256]{1,0:T(8,128)(2,1)S(1)} %multiply_convert_fusion.2.refs_1_.refs_0_, ...), custom_call_target="tpu_custom_call" | custom-call | tf_op jit(solution)/shard_map/pallas_call | solution.py:115
  111.0 1.6 %collective-permute-start.21 = (bf16[1,4,128,256]{3,2,1,0:T(8,128)(2,1)S(1)}, bf16[1,4,128,256]{3,2,1,0:T(8,128)(2,1)S(1)}, u32[]{:S(2)}, u32[]{:S(2)}) collective-permute-start(bf16[1,4,128,256]{3,2,1,0:T(8,128)(2,1)S(1)} %slice.70), channel_id=1, source_target_pairs={{0,16},{8,24},{16,0},{24,8},{1,17},{9,25},{17,1},{25,9},{2,18},{10... | collective-permute-start | bytes 786440 | tf_op jit(solution)/shard_map/ppermute | solution.py:22
  112.7 6.6 %collective-permute-done.21 = bf16[1,4,128,256]{3,2,1,0:T(8,128)(2,1)S(1)} collective-permute-done((bf16[1,4,128,256]{3,2,1,0:T(8,128)(2,1)S(1)}, bf16[1,4,128,256]{3,2,1,0:T(8,128)(2,1)S(1)}, u32[]{:S(2)}, u32[]{:S(2)}) %collective-permute-start.21) | collective-permute-done | bytes 262176 | tf_op jit(solution)/shard_map/ppermute | solution.py:22
  121.7 10.8 %collective-permute-done.23 = bf16[4,128,256]{2,1,0:T(8,128)(2,1)S(1)} collective-permute-done((bf16[4,128,256]{2,1,0:T(8,128)(2,1)S(1)}, bf16[4,128,256]{2,1,0:T(8,128)(2,1)S(1)}, u32[]{:S(2)}, u32[]{:S(2)}) %collective-permute-start.23) | collective-permute-done | bytes 262176 | tf_op jit(solution)/shard_map/ppermute | solution.py:22
  (68 shorter events, 18.7 us)
Async XLA Ops:
  2.4 27.4 %collective-permute-start = (bf16[1024,256]{1,0:T(8,128)(2,1)S(1)}, bf16[1024,256]{1,0:T(8,128)(2,1)S(1)}, u32[]{:S(2)}, u32[]{:S(2)}) collective-permute-start(bf16[1024,256]{1,0:T(8,128)(2,1)S(1)} %get-tuple-element.59), channel_id=1, source_target_pairs={{0,4},{1,5},{2,6},{3,7},{4,0},{5,1},{6,2},{7,3},{8,12},{9,13},{10,... | collective-permute-start | bytes 1572872 | tf_op jit(solution)/shard_map/ppermute | solution.py:22
  6.5 23.5 %collective-permute-start.1 = (bf16[1024,256]{1,0:T(8,128)(2,1)S(1)}, bf16[1024,256]{1,0:T(8,128)(2,1)S(1)}, u32[]{:S(2)}, u32[]{:S(2)}) collective-permute-start(bf16[1024,256]{1,0:T(8,128)(2,1)S(1)} %get-tuple-element.60.refs_0_), channel_id=1, source_target_pairs={{0,2},{1,3},{2,0},{3,1},{4,6},{5,7},{6,4},{7,5},{8,10},{9,11},{10,... | collective-permute-start | bytes 1572872 | tf_op jit(solution)/shard_map/ppermute | solution.py:22
  8.3 23.2 %collective-permute-start.6 = (bf16[1024,256]{1,0:T(8,128)(2,1)S(1)}, bf16[1024,256]{1,0:T(8,128)(2,1)S(1)}, u32[]{:S(2)}, u32[]{:S(2)}) collective-permute-start(bf16[1024,256]{1,0:T(8,128)(2,1)S(1)} %multiply_convert_fusion.2.refs_1_.refs_0_), channel_id=1, source_target_pairs={{0,1},{1,0},{2,3},{3,2},{4,5},{5,4},{6,7},{7,6},{8,9},{9,8},{10,11... | collective-permute-start | bytes 1572872 | tf_op jit(solution)/shard_map/ppermute | solution.py:22
  9.9 26.4 %collective-permute-start.5 = (bf16[1024,256]{1,0:T(8,128)(2,1)S(1)}, bf16[1024,256]{1,0:T(8,128)(2,1)S(1)}, u32[]{:S(2)}, u32[]{:S(2)}) collective-permute-start(bf16[1024,256]{1,0:T(8,128)(2,1)S(1)} %get-tuple-element.60.refs_0_), channel_id=1, source_target_pairs={{0,1},{1,0},{2,3},{3,2},{4,5},{5,4},{6,7},{7,6},{8,9},{9,8},{10,11... | collective-permute-start | bytes 1572872 | tf_op jit(solution)/shard_map/ppermute | solution.py:22
  30.0 21.6 %collective-permute-start.2 = (bf16[1024,256]{1,0:T(8,128)(2,1)S(1)}, bf16[1024,256]{1,0:T(8,128)(2,1)}, u32[]{:S(2)}, u32[]{:S(2)}) collective-permute-start(bf16[1024,256]{1,0:T(8,128)(2,1)S(1)} %collective-permute-done.refs_2_.refs_4_), channel_id=1, source_target_pairs={{0,2},{1,3},{2,0},{3,1},{4,6},{5,7},{6,4},{7,5},{8,10},{9,11},{10,... | collective-permute-start | bytes 1572872 | tf_op jit(solution)/shard_map/ppermute | solution.py:22
  31.5 20.1 %collective-permute-start.7 = (bf16[1024,256]{1,0:T(8,128)(2,1)S(1)}, bf16[1024,256]{1,0:T(8,128)(2,1)S(1)}, u32[]{:S(2)}, u32[]{:S(2)}) collective-permute-start(bf16[1024,256]{1,0:T(8,128)(2,1)S(1)} %collective-permute-done.1.refs_2_), channel_id=1, source_target_pairs={{0,1},{1,0},{2,3},{3,2},{4,5},{5,4},{6,7},{7,6},{8,9},{9,8},{10,11... | collective-permute-start | bytes 1572872 | tf_op jit(solution)/shard_map/ppermute | solution.py:22
  34.0 25.5 %collective-permute-start.4 = (bf16[1024,256]{1,0:T(8,128)(2,1)}, bf16[1024,256]{1,0:T(8,128)(2,1)S(1)}, u32[]{:S(2)}, u32[]{:S(2)}) collective-permute-start(bf16[1024,256]{1,0:T(8,128)(2,1)} %multiply_convert_fusion), channel_id=1, source_target_pairs={{0,4},{1,5},{2,6},{3,7},{4,0},{5,1},{6,2},{7,3},{8,12},{9,13},{10,... | collective-permute-start | bytes 1572872 | tf_op jit(solution)/shard_map/ppermute | solution.py:22
  37.1 22.3 %collective-permute-start.8 = (bf16[1024,256]{1,0:T(8,128)(2,1)S(1)}, bf16[1024,256]{1,0:T(8,128)(2,1)}, u32[]{:S(2)}, u32[]{:S(2)}) collective-permute-start(bf16[1024,256]{1,0:T(8,128)(2,1)S(1)} %collective-permute-done.refs_2_.refs_4_), channel_id=1, source_target_pairs={{0,1},{1,0},{2,3},{3,2},{4,5},{5,4},{6,7},{7,6},{8,9},{9,8},{10,11... | collective-permute-start | bytes 1572872 | tf_op jit(solution)/shard_map/ppermute | solution.py:22
  51.5 14.6 %collective-permute-start.3 = (bf16[1024,256]{1,0:T(8,128)(2,1)S(1)}, bf16[1024,256]{1,0:T(8,128)(2,1)S(1)}, u32[]{:S(2)}, u32[]{:S(2)}) collective-permute-start(bf16[1024,256]{1,0:T(8,128)(2,1)S(1)} %multiply_convert_fusion.2.refs_1_.refs_0_), channel_id=1, source_target_pairs={{0,2},{1,3},{2,0},{3,1},{4,6},{5,7},{6,4},{7,5},{8,10},{9,11},{10,... | collective-permute-start | bytes 1572872 | tf_op jit(solution)/shard_map/ppermute | solution.py:22
  52.3 16.0 %collective-permute-start.9 = (bf16[1024,256]{1,0:T(8,128)(2,1)}, bf16[1024,256]{1,0:T(8,128)(2,1)}, u32[]{:S(2)}, u32[]{:S(2)}) collective-permute-start(bf16[1024,256]{1,0:T(8,128)(2,1)} %collective-permute-done.2.refs_6_), channel_id=1, source_target_pairs={{0,1},{1,0},{2,3},{3,2},{4,5},{5,4},{6,7},{7,6},{8,9},{9,8},{10,11... | collective-permute-start | bytes 1572872 | tf_op jit(solution)/shard_map/ppermute | solution.py:22
  59.4 18.3 %collective-permute-start.13 = (bf16[1024,256]{1,0:T(8,128)(2,1)S(1)}, bf16[1024,256]{1,0:T(8,128)(2,1)S(1)}, u32[]{:S(2)}, u32[]{:S(2)}) collective-permute-start(bf16[1024,256]{1,0:T(8,128)(2,1)S(1)} %collective-permute-done.4.refs_3_.refs_4_), channel_id=1, source_target_pairs={{0,1},{1,0},{2,3},{3,2},{4,5},{5,4},{6,7},{7,6},{8,9},{9,8},{10,11... | collective-permute-start | bytes 1572872 | tf_op jit(solution)/shard_map/ppermute | solution.py:22
  71.3 8.3 %collective-permute-start.11 = (bf16[2,4,128,256]{3,2,1,0:T(8,128)(2,1)S(1)}, bf16[2,4,128,256]{3,2,1,0:T(8,128)(2,1)S(1)}, u32[]{:S(2)}, u32[]{:S(2)}) collective-permute-start(bf16[2,4,128,256]{3,2,1,0:T(8,128)(2,1)S(1)} %get-tuple-element.40), channel_id=1, source_target_pairs={{0,8},{8,0},{16,24},{24,16},{1,9},{9,1},{17,25},{25,17},{2,10},{10... | collective-permute-start | bytes 1572872 | tf_op jit(solution)/shard_map/ppermute | solution.py:22
  74.4 7.0 %collective-permute-start.10 = (bf16[2,4,128,256]{3,2,1,0:T(8,128)(2,1)S(1)}, bf16[2,4,128,256]{3,2,1,0:T(8,128)(2,1)S(1)}, u32[]{:S(2)}, u32[]{:S(2)}) collective-permute-start(bf16[2,4,128,256]{3,2,1,0:T(8,128)(2,1)S(1)} %get-tuple-element.43), channel_id=1, source_target_pairs={{0,8},{8,0},{16,24},{24,16},{1,9},{9,1},{17,25},{25,17},{2,10},{10... | collective-permute-start | bytes 1572872 | tf_op jit(solution)/shard_map/ppermute | solution.py:22
  77.7 12.2 %collective-permute-start.14 = (bf16[1024,256]{1,0:T(8,128)(2,1)S(1)}, bf16[1024,256]{1,0:T(8,128)(2,1)S(1)}, u32[]{:S(2)}, u32[]{:S(2)}) collective-permute-start(bf16[1024,256]{1,0:T(8,128)(2,1)S(1)} %collective-permute-done.3.refs_2_), channel_id=1, source_target_pairs={{0,1},{1,0},{2,3},{3,2},{4,5},{5,4},{6,7},{7,6},{8,9},{9,8},{10,11... | collective-permute-start | bytes 1572872 | tf_op jit(solution)/shard_map/ppermute | solution.py:22
  79.2 17.5 %collective-permute-start.17 = (bf16[1024,256]{1,0:T(8,128)(2,1)S(1)}, bf16[1024,256]{1,0:T(8,128)(2,1)S(1)}, u32[]{:S(2)}, u32[]{:S(2)}) collective-permute-start(bf16[1024,256]{1,0:T(8,128)(2,1)S(1)} %collective-permute-done.4.refs_3_.refs_4_), channel_id=1, source_target_pairs={{0,2},{1,3},{2,0},{3,1},{4,6},{5,7},{6,4},{7,5},{8,10},{9,11},{10,... | collective-permute-start | bytes 1572872 | tf_op jit(solution)/shard_map/ppermute | solution.py:22
  79.7 6.6 %collective-permute-start.12 = (bf16[1,4,128,256]{3,2,1,0:T(8,128)(2,1)S(1)}, bf16[1,4,128,256]{3,2,1,0:T(8,128)(2,1)S(1)}, u32[]{:S(2)}, u32[]{:S(2)}) collective-permute-start(bf16[1,4,128,256]{3,2,1,0:T(8,128)(2,1)S(1)} %slice.72), channel_id=1, source_target_pairs={{0,16},{8,24},{16,0},{24,8},{1,17},{9,25},{17,1},{25,9},{2,18},{10... | collective-permute-start | bytes 786440 | tf_op jit(solution)/shard_map/ppermute | solution.py:22
  86.4 10.6 %collective-permute-start.16 = (bf16[4,128,256]{2,1,0:T(8,128)(2,1)S(1)}, bf16[4,128,256]{2,1,0:T(8,128)(2,1)S(1)}, u32[]{:S(2)}, u32[]{:S(2)}) collective-permute-start(bf16[4,128,256]{2,1,0:T(8,128)(2,1)S(1)} %fusion.3), channel_id=1, source_target_pairs={{0,4},{1,5},{2,6},{3,7},{4,0},{5,1},{6,2},{7,3},{8,12},{9,13},{10,... | collective-permute-start | bytes 786440 | tf_op jit(solution)/shard_map/ppermute | solution.py:22
  89.9 7.1 %collective-permute-start.15 = (bf16[1,4,128,256]{3,2,1,0:T(8,128)(2,1)S(1)}, bf16[1,4,128,256]{3,2,1,0:T(8,128)(2,1)S(1)}, u32[]{:S(2)}, u32[]{:S(2)}) collective-permute-start(bf16[1,4,128,256]{3,2,1,0:T(8,128)(2,1)S(1)} %slice.73), channel_id=1, source_target_pairs={{0,16},{8,24},{16,0},{24,8},{1,17},{9,25},{17,1},{25,9},{2,18},{10... | collective-permute-start | bytes 786440 | tf_op jit(solution)/shard_map/ppermute | solution.py:22
  96.7 9.2 %collective-permute-start.18 = (bf16[1024,256]{1,0:T(8,128)(2,1)S(1)}, bf16[1024,256]{1,0:T(8,128)(2,1)S(1)}, u32[]{:S(2)}, u32[]{:S(2)}) collective-permute-start(bf16[1024,256]{1,0:T(8,128)(2,1)S(1)} %collective-permute-done.17.refs_6_), channel_id=1, source_target_pairs={{0,1},{1,0},{2,3},{3,2},{4,5},{5,4},{6,7},{7,6},{8,9},{9,8},{10,11... | collective-permute-start | bytes 1572872 | tf_op jit(solution)/shard_map/ppermute | solution.py:22
  108.0 2.8 %collective-permute-start.20 = (bf16[2,4,128,256]{3,2,1,0:T(8,128)(2,1)S(1)}, bf16[2,4,128,256]{3,2,1,0:T(8,128)(2,1)S(1)}, u32[]{:S(2)}, u32[]{:S(2)}) collective-permute-start(bf16[2,4,128,256]{3,2,1,0:T(8,128)(2,1)S(1)} %get-tuple-element.51), channel_id=1, source_target_pairs={{0,8},{8,0},{16,24},{24,16},{1,9},{9,1},{17,25},{25,17},{2,10},{10... | collective-permute-start | bytes 1572872 | tf_op jit(solution)/shard_map/ppermute | solution.py:22
  110.2 2.3 %collective-permute-start.19 = (bf16[2,4,128,256]{3,2,1,0:T(8,128)(2,1)S(1)}, bf16[2,4,128,256]{3,2,1,0:T(8,128)(2,1)S(1)}, u32[]{:S(2)}, u32[]{:S(2)}) collective-permute-start(bf16[2,4,128,256]{3,2,1,0:T(8,128)(2,1)S(1)} %get-tuple-element.54), channel_id=1, source_target_pairs={{0,8},{8,0},{16,24},{24,16},{1,9},{9,1},{17,25},{25,17},{2,10},{10... | collective-permute-start | bytes 1572872 | tf_op jit(solution)/shard_map/ppermute | solution.py:22
  111.0 8.3 %collective-permute-start.21 = (bf16[1,4,128,256]{3,2,1,0:T(8,128)(2,1)S(1)}, bf16[1,4,128,256]{3,2,1,0:T(8,128)(2,1)S(1)}, u32[]{:S(2)}, u32[]{:S(2)}) collective-permute-start(bf16[1,4,128,256]{3,2,1,0:T(8,128)(2,1)S(1)} %slice.70), channel_id=1, source_target_pairs={{0,16},{8,24},{16,0},{24,8},{1,17},{9,25},{17,1},{25,9},{2,18},{10... | collective-permute-start | bytes 786440 | tf_op jit(solution)/shard_map/ppermute | solution.py:22
  119.3 13.1 %collective-permute-start.23 = (bf16[4,128,256]{2,1,0:T(8,128)(2,1)S(1)}, bf16[4,128,256]{2,1,0:T(8,128)(2,1)S(1)}, u32[]{:S(2)}, u32[]{:S(2)}) collective-permute-start(bf16[4,128,256]{2,1,0:T(8,128)(2,1)S(1)} %fusion), channel_id=1, source_target_pairs={{0,4},{1,5},{2,6},{3,7},{4,0},{5,1},{6,2},{7,3},{8,12},{9,13},{10,... | collective-permute-start | bytes 786440 | tf_op jit(solution)/shard_map/ppermute | solution.py:22
  120.7 11.8 %collective-permute-start.22 = (bf16[1,4,128,256]{3,2,1,0:T(8,128)(2,1)S(1)}, bf16[1,4,128,256]{3,2,1,0:T(8,128)(2,1)S(1)}, u32[]{:S(2)}, u32[]{:S(2)}) collective-permute-start(bf16[1,4,128,256]{3,2,1,0:T(8,128)(2,1)S(1)} %slice.71), channel_id=1, source_target_pairs={{0,16},{8,24},{16,0},{24,8},{1,17},{9,25},{17,1},{25,9},{2,18},{10... | collective-permute-start | bytes 786440 | tf_op jit(solution)/shard_map/ppermute | solution.py:22
  (8 other events, 125.4 us)
